TPU v7x, 512 devices: a whole 4x8x8 slice. The times are simulated.
512 devices in a mesh: ctx: 64 (over z_hi, y, x), tp: 8 (over z_lo, core).
Axes of the slice: x: 4, y: 8, z: 8 (z_hi: 2, z_lo: 4; z = z_hi * 4 + z_lo), core: 2. Of those that a mesh axis runs over, the one named last changes fastest.
Arguments:
- hidden_in: bfloat16 [10240, 2048], P('ctx'), may hold values from -8 to 8
- norm_gain: float32 [2048], replicated, may hold values from 0.1 to 1.9
- snap_qkv: bfloat16 [64, 3, 2048, 2048], P('ctx', None, None, 'tp'), may hold values from -1 to 1
- snap_out: bfloat16 [64, 2048, 2048], P('ctx', 'tp'), may hold values from -0.125 to 0.125
- owner_index: int32 [1], replicated, may hold values from 0 to 63
- block_order: int32 [64], replicated, may hold values from 0 to 63, each once
Outputs:
- attention_out: bfloat16 [10240, 2048], P('ctx', 'tp')
Inputs may be any that keep to these rules, and one draw needn't show every extreme that they name: `block_order`: each block appears once.
All inputs are finite; a program needn't handle non-finite values.
Results may differ from a plain program's by a relative error of at most 0.02.
Values may be sent and summed in bfloat16 or wider, within the bound.
No kernel may reach another device: no remote copies, remote signals or barrier semaphores. Data moves between devices by JAX's collectives and lax.ppermute only.
A program may use at most 128 MiB of HBM per device.

v0:
```python
import jax
import jax.numpy as jnp
from jax import lax
from jax.sharding import PartitionSpec as P

HD = 128


def from_root(block, axis, holder):
    block = jnp.where(lax.axis_index(axis) == holder, block, jnp.zeros_like(block))
    return lax.psum(block, axis)


def shifted(block, axis, distance):
    devices = range(lax.axis_size(axis))
    route = [((i - distance) % len(devices), i) for i in devices]
    return lax.ppermute(block, axis, route)


def attend(state_in, queries, pair, query_pos, key_pos):
    row_max, totals, weighted = state_in
    count_rows = pair.shape[1]
    head_count = queries.shape[1]
    head_size = queries.shape[2]
    keys = pair[0].reshape(count_rows, head_count, head_size)
    values = pair[1].reshape(count_rows, head_count, head_size)
    scores = jnp.einsum("thd,shd->ths", queries, keys, preferred_element_type=jnp.float32) * (
        1.0 / head_size**0.5
    )
    allowed = key_pos[None, None, :] <= query_pos[:, None, None]
    scores = jnp.where(allowed, scores, -1e30)
    new_max = jnp.maximum(row_max, jnp.max(scores, axis=-1))
    factor = jnp.exp(row_max - new_max)
    weights = jnp.where(allowed, jnp.exp(scores - new_max[..., None]), 0.0)
    totals = totals * factor + jnp.sum(weights, axis=-1)
    weighted = weighted * factor[..., None] + jnp.einsum(
        "ths,shd->thd", weights.astype(jnp.bfloat16), values, preferred_element_type=jnp.float32
    )
    return (new_max, totals, weighted)


def shards(hidden_in, norm_gain, snap_qkv, snap_out, owner_index, block_order):
    rows = hidden_in.shape[0]
    local_cols = snap_qkv.shape[3]
    head_size = HD
    head_count = local_cols // head_size
    widened = hidden_in.astype(jnp.float32)
    normed = (
        widened * lax.rsqrt(jnp.mean(widened * widened, axis=-1, keepdims=True) + 1e-06) * norm_gain
    ).astype(jnp.bfloat16)
    qkv_slot, out_slot = (
        from_root(snap_qkv, "ctx", owner_index[0]),
        from_root(snap_out, "ctx", owner_index[0]),
    )
    projected = jnp.einsum(
        "td,jdc->jtc", normed, qkv_slot[0], preferred_element_type=jnp.float32
    ).astype(jnp.bfloat16)
    queries = projected[0].reshape(rows, head_count, head_size)
    pair = projected[1:]
    here = lax.axis_index("ctx")
    count = lax.axis_size("ctx")
    offsets = jnp.arange(rows, dtype=jnp.int32)
    my_block = block_order[here]
    query_pos = my_block * rows + offsets
    initial = (
        jnp.full((rows, head_count), -1e30, jnp.float32),
        jnp.zeros((rows, head_count), jnp.float32),
        jnp.zeros((rows, head_count, head_size), jnp.float32),
    )
    state = attend(initial, queries, pair, query_pos, query_pos)

    def rotate(turn_index, packed):
        moving, state_in = packed
        moving = shifted(moving, "ctx", 1)
        source = (here - turn_index) % count
        their_block = block_order[source]
        key_pos = their_block * rows + offsets
        state_out = lax.cond(
            their_block <= my_block,
            lambda held: attend(held, queries, moving, query_pos, key_pos),
            lambda held: held,
            state_in,
        )
        return (moving, state_out)

    moving_end, state = lax.fori_loop(1, count, rotate, (pair, state))
    row_max, totals, weighted = state
    context = (weighted / totals[..., None]).astype(jnp.bfloat16).reshape(rows, local_cols)
    terms = jnp.dot(context, out_slot[0], preferred_element_type=jnp.float32)
    return lax.psum_scatter(terms.astype(jnp.bfloat16), "tp", scatter_dimension=1, tiled=True)


def solution(mesh):
    in_specs = (P("ctx", None), P(), P("ctx", None, None, "tp"), P("ctx", "tp", None), P(), P())
    out_specs = P("ctx", "tp")
    return jax.shard_map(shards, mesh=mesh, in_specs=in_specs, out_specs=out_specs, check_vma=False)
```

profile of v0, /device:TPU:1, one launch (start us, length us, event | category | flops | bytes accessed | tf_op | source)
XLA Modules:
  0.0 2027.5 jit_solution(10455677318684447342)
XLA Ops:
  12.2 819.4 %all-reduce.3.cloned.1.call-done = (bf16[256,2048]{1,0:T(8,128)(2,1)}, bf16[3,2048,256]{2,1,0:T(8,128)(2,1)}) async-done(((bf16[256,2048]{1,0:T(8,128)(2,1)}, bf16[3,2048,256]{2,1,0:T(8,128)(2,1)}), (bf16[256,2048]{1,0:T(8,128)(2,1)}, bf16[3,2048,256]{2,1,0:T(8,128)(2,1)})) %all-reduce.3.cloned.1.call-update) | async-done | bytes 4194320 | tf_op jit(solution)/shard_map/psum | solution.py:11
  835.0 1035.9 %while.22 = (s32[]{:T(128)}, bf16[2,160,256]{2,1,0:T(8,128)(2,1)S(1)}, f32[160,2]{0,1:T(2,128)S(1)}, f32[160,2]{0,1:T(2,128)S(1)}, f32[160,2,128]{2,0,1:T(8,128)...) while((s32[]{:T(128)}, ...), condition=%wide.region_9.10_spmd.clone, body=%wide.region_4.9_spmd.clone.sunk | while | flops 26783700 | bytes 2954102 | solution.py:86
  855.8 11.7 collective-permute-done
  872.8 11.3 collective-permute-done
  887.9 12.1 collective-permute-done
  903.9 14.0 collective-permute-done
  921.7 12.4 collective-permute-done
  937.9 11.6 collective-permute-done
  1060.6 12.0 collective-permute-done
  1077.9 12.0 collective-permute-done
  1093.7 11.0 collective-permute-done
  1108.5 12.0 collective-permute-done
  1124.4 13.2 collective-permute-done
  1142.9 12.3 collective-permute-done
  1160.6 12.5 collective-permute-done
  1178.3 12.8 collective-permute-done
  1195.0 12.1 collective-permute-done
  1210.9 10.9 collective-permute-done
  1227.1 10.9 collective-permute-done
  1290.5 11.7 collective-permute-done
  1307.4 12.0 collective-permute-done
  1324.7 13.3 collective-permute-done
  1341.9 15.2 collective-permute-done
  1362.5 13.9 collective-permute-done
  1380.2 12.5 collective-permute-done
  1396.5 11.5 collective-permute-done
  1411.9 11.6 collective-permute-done
  1427.3 12.1 collective-permute-done
  1443.2 11.4 collective-permute-done
  1460.0 11.9 collective-permute-done
  1477.2 11.9 collective-permute-done
  1494.4 11.0 collective-permute-done
  1555.3 12.0 collective-permute-done
  1588.8 11.4 collective-permute-done
  1604.0 14.1 collective-permute-done
  1622.0 11.7 collective-permute-done
  1637.5 12.3 collective-permute-done
  1653.7 12.4 collective-permute-done
  1671.4 12.0 collective-permute-done
  1688.8 11.0 collective-permute-done
  1750.7 12.1 collective-permute-done
  1768.2 12.1 collective-permute-done
  1784.1 11.4 collective-permute-done
  1800.8 11.8 collective-permute-done
  1817.9 12.6 collective-permute-done
  1835.9 13.8 collective-permute-done
  1855.0 14.5 collective-permute-done
  1872.2 148.4 %reduce-scatter.2.cloned.1.call-done = bf16[160,256]{1,0:T(8,128)(2,1)} async-done(((bf16[160,2048]{1,0:T(8,128)(2,1)}), bf16[160,256]{1,0:T(8,128)(2,1)}) %reduce-scatter.2.cloned.1.call-update) | async-done | bytes 81936 | tf_op jit(solution)/shard_map/reduce_scatter | solution.py:90
  (761 shorter events, 444.2 us)
Async XLA Ops:
  6.5 825.1 %all-reduce.3.cloned.1.call-start = ((), (), s32[]{:S(2)}) async-start(), calls=%async_computation.2 | async-start | bytes 8388608 | tf_op jit(solution)/shard_map/psum | solution.py:11
  10.2 2010.5 %reduce-scatter.2.cloned.1.call-start = ((), (), s32[]{:S(2)}) async-start(), calls=%async_computation.1 | async-start | bytes 737280 | tf_op jit(solution)/shard_map/reduce_scatter | solution.py:90
  835.1 15.4 collective-permute-start
  852.0 15.5 collective-permute-start
  869.0 15.1 collective-permute-start
  884.1 15.9 collective-permute-start
  900.1 17.8 collective-permute-start
  917.9 16.2 collective-permute-start
  934.1 15.4 collective-permute-start
  1056.8 15.8 collective-permute-start
  1074.1 15.8 collective-permute-start
  1089.9 14.8 collective-permute-start
  1104.7 15.8 collective-permute-start
  1120.6 17.0 collective-permute-start
  1139.1 16.1 collective-permute-start
  1156.8 16.3 collective-permute-start
  1174.5 16.6 collective-permute-start
  1191.2 15.9 collective-permute-start
  1207.1 14.7 collective-permute-start
  1223.3 14.7 collective-permute-start
  1286.7 15.5 collective-permute-start
  1303.7 15.8 collective-permute-start
  1320.9 17.1 collective-permute-start
  1338.1 19.0 collective-permute-start
  1358.7 17.7 collective-permute-start
  1376.4 16.3 collective-permute-start
  1392.7 15.3 collective-permute-start
  1408.1 15.4 collective-permute-start
  1423.5 15.9 collective-permute-start
  1439.4 15.2 collective-permute-start
  1456.2 15.7 collective-permute-start
  1473.4 15.7 collective-permute-start
  1490.6 14.8 collective-permute-start
  1551.5 15.8 collective-permute-start
  1585.0 15.2 collective-permute-start
  1600.2 17.9 collective-permute-start
  1618.2 15.5 collective-permute-start
  1633.7 16.1 collective-permute-start
  1649.9 16.2 collective-permute-start
  1667.6 15.8 collective-permute-start
  1685.0 14.8 collective-permute-start
  1747.0 15.9 collective-permute-start
  1764.4 15.9 collective-permute-start
  1780.3 15.2 collective-permute-start
  1797.0 15.6 collective-permute-start
  1814.1 16.4 collective-permute-start
  1832.1 17.6 collective-permute-start
  1851.2 18.3 collective-permute-start
  (21 other events, 2103.7 us)
Sparse Core Ops, SparseCore 0:
  10.3 821.2 all-reduce.2
  1872.4 148.2 reduce-scatter.1
where the time goes:
time: 2030 us
  waiting for transfers between devices  1710 us (84%)
  starting transfers between devices  122 us (6%)
  loops' own time  104 us (5%)
  local copies, waits for them, and re-layouts  45.7 us (2%)
  matrix products  22.4 us (1%)
    psum x1, waiting for transfers between devices, from_root(): return lax.psum(block, axis)  819 us
    ppermute x63, waiting for transfers between devices, shifted(): return lax.ppermute(block, axis, route)  740 us
    reduce_scatter x1, waiting for transfers between devices, shards(): lax.psum_scatter(terms.astype(jnp.bfloat16), 'tp', scatter_dimension=1, t...  148 us
    ppermute x63, starting transfers between devices, shifted(): return lax.ppermute(block, axis, route)  122 us
    another operation x1, loops' own time, shards(): moving_end, state = lax.fori_loop(1, count, rotate, (pair, state))  78.5 us
    dynamic_slice x63, local copies, waits for them, and re-layouts, rotate(): their_block = block_order[source]  41.3 us
  transfers between devices with their start and end apart: 65, of which 65 were waited for; matrix products, arithmetic and copies ran while one was open for 2% of the time, Pallas kernels for 0%

commit v1 on v0

v1 whole, which is shorter than its diff:
```python
import jax
import jax.numpy as jnp
import numpy as np
from jax import lax
from jax.experimental import pallas as pl
from jax.experimental.pallas import tpu as pltpu
from jax.sharding import Mesh
from jax.sharding import PartitionSpec as P

HD = 128
HIDE = -1e30
TILE = 160
CHUNK = 640


def attend_kernel(q_ref, kv_ref, qpos_ref, kpos_ref, o_ref, stat_ref, s_ref):
    factor = float(np.log2(np.e) / HD**0.5)
    rows = q_ref.shape[0]
    count = kv_ref.shape[0] // CHUNK
    q = q_ref[...]
    qpos = qpos_ref[...]
    high = jnp.full((rows, HD), HIDE, jnp.float32)
    for j in range(count):
        span = pl.ds(j * CHUNK, CHUNK)
        s = lax.dot_general(
            q, kv_ref[span, :HD], (((1,), (1,)), ((), ())), preferred_element_type=jnp.float32
        )
        s = jnp.where(kpos_ref[:, span] <= qpos, s * factor, HIDE)
        s_ref[:, span] = s
        for t in range(CHUNK // HD):
            high = jnp.maximum(high, s[:, t * HD : (t + 1) * HD])
    top = jnp.max(high, axis=1, keepdims=True)
    base = jnp.where(top <= 0.5 * HIDE, 0.0, top)
    total = jnp.zeros((rows, HD), jnp.float32)
    acc = jnp.zeros((rows, HD), jnp.float32)
    for j in range(count):
        span = pl.ds(j * CHUNK, CHUNK)
        p = jnp.exp2(s_ref[:, span] - base)
        for t in range(CHUNK // HD):
            total = total + p[:, t * HD : (t + 1) * HD]
        acc = acc + jnp.dot(
            p.astype(jnp.bfloat16), kv_ref[span, HD:], preferred_element_type=jnp.float32
        )
    total = jnp.sum(total, axis=1, keepdims=True)
    o_ref[...] = acc / jnp.where(total == 0.0, 1.0, total)
    lane = lax.broadcasted_iota(jnp.int32, (rows, HD), 1)
    stat_ref[...] = jnp.where(lane == 0, top, total)


def attend(q, kv, qpos, kpos):
    nq, nk = q.shape[0], kv.shape[0]
    return pl.pallas_call(
        attend_kernel,
        grid=(nq // TILE,),
        in_specs=[
            pl.BlockSpec((TILE, HD), lambda i: (i, 0)),
            pl.BlockSpec((nk, 2 * HD), lambda i: (0, 0)),
            pl.BlockSpec((TILE, 1), lambda i: (i, 0)),
            pl.BlockSpec((1, nk), lambda i: (0, 0)),
        ],
        out_specs=[
            pl.BlockSpec((TILE, HD), lambda i: (i, 0)),
            pl.BlockSpec((TILE, HD), lambda i: (i, 0)),
        ],
        out_shape=[
            jax.ShapeDtypeStruct((nq, HD), jnp.float32),
            jax.ShapeDtypeStruct((nq, HD), jnp.float32),
        ],
        scratch_shapes=[pltpu.VMEM((TILE, nk), jnp.float32)],
        compiler_params=pltpu.CompilerParams(vmem_limit_bytes=48 * 1024 * 1024),
        cost_estimate=pl.CostEstimate(
            flops=4 * nq * nk * HD, bytes_accessed=nk * HD * 4, transcendentals=nq * nk
        ),
    )(q, kv, qpos, kpos)


def swap(block, axis):
    return lax.ppermute(block, axis, [(0, 1), (1, 0)])


def exchange(block, axis):
    return lax.all_to_all(block, axis, 0, 0, tiled=True)


def pick(blocks, index):
    return lax.dynamic_index_in_dim(blocks, index, 0, keepdims=False)


def shards(hidden_in, norm_gain, snap_qkv, snap_out, owner_index, block_order):
    rows, width = hidden_in.shape
    zh, y, x, c = (lax.axis_index(name) for name in ("zh", "y", "x", "c"))
    ny, nx, nl = 8, 4, 4
    half = rows // 2
    owner = owner_index[0]
    zh0, y0, x0 = owner // (ny * nx), (owner // nx) % ny, owner % nx

    part = width // (2 * ny)
    w = snap_qkv[0].reshape(3, ny, 2, part, 2, HD)
    w = jnp.transpose(w, (2, 4, 1, 3, 0, 5)).reshape(2, 2, ny, part, 3 * HD)
    w = exchange(w, "c").reshape(nx, ny, part, 3 * HD)
    w = pick(exchange(w, "x"), x0)
    w = pick(exchange(w, "y"), y0)
    w = jnp.where(zh == zh0, w, swap(w, "zh"))
    w, snap_out = lax.optimization_barrier((w, snap_out))
    w = lax.all_gather(w, ("y", "c"), axis=0, tiled=True)
    w = w.reshape(width, 3 * HD)

    mine = lax.dynamic_slice_in_dim(hidden_in, c * half, half, 0).astype(jnp.float32)
    normed = (
        mine * lax.rsqrt(jnp.mean(mine * mine, axis=-1, keepdims=True) + 1e-06) * norm_gain
    ).astype(jnp.bfloat16)
    normed = lax.all_gather(normed, "x", axis=0, tiled=True)

    qkv = jnp.dot(normed, w, preferred_element_type=jnp.float32).astype(jnp.bfloat16)
    q, kv = qkv[:, :HD], qkv[:, HD:]
    q_other = swap(q, "zh")
    kv = lax.all_gather(kv, ("y", "c"), axis=0, tiled=True)

    order = block_order.reshape(2, ny, nx) * rows
    offsets = jnp.arange(half, dtype=jnp.int32)
    halves = jnp.arange(2, dtype=jnp.int32) * half
    kpos = pick(order, zh)[:, None, :, None] + halves[None, :, None, None] + offsets
    here = lax.dynamic_index_in_dim(order, y, 1, keepdims=False)
    here = jnp.stack([pick(here, zh), pick(here, 1 - zh)])
    qpos = here[:, :, None] + c * half + offsets

    cols = snap_out.shape[2] // nx
    wo = snap_out[0].reshape(ny, -1, nx, cols)
    wo = jnp.transpose(wo, (2, 0, 1, 3))
    wo = pick(exchange(wo, "x"), x0)
    wo = pick(exchange(wo, "y"), y0)
    wo = jnp.where(zh == zh0, wo, swap(wo, "zh"))
    wo = lax.all_gather(wo, ("c", "y"), axis=0, tiled=True)
    wo = lax.all_gather(wo, "x", axis=0, tiled=False)

    o, stat = attend(
        jnp.concatenate([q, q_other]), kv, qpos.reshape(-1, 1), kpos.reshape(1, -1)
    )
    n = q.shape[0]
    m, t = stat[:, 0], stat[:, 1]
    o_in = swap(o[n:].astype(jnp.bfloat16), "zh").astype(jnp.float32)
    stat_in = swap(jnp.stack([m[n:], t[n:]]), "zh")
    m_all = jnp.maximum(m[:n], stat_in[0])
    a = t[:n] * jnp.exp2(m[:n] - m_all)
    b = stat_in[1] * jnp.exp2(stat_in[0] - m_all)
    context = (o[:n] * (a / (a + b))[:, None] + o_in * (b / (a + b))[:, None]).astype(jnp.bfloat16)

    context = exchange(context.reshape(nx, half, HD), "x")
    context = jnp.transpose(context, (1, 0, 2)).reshape(half, nx * HD)
    terms = jnp.einsum("tk,nkc->ntc", context, wo.reshape(nl, -1, cols), preferred_element_type=jnp.float32)
    terms = exchange(terms.astype(jnp.bfloat16), "zl")
    out = jnp.sum(terms.astype(jnp.float32), axis=0).astype(jnp.bfloat16)
    out = jnp.transpose(out.reshape(half, 2, -1), (1, 0, 2))
    return exchange(out, "c").reshape(rows, -1)


def solution(mesh):
    fine = Mesh(mesh.devices.reshape(2, 8, 4, 4, 2), ("zh", "y", "x", "zl", "c"))
    ctx, tp = ("zh", "y", "x"), ("zl", "c")
    in_specs = (P(ctx, None), P(), P(ctx, None, None, tp), P(ctx, tp, None), P(), P())
    return jax.shard_map(shards, mesh=fine, in_specs=in_specs, out_specs=P(ctx, tp), check_vma=False)
```

time: 2030 us -> 320 us (0.16)
  waiting for transfers between devices: 1710 us -> 120 us
  blocking collectives: 0 us -> 109 us
  loops' own time: 104 us -> 0 us
  starting transfers between devices: 122 us -> 39.8 us
  local copies, waits for them, and re-layouts: 45.7 us -> 18.9 us
    psum x1 -> x0, waiting for transfers between devices: 819 us -> none  [from_root(): return lax.psum(block, axis)]
    ppermute x63 -> x5, waiting for transfers between devices: 740 us -> 12.4 us  [swap(): return lax.ppermute(block, axis, [(0, 1), (1, 0)])]
    reduce_scatter x1 -> x0, waiting for transfers between devices: 148 us -> none  [shards(): lax.psum_scatter(terms.astype(jnp.bfloat16), 'tp', scatter_dimension=1, t...]
    another operation x64 -> x0, loops' own time: 104 us -> none  [the longest x1 78.5 us: shards(): moving_end, state = lax.fori_loop(1, count, rotate, (pair, state))]
    ppermute x63 -> x5, starting transfers between devices: 122 us -> 32.3 us  [swap(): return lax.ppermute(block, axis, [(0, 1), (1, 0)])]
    all_to_all x0 -> x6, blocking collectives: none -> 76.2 us  [exchange(): return lax.all_to_all(block, axis, 0, 0, tiled=True)]
    all_to_all x0 -> x2, waiting for transfers between devices: none -> 67.4 us  [exchange(): return lax.all_to_all(block, axis, 0, 0, tiled=True)]
    dynamic_slice x64 -> x0, local copies, waits for them, and re-layouts: 41.8 us -> none  [the longest x63 41.3 us: rotate(): their_block = block_order[source]]
  transfers between devices with their start and end apart: 65 -> 11, of which waited for: 65 -> 7; matrix products, arithmetic and copies ran while one was open for 2% -> 2% of each run, Pallas kernels for 0% -> 2%
where the time goes in v1:
time: 320 us; the launch traced here: 319 us
  waiting for transfers between devices  120 us (38%)
  blocking collectives  109 us (34%)
  starting transfers between devices  39.8 us (12%)
  local copies, waits for them, and re-layouts  18.9 us (6%)
  between operations  14.3 us (4%)
  Pallas kernels  7.25 us (2%)
  matrix products  4.74 us (1%)
  other arithmetic  4.41 us (1%)
    all_to_all x6, blocking collectives, exchange(): return lax.all_to_all(block, axis, 0, 0, tiled=True)  76.2 us
    all_to_all x2, waiting for transfers between devices, exchange(): return lax.all_to_all(block, axis, 0, 0, tiled=True)  67.4 us
    all_gather x1, waiting for transfers between devices, shards(): w = lax.all_gather(w, ('y', 'c'), axis=0, tiled=True)  40.1 us
    all_gather x1, blocking collectives, shards(): wo = lax.all_gather(wo, ('c', 'y'), axis=0, tiled=True)  33 us
    ppermute x5, starting transfers between devices, swap(): return lax.ppermute(block, axis, [(0, 1), (1, 0)])  32.3 us
    ppermute x5, waiting for transfers between devices, swap(): return lax.ppermute(block, axis, [(0, 1), (1, 0)])  12.4 us
    all_to_all x2, starting transfers between devices, exchange(): return lax.all_to_all(block, axis, 0, 0, tiled=True)  7.38 us
    transpose x1, local copies, waits for them, and re-layouts, shards(): w = jnp.transpose(w, (2, 4, 1, 3, 0, 5)).reshape(2, 2, ny, part, 3 * HD)  7.3 us
  transfers between devices with their start and end apart: 11, of which 7 were waited for; matrix products, arithmetic and copies ran while one was open for 2% of the time, Pallas kernels for 2%

profile of v1, /device:TPU:1, one launch (start us, length us, event | category | flops | bytes accessed | tf_op | source)
XLA Modules:
  0.0 318.6 jit_solution(14926186506688679453)
XLA Ops:
  6.5 5.5 %reshape_squeeze.6 = bf16[3,8,2,128,2,128]{5,4,3,2,1,0:T(2,128)(2,1)} reshape(bf16[1,3,2048,256]{3,2,1,0:T(8,128)(2,1)} %param.8) | data formatting | bytes 6291456 | tf_op jit(solution)/shard_map/reshape;squeeze | solution.py:98
  12.1 7.3 %copy.36 = bf16[2,2,8,128,3,128]{3,5,4,2,1,0:T(8,128)(2,1)S(1)} copy(bf16[2,2,8,128,3,128]{5,1,3,0,2,4:T(2,128)(2,1)} %bitcast.45) | data formatting | bytes 6291456 | tf_op jit(solution)/shard_map/transpose | solution.py:99
  19.4 13.7 %all_to_all.40 = bf16[2,2,8,128,384]{3,4,2,1,0:T(8,128)(2,1)} all-to-all(bf16[2,2,8,128,384]{3,4,2,1,0:T(8,128)(2,1)S(1)} %bitcast.44), channel_id=1, replica_groups=mesh['zh'=2,'y'=8,'x'=4,'zl'=4,'c'=2] {'c'}, dimensions={0} | all-to-all | bytes 6291456 | tf_op jit(solution)/shard_map/all_to_all | solution.py:82
  33.1 3.8 %all-to-all-start.1 = ((bf16[4,8,128,384]{2,3,1,0:T(8,128)(2,1)}), bf16[4,8,128,384]{2,3,1,0:T(8,128)(2,1)S(1)}, u32[]{:S(2)}, u32[]{:S(2)}) async-start(bf16[4,8,128,384]{2,3,1,0:T(8,128)(2,1)} %bitcast.3), calls=%async_computation.1 | async-start | bytes 6291456 | tf_op jit(solution)/shard_map/all_to_all | solution.py:82
  37.0 1.1 fusion.1
  38.2 1.9 fusion.3
  40.7 44.0 %all-to-all-done.1 = bf16[4,8,128,384]{2,3,1,0:T(8,128)(2,1)S(1)} async-done(((bf16[4,8,128,384]{2,3,1,0:T(8,128)(2,1)}), bf16[4,8,128,384]{2,3,1,0:T(8,128)(2,1)S(1)}, u32[]{:S(2)}, u32[]{:S(2)}) %all-to-all-start.1) | async-done | bytes 3145760 | tf_op jit(solution)/shard_map/all_to_all | solution.py:82
  84.8 0.9 dynamic-slice_bitcast_fusion
  85.7 3.5 %all-to-all-start.2 = ((bf16[8,128,384]{1,2,0:T(8,128)(2,1)}), bf16[8,128,384]{1,2,0:T(8,128)(2,1)S(1)}, u32[]{:S(2)}, u32[]{:S(2)}) async-start(bf16[8,128,384]{1,2,0:T(8,128)(2,1)} %dynamic-slice_bitcast_fusion), calls=%async_computation.2 | async-start | bytes 1572864 | tf_op jit(solution)/shard_map/all_to_all | solution.py:82
  89.3 0.0 all-gather.8.cloned.1.call-start
  89.4 23.4 %all-to-all-done.2 = bf16[8,128,384]{1,2,0:T(8,128)(2,1)S(1)} async-done(((bf16[8,128,384]{1,2,0:T(8,128)(2,1)}), bf16[8,128,384]{1,2,0:T(8,128)(2,1)S(1)}, u32[]{:S(2)}, u32[]{:S(2)}) %all-to-all-start.2) | async-done | bytes 786464 | tf_op jit(solution)/shard_map/all_to_all | solution.py:82
  112.8 7.4 %collective-permute-start = (bf16[128,384]{0,1:T(8,128)(2,1)S(1)}, bf16[128,384]{0,1:T(8,128)(2,1)S(1)}, u32[]{:S(2)}, u32[]{:S(2)}) collective-permute-start(bf16[128,384]{0,1:T(8,128)(2,1)S(1)} %dynamic-slice_bitcast_fusion.2), channel_id=1, source_target_pairs={{0,256},{256,0},{1,257},{257,1},{2,258},{258,2},{3,259},{259,3},{4... | collective-permute-start | bytes 294920 | tf_op jit(solution)/shard_map/ppermute | solution.py:78
  120.2 2.1 collective-permute-done
  122.3 0.7 broadcast_select_fusion
  123.0 0.0 all-gather.10.cloned.1.call-start
  123.1 40.1 %all-gather.8.cloned.1.call-done = bf16[2048,384]{0,1:T(8,128)(2,1)} async-done(((bf16[128,384]{0,1:T(8,128)(2,1)}), bf16[2048,384]{0,1:T(8,128)(2,1)}) %all-gather.8.cloned.1.call-update) | async-done | bytes 1572880 | tf_op jit(solution)/shard_map/all_gather | solution.py:105
  163.1 2.7 convolution_convert_fusion.1
  165.8 0.7 slice.54
  166.6 0.8 reshape_squeeze.7
  167.4 0.2 copy.37
  167.6 18.3 %all_to_all.41 = bf16[4,8,32,512]{3,2,1,0:T(8,128)(2,1)S(1)} all-to-all(bf16[4,8,32,512]{3,2,1,0:T(8,128)(2,1)S(1)} %copy.37), channel_id=1, replica_groups=mesh['zh'=2,'y'=8,'x'=4,'zl'=4,'c'=2] {'x'}, dimensions={0} | all-to-all | bytes 2097152 | tf_op jit(solution)/shard_map/all_to_all | solution.py:82
  186.0 17.1 %all_to_all.42 = bf16[8,32,512]{2,1,0:T(8,128)(2,1)S(1)} all-to-all(bf16[8,32,512]{2,1,0:T(8,128)(2,1)S(1)} %dynamic-slice_bitcast_fusion.1), channel_id=1, replica_groups=mesh['zh'=2,'y'=8,'x'=4,'zl'=4,'c'=2] {'y'}, dimensions={0} | all-to-all | bytes 524288 | tf_op jit(solution)/shard_map/all_to_all | solution.py:82
  203.1 7.9 %collective-permute-start.1 = (bf16[32,512]{1,0:T(8,128)(2,1)S(1)}, bf16[32,512]{1,0:T(8,128)(2,1)S(1)}, u32[]{:S(2)}, u32[]{:S(2)}) collective-permute-start(bf16[32,512]{1,0:T(8,128)(2,1)S(1)} %dynamic-slice_bitcast_fusion.3), channel_id=1, source_target_pairs={{0,256},{256,0},{1,257},{257,1},{2,258},{258,2},{3,259},{259,3},{4... | collective-permute-start | bytes 98312 | tf_op jit(solution)/shard_map/ppermute | solution.py:78
  211.1 1.4 collective-permute-done.1
  212.5 33.0 %all_gather.18 = bf16[512,512]{1,0:T(8,128)(2,1)} all-gather(bf16[32,512]{1,0:T(8,128)(2,1)S(1)} %broadcast_select_fusion.1), channel_id=1, replica_groups=mesh['zh'=2,'y'=8,'x'=4,'zl'=4,'c'=2] {'c','y'}, dimensions={0}, use_global_device_ids=true | all-gather | bytes 557056 | tf_op jit(solution)/shard_map/all_gather | solution.py:133
  245.5 0.1 mul.77
  245.7 0.1 broadcast_add_fusion
  245.7 0.1 iota_add_fusion
  245.8 7.7 %collective-permute-start.2 = (bf16[320,128]{1,0:T(8,128)(2,1)S(1)}, bf16[320,128]{1,0:T(8,128)(2,1)S(1)}, u32[]{:S(2)}, u32[]{:S(2)}) collective-permute-start(bf16[320,128]{1,0:T(8,128)(2,1)S(1)} %slice.53), channel_id=1, source_target_pairs={{0,256},{256,0},{1,257},{257,1},{2,258},{258,2},{3,259},{259,3},{4... | collective-permute-start | bytes 245768 | tf_op jit(solution)/shard_map/ppermute | solution.py:78
  253.5 0.1 iota_add_fusion.1
  253.6 0.2 add.167.qpos_ref
  253.8 0.1 add.164.kpos_ref
  253.9 2.6 collective-permute-done.2
  256.6 1.7 copy-done
  258.3 7.3 %shard_map.64 = (f32[640,128]{1,0:T(8,128)S(1)}, f32[640,128]{1,0:T(8,128)S(1)}) custom-call(bf16[640,128]{1,0:T(8,128)(2,1)S(1)} %pad_maximum_fusion.q_ref, bf16[5120,256]{1,0:T(8,128)(2,1)S(1)} %copy-done, s32[640,1]{1,0:T(8,128)S(1)} %add.167.qpos_ref, s32[1,5120]{1,0:T(1,128)S(1)} %add.164.kpos_ref), custom_call_target="tpu_custom_call" | custom-call | flops 1677721600 | bytes 2621440 | tf_op jit(solution)/shard_map/pallas_call | solution.py:52
  265.6 0.2 slice_reduce_fusion.1
  265.8 7.0 %collective-permute-start.3 = (f32[2,320]{1,0:T(2,128)S(1)}, f32[2,320]{1,0:T(2,128)S(1)}, u32[]{:S(2)}, u32[]{:S(2)}) collective-permute-start(f32[2,320]{1,0:T(2,128)S(1)} %pad_maximum_fusion.1), channel_id=1, source_target_pairs={{0,256},{256,0},{1,257},{257,1},{2,258},{258,2},{3,259},{259,3},{4... | collective-permute-start | bytes 7688 | tf_op jit(solution)/shard_map/ppermute | solution.py:78
  272.9 2.2 collective-permute-start.4
  275.1 0.1 copy.41
  275.2 0.1 copy.43
  275.4 0.3 fusion.10
  275.7 6.3 %collective-permute-done.4 = bf16[320,128]{1,0:T(8,128)(2,1)S(1)} collective-permute-done((bf16[320,128]{1,0:T(8,128)(2,1)S(1)}, bf16[320,128]{1,0:T(8,128)(2,1)S(1)}, u32[]{:S(2)}, u32[]{:S(2)}) %collective-permute-start.4) | collective-permute-done | bytes 81952 | tf_op jit(solution)/shard_map/ppermute | solution.py:78
  282.0 0.2 add_convert_fusion
  282.1 8.6 %all_to_all.43 = bf16[4,80,128]{2,1,0:T(8,128)(2,1)S(1)} all-to-all(bf16[4,80,128]{2,1,0:T(8,128)(2,1)S(1)} %bitcast.51), channel_id=1, replica_groups=mesh['zh'=2,'y'=8,'x'=4,'zl'=4,'c'=2] {'x'}, dimensions={0} | all-to-all | bytes 163840 | tf_op jit(solution)/shard_map/all_to_all | solution.py:82
  290.8 2.1 fusion
  292.9 9.2 %all_to_all.44 = bf16[4,80,512]{2,1,0:T(8,128)(2,1)S(1)} all-to-all(bf16[4,80,512]{2,1,0:T(8,128)(2,1)S(1)} %fusion), channel_id=1, replica_groups=mesh['zh'=2,'y'=8,'x'=4,'zl'=4,'c'=2] {'zl'}, dimensions={0} | all-to-all | bytes 655360 | tf_op jit(solution)/shard_map/all_to_all | solution.py:82
  302.2 9.2 %all_to_all.45 = bf16[2,80,256]{2,1,0:T(8,128)(2,1)S(1)} all-to-all(bf16[2,80,256]{2,1,0:T(8,128)(2,1)S(1)} %copy.45), channel_id=1, replica_groups=mesh['zh'=2,'y'=8,'x'=4,'zl'=4,'c'=2] {'c'}, dimensions={0} | all-to-all | bytes 163840 | tf_op jit(solution)/shard_map/all_to_all | solution.py:82
  311.4 0.6 copy.49
  (39 shorter events, 0.5 us)
Async XLA Ops:
  33.1 5.1 %copy-start.2 = (f32[2048]{0:T(1024)S(1)}, f32[2048]{0:T(1024)}, u32[]{:S(2)}) copy-start(f32[2048]{0:T(1024)} %param.7) | copy-start | bytes 24580
  33.1 51.7 %all-to-all-start.1 = ((bf16[4,8,128,384]{2,3,1,0:T(8,128)(2,1)}), bf16[4,8,128,384]{2,3,1,0:T(8,128)(2,1)S(1)}, u32[]{:S(2)}, u32[]{:S(2)}) async-start(bf16[4,8,128,384]{2,3,1,0:T(8,128)(2,1)} %bitcast.3), calls=%async_computation.1 | async-start | bytes 6291456 | tf_op jit(solution)/shard_map/all_to_all | solution.py:82
  37.0 86.1 %all-gather.6.cloned.1.call-start = ((), (), s32[]{:S(2)}) async-start(), calls=%async_computation.8 | async-start | bytes 1638400 | tf_op jit(solution)/shard_map/all_gather | solution.py:112
  85.7 27.0 %all-to-all-start.2 = ((bf16[8,128,384]{1,2,0:T(8,128)(2,1)}), bf16[8,128,384]{1,2,0:T(8,128)(2,1)S(1)}, u32[]{:S(2)}, u32[]{:S(2)}) async-start(bf16[8,128,384]{1,2,0:T(8,128)(2,1)} %dynamic-slice_bitcast_fusion), calls=%async_computation.2 | async-start | bytes 1572864 | tf_op jit(solution)/shard_map/all_to_all | solution.py:82
  89.3 73.9 %all-gather.8.cloned.1.call-start = ((), (), s32[]{:S(2)}) async-start(), calls=%async_computation.9 | async-start | bytes 1671168 | tf_op jit(solution)/shard_map/all_gather | solution.py:105
  112.8 9.5 %collective-permute-start = (bf16[128,384]{0,1:T(8,128)(2,1)S(1)}, bf16[128,384]{0,1:T(8,128)(2,1)S(1)}, u32[]{:S(2)}, u32[]{:S(2)}) collective-permute-start(bf16[128,384]{0,1:T(8,128)(2,1)S(1)} %dynamic-slice_bitcast_fusion.2), channel_id=1, source_target_pairs={{0,256},{256,0},{1,257},{257,1},{2,258},{258,2},{3,259},{259,3},{4... | collective-permute-start | bytes 294920 | tf_op jit(solution)/shard_map/ppermute | solution.py:78
  123.0 43.6 %copy-start.1 = (bf16[1,256,2048]{2,1,0:T(8,128)(2,1)S(1)}, bf16[1,256,2048]{2,1,0:T(8,128)(2,1)}, u32[]{:S(2)}) copy-start(bf16[1,256,2048]{2,1,0:T(8,128)(2,1)} %param.9) | copy-start | bytes 3145732
  123.0 133.5 %all-gather.10.cloned.1.call-start = ((), (), s32[]{:S(2)}) async-start(), calls=%async_computation.10 | async-start | bytes 2785280 | tf_op jit(solution)/shard_map/all_gather | solution.py:117
  166.5 124.3 %all-gather.12.cloned.1.call-start = ((), (), s32[]{:S(2)}) async-start(), calls=%async_computation.11 | async-start | bytes 2621440 | tf_op jit(solution)/shard_map/all_gather | solution.py:134
  167.6 77.9 %copy-start.3 = (s32[64]{0:T(128)S(1)}, s32[64]{0:T(128)}, u32[]{:S(2)}) copy-start(s32[64]{0:T(128)} %param.11) | copy-start | bytes 772
  203.1 9.3 %collective-permute-start.1 = (bf16[32,512]{1,0:T(8,128)(2,1)S(1)}, bf16[32,512]{1,0:T(8,128)(2,1)S(1)}, u32[]{:S(2)}, u32[]{:S(2)}) collective-permute-start(bf16[32,512]{1,0:T(8,128)(2,1)S(1)} %dynamic-slice_bitcast_fusion.3), channel_id=1, source_target_pairs={{0,256},{256,0},{1,257},{257,1},{2,258},{258,2},{3,259},{259,3},{4... | collective-permute-start | bytes 98312 | tf_op jit(solution)/shard_map/ppermute | solution.py:78
  245.8 10.7 %collective-permute-start.2 = (bf16[320,128]{1,0:T(8,128)(2,1)S(1)}, bf16[320,128]{1,0:T(8,128)(2,1)S(1)}, u32[]{:S(2)}, u32[]{:S(2)}) collective-permute-start(bf16[320,128]{1,0:T(8,128)(2,1)S(1)} %slice.53), channel_id=1, source_target_pairs={{0,256},{256,0},{1,257},{257,1},{2,258},{258,2},{3,259},{259,3},{4... | collective-permute-start | bytes 245768 | tf_op jit(solution)/shard_map/ppermute | solution.py:78
  256.6 1.7 copy-start
  265.8 9.2 %collective-permute-start.3 = (f32[2,320]{1,0:T(2,128)S(1)}, f32[2,320]{1,0:T(2,128)S(1)}, u32[]{:S(2)}, u32[]{:S(2)}) collective-permute-start(f32[2,320]{1,0:T(2,128)S(1)} %pad_maximum_fusion.1), channel_id=1, source_target_pairs={{0,256},{256,0},{1,257},{257,1},{2,258},{258,2},{3,259},{259,3},{4... | collective-permute-start | bytes 7688 | tf_op jit(solution)/shard_map/ppermute | solution.py:78
  272.9 9.1 %collective-permute-start.4 = (bf16[320,128]{1,0:T(8,128)(2,1)S(1)}, bf16[320,128]{1,0:T(8,128)(2,1)S(1)}, u32[]{:S(2)}, u32[]{:S(2)}) collective-permute-start(bf16[320,128]{1,0:T(8,128)(2,1)S(1)} %slice.79), channel_id=1, source_target_pairs={{0,256},{256,0},{1,257},{257,1},{2,258},{258,2},{3,259},{259,3},{4... | collective-permute-start | bytes 245768 | tf_op jit(solution)/shard_map/ppermute | solution.py:78
Sparse Core Ops, SparseCore 0:
  40.2 40.8 all-gather.5
  123.1 39.9 all-gather.7
  166.6 44.9 all-gather.9
  245.6 34.7 all-gather.11

commit v2 on v1

v2 whole, which is shorter than its diff:
```python
import jax
import jax.numpy as jnp
import numpy as np
from jax import lax
from jax.experimental import pallas as pl
from jax.experimental.pallas import tpu as pltpu
from jax.sharding import Mesh
from jax.sharding import PartitionSpec as P

HD = 128
HIDE = -1e30
CHUNK = 640
EXTRA = 16
LIMIT = pltpu.CompilerParams(vmem_limit_bytes=48 * 1024 * 1024)


def fold_kernel(w_ref, o_ref):
    part = o_ref.shape[3]
    for c in range(2):
        for h in range(2):
            for j in range(3):
                o_ref[c, h, 0, :, j * HD : (j + 1) * HD] = w_ref[
                    j, c * part : (c + 1) * part, h * HD : (h + 1) * HD
                ]


def fold(w, ny):
    part = w.shape[1] // (2 * ny)
    return pl.pallas_call(
        fold_kernel,
        grid=(ny,),
        in_specs=[pl.BlockSpec((3, 2 * part, 2 * HD), lambda i: (0, i, 0))],
        out_specs=pl.BlockSpec((2, 2, 1, part, 3 * HD), lambda i: (0, 0, i, 0, 0)),
        out_shape=jax.ShapeDtypeStruct((2, 2, ny, part, 3 * HD), w.dtype),
        compiler_params=LIMIT,
        cost_estimate=pl.CostEstimate(flops=0, bytes_accessed=4 * w.size, transcendentals=0),
    )(w)


def project_kernel(x_ref, w_ref, q_ref, kv_ref):
    out = jnp.dot(x_ref[...], w_ref[...], preferred_element_type=jnp.float32)
    q_ref[...] = out[:, :HD].astype(q_ref.dtype)
    kv_ref[...] = out[:, HD:].astype(kv_ref.dtype)


def project(x, w):
    n = x.shape[0]
    return pl.pallas_call(
        project_kernel,
        out_shape=[
            jax.ShapeDtypeStruct((n, HD), jnp.bfloat16),
            jax.ShapeDtypeStruct((n, 2 * HD), jnp.bfloat16),
        ],
        compiler_params=LIMIT,
        cost_estimate=pl.CostEstimate(
            flops=2 * n * w.size, bytes_accessed=2 * (x.size + w.size), transcendentals=0
        ),
    )(x, w)


def three_parts(value):
    first = value.astype(jnp.bfloat16).astype(jnp.float32)
    rest = value - first
    second = rest.astype(jnp.bfloat16).astype(jnp.float32)
    return first, second, rest - second


def attend_kernel(q_ref, kv_ref, qpos_ref, kpos_ref, o_ref, s_ref):
    factor = float(np.log2(np.e) / HD**0.5)
    rows = q_ref.shape[0]
    count = kv_ref.shape[0] // CHUNK
    q = q_ref[...]
    qpos = qpos_ref[...]
    high = jnp.full((rows, HD), HIDE, jnp.float32)
    for j in range(count):
        span = pl.ds(j * CHUNK, CHUNK)
        s = lax.dot_general(
            q, kv_ref[span, :HD], (((1,), (1,)), ((), ())), preferred_element_type=jnp.float32
        )
        s = jnp.where(kpos_ref[:, span] <= qpos, s * factor, HIDE)
        s_ref[:, span] = s
        for t in range(CHUNK // HD):
            high = jnp.maximum(high, s[:, t * HD : (t + 1) * HD])
    top = jnp.max(high, axis=1, keepdims=True)
    base = jnp.where(top <= 0.5 * HIDE, 0.0, top)
    total = jnp.zeros((rows, HD), jnp.float32)
    acc = jnp.zeros((rows, HD), jnp.float32)
    for j in range(count):
        span = pl.ds(j * CHUNK, CHUNK)
        p = jnp.exp2(s_ref[:, span] - base)
        for t in range(CHUNK // HD):
            total = total + p[:, t * HD : (t + 1) * HD]
        acc = acc + jnp.dot(
            p.astype(jnp.bfloat16), kv_ref[span, HD:], preferred_element_type=jnp.float32
        )
    total = jnp.sum(total, axis=1, keepdims=True)
    o = acc / jnp.where(total == 0.0, 1.0, total)
    lane = lax.broadcasted_iota(jnp.int32, (rows, HD), 1)
    stat = jnp.zeros((rows, HD), jnp.float32)
    for k, piece in enumerate(three_parts(top) + three_parts(total)):
        stat = jnp.where(lane == k, piece, stat)
    blocks, half = o_ref.shape[0], o_ref.shape[1] - EXTRA
    for b in range(blocks):
        o_ref[b, :half, :] = o[b * half : (b + 1) * half].astype(o_ref.dtype)
        block = jnp.concatenate(
            [stat[b * half : (b + 1) * half], jnp.zeros((HD - half, HD), jnp.float32)]
        )
        o_ref[b, half:, :] = block.T[:EXTRA].astype(o_ref.dtype)


def attend(q, kv, qpos, kpos, half):
    nq, nk = q.shape[0], kv.shape[0]
    tile = 2 * half
    return pl.pallas_call(
        attend_kernel,
        grid=(nq // tile,),
        in_specs=[
            pl.BlockSpec((tile, HD), lambda i: (i, 0)),
            pl.BlockSpec((nk, 2 * HD), lambda i: (0, 0)),
            pl.BlockSpec((tile, 1), lambda i: (i, 0)),
            pl.BlockSpec((1, nk), lambda i: (0, 0)),
        ],
        out_specs=pl.BlockSpec((2, half + EXTRA, HD), lambda i: (i, 0, 0)),
        out_shape=jax.ShapeDtypeStruct((nq // half, half + EXTRA, HD), jnp.bfloat16),
        scratch_shapes=[pltpu.VMEM((tile, nk), jnp.float32)],
        compiler_params=LIMIT,
        cost_estimate=pl.CostEstimate(
            flops=4 * nq * nk * HD, bytes_accessed=nk * HD * 4, transcendentals=nq * nk
        ),
    )(q, kv, qpos, kpos)


def finish_kernel(c_ref, part_ref, mine_ref, other_ref, out_ref):
    heads, half = part_ref.shape[1], part_ref.shape[2] - EXTRA
    context = []
    for h in range(heads):
        weight, values = [], []
        for k in range(2):
            stat = part_ref[k, h, half:, :].astype(jnp.float32)
            stat = jnp.concatenate([stat, jnp.zeros((HD - EXTRA, HD), jnp.float32)]).T[:half]
            weight.append((stat[:, 0:1] + stat[:, 1:2] + stat[:, 2:3], stat[:, 3:4] + stat[:, 4:5] + stat[:, 5:6]))
            values.append(part_ref[k, h, :half, :].astype(jnp.float32))
        top = jnp.maximum(weight[0][0], weight[1][0])
        a = weight[0][1] * jnp.exp2(weight[0][0] - top)
        b = weight[1][1] * jnp.exp2(weight[1][0] - top)
        context.append(((values[0] * a + values[1] * b) / (a + b)).astype(jnp.bfloat16))
    low = jnp.concatenate(context[: heads // 2], axis=1)
    high = jnp.concatenate(context[heads // 2 :], axis=1)
    first = c_ref[0] == 0
    near = jnp.where(first, low, high)
    far = jnp.where(first, high, low)
    for n in range(mine_ref.shape[0]):
        terms = jnp.dot(near, mine_ref[n], preferred_element_type=jnp.float32)
        terms += jnp.dot(far, other_ref[n], preferred_element_type=jnp.float32)
        terms = terms.astype(out_ref.dtype)
        width = out_ref.shape[2]
        out_ref[2 * n] = terms[:, :width]
        out_ref[2 * n + 1] = terms[:, width:]


def finish(core, parts, mine, other):
    half = parts.shape[2] - EXTRA
    blocks, _, cols = mine.shape
    vmem = pl.BlockSpec(memory_space=pltpu.VMEM)
    return pl.pallas_call(
        finish_kernel,
        in_specs=[pl.BlockSpec(memory_space=pltpu.SMEM), vmem, vmem, vmem],
        out_specs=vmem,
        out_shape=jax.ShapeDtypeStruct((2 * blocks, half, cols // 2), jnp.bfloat16),
        compiler_params=LIMIT,
        cost_estimate=pl.CostEstimate(
            flops=4 * half * mine.size, bytes_accessed=4 * mine.size, transcendentals=0
        ),
    )(core, parts, mine, other)


def swap(block, axis):
    return lax.ppermute(block, axis, [(0, 1), (1, 0)])


def exchange(block, axis):
    return lax.all_to_all(block, axis, 0, 0, tiled=True)


def gather(block, axis):
    count = lax.axis_size(axis)
    return exchange(jnp.broadcast_to(block[None], (count,) + block.shape), axis)


def pick(blocks, index):
    return lax.dynamic_index_in_dim(blocks, index, 0, keepdims=False)


def shards(hidden_in, norm_gain, snap_qkv, snap_out, owner_index, block_order):
    rows, width = hidden_in.shape
    zh, y, x, c = (lax.axis_index(name) for name in ("zh", "y", "x", "c"))
    ny, nx = 8, 4
    half = rows // 2
    owner = owner_index[0]
    zh0, y0, x0 = owner // (ny * nx), (owner // nx) % ny, owner % nx

    mine = lax.dynamic_slice_in_dim(hidden_in, c * half, half, 0).astype(jnp.float32)
    normed = (
        mine * lax.rsqrt(jnp.mean(mine * mine, axis=-1, keepdims=True) + 1e-06) * norm_gain
    ).astype(jnp.bfloat16)

    part = width // (2 * ny)
    w = exchange(fold(snap_qkv[0], ny), "c").reshape(nx, ny, part, 3 * HD)
    w = pick(exchange(w, "x"), x0)
    normed = lax.all_gather(normed, "x", axis=0, tiled=True)
    wo = jnp.where(x == x0, snap_out[0], jnp.zeros_like(snap_out[0]))
    wo = jnp.transpose(wo.reshape(wo.shape[0], nx, -1), (1, 0, 2))
    w, wo, normed = lax.optimization_barrier((w, wo, normed))
    wo = lax.psum_scatter(wo, "x", scatter_dimension=0)
    w = pick(exchange(w, "y"), y0)
    w = jnp.where(zh == zh0, w, swap(w, "zh"))
    w, wo = lax.optimization_barrier((w, wo))
    w = lax.all_gather(w, ("y", "c"), axis=0, tiled=True)
    wo = pick(exchange(wo.reshape(ny, -1, wo.shape[1]), "y"), y0)
    wo = jnp.where(zh == zh0, wo, swap(wo, "zh"))
    w, wo = lax.optimization_barrier((w, wo))
    wo = gather(wo, "y").reshape(-1, wo.shape[1])

    q, kv = project(normed, w)
    kv = lax.all_gather(kv, ("y", "c"), axis=0, tiled=True)
    q_other = swap(q, "zh")
    wo = gather(wo, "x")
    wo_other = swap(wo, "c")
    q0, q1 = jnp.where(zh == 0, q, q_other), jnp.where(zh == 0, q_other, q)
    q_all = jnp.concatenate([q0, q1])

    order = block_order.reshape(2, ny, nx) * rows
    offsets = jnp.arange(half, dtype=jnp.int32)
    halves = jnp.arange(2, dtype=jnp.int32) * half
    kpos = pick(order, zh)[:, None, :, None] + halves[None, :, None, None] + offsets
    here = lax.dynamic_index_in_dim(order, y, 1, keepdims=False)
    qpos = here[:, :, None] + c * half + offsets

    parts = attend(q_all, kv, qpos.reshape(-1, 1), kpos.reshape(1, -1), half)
    parts = exchange(parts, ("zh", "x")).reshape((2, nx) + parts.shape[1:])
    terms = finish(c.reshape(1), parts, wo, wo_other)
    terms = exchange(terms, ("zl", "c")).reshape(-1, rows, terms.shape[2])
    return jnp.sum(terms.astype(jnp.float32), axis=0).astype(jnp.bfloat16)


def solution(mesh):
    fine = Mesh(mesh.devices.reshape(2, 8, 4, 4, 2), ("zh", "y", "x", "zl", "c"))
    ctx, tp = ("zh", "y", "x"), ("zl", "c")
    in_specs = (P(ctx, None), P(), P(ctx, None, None, tp), P(ctx, tp, None), P(), P())
    return jax.shard_map(shards, mesh=fine, in_specs=in_specs, out_specs=P(ctx, tp), check_vma=False)
```

time: 320 us -> 255 us (0.80)
  blocking collectives: 109 us -> 57.5 us
  waiting for transfers between devices: 120 us -> 103 us
  local copies, waits for them, and re-layouts: 18.9 us -> 8.94 us
  starting transfers between devices: 39.8 us -> 48.8 us
  Pallas kernels: 7.25 us -> 15.1 us
  matrix products: 4.74 us -> 0 us
    all_gather x1 -> x0, blocking collectives: 33 us -> none  [shards(): wo = lax.all_gather(wo, ('c', 'y'), axis=0, tiled=True)]
    all_gather x1, waiting for transfers between devices: 40.1 us -> 18.9 us  [shards(): w = lax.all_gather(w, ('y', 'c'), axis=0, tiled=True)]
    all_to_all x6 -> x4, blocking collectives: 76.2 us -> 57.5 us  [exchange(): return lax.all_to_all(block, axis, 0, 0, tiled=True)]
    all_to_all x2 -> x4, starting transfers between devices: 7.38 us -> 21.2 us  [exchange(): return lax.all_to_all(block, axis, 0, 0, tiled=True)]
    all_to_all x2 -> x4, waiting for transfers between devices: 67.4 us -> 78.4 us  [exchange(): return lax.all_to_all(block, axis, 0, 0, tiled=True)]
    ppermute x5 -> x4, waiting for transfers between devices: 12.4 us -> 3.35 us  [swap(): return lax.ppermute(block, axis, [(0, 1), (1, 0)])]
    pallas_call x1 -> x4, Pallas kernels: 7.25 us -> 15.1 us  [the longest x1 7.92 us: attend(): pl.pallas_call(attend_kernel, grid=(nq // tile,), in_specs=[pl.BlockSpec(...]
    transpose x4 -> x0, local copies, waits for them, and re-layouts: 7.57 us -> none  [the longest x1 7.3 us: shards(): w = jnp.transpose(w, (2, 4, 1, 3, 0, 5)).reshape(2, 2, ny, part, 3 * HD)]
  transfers between devices with their start and end apart: 11 -> 12, of which waited for: 7 -> 8; matrix products, arithmetic and copies ran while one was open for 2% -> 4% of each run, Pallas kernels for 2% -> 3%
where the time goes in v2:
time: 255 us; the launch traced here: 254 us
  waiting for transfers between devices  103 us (40%)
  blocking collectives  57.5 us (23%)
  starting transfers between devices  48.8 us (19%)
  Pallas kernels  15.1 us (6%)
  between operations  14.1 us (6%)
  local copies, waits for them, and re-layouts  8.94 us (4%)
  other arithmetic  6.94 us (3%)
    all_to_all x4, waiting for transfers between devices, exchange(): return lax.all_to_all(block, axis, 0, 0, tiled=True)  78.4 us
    all_to_all x4, blocking collectives, exchange(): return lax.all_to_all(block, axis, 0, 0, tiled=True)  57.5 us
    ppermute x4, starting transfers between devices, swap(): return lax.ppermute(block, axis, [(0, 1), (1, 0)])  27.4 us
    all_to_all x4, starting transfers between devices, exchange(): return lax.all_to_all(block, axis, 0, 0, tiled=True)  21.2 us
    all_gather x1, waiting for transfers between devices, shards(): w = lax.all_gather(w, ('y', 'c'), axis=0, tiled=True)  18.9 us
    pallas_call x1, Pallas kernels, attend(): pl.pallas_call(attend_kernel, grid=(nq // tile,), in_specs=[pl.BlockSpec(...  7.92 us
    unnamed x11, local copies, waits for them, and re-layouts  5.43 us
  transfers between devices with their start and end apart: 12, of which 8 were waited for; matrix products, arithmetic and copies ran while one was open for 4% of the time, Pallas kernels for 3%

profile of v2, /device:TPU:1, one launch (start us, length us, event | category | flops | bytes accessed | tf_op | source)
XLA Modules:
  0.0 254.5 jit_solution(11734246987251346305)
XLA Ops:
  6.5 4.7 %shard_map.64 = bf16[2,2,8,128,384]{4,3,2,1,0:T(8,128)(2,1)S(1)} custom-call(bf16[3,2048,256]{2,1,0:T(8,128)(2,1)} %bitcast.33), custom_call_target="tpu_custom_call" | custom-call | bytes 6291456 | tf_op jit(solution)/shard_map/pallas_call | solution.py:29
  11.2 13.7 %all_to_all.40 = bf16[2,2,8,128,384]{4,3,2,1,0:T(8,128)(2,1)} all-to-all(bf16[2,2,8,128,384]{4,3,2,1,0:T(8,128)(2,1)S(1)} %shard_map.64), channel_id=1, replica_groups=mesh['zh'=2,'y'=8,'x'=4,'zl'=4,'c'=2] {'c'}, dimensions={0} | all-to-all | bytes 6291456 | tf_op jit(solution)/shard_map/all_to_all | solution.py:182
  25.0 3.8 %all-to-all-start.1 = ((bf16[4,8,128,384]{3,2,1,0:T(8,128)(2,1)}), bf16[4,8,128,384]{3,2,1,0:T(8,128)(2,1)S(1)}, u32[]{:S(2)}, u32[]{:S(2)}) async-start(bf16[4,8,128,384]{3,2,1,0:T(8,128)(2,1)} %bitcast.2), calls=%async_computation.1 | async-start | bytes 6291456 | tf_op jit(solution)/shard_map/all_to_all | solution.py:182
  28.8 0.0 all-gather.4.cloned.1.call-start
  28.9 1.1 fusion
  30.0 1.9 fusion.2
  31.9 0.0 all-gather.4.cloned.1.call-update
  31.9 0.0 reduce-scatter.2.cloned.1.call-start
  32.6 2.3 copy.12
  34.9 2.3 broadcast_select_fusion
  37.2 39.4 %all-to-all-done.1 = bf16[4,8,128,384]{3,2,1,0:T(8,128)(2,1)S(1)} async-done(((bf16[4,8,128,384]{3,2,1,0:T(8,128)(2,1)}), bf16[4,8,128,384]{3,2,1,0:T(8,128)(2,1)S(1)}, u32[]{:S(2)}, u32[]{:S(2)}) %all-to-all-start.1) | async-done | bytes 3145760 | tf_op jit(solution)/shard_map/all_to_all | solution.py:182
  76.6 1.0 dynamic-slice_bitcast_fusion
  77.6 0.0 reduce-scatter.2.cloned.1.call-update
  77.6 3.7 %all-to-all-start.2 = ((bf16[8,128,384]{2,1,0:T(8,128)(2,1)}), bf16[8,128,384]{2,1,0:T(8,128)(2,1)S(1)}, u32[]{:S(2)}, u32[]{:S(2)}) async-start(bf16[8,128,384]{2,1,0:T(8,128)(2,1)} %dynamic-slice_bitcast_fusion), calls=%async_computation.2 | async-start | bytes 1572864 | tf_op jit(solution)/shard_map/all_to_all | solution.py:182
  81.3 0.0 all-gather.6.cloned.1.call-start
  81.4 23.4 %all-to-all-done.2 = bf16[8,128,384]{2,1,0:T(8,128)(2,1)S(1)} async-done(((bf16[8,128,384]{2,1,0:T(8,128)(2,1)}), bf16[8,128,384]{2,1,0:T(8,128)(2,1)S(1)}, u32[]{:S(2)}, u32[]{:S(2)}) %all-to-all-start.2) | async-done | bytes 786464 | tf_op jit(solution)/shard_map/all_to_all | solution.py:182
  104.8 7.4 %collective-permute-start = (bf16[128,384]{1,0:T(8,128)(2,1)S(1)}, bf16[128,384]{1,0:T(8,128)(2,1)S(1)}, u32[]{:S(2)}, u32[]{:S(2)}) collective-permute-start(bf16[128,384]{1,0:T(8,128)(2,1)S(1)} %dynamic-slice_bitcast_fusion.1), channel_id=1, source_target_pairs={{0,256},{256,0},{1,257},{257,1},{2,258},{258,2},{3,259},{259,3},{4... | collective-permute-start | bytes 294920 | tf_op jit(solution)/shard_map/ppermute | solution.py:178
  112.3 2.1 collective-permute-done
  114.4 0.7 broadcast_select_fusion.1
  115.0 1.1 copy.13
  116.1 0.0 all-gather.6.cloned.1.call-update
  116.2 0.0 all-gather.8.cloned.1.call-start
  116.2 11.8 %all_to_all.41 = bf16[8,32,512]{2,1,0:T(8,128)(2,1)S(1)} all-to-all(bf16[8,32,512]{2,1,0:T(8,128)(2,1)S(1)} %bitcast.36), channel_id=1, replica_groups=mesh['zh'=2,'y'=8,'x'=4,'zl'=4,'c'=2] {'y'}, dimensions={0} | all-to-all | bytes 524288 | tf_op jit(solution)/shard_map/all_to_all | solution.py:182
  128.1 8.1 %collective-permute-start.1 = (bf16[32,512]{1,0:T(8,128)(2,1)S(1)}, bf16[32,512]{1,0:T(8,128)(2,1)S(1)}, u32[]{:S(2)}, u32[]{:S(2)}) collective-permute-start(bf16[32,512]{1,0:T(8,128)(2,1)S(1)} %dynamic-slice_bitcast_fusion.2), channel_id=1, source_target_pairs={{0,256},{256,0},{1,257},{257,1},{2,258},{258,2},{3,259},{259,3},{4... | collective-permute-start | bytes 98312 | tf_op jit(solution)/shard_map/ppermute | solution.py:178
  136.2 1.3 collective-permute-done.1
  137.5 18.9 %all-gather.6.cloned.1.call-done.w_ref = bf16[2048,384]{1,0:T(8,128)(2,1)} async-done(((bf16[128,384]{1,0:T(8,128)(2,1)}), bf16[2048,384]{1,0:T(8,128)(2,1)}) %all-gather.6.cloned.1.call-update) | async-done | bytes 1572880 | tf_op jit(solution)/shard_map/all_gather | solution.py:218
  156.4 1.4 copy-done
  157.8 1.5 shard_map.65
  159.3 15.9 %all_to_all.42 = bf16[8,32,512]{2,1,0:T(8,128)(2,1)S(1)} all-to-all(bf16[8,32,512]{2,1,0:T(8,128)(2,1)S(1)} %broadcast_in_dim.9), channel_id=1, replica_groups=mesh['zh'=2,'y'=8,'x'=4,'zl'=4,'c'=2] {'y'}, dimensions={0} | all-to-all | bytes 524288 | tf_op jit(solution)/shard_map/all_to_all | solution.py:182
  175.2 1.0 broadcast_in_dim.11
  176.3 4.0 %all-to-all-start.6 = ((bf16[4,256,512]{2,1,0:T(8,128)(2,1)}), bf16[4,256,512]{2,1,0:T(8,128)(2,1)S(1)}, u32[]{:S(2)}, u32[]{:S(2)}) async-start(bf16[4,256,512]{2,1,0:T(8,128)(2,1)} %broadcast_in_dim.11), calls=%async_computation.7 | async-start | bytes 2097152 | tf_op jit(solution)/shard_map/all_to_all | solution.py:182
  180.2 0.1 mul.47
  180.4 0.1 broadcast_add_fusion
  180.4 0.1 iota_add_fusion
  180.5 7.8 %collective-permute-start.2 = (bf16[320,128]{1,0:T(8,128)(2,1)S(1)}, bf16[320,128]{1,0:T(8,128)(2,1)S(1)}, u32[]{:S(2)}, u32[]{:S(2)}) collective-permute-start(bf16[320,128]{1,0:T(8,128)(2,1)S(1)} %get-tuple-element.20), channel_id=1, source_target_pairs={{0,256},{256,0},{1,257},{257,1},{2,258},{258,2},{3,259},{259,3},{4... | collective-permute-start | bytes 245768 | tf_op jit(solution)/shard_map/ppermute | solution.py:178
  188.3 5.8 %all-to-all-done.6.mine_ref = bf16[4,256,512]{2,1,0:T(8,128)(2,1)S(1)} async-done(((bf16[4,256,512]{2,1,0:T(8,128)(2,1)}), bf16[4,256,512]{2,1,0:T(8,128)(2,1)S(1)}, u32[]{:S(2)}, u32[]{:S(2)}) %all-to-all-start.6) | async-done | bytes 1048608 | tf_op jit(solution)/shard_map/all_to_all | solution.py:182
  194.1 4.1 %collective-permute-start.3 = (bf16[4,256,512]{2,1,0:T(8,128)(2,1)S(1)}, bf16[4,256,512]{2,1,0:T(8,128)(2,1)S(1)}, u32[]{:S(2)}, u32[]{:S(2)}) collective-permute-start(bf16[4,256,512]{2,1,0:T(8,128)(2,1)S(1)} %all-to-all-done.6.mine_ref), channel_id=1, source_target_pairs={{0,1},{1,0},{2,3},{3,2},{4,5},{5,4},{6,7},{7,6},{8,9},{9,8},{10,11... | collective-permute-start | bytes 3145736 | tf_op jit(solution)/shard_map/ppermute | solution.py:178
  198.2 0.1 iota_add_fusion.1
  198.3 0.2 add.147.qpos_ref
  198.4 0.1 add.146.kpos_ref
  198.6 2.5 all-gather.8.cloned.1.call-done.kv_ref
  201.1 1.7 copy-done.2
  202.8 7.9 %shard_map.66 = bf16[8,96,128]{2,1,0:T(8,128)(2,1)} custom-call(bf16[640,128]{1,0:T(8,128)(2,1)S(1)} %pad_maximum_fusion.q_ref, bf16[5120,256]{1,0:T(8,128)(2,1)S(1)} %copy-done.2, s32[640,1]{1,0:T(8,128)S(1)} %add.147.qpos_ref, s32[1,5120]{1,0:T(1,128)S(1)} %add.146.kpos_ref), custom_call_target="tpu_custom_call" | custom-call | flops 1677721600 | bytes 2621440 | tf_op jit(solution)/shard_map/pallas_call | solution.py:114
  210.7 9.7 %all-to-all-start.4 = ((bf16[8,96,128]{2,1,0:T(8,128)(2,1)}), bf16[8,96,128]{2,1,0:T(8,128)(2,1)S(1)}, u32[]{:S(2)}, u32[]{:S(2)}) async-start(bf16[8,96,128]{2,1,0:T(8,128)(2,1)} %shard_map.66), calls=%async_computation.5 | async-start | bytes 393216 | tf_op jit(solution)/shard_map/all_to_all | solution.py:182
  220.5 9.8 %all-to-all-done.4 = bf16[8,96,128]{2,1,0:T(8,128)(2,1)S(1)} async-done(((bf16[8,96,128]{2,1,0:T(8,128)(2,1)}), bf16[8,96,128]{2,1,0:T(8,128)(2,1)S(1)}, u32[]{:S(2)}, u32[]{:S(2)}) %all-to-all-start.4) | async-done | bytes 196640 | tf_op jit(solution)/shard_map/all_to_all | solution.py:182
  230.2 0.9 shard_map.67
  231.2 16.1 %all_to_all.43 = bf16[8,80,256]{2,1,0:T(8,128)(2,1)S(1)} all-to-all(bf16[8,80,256]{2,1,0:T(8,128)(2,1)S(1)} %shard_map.67), channel_id=1, replica_groups=mesh['zh'=2,'y'=8,'x'=4,'zl'=4,'c'=2] {'zl','c'}, dimensions={0} | all-to-all | bytes 655360 | tf_op jit(solution)/shard_map/all_to_all | solution.py:182
  247.3 0.7 bitcast_reduce_fusion
  (24 shorter events, 0.1 us)
Async XLA Ops:
  25.0 5.1 %copy-start.3 = (f32[2048]{0:T(1024)S(1)}, f32[2048]{0:T(1024)}, u32[]{:S(2)}) copy-start(f32[2048]{0:T(1024)} %param.7) | copy-start | bytes 24580
  25.0 51.7 %all-to-all-start.1 = ((bf16[4,8,128,384]{3,2,1,0:T(8,128)(2,1)}), bf16[4,8,128,384]{3,2,1,0:T(8,128)(2,1)S(1)}, u32[]{:S(2)}, u32[]{:S(2)}) async-start(bf16[4,8,128,384]{3,2,1,0:T(8,128)(2,1)} %bitcast.2), calls=%async_computation.1 | async-start | bytes 6291456 | tf_op jit(solution)/shard_map/all_to_all | solution.py:182
  28.8 48.8 %all-gather.4.cloned.1.call-start = ((), (), s32[]{:S(2)}) async-start(), calls=%async_computation.9 | async-start | bytes 1638400 | tf_op jit(solution)/shard_map/all_gather | solution.py:210
  31.9 83.1 %reduce-scatter.2.cloned.1.call-start = ((), (), s32[]{:S(2)}) async-start(), calls=%async_computation.10 | async-start | bytes 1310720 | tf_op jit(solution)/shard_map/reduce_scatter | solution.py:214
  77.6 78.8 %copy-start.1 = (bf16[320,2048]{1,0:T(8,128)(2,1)S(1)}, bf16[320,2048]{1,0:T(8,128)(2,1)}, u32[]{:S(2)}) copy-start(bf16[320,2048]{1,0:T(8,128)(2,1)} %all-gather.4.cloned.1.call-done.x_ref) | copy-start | bytes 3932164
  77.6 27.2 %all-to-all-start.2 = ((bf16[8,128,384]{2,1,0:T(8,128)(2,1)}), bf16[8,128,384]{2,1,0:T(8,128)(2,1)S(1)}, u32[]{:S(2)}, u32[]{:S(2)}) async-start(bf16[8,128,384]{2,1,0:T(8,128)(2,1)} %dynamic-slice_bitcast_fusion), calls=%async_computation.2 | async-start | bytes 1572864 | tf_op jit(solution)/shard_map/all_to_all | solution.py:182
  81.3 75.0 %all-gather.6.cloned.1.call-start = ((), (), s32[]{:S(2)}) async-start(), calls=%async_computation.11 | async-start | bytes 1671168 | tf_op jit(solution)/shard_map/all_gather | solution.py:218
  104.8 9.5 %collective-permute-start = (bf16[128,384]{1,0:T(8,128)(2,1)S(1)}, bf16[128,384]{1,0:T(8,128)(2,1)S(1)}, u32[]{:S(2)}, u32[]{:S(2)}) collective-permute-start(bf16[128,384]{1,0:T(8,128)(2,1)S(1)} %dynamic-slice_bitcast_fusion.1), channel_id=1, source_target_pairs={{0,256},{256,0},{1,257},{257,1},{2,258},{258,2},{3,259},{259,3},{4... | collective-permute-start | bytes 294920 | tf_op jit(solution)/shard_map/ppermute | solution.py:178
  116.2 84.9 %all-gather.8.cloned.1.call-start = ((), (), s32[]{:S(2)}) async-start(), calls=%async_computation.12 | async-start | bytes 2785280 | tf_op jit(solution)/shard_map/all_gather | solution.py:225
  128.1 9.4 %collective-permute-start.1 = (bf16[32,512]{1,0:T(8,128)(2,1)S(1)}, bf16[32,512]{1,0:T(8,128)(2,1)S(1)}, u32[]{:S(2)}, u32[]{:S(2)}) collective-permute-start(bf16[32,512]{1,0:T(8,128)(2,1)S(1)} %dynamic-slice_bitcast_fusion.2), channel_id=1, source_target_pairs={{0,256},{256,0},{1,257},{257,1},{2,258},{258,2},{3,259},{259,3},{4... | collective-permute-start | bytes 98312 | tf_op jit(solution)/shard_map/ppermute | solution.py:178
  156.4 1.4 copy-start
  157.8 22.5 %copy-start.4 = (s32[64]{0:T(128)S(1)}, s32[64]{0:T(128)}, u32[]{:S(2)}) copy-start(s32[64]{0:T(128)} %param.11) | copy-start | bytes 772
  176.3 17.8 %all-to-all-start.6 = ((bf16[4,256,512]{2,1,0:T(8,128)(2,1)}), bf16[4,256,512]{2,1,0:T(8,128)(2,1)S(1)}, u32[]{:S(2)}, u32[]{:S(2)}) async-start(bf16[4,256,512]{2,1,0:T(8,128)(2,1)} %broadcast_in_dim.11), calls=%async_computation.7 | async-start | bytes 2097152 | tf_op jit(solution)/shard_map/all_to_all | solution.py:182
  180.5 18.0 %collective-permute-start.2 = (bf16[320,128]{1,0:T(8,128)(2,1)S(1)}, bf16[320,128]{1,0:T(8,128)(2,1)S(1)}, u32[]{:S(2)}, u32[]{:S(2)}) collective-permute-start(bf16[320,128]{1,0:T(8,128)(2,1)S(1)} %get-tuple-element.20), channel_id=1, source_target_pairs={{0,256},{256,0},{1,257},{257,1},{2,258},{258,2},{3,259},{259,3},{4... | collective-permute-start | bytes 245768 | tf_op jit(solution)/shard_map/ppermute | solution.py:178
  194.1 26.4 %collective-permute-start.3 = (bf16[4,256,512]{2,1,0:T(8,128)(2,1)S(1)}, bf16[4,256,512]{2,1,0:T(8,128)(2,1)S(1)}, u32[]{:S(2)}, u32[]{:S(2)}) collective-permute-start(bf16[4,256,512]{2,1,0:T(8,128)(2,1)S(1)} %all-to-all-done.6.mine_ref), channel_id=1, source_target_pairs={{0,1},{1,0},{2,3},{3,2},{4,5},{5,4},{6,7},{7,6},{8,9},{9,8},{10,11... | collective-permute-start | bytes 3145736 | tf_op jit(solution)/shard_map/ppermute | solution.py:178
  201.1 1.7 copy-start.2
  210.7 19.5 %all-to-all-start.4 = ((bf16[8,96,128]{2,1,0:T(8,128)(2,1)}), bf16[8,96,128]{2,1,0:T(8,128)(2,1)S(1)}, u32[]{:S(2)}, u32[]{:S(2)}) async-start(bf16[8,96,128]{2,1,0:T(8,128)(2,1)} %shard_map.66), calls=%async_computation.5 | async-start | bytes 393216 | tf_op jit(solution)/shard_map/all_to_all | solution.py:182
Sparse Core Ops, SparseCore 0:
  32.0 40.8 all-gather.3
  77.8 27.2 reduce-scatter.1
  116.3 40.0 all-gather.5
  159.4 41.5 all-gather.7

commit v3 on v2

--- a/solution.py
+++ b/solution.py
@@ -15,13 +15,10 @@
 
 
 def fold_kernel(w_ref, o_ref):
-    part = o_ref.shape[3]
     for c in range(2):
         for h in range(2):
             for j in range(3):
-                o_ref[c, h, 0, :, j * HD : (j + 1) * HD] = w_ref[
-                    j, c * part : (c + 1) * part, h * HD : (h + 1) * HD
-                ]
+                o_ref[c, h, 0, :, j * HD : (j + 1) * HD] = w_ref[j, c, :, h * HD : (h + 1) * HD]
 
 
 def fold(w, ny):
@@ -29,33 +26,55 @@
     return pl.pallas_call(
         fold_kernel,
         grid=(ny,),
-        in_specs=[pl.BlockSpec((3, 2 * part, 2 * HD), lambda i: (0, i, 0))],
+        in_specs=[pl.BlockSpec((3, 2, part, 2 * HD), lambda i: (0, 0, i, 0))],
         out_specs=pl.BlockSpec((2, 2, 1, part, 3 * HD), lambda i: (0, 0, i, 0, 0)),
         out_shape=jax.ShapeDtypeStruct((2, 2, ny, part, 3 * HD), w.dtype),
         compiler_params=LIMIT,
         cost_estimate=pl.CostEstimate(flops=0, bytes_accessed=4 * w.size, transcendentals=0),
-    )(w)
-
-
-def project_kernel(x_ref, w_ref, q_ref, kv_ref):
-    out = jnp.dot(x_ref[...], w_ref[...], preferred_element_type=jnp.float32)
+    )(w.reshape(3, 2, ny * part, 2 * HD))
+
+
+def near_kernel(c_ref, x_ref, w_ref, out_ref):
+    depth = w_ref.shape[0]
+    span = pl.ds(pl.multiple_of(c_ref[0] * depth, depth), depth)
+    w = w_ref[:, : out_ref.shape[1]]
+    out_ref[...] = jnp.dot(x_ref[:, span], w, preferred_element_type=jnp.float32)
+
+
+def far_kernel(c_ref, x_ref, w_ref, sum_ref, q_ref, kv_ref):
+    depth = w_ref.shape[0]
+    span = pl.ds(pl.multiple_of((1 - c_ref[0]) * depth, depth), depth)
+    w = w_ref[:, : sum_ref.shape[1]]
+    out = sum_ref[...] + jnp.dot(x_ref[:, span], w, preferred_element_type=jnp.float32)
     q_ref[...] = out[:, :HD].astype(q_ref.dtype)
     kv_ref[...] = out[:, HD:].astype(kv_ref.dtype)
 
 
-def project(x, w):
-    n = x.shape[0]
+def project(core, x, near, far):
+    n, cols = x.shape[0], 3 * HD
+    smem, vmem = pl.BlockSpec(memory_space=pltpu.SMEM), pl.BlockSpec(memory_space=pltpu.VMEM)
+    cost = pl.CostEstimate(
+        flops=2 * n * near.shape[0] * cols, bytes_accessed=2 * (x.size + near.size), transcendentals=0
+    )
+    total = pl.pallas_call(
+        near_kernel,
+        in_specs=[smem, vmem, vmem],
+        out_specs=vmem,
+        out_shape=jax.ShapeDtypeStruct((n, cols), jnp.float32),
+        compiler_params=LIMIT,
+        cost_estimate=cost,
+    )(core, x, near)
     return pl.pallas_call(
-        project_kernel,
+        far_kernel,
+        in_specs=[smem, vmem, vmem, vmem],
+        out_specs=[vmem, vmem],
         out_shape=[
             jax.ShapeDtypeStruct((n, HD), jnp.bfloat16),
             jax.ShapeDtypeStruct((n, 2 * HD), jnp.bfloat16),
         ],
         compiler_params=LIMIT,
-        cost_estimate=pl.CostEstimate(
-            flops=2 * n * w.size, bytes_accessed=2 * (x.size + w.size), transcendentals=0
-        ),
-    )(x, w)
+        cost_estimate=cost,
+    )(core, x, far, total)
 
 
 def three_parts(value):
@@ -65,17 +84,21 @@
     return first, second, rest - second
 
 
-def attend_kernel(q_ref, kv_ref, qpos_ref, kpos_ref, o_ref, s_ref):
+def attend_kernel(q_ref, near_ref, far_ref, qpos_ref, kpos_ref, o_ref, s_ref):
     factor = float(np.log2(np.e) / HD**0.5)
     rows = q_ref.shape[0]
-    count = kv_ref.shape[0] // CHUNK
+    pieces = [
+        (ref, j * CHUNK, i * ref.shape[0] + j * CHUNK)
+        for i, ref in enumerate((near_ref, far_ref))
+        for j in range(ref.shape[0] // CHUNK)
+    ]
     q = q_ref[...]
     qpos = qpos_ref[...]
     high = jnp.full((rows, HD), HIDE, jnp.float32)
-    for j in range(count):
-        span = pl.ds(j * CHUNK, CHUNK)
+    for ref, at, column in pieces:
+        span = pl.ds(column, CHUNK)
         s = lax.dot_general(
-            q, kv_ref[span, :HD], (((1,), (1,)), ((), ())), preferred_element_type=jnp.float32
+            q, ref[pl.ds(at, CHUNK), :HD], (((1,), (1,)), ((), ())), preferred_element_type=jnp.float32
         )
         s = jnp.where(kpos_ref[:, span] <= qpos, s * factor, HIDE)
         s_ref[:, span] = s
@@ -85,13 +108,13 @@
     base = jnp.where(top <= 0.5 * HIDE, 0.0, top)
     total = jnp.zeros((rows, HD), jnp.float32)
     acc = jnp.zeros((rows, HD), jnp.float32)
-    for j in range(count):
-        span = pl.ds(j * CHUNK, CHUNK)
+    for ref, at, column in pieces:
+        span = pl.ds(column, CHUNK)
         p = jnp.exp2(s_ref[:, span] - base)
         for t in range(CHUNK // HD):
             total = total + p[:, t * HD : (t + 1) * HD]
         acc = acc + jnp.dot(
-            p.astype(jnp.bfloat16), kv_ref[span, HD:], preferred_element_type=jnp.float32
+            p.astype(jnp.bfloat16), ref[pl.ds(at, CHUNK), HD:], preferred_element_type=jnp.float32
         )
     total = jnp.sum(total, axis=1, keepdims=True)
     o = acc / jnp.where(total == 0.0, 1.0, total)
@@ -108,15 +131,16 @@
         o_ref[b, half:, :] = block.T[:EXTRA].astype(o_ref.dtype)
 
 
-def attend(q, kv, qpos, kpos, half):
-    nq, nk = q.shape[0], kv.shape[0]
+def attend(q, near, far, qpos, kpos, half):
+    nq, nk = q.shape[0], 2 * near.shape[0]
     tile = 2 * half
     return pl.pallas_call(
         attend_kernel,
         grid=(nq // tile,),
         in_specs=[
             pl.BlockSpec((tile, HD), lambda i: (i, 0)),
-            pl.BlockSpec((nk, 2 * HD), lambda i: (0, 0)),
+            pl.BlockSpec((nk // 2, 2 * HD), lambda i: (0, 0)),
+            pl.BlockSpec((nk // 2, 2 * HD), lambda i: (0, 0)),
             pl.BlockSpec((tile, 1), lambda i: (i, 0)),
             pl.BlockSpec((1, nk), lambda i: (0, 0)),
         ],
@@ -127,7 +151,7 @@
         cost_estimate=pl.CostEstimate(
             flops=4 * nq * nk * HD, bytes_accessed=nk * HD * 4, transcendentals=nq * nk
         ),
-    )(q, kv, qpos, kpos)
+    )(q, near, far, qpos, kpos)
 
 
 def finish_kernel(c_ref, part_ref, mine_ref, other_ref, out_ref):
@@ -182,13 +206,41 @@
     return lax.all_to_all(block, axis, 0, 0, tiled=True)
 
 
-def gather(block, axis):
+def pick(blocks, index):
+    return lax.dynamic_index_in_dim(blocks, index, 0, keepdims=False)
+
+
+def spread(block, axis):
     count = lax.axis_size(axis)
     return exchange(jnp.broadcast_to(block[None], (count,) + block.shape), axis)
 
 
-def pick(blocks, index):
-    return lax.dynamic_index_in_dim(blocks, index, 0, keepdims=False)
+def shift(block, axis, distance):
+    count = lax.axis_size(axis)
+    return lax.ppermute(block, axis, [(i, (i + distance) % count) for i in range(count)])
+
+
+def distances(axis):
+    count = lax.axis_size(axis)
+    return sorted(range(1, count), key=lambda s: -min(s, count - s))
+
+
+def scatter_by_shifts(blocks, axis, source):
+    here, count = lax.axis_index(axis), blocks.shape[0]
+    result = pick(blocks, here)
+    for s in distances(axis):
+        got = shift(pick(blocks, (here + s) % count), axis, s)
+        result = jnp.where((here - source) % count == s, got, result)
+    return result
+
+
+def gather_by_shifts(block, axis):
+    here, count = lax.axis_index(axis), lax.axis_size(axis)
+    got = {0: block}
+    for s in distances(axis):
+        got[s] = shift(block, axis, s)
+    got = jnp.stack([got[s] for s in range(count)])
+    return jnp.stack([pick(got, (here - i) % count) for i in range(count)])
 
 
 def shards(hidden_in, norm_gain, snap_qkv, snap_out, owner_index, block_order):
@@ -196,6 +248,7 @@
     zh, y, x, c = (lax.axis_index(name) for name in ("zh", "y", "x", "c"))
     ny, nx = 8, 4
     half = rows // 2
+    core = c.reshape(1)
     owner = owner_index[0]
     zh0, y0, x0 = owner // (ny * nx), (owner // nx) % ny, owner % nx
 
@@ -206,39 +259,42 @@
 
     part = width // (2 * ny)
     w = exchange(fold(snap_qkv[0], ny), "c").reshape(nx, ny, part, 3 * HD)
+    wo = snap_out[0].reshape(ny, -1, snap_out.shape[2])
     w = pick(exchange(w, "x"), x0)
-    normed = lax.all_gather(normed, "x", axis=0, tiled=True)
-    wo = jnp.where(x == x0, snap_out[0], jnp.zeros_like(snap_out[0]))
+    wo = scatter_by_shifts(wo, "y", y0)
+    w, wo, normed = lax.optimization_barrier((w, wo, normed))
+    w = pick(exchange(w, "y"), y0)
+    normed = gather_by_shifts(normed, "x").reshape(-1, width)
     wo = jnp.transpose(wo.reshape(wo.shape[0], nx, -1), (1, 0, 2))
-    w, wo, normed = lax.optimization_barrier((w, wo, normed))
-    wo = lax.psum_scatter(wo, "x", scatter_dimension=0)
-    w = pick(exchange(w, "y"), y0)
+    wo = scatter_by_shifts(wo, "x", x0)
+    wo = jnp.transpose(wo.reshape(wo.shape[0], nx, HD), (1, 0, 2)).reshape(part, HD)
+    w = jnp.concatenate([w, wo], axis=1)
+    w, normed = lax.optimization_barrier((w, normed))
     w = jnp.where(zh == zh0, w, swap(w, "zh"))
-    w, wo = lax.optimization_barrier((w, wo))
-    w = lax.all_gather(w, ("y", "c"), axis=0, tiled=True)
-    wo = pick(exchange(wo.reshape(ny, -1, wo.shape[1]), "y"), y0)
-    wo = jnp.where(zh == zh0, wo, swap(wo, "zh"))
-    w, wo = lax.optimization_barrier((w, wo))
-    wo = gather(wo, "y").reshape(-1, wo.shape[1])
-
-    q, kv = project(normed, w)
-    kv = lax.all_gather(kv, ("y", "c"), axis=0, tiled=True)
+    w = spread(w, "y").reshape(ny * part, 4 * HD)
+    q, kv = project(core, normed, w, swap(w, "c"))
+    wo = w[:, 3 * HD :].reshape(ny, nx, part // nx, HD)
+    wo = jnp.transpose(wo, (0, 2, 1, 3)).reshape(ny * part // nx, nx * HD)
+    q, kv, wo = lax.optimization_barrier((q, kv, wo))
+
+    near = spread(kv, "y").reshape(-1, 2 * HD)
     q_other = swap(q, "zh")
-    wo = gather(wo, "x")
-    wo_other = swap(wo, "c")
-    q0, q1 = jnp.where(zh == 0, q, q_other), jnp.where(zh == 0, q_other, q)
-    q_all = jnp.concatenate([q0, q1])
+    q_all = jnp.concatenate([jnp.where(zh == 0, q, q_other), jnp.where(zh == 0, q_other, q)])
+    wo = gather_by_shifts(wo, "x")
+    near, q_all, wo = lax.optimization_barrier((near, q_all, wo))
+    far = swap(near, "c")
+    wo_far = swap(wo, "c")
 
     order = block_order.reshape(2, ny, nx) * rows
     offsets = jnp.arange(half, dtype=jnp.int32)
-    halves = jnp.arange(2, dtype=jnp.int32) * half
-    kpos = pick(order, zh)[:, None, :, None] + halves[None, :, None, None] + offsets
+    kpos = (pick(order, zh)[:, :, None] + offsets).reshape(-1)
+    kpos = jnp.concatenate([kpos + c * half, kpos + (1 - c) * half])
     here = lax.dynamic_index_in_dim(order, y, 1, keepdims=False)
     qpos = here[:, :, None] + c * half + offsets
 
-    parts = attend(q_all, kv, qpos.reshape(-1, 1), kpos.reshape(1, -1), half)
+    parts = attend(q_all, near, far, qpos.reshape(-1, 1), kpos.reshape(1, -1), half)
     parts = exchange(parts, ("zh", "x")).reshape((2, nx) + parts.shape[1:])
-    terms = finish(c.reshape(1), parts, wo, wo_other)
+    terms = finish(core, parts, wo, wo_far)
     terms = exchange(terms, ("zl", "c")).reshape(-1, rows, terms.shape[2])
     return jnp.sum(terms.astype(jnp.float32), axis=0).astype(jnp.bfloat16)
 

time: 255 us -> 243 us (0.953)
  waiting for transfers between devices: 103 us -> 42.5 us
  starting transfers between devices: 48.8 us -> 106 us
  between operations: 14.1 us -> 1.57 us
  blocking collectives: 57.5 us -> 60.7 us
    all_to_all x4, waiting for transfers between devices: 78.4 us -> 13.3 us  [exchange(): return lax.all_to_all(block, axis, 0, 0, tiled=True)]
    ppermute x0 -> x16, starting transfers between devices: none -> 51.9 us  [shift(): lax.ppermute(block, axis, [(i, (i + distance) % count) for i in range(cou...]
    ppermute x0 -> x16, waiting for transfers between devices: none -> 25.3 us  [shift(): lax.ppermute(block, axis, [(i, (i + distance) % count) for i in range(cou...]
    all_gather x3 -> x0, waiting for transfers between devices: 21.3 us -> none  [the longest x1 18.9 us: shards(): w = lax.all_gather(w, ('y', 'c'), axis=0, tiled=True)]
    all_to_all x4, starting transfers between devices: 21.2 us -> 25.7 us  [exchange(): return lax.all_to_all(block, axis, 0, 0, tiled=True)]
    all_to_all x4 -> x3, blocking collectives: 57.5 us -> 60.7 us  [exchange(): return lax.all_to_all(block, axis, 0, 0, tiled=True)]
    unnamed x11 -> x20, local copies, waits for them, and re-layouts: 5.43 us -> 3.26 us
    ppermute x4 -> x5, starting transfers between devices: 27.4 us -> 28.6 us  [swap(): return lax.ppermute(block, axis, [(0, 1), (1, 0)])]
  transfers between devices with their start and end apart: 12 -> 25, of which waited for: 8 -> 9; matrix products, arithmetic and copies ran while one was open for 4% -> 4% of each run, Pallas kernels for 3% -> 4%
where the time goes in v3:
time: 243 us; the launch traced here: 242 us
  starting transfers between devices  106 us (44%)
  blocking collectives  60.7 us (25%)
  waiting for transfers between devices  42.5 us (17%)
  Pallas kernels  15.3 us (6%)
  local copies, waits for them, and re-layouts  9.62 us (4%)
  other arithmetic  6.15 us (3%)
    all_to_all x3, blocking collectives, exchange(): return lax.all_to_all(block, axis, 0, 0, tiled=True)  60.7 us
    ppermute x16, starting transfers between devices, shift(): lax.ppermute(block, axis, [(i, (i + distance) % count) for i in range(cou...  51.9 us
    ppermute x5, starting transfers between devices, swap(): return lax.ppermute(block, axis, [(0, 1), (1, 0)])  28.6 us
    all_to_all x4, starting transfers between devices, exchange(): return lax.all_to_all(block, axis, 0, 0, tiled=True)  25.7 us
    ppermute x16, waiting for transfers between devices, shift(): lax.ppermute(block, axis, [(i, (i + distance) % count) for i in range(cou...  25.3 us
    all_to_all x4, waiting for transfers between devices, exchange(): return lax.all_to_all(block, axis, 0, 0, tiled=True)  13.3 us
    pallas_call x1, Pallas kernels, attend(): pl.pallas_call(attend_kernel, grid=(nq // tile,), in_specs=[pl.BlockSpec(...  8.62 us
  transfers between devices with their start and end apart: 25, of which 9 were waited for; matrix products, arithmetic and copies ran while one was open for 4% of the time, Pallas kernels for 4%

profile of v3, /device:TPU:1, one launch (start us, length us, event | category | flops | bytes accessed | tf_op | source)
XLA Modules:
  0.0 242.0 jit_solution(7562902049001953407)
XLA Ops:
  0.0 4.7 %shard_map.64 = bf16[2,2,8,128,384]{4,3,2,1,0:T(8,128)(2,1)S(1)} custom-call(bf16[3,2,1024,256]{3,2,1,0:T(8,128)(2,1)} %bitcast.93), custom_call_target="tpu_custom_call" | custom-call | bytes 6291456 | tf_op jit(solution)/shard_map/pallas_call | solution.py:26
  4.7 13.8 %all_to_all.35 = bf16[2,2,8,128,384]{4,3,2,1,0:T(8,128)(2,1)} all-to-all(bf16[2,2,8,128,384]{4,3,2,1,0:T(8,128)(2,1)S(1)} %shard_map.64), channel_id=1, replica_groups=mesh['zh'=2,'y'=8,'x'=4,'zl'=4,'c'=2] {'c'}, dimensions={0} | all-to-all | bytes 6291456 | tf_op jit(solution)/shard_map/all_to_all | solution.py:206
  18.5 3.7 %all-to-all-start.1 = ((bf16[4,8,128,384]{3,2,1,0:T(8,128)(2,1)}), bf16[4,8,128,384]{3,2,1,0:T(8,128)(2,1)S(1)}, u32[]{:S(2)}, u32[]{:S(2)}) async-start(bf16[4,8,128,384]{3,2,1,0:T(8,128)(2,1)} %bitcast.2), calls=%async_computation.1 | async-start | bytes 6291456 | tf_op jit(solution)/shard_map/all_to_all | solution.py:206
  22.3 2.2 dynamic-slice_bitcast_fusion.1
  24.5 1.9 collective-permute-start
  26.4 3.4 %collective-permute-start.1 = (bf16[32,2048]{1,0:T(8,128)(2,1)}, bf16[32,2048]{1,0:T(8,128)(2,1)S(1)}, u32[]{:S(2)}, u32[]{:S(2)}) collective-permute-start(bf16[32,2048]{1,0:T(8,128)(2,1)} %get-tuple-element.44), channel_id=1, source_target_pairs={{0,32},{32,64},{64,96},{96,128},{128,160},{160,192},{192,224},{224... | collective-permute-start | bytes 393224 | tf_op jit(solution)/shard_map/ppermute | solution.py:220
  29.8 1.9 collective-permute-start.2
  31.7 4.3 %collective-permute-start.3 = (bf16[32,2048]{1,0:T(8,128)(2,1)}, bf16[32,2048]{1,0:T(8,128)(2,1)}, u32[]{:S(2)}, u32[]{:S(2)}) collective-permute-start(bf16[32,2048]{1,0:T(8,128)(2,1)} %get-tuple-element.42), channel_id=1, source_target_pairs={{0,64},{32,96},{64,128},{96,160},{128,192},{160,224},{192,0},{224,... | collective-permute-start | bytes 393224 | tf_op jit(solution)/shard_map/ppermute | solution.py:220
  36.0 2.9 %collective-permute-start.4 = (bf16[32,2048]{1,0:T(8,128)(2,1)}, bf16[32,2048]{1,0:T(8,128)(2,1)}, u32[]{:S(2)}, u32[]{:S(2)}) collective-permute-start(bf16[32,2048]{1,0:T(8,128)(2,1)} %get-tuple-element.41), channel_id=1, source_target_pairs={{0,160},{32,192},{64,224},{96,0},{128,32},{160,64},{192,96},{224,1... | collective-permute-start | bytes 393224 | tf_op jit(solution)/shard_map/ppermute | solution.py:220
  38.8 1.1 fusion
  40.0 4.2 %collective-permute-start.5 = (bf16[32,2048]{1,0:T(8,128)(2,1)}, bf16[32,2048]{1,0:T(8,128)(2,1)}, u32[]{:S(2)}, u32[]{:S(2)}) collective-permute-start(bf16[32,2048]{1,0:T(8,128)(2,1)} %get-tuple-element.40), channel_id=1, source_target_pairs={{0,96},{32,128},{64,160},{96,192},{128,224},{160,0},{192,32},{224,... | collective-permute-start | bytes 393224 | tf_op jit(solution)/shard_map/ppermute | solution.py:220
  44.9 4.1 %collective-permute-start.6 = (bf16[32,2048]{1,0:T(8,128)(2,1)}, bf16[32,2048]{1,0:T(8,128)(2,1)}, u32[]{:S(2)}, u32[]{:S(2)}) collective-permute-start(bf16[32,2048]{1,0:T(8,128)(2,1)} %get-tuple-element.39), channel_id=1, source_target_pairs={{0,128},{32,160},{64,192},{96,224},{128,0},{160,32},{192,64},{224,... | collective-permute-start | bytes 393224 | tf_op jit(solution)/shard_map/ppermute | solution.py:220
  49.0 1.1 fusion.2
  50.9 8.0 %collective-permute-done.5 = bf16[32,2048]{1,0:T(8,128)(2,1)} collective-permute-done((bf16[32,2048]{1,0:T(8,128)(2,1)}, bf16[32,2048]{1,0:T(8,128)(2,1)}, u32[]{:S(2)}, u32[]{:S(2)}) %collective-permute-start.5) | collective-permute-done | bytes 131104 | tf_op jit(solution)/shard_map/ppermute | solution.py:220
  58.9 1.7 fusion.8
  60.6 1.0 dynamic-slice_bitcast_fusion
  61.5 7.6 %all-to-all-start.2 = ((bf16[8,128,384]{2,1,0:T(8,128)(2,1)}), bf16[8,128,384]{2,1,0:T(8,128)(2,1)S(1)}, u32[]{:S(2)}, u32[]{:S(2)}) async-start(bf16[8,128,384]{2,1,0:T(8,128)(2,1)} %dynamic-slice_bitcast_fusion), calls=%async_computation.2 | async-start | bytes 1572864 | tf_op jit(solution)/shard_map/all_to_all | solution.py:206
  69.2 4.5 %collective-permute-start.12 = (bf16[80,2048]{1,0:T(8,128)(2,1)S(1)}, bf16[80,2048]{1,0:T(8,128)(2,1)S(1)}, u32[]{:S(2)}, u32[]{:S(2)}) collective-permute-start(bf16[80,2048]{1,0:T(8,128)(2,1)S(1)} %fusion.2), channel_id=1, source_target_pairs={{0,24},{8,0},{16,8},{24,16},{1,25},{9,1},{17,9},{25,17},{2,26},{10... | collective-permute-start | bytes 983048 | tf_op jit(solution)/shard_map/ppermute | solution.py:220
  73.7 2.5 %collective-permute-start.11 = (bf16[80,2048]{1,0:T(8,128)(2,1)S(1)}, bf16[80,2048]{1,0:T(8,128)(2,1)S(1)}, u32[]{:S(2)}, u32[]{:S(2)}) collective-permute-start(bf16[80,2048]{1,0:T(8,128)(2,1)S(1)} %fusion.2), channel_id=1, source_target_pairs={{0,16},{8,24},{16,0},{24,8},{1,17},{9,25},{17,1},{25,9},{2,18},{10... | collective-permute-start | bytes 983048 | tf_op jit(solution)/shard_map/ppermute | solution.py:220
  76.2 2.5 %collective-permute-start.10 = (bf16[80,2048]{1,0:T(8,128)(2,1)S(1)}, bf16[80,2048]{1,0:T(8,128)(2,1)S(1)}, u32[]{:S(2)}, u32[]{:S(2)}) collective-permute-start(bf16[80,2048]{1,0:T(8,128)(2,1)S(1)} %fusion.2), channel_id=1, source_target_pairs={{0,8},{8,16},{16,24},{24,0},{1,9},{9,17},{17,25},{25,1},{2,10},{10... | collective-permute-start | bytes 983048 | tf_op jit(solution)/shard_map/ppermute | solution.py:220
  79.1 4.0 %collective-permute-start.7 = (bf16[32,512]{1,0:T(8,128)(2,1)S(1)}, bf16[32,512]{1,0:T(8,128)(2,1)S(1)}, u32[]{:S(2)}, u32[]{:S(2)}) collective-permute-start(bf16[32,512]{1,0:T(8,128)(2,1)S(1)} %bitcast.114), channel_id=1, source_target_pairs={{0,24},{8,0},{16,8},{24,16},{1,25},{9,1},{17,9},{25,17},{2,26},{10... | collective-permute-start | bytes 98312 | tf_op jit(solution)/shard_map/ppermute | solution.py:220
  83.1 1.9 collective-permute-start.8
  85.0 2.5 %collective-permute-done.7 = bf16[32,512]{1,0:T(8,128)(2,1)S(1)} collective-permute-done((bf16[32,512]{1,0:T(8,128)(2,1)S(1)}, bf16[32,512]{1,0:T(8,128)(2,1)S(1)}, u32[]{:S(2)}, u32[]{:S(2)}) %collective-permute-start.7) | collective-permute-done | bytes 32800 | tf_op jit(solution)/shard_map/ppermute | solution.py:220
  87.5 4.4 %collective-permute-start.9 = (bf16[32,512]{1,0:T(8,128)(2,1)S(1)}, bf16[32,512]{1,0:T(8,128)(2,1)S(1)}, u32[]{:S(2)}, u32[]{:S(2)}) collective-permute-start(bf16[32,512]{1,0:T(8,128)(2,1)S(1)} %bitcast.113), channel_id=1, source_target_pairs={{0,16},{8,24},{16,0},{24,8},{1,17},{9,25},{17,1},{25,9},{2,18},{10... | collective-permute-start | bytes 98312 | tf_op jit(solution)/shard_map/ppermute | solution.py:220
  92.1 2.7 %collective-permute-done.8 = bf16[32,512]{1,0:T(8,128)(2,1)S(1)} collective-permute-done((bf16[32,512]{1,0:T(8,128)(2,1)S(1)}, bf16[32,512]{1,0:T(8,128)(2,1)S(1)}, u32[]{:S(2)}, u32[]{:S(2)}) %collective-permute-start.8) | collective-permute-done | bytes 32800 | tf_op jit(solution)/shard_map/ppermute | solution.py:220
  95.4 7.4 %collective-permute-start.13 = (bf16[128,512]{1,0:T(8,128)(2,1)S(1)}, bf16[128,512]{1,0:T(8,128)(2,1)S(1)}, u32[]{:S(2)}, u32[]{:S(2)}) collective-permute-start(bf16[128,512]{1,0:T(8,128)(2,1)S(1)} %pad_maximum_fusion.5), channel_id=1, source_target_pairs={{0,256},{256,0},{1,257},{257,1},{2,258},{258,2},{3,259},{259,3},{4... | collective-permute-start | bytes 393224 | tf_op jit(solution)/shard_map/ppermute | solution.py:202
  102.9 2.4 collective-permute-done.13
  105.4 29.7 %all_to_all.36 = bf16[8,128,512]{2,1,0:T(8,128)(2,1)S(1)} all-to-all(bf16[8,128,512]{2,1,0:T(8,128)(2,1)S(1)} %broadcast_in_dim.4), channel_id=1, replica_groups=mesh['zh'=2,'y'=8,'x'=4,'zl'=4,'c'=2] {'y'}, dimensions={0} | all-to-all | bytes 2097152 | tf_op jit(solution)/shard_map/all_to_all | solution.py:206
  135.1 8.3 %collective-permute-start.14 = (bf16[1024,512]{1,0:T(8,128)(2,1)S(1)}, bf16[1024,512]{1,0:T(8,128)(2,1)S(1)}, u32[]{:S(2)}, u32[]{:S(2)}) collective-permute-start(bf16[1024,512]{1,0:T(8,128)(2,1)S(1)} %bitcast.86), channel_id=1, source_target_pairs={{0,1},{1,0},{2,3},{3,2},{4,5},{5,4},{6,7},{7,6},{8,9},{9,8},{10,11... | collective-permute-start | bytes 3145736 | tf_op jit(solution)/shard_map/ppermute | solution.py:202
  144.2 1.5 collective-permute-done.14.w_ref
  146.2 1.2 broadcast_in_dim.5
  147.4 3.6 %all-to-all-start.4 = ((bf16[8,320,256]{2,1,0:T(8,128)(2,1)}), bf16[8,320,256]{2,1,0:T(8,128)(2,1)S(1)}, u32[]{:S(2)}, u32[]{:S(2)}) async-start(bf16[8,320,256]{2,1,0:T(8,128)(2,1)} %broadcast_in_dim.5), calls=%async_computation.4 | async-start | bytes 2621440 | tf_op jit(solution)/shard_map/all_to_all | solution.py:206
  151.0 8.6 %collective-permute-start.15 = (bf16[320,128]{1,0:T(8,128)(2,1)S(1)}, bf16[320,128]{1,0:T(8,128)(2,1)S(1)}, u32[]{:S(2)}, u32[]{:S(2)}) collective-permute-start(bf16[320,128]{1,0:T(8,128)(2,1)S(1)} %get-tuple-element.26), channel_id=1, source_target_pairs={{0,256},{256,0},{1,257},{257,1},{2,258},{258,2},{3,259},{259,3},{4... | collective-permute-start | bytes 245768 | tf_op jit(solution)/shard_map/ppermute | solution.py:202
  159.5 5.0 %collective-permute-start.18 = (bf16[256,512]{1,0:T(8,128)(2,1)S(1)}, bf16[256,512]{1,0:T(8,128)(2,1)S(1)}, u32[]{:S(2)}, u32[]{:S(2)}) collective-permute-start(bf16[256,512]{1,0:T(8,128)(2,1)S(1)} %bitcast.100), channel_id=1, source_target_pairs={{0,24},{8,0},{16,8},{24,16},{1,25},{9,1},{17,9},{25,17},{2,26},{10... | collective-permute-start | bytes 786440 | tf_op jit(solution)/shard_map/ppermute | solution.py:220
  164.6 1.9 collective-permute-start.17
  166.5 2.5 %collective-permute-start.16 = (bf16[256,512]{1,0:T(8,128)(2,1)S(1)}, bf16[256,512]{1,0:T(8,128)(2,1)S(1)}, u32[]{:S(2)}, u32[]{:S(2)}) collective-permute-start(bf16[256,512]{1,0:T(8,128)(2,1)S(1)} %bitcast.102), channel_id=1, source_target_pairs={{0,8},{8,16},{16,24},{24,0},{1,9},{9,17},{17,25},{25,1},{2,10},{10... | collective-permute-start | bytes 786440 | tf_op jit(solution)/shard_map/ppermute | solution.py:220
  169.7 5.3 %collective-permute-done.18 = bf16[256,512]{1,0:T(8,128)(2,1)S(1)} collective-permute-done((bf16[256,512]{1,0:T(8,128)(2,1)S(1)}, bf16[256,512]{1,0:T(8,128)(2,1)S(1)}, u32[]{:S(2)}, u32[]{:S(2)}) %collective-permute-start.18) | collective-permute-done | bytes 262176 | tf_op jit(solution)/shard_map/ppermute | solution.py:220
  175.1 6.8 %collective-permute-done.16 = bf16[256,512]{1,0:T(8,128)(2,1)S(1)} collective-permute-done((bf16[256,512]{1,0:T(8,128)(2,1)S(1)}, bf16[256,512]{1,0:T(8,128)(2,1)S(1)}, u32[]{:S(2)}, u32[]{:S(2)}) %collective-permute-start.16) | collective-permute-done | bytes 262176 | tf_op jit(solution)/shard_map/ppermute | solution.py:220
  182.2 3.5 %all-to-all-done.4 = bf16[8,320,256]{2,1,0:T(8,128)(2,1)S(1)} async-done(((bf16[8,320,256]{2,1,0:T(8,128)(2,1)}), bf16[8,320,256]{2,1,0:T(8,128)(2,1)S(1)}, u32[]{:S(2)}, u32[]{:S(2)}) %all-to-all-start.4) | async-done | bytes 1310752 | tf_op jit(solution)/shard_map/all_to_all | solution.py:206
  185.7 2.4 collective-permute-start.19
  188.2 1.9 collective-permute-start.20
  191.4 1.0 copy-done
  192.4 0.9 copy-done.2
  193.3 8.6 %shard_map.67 = bf16[8,96,128]{2,1,0:T(8,128)(2,1)S(1)} custom-call(bf16[640,128]{1,0:T(8,128)(2,1)S(1)} %copy-done.2, bf16[2560,256]{1,0:T(8,128)(2,1)S(1)} %bitcast.90, bf16[2560,256]{1,0:T(8,128)(2,1)} %collective-permute-done.19.far_ref, s32[640,1]{1,0:T(8,128)S(1)} %copy-done, s32[1,5120]{1,0:T(1,128)S(1)} %bitcast.92), custom_call_target="tpu_custom_call" | custom-call | flops 1677721600 | bytes 2621440 | tf_op jit(solution)/shard_map/pallas_call | solution.py:137
  202.6 10.8 %all-to-all-start.5 = ((bf16[8,96,128]{2,1,0:T(8,128)(2,1)}), bf16[8,96,128]{2,1,0:T(8,128)(2,1)S(1)}, u32[]{:S(2)}, u32[]{:S(2)}) async-start(bf16[8,96,128]{2,1,0:T(8,128)(2,1)} %copy-done.1), calls=%async_computation.5 | async-start | bytes 393216 | tf_op jit(solution)/shard_map/all_to_all | solution.py:206
  213.4 9.8 %all-to-all-done.5 = bf16[8,96,128]{2,1,0:T(8,128)(2,1)S(1)} async-done(((bf16[8,96,128]{2,1,0:T(8,128)(2,1)}), bf16[8,96,128]{2,1,0:T(8,128)(2,1)S(1)}, u32[]{:S(2)}, u32[]{:S(2)}) %all-to-all-start.5) | async-done | bytes 196640 | tf_op jit(solution)/shard_map/all_to_all | solution.py:206
  223.2 0.9 shard_map.68
  224.1 17.2 %all_to_all.37 = bf16[8,80,256]{2,1,0:T(8,128)(2,1)S(1)} all-to-all(bf16[8,80,256]{2,1,0:T(8,128)(2,1)S(1)} %shard_map.68), channel_id=1, replica_groups=mesh['zh'=2,'y'=8,'x'=4,'zl'=4,'c'=2] {'zl','c'}, dimensions={0} | all-to-all | bytes 655360 | tf_op jit(solution)/shard_map/all_to_all | solution.py:206
  (67 shorter events, 6.7 us)
Async XLA Ops:
  18.5 42.1 %all-to-all-start.1 = ((bf16[4,8,128,384]{3,2,1,0:T(8,128)(2,1)}), bf16[4,8,128,384]{3,2,1,0:T(8,128)(2,1)S(1)}, u32[]{:S(2)}, u32[]{:S(2)}) async-start(bf16[4,8,128,384]{3,2,1,0:T(8,128)(2,1)} %bitcast.2), calls=%async_computation.1 | async-start | bytes 6291456 | tf_op jit(solution)/shard_map/all_to_all | solution.py:206
  22.2 26.8 %copy-start.6 = (f32[2048]{0:T(1024)S(1)}, f32[2048]{0:T(1024)}, u32[]{:S(2)}) copy-start(f32[2048]{0:T(1024)} %param.7) | copy-start | bytes 24580
  24.5 15.5 %collective-permute-start = (bf16[32,2048]{1,0:T(8,128)(2,1)}, bf16[32,2048]{1,0:T(8,128)(2,1)S(1)}, u32[]{:S(2)}, u32[]{:S(2)}) collective-permute-start(bf16[32,2048]{1,0:T(8,128)(2,1)} %get-tuple-element.45), channel_id=1, source_target_pairs={{0,224},{32,0},{64,32},{96,64},{128,96},{160,128},{192,160},{224,1... | collective-permute-start | bytes 393224 | tf_op jit(solution)/shard_map/ppermute | solution.py:220
  26.4 17.9 %collective-permute-start.1 = (bf16[32,2048]{1,0:T(8,128)(2,1)}, bf16[32,2048]{1,0:T(8,128)(2,1)S(1)}, u32[]{:S(2)}, u32[]{:S(2)}) collective-permute-start(bf16[32,2048]{1,0:T(8,128)(2,1)} %get-tuple-element.44), channel_id=1, source_target_pairs={{0,32},{32,64},{64,96},{96,128},{128,160},{160,192},{192,224},{224... | collective-permute-start | bytes 393224 | tf_op jit(solution)/shard_map/ppermute | solution.py:220
  29.8 21.1 %collective-permute-start.2 = (bf16[32,2048]{1,0:T(8,128)(2,1)}, bf16[32,2048]{1,0:T(8,128)(2,1)}, u32[]{:S(2)}, u32[]{:S(2)}) collective-permute-start(bf16[32,2048]{1,0:T(8,128)(2,1)} %get-tuple-element.43), channel_id=1, source_target_pairs={{0,192},{32,224},{64,0},{96,32},{128,64},{160,96},{192,128},{224,1... | collective-permute-start | bytes 393224 | tf_op jit(solution)/shard_map/ppermute | solution.py:220
  31.7 19.2 %collective-permute-start.3 = (bf16[32,2048]{1,0:T(8,128)(2,1)}, bf16[32,2048]{1,0:T(8,128)(2,1)}, u32[]{:S(2)}, u32[]{:S(2)}) collective-permute-start(bf16[32,2048]{1,0:T(8,128)(2,1)} %get-tuple-element.42), channel_id=1, source_target_pairs={{0,64},{32,96},{64,128},{96,160},{128,192},{160,224},{192,0},{224,... | collective-permute-start | bytes 393224 | tf_op jit(solution)/shard_map/ppermute | solution.py:220
  36.0 14.9 %collective-permute-start.4 = (bf16[32,2048]{1,0:T(8,128)(2,1)}, bf16[32,2048]{1,0:T(8,128)(2,1)}, u32[]{:S(2)}, u32[]{:S(2)}) collective-permute-start(bf16[32,2048]{1,0:T(8,128)(2,1)} %get-tuple-element.41), channel_id=1, source_target_pairs={{0,160},{32,192},{64,224},{96,0},{128,32},{160,64},{192,96},{224,1... | collective-permute-start | bytes 393224 | tf_op jit(solution)/shard_map/ppermute | solution.py:220
  40.0 4.3 %copy-start.4 = (bf16[32,2048]{1,0:T(8,128)(2,1)}, bf16[32,2048]{1,0:T(8,128)(2,1)S(1)}, u32[]{:S(2)}) copy-start(bf16[32,2048]{1,0:T(8,128)(2,1)S(1)} %collective-permute-done) | copy-start | bytes 393220
  40.0 18.8 %collective-permute-start.5 = (bf16[32,2048]{1,0:T(8,128)(2,1)}, bf16[32,2048]{1,0:T(8,128)(2,1)}, u32[]{:S(2)}, u32[]{:S(2)}) collective-permute-start(bf16[32,2048]{1,0:T(8,128)(2,1)} %get-tuple-element.40), channel_id=1, source_target_pairs={{0,96},{32,128},{64,160},{96,192},{128,224},{160,0},{192,32},{224,... | collective-permute-start | bytes 393224 | tf_op jit(solution)/shard_map/ppermute | solution.py:220
  44.3 0.7 copy-start.5
  44.9 14.0 %collective-permute-start.6 = (bf16[32,2048]{1,0:T(8,128)(2,1)}, bf16[32,2048]{1,0:T(8,128)(2,1)}, u32[]{:S(2)}, u32[]{:S(2)}) collective-permute-start(bf16[32,2048]{1,0:T(8,128)(2,1)} %get-tuple-element.39), channel_id=1, source_target_pairs={{0,128},{32,160},{64,192},{96,224},{128,0},{160,32},{192,64},{224,... | collective-permute-start | bytes 393224 | tf_op jit(solution)/shard_map/ppermute | solution.py:220
  61.5 17.1 %copy-start.3 = (bf16[32,2048]{1,0:T(8,128)(2,1)S(1)}, bf16[32,2048]{1,0:T(8,128)(2,1)}, u32[]{:S(2)}) copy-start(bf16[32,2048]{1,0:T(8,128)(2,1)} %fusion.8) | copy-start | bytes 393220
  61.5 33.8 %all-to-all-start.2 = ((bf16[8,128,384]{2,1,0:T(8,128)(2,1)}), bf16[8,128,384]{2,1,0:T(8,128)(2,1)S(1)}, u32[]{:S(2)}, u32[]{:S(2)}) async-start(bf16[8,128,384]{2,1,0:T(8,128)(2,1)} %dynamic-slice_bitcast_fusion), calls=%async_computation.2 | async-start | bytes 1572864 | tf_op jit(solution)/shard_map/all_to_all | solution.py:206
  69.2 25.7 %collective-permute-start.12 = (bf16[80,2048]{1,0:T(8,128)(2,1)S(1)}, bf16[80,2048]{1,0:T(8,128)(2,1)S(1)}, u32[]{:S(2)}, u32[]{:S(2)}) collective-permute-start(bf16[80,2048]{1,0:T(8,128)(2,1)S(1)} %fusion.2), channel_id=1, source_target_pairs={{0,24},{8,0},{16,8},{24,16},{1,25},{9,1},{17,9},{25,17},{2,26},{10... | collective-permute-start | bytes 983048 | tf_op jit(solution)/shard_map/ppermute | solution.py:220
  73.7 21.2 %collective-permute-start.11 = (bf16[80,2048]{1,0:T(8,128)(2,1)S(1)}, bf16[80,2048]{1,0:T(8,128)(2,1)S(1)}, u32[]{:S(2)}, u32[]{:S(2)}) collective-permute-start(bf16[80,2048]{1,0:T(8,128)(2,1)S(1)} %fusion.2), channel_id=1, source_target_pairs={{0,16},{8,24},{16,0},{24,8},{1,17},{9,25},{17,1},{25,9},{2,18},{10... | collective-permute-start | bytes 983048 | tf_op jit(solution)/shard_map/ppermute | solution.py:220
  76.2 18.7 %collective-permute-start.10 = (bf16[80,2048]{1,0:T(8,128)(2,1)S(1)}, bf16[80,2048]{1,0:T(8,128)(2,1)S(1)}, u32[]{:S(2)}, u32[]{:S(2)}) collective-permute-start(bf16[80,2048]{1,0:T(8,128)(2,1)S(1)} %fusion.2), channel_id=1, source_target_pairs={{0,8},{8,16},{16,24},{24,0},{1,9},{9,17},{17,25},{25,1},{2,10},{10... | collective-permute-start | bytes 983048 | tf_op jit(solution)/shard_map/ppermute | solution.py:220
  79.1 8.4 %collective-permute-start.7 = (bf16[32,512]{1,0:T(8,128)(2,1)S(1)}, bf16[32,512]{1,0:T(8,128)(2,1)S(1)}, u32[]{:S(2)}, u32[]{:S(2)}) collective-permute-start(bf16[32,512]{1,0:T(8,128)(2,1)S(1)} %bitcast.114), channel_id=1, source_target_pairs={{0,24},{8,0},{16,8},{24,16},{1,25},{9,1},{17,9},{25,17},{2,26},{10... | collective-permute-start | bytes 98312 | tf_op jit(solution)/shard_map/ppermute | solution.py:220
  83.1 11.7 %collective-permute-start.8 = (bf16[32,512]{1,0:T(8,128)(2,1)S(1)}, bf16[32,512]{1,0:T(8,128)(2,1)S(1)}, u32[]{:S(2)}, u32[]{:S(2)}) collective-permute-start(bf16[32,512]{1,0:T(8,128)(2,1)S(1)} %bitcast.112), channel_id=1, source_target_pairs={{0,8},{8,16},{16,24},{24,0},{1,9},{9,17},{17,25},{25,1},{2,10},{10... | collective-permute-start | bytes 98312 | tf_op jit(solution)/shard_map/ppermute | solution.py:220
  87.5 7.3 %collective-permute-start.9 = (bf16[32,512]{1,0:T(8,128)(2,1)S(1)}, bf16[32,512]{1,0:T(8,128)(2,1)S(1)}, u32[]{:S(2)}, u32[]{:S(2)}) collective-permute-start(bf16[32,512]{1,0:T(8,128)(2,1)S(1)} %bitcast.113), channel_id=1, source_target_pairs={{0,16},{8,24},{16,0},{24,8},{1,17},{9,25},{17,1},{25,9},{2,18},{10... | collective-permute-start | bytes 98312 | tf_op jit(solution)/shard_map/ppermute | solution.py:220
  95.4 9.8 %collective-permute-start.13 = (bf16[128,512]{1,0:T(8,128)(2,1)S(1)}, bf16[128,512]{1,0:T(8,128)(2,1)S(1)}, u32[]{:S(2)}, u32[]{:S(2)}) collective-permute-start(bf16[128,512]{1,0:T(8,128)(2,1)S(1)} %pad_maximum_fusion.5), channel_id=1, source_target_pairs={{0,256},{256,0},{1,257},{257,1},{2,258},{258,2},{3,259},{259,3},{4... | collective-permute-start | bytes 393224 | tf_op jit(solution)/shard_map/ppermute | solution.py:202
  135.1 10.6 %collective-permute-start.14 = (bf16[1024,512]{1,0:T(8,128)(2,1)S(1)}, bf16[1024,512]{1,0:T(8,128)(2,1)S(1)}, u32[]{:S(2)}, u32[]{:S(2)}) collective-permute-start(bf16[1024,512]{1,0:T(8,128)(2,1)S(1)} %bitcast.86), channel_id=1, source_target_pairs={{0,1},{1,0},{2,3},{3,2},{4,5},{5,4},{6,7},{7,6},{8,9},{9,8},{10,11... | collective-permute-start | bytes 3145736 | tf_op jit(solution)/shard_map/ppermute | solution.py:202
  147.4 38.3 %all-to-all-start.4 = ((bf16[8,320,256]{2,1,0:T(8,128)(2,1)}), bf16[8,320,256]{2,1,0:T(8,128)(2,1)S(1)}, u32[]{:S(2)}, u32[]{:S(2)}) async-start(bf16[8,320,256]{2,1,0:T(8,128)(2,1)} %broadcast_in_dim.5), calls=%async_computation.4 | async-start | bytes 2621440 | tf_op jit(solution)/shard_map/all_to_all | solution.py:206
  151.0 18.1 %collective-permute-start.15 = (bf16[320,128]{1,0:T(8,128)(2,1)S(1)}, bf16[320,128]{1,0:T(8,128)(2,1)S(1)}, u32[]{:S(2)}, u32[]{:S(2)}) collective-permute-start(bf16[320,128]{1,0:T(8,128)(2,1)S(1)} %get-tuple-element.26), channel_id=1, source_target_pairs={{0,256},{256,0},{1,257},{257,1},{2,258},{258,2},{3,259},{259,3},{4... | collective-permute-start | bytes 245768 | tf_op jit(solution)/shard_map/ppermute | solution.py:202
  159.5 15.5 %collective-permute-start.18 = (bf16[256,512]{1,0:T(8,128)(2,1)S(1)}, bf16[256,512]{1,0:T(8,128)(2,1)S(1)}, u32[]{:S(2)}, u32[]{:S(2)}) collective-permute-start(bf16[256,512]{1,0:T(8,128)(2,1)S(1)} %bitcast.100), channel_id=1, source_target_pairs={{0,24},{8,0},{16,8},{24,16},{1,25},{9,1},{17,9},{25,17},{2,26},{10... | collective-permute-start | bytes 786440 | tf_op jit(solution)/shard_map/ppermute | solution.py:220
  164.6 10.5 %collective-permute-start.17 = (bf16[256,512]{1,0:T(8,128)(2,1)S(1)}, bf16[256,512]{1,0:T(8,128)(2,1)S(1)}, u32[]{:S(2)}, u32[]{:S(2)}) collective-permute-start(bf16[256,512]{1,0:T(8,128)(2,1)S(1)} %bitcast.101), channel_id=1, source_target_pairs={{0,16},{8,24},{16,0},{24,8},{1,17},{9,25},{17,1},{25,9},{2,18},{10... | collective-permute-start | bytes 786440 | tf_op jit(solution)/shard_map/ppermute | solution.py:220
  166.5 15.3 %collective-permute-start.16 = (bf16[256,512]{1,0:T(8,128)(2,1)S(1)}, bf16[256,512]{1,0:T(8,128)(2,1)S(1)}, u32[]{:S(2)}, u32[]{:S(2)}) collective-permute-start(bf16[256,512]{1,0:T(8,128)(2,1)S(1)} %bitcast.102), channel_id=1, source_target_pairs={{0,8},{8,16},{16,24},{24,0},{1,9},{9,17},{17,25},{25,1},{2,10},{10... | collective-permute-start | bytes 786440 | tf_op jit(solution)/shard_map/ppermute | solution.py:220
  182.1 6.0 %copy-start.7 = (s32[64]{0:T(128)S(1)}, s32[64]{0:T(128)}, u32[]{:S(2)}) copy-start(s32[64]{0:T(128)} %param.11) | copy-start | bytes 772
  185.7 5.7 %collective-permute-start.19 = (bf16[2560,256]{1,0:T(8,128)(2,1)S(1)}, bf16[2560,256]{1,0:T(8,128)(2,1)}, u32[]{:S(2)}, u32[]{:S(2)}) collective-permute-start(bf16[2560,256]{1,0:T(8,128)(2,1)S(1)} %bitcast.89), channel_id=1, source_target_pairs={{0,1},{1,0},{2,3},{3,2},{4,5},{5,4},{6,7},{7,6},{8,9},{9,8},{10,11... | collective-permute-start | bytes 3932168 | tf_op jit(solution)/shard_map/ppermute | solution.py:202
  188.2 25.2 %collective-permute-start.20 = (bf16[4,256,512]{2,1,0:T(8,128)(2,1)S(1)}, bf16[4,256,512]{2,1,0:T(8,128)(2,1)S(1)}, u32[]{:S(2)}, u32[]{:S(2)}) collective-permute-start(bf16[4,256,512]{2,1,0:T(8,128)(2,1)S(1)} %pad_maximum_fusion.3.mine_ref), channel_id=1, source_target_pairs={{0,1},{1,0},{2,3},{3,2},{4,5},{5,4},{6,7},{7,6},{8,9},{9,8},{10,11... | collective-permute-start | bytes 3145736 | tf_op jit(solution)/shard_map/ppermute | solution.py:202
  191.4 1.0 copy-start
  192.4 0.9 copy-start.2
  201.9 0.7 copy-start.1
  202.6 20.6 %all-to-all-start.5 = ((bf16[8,96,128]{2,1,0:T(8,128)(2,1)}), bf16[8,96,128]{2,1,0:T(8,128)(2,1)S(1)}, u32[]{:S(2)}, u32[]{:S(2)}) async-start(bf16[8,96,128]{2,1,0:T(8,128)(2,1)} %copy-done.1), calls=%async_computation.5 | async-start | bytes 393216 | tf_op jit(solution)/shard_map/all_to_all | solution.py:206

commit v4 on v3

--- a/solution.py
+++ b/solution.py
@@ -14,24 +14,32 @@
 LIMIT = pltpu.CompilerParams(vmem_limit_bytes=48 * 1024 * 1024)
 
 
-def fold_kernel(w_ref, o_ref):
-    for c in range(2):
-        for h in range(2):
+def fold_kernel(w_ref, wo_ref, out_ref):
+    span, cols = wo_ref.shape[0], wo_ref.shape[1] // 4
+    for h in range(2):
+        for r in range(2):
             for j in range(3):
-                o_ref[c, h, 0, :, j * HD : (j + 1) * HD] = w_ref[j, c, :, h * HD : (h + 1) * HD]
-
-
-def fold(w, ny):
+                out_ref[2 * h + r, 0, :, j * HD : (j + 1) * HD] = w_ref[j, r, :, h * HD : (h + 1) * HD]
+    for x in range(4):
+        for k in range(4):
+            at = x * cols + k * HD
+            out_ref[x, 0, k * span : (k + 1) * span, 3 * HD :] = wo_ref[:, at : at + HD]
+
+
+def fold(w, wo, ny):
     part = w.shape[1] // (2 * ny)
     return pl.pallas_call(
         fold_kernel,
         grid=(ny,),
-        in_specs=[pl.BlockSpec((3, 2, part, 2 * HD), lambda i: (0, 0, i, 0))],
-        out_specs=pl.BlockSpec((2, 2, 1, part, 3 * HD), lambda i: (0, 0, i, 0, 0)),
-        out_shape=jax.ShapeDtypeStruct((2, 2, ny, part, 3 * HD), w.dtype),
-        compiler_params=LIMIT,
-        cost_estimate=pl.CostEstimate(flops=0, bytes_accessed=4 * w.size, transcendentals=0),
-    )(w.reshape(3, 2, ny * part, 2 * HD))
+        in_specs=[
+            pl.BlockSpec((3, 2, part, 2 * HD), lambda i: (0, 0, i, 0)),
+            pl.BlockSpec((wo.shape[0] // ny, wo.shape[1]), lambda i: (i, 0)),
+        ],
+        out_specs=pl.BlockSpec((4, 1, part, 4 * HD), lambda i: (0, i, 0, 0)),
+        out_shape=jax.ShapeDtypeStruct((4, ny, part, 4 * HD), w.dtype),
+        compiler_params=LIMIT,
+        cost_estimate=pl.CostEstimate(flops=0, bytes_accessed=4 * (w.size + wo.size), transcendentals=0),
+    )(w.reshape(3, 2, ny * part, 2 * HD), wo)
 
 
 def near_kernel(c_ref, x_ref, w_ref, out_ref):
@@ -84,16 +92,21 @@
     return first, second, rest - second
 
 
-def attend_kernel(q_ref, near_ref, far_ref, qpos_ref, kpos_ref, o_ref, s_ref):
+def attend_kernel(start_ref, q_ref, near_ref, far_ref, kpos_ref, o_ref, s_ref):
     factor = float(np.log2(np.e) / HD**0.5)
     rows = q_ref.shape[0]
+    blocks, half = o_ref.shape[0], o_ref.shape[1] - EXTRA
+    row = lax.broadcasted_iota(jnp.int32, (rows, 1), 0)
+    first = blocks * pl.program_id(0)
+    qpos = row + start_ref[first]
+    for b in range(1, blocks):
+        qpos = jnp.where(row < b * half, qpos, row - b * half + start_ref[first + b])
     pieces = [
         (ref, j * CHUNK, i * ref.shape[0] + j * CHUNK)
         for i, ref in enumerate((near_ref, far_ref))
         for j in range(ref.shape[0] // CHUNK)
     ]
     q = q_ref[...]
-    qpos = qpos_ref[...]
     high = jnp.full((rows, HD), HIDE, jnp.float32)
     for ref, at, column in pieces:
         span = pl.ds(column, CHUNK)
@@ -122,7 +135,6 @@
     stat = jnp.zeros((rows, HD), jnp.float32)
     for k, piece in enumerate(three_parts(top) + three_parts(total)):
         stat = jnp.where(lane == k, piece, stat)
-    blocks, half = o_ref.shape[0], o_ref.shape[1] - EXTRA
     for b in range(blocks):
         o_ref[b, :half, :] = o[b * half : (b + 1) * half].astype(o_ref.dtype)
         block = jnp.concatenate(
@@ -131,17 +143,17 @@
         o_ref[b, half:, :] = block.T[:EXTRA].astype(o_ref.dtype)
 
 
-def attend(q, near, far, qpos, kpos, half):
+def attend(start, q, near, far, kpos, half):
     nq, nk = q.shape[0], 2 * near.shape[0]
     tile = 2 * half
     return pl.pallas_call(
         attend_kernel,
         grid=(nq // tile,),
         in_specs=[
+            pl.BlockSpec(memory_space=pltpu.SMEM),
             pl.BlockSpec((tile, HD), lambda i: (i, 0)),
             pl.BlockSpec((nk // 2, 2 * HD), lambda i: (0, 0)),
             pl.BlockSpec((nk // 2, 2 * HD), lambda i: (0, 0)),
-            pl.BlockSpec((tile, 1), lambda i: (i, 0)),
             pl.BlockSpec((1, nk), lambda i: (0, 0)),
         ],
         out_specs=pl.BlockSpec((2, half + EXTRA, HD), lambda i: (i, 0, 0)),
@@ -151,35 +163,36 @@
         cost_estimate=pl.CostEstimate(
             flops=4 * nq * nk * HD, bytes_accessed=nk * HD * 4, transcendentals=nq * nk
         ),
-    )(q, near, far, qpos, kpos)
-
-
-def finish_kernel(c_ref, part_ref, mine_ref, other_ref, out_ref):
-    heads, half = part_ref.shape[1], part_ref.shape[2] - EXTRA
+    )(start, q, near, far, kpos)
+
+
+def finish_kernel(c_ref, part_ref, near_ref, far_ref, out_ref):
+    count, nx, half = part_ref.shape[0], part_ref.shape[1], part_ref.shape[2] - EXTRA
     context = []
-    for h in range(heads):
-        weight, values = [], []
-        for k in range(2):
-            stat = part_ref[k, h, half:, :].astype(jnp.float32)
+    for x in range(nx):
+        tops, totals = [], []
+        for k in range(count):
+            stat = part_ref[k, x, half:, :].astype(jnp.float32)
             stat = jnp.concatenate([stat, jnp.zeros((HD - EXTRA, HD), jnp.float32)]).T[:half]
-            weight.append((stat[:, 0:1] + stat[:, 1:2] + stat[:, 2:3], stat[:, 3:4] + stat[:, 4:5] + stat[:, 5:6]))
-            values.append(part_ref[k, h, :half, :].astype(jnp.float32))
-        top = jnp.maximum(weight[0][0], weight[1][0])
-        a = weight[0][1] * jnp.exp2(weight[0][0] - top)
-        b = weight[1][1] * jnp.exp2(weight[1][0] - top)
-        context.append(((values[0] * a + values[1] * b) / (a + b)).astype(jnp.bfloat16))
-    low = jnp.concatenate(context[: heads // 2], axis=1)
-    high = jnp.concatenate(context[heads // 2 :], axis=1)
-    first = c_ref[0] == 0
-    near = jnp.where(first, low, high)
-    far = jnp.where(first, high, low)
-    for n in range(mine_ref.shape[0]):
-        terms = jnp.dot(near, mine_ref[n], preferred_element_type=jnp.float32)
-        terms += jnp.dot(far, other_ref[n], preferred_element_type=jnp.float32)
-        terms = terms.astype(out_ref.dtype)
-        width = out_ref.shape[2]
-        out_ref[2 * n] = terms[:, :width]
-        out_ref[2 * n + 1] = terms[:, width:]
+            tops.append(stat[:, 0:1] + stat[:, 1:2] + stat[:, 2:3])
+            totals.append(stat[:, 3:4] + stat[:, 4:5] + stat[:, 5:6])
+        top = tops[0]
+        for k in range(1, count):
+            top = jnp.maximum(top, tops[k])
+        weights = [totals[k] * jnp.exp2(tops[k] - top) for k in range(count)]
+        mixed = sum(part_ref[k, x, :half, :].astype(jnp.float32) * weights[k] for k in range(count))
+        context.append((mixed / sum(weights)).astype(jnp.bfloat16))
+    low = jnp.concatenate([context[0], context[2]], axis=1)
+    high = jnp.concatenate([context[1], context[3]], axis=1)
+    width = out_ref.shape[2]
+    for ref, odd in ((near_ref, c_ref[0]), (far_ref, 1 - c_ref[0])):
+        for h in range(2):
+            terms = jnp.dot(low, ref[2 * h], preferred_element_type=jnp.float32)
+            terms += jnp.dot(high, ref[2 * h + 1], preferred_element_type=jnp.float32)
+            terms = terms.astype(out_ref.dtype)
+            at = 2 * (2 * h + odd)
+            out_ref[at] = terms[:, :width]
+            out_ref[at + 1] = terms[:, width:]
 
 
 def finish(core, parts, mine, other):
@@ -225,15 +238,6 @@
     return sorted(range(1, count), key=lambda s: -min(s, count - s))
 
 
-def scatter_by_shifts(blocks, axis, source):
-    here, count = lax.axis_index(axis), blocks.shape[0]
-    result = pick(blocks, here)
-    for s in distances(axis):
-        got = shift(pick(blocks, (here + s) % count), axis, s)
-        result = jnp.where((here - source) % count == s, got, result)
-    return result
-
-
 def gather_by_shifts(block, axis):
     here, count = lax.axis_index(axis), lax.axis_size(axis)
     got = {0: block}
@@ -243,10 +247,27 @@
     return jnp.stack([pick(got, (here - i) % count) for i in range(count)])
 
 
+def trade(block, across):
+    route = []
+    for z in range(2):
+        for x in range(4):
+            for c in range(2):
+                to = ((z ^ across) * 4 + x - x % 2 + c) * 2 + x % 2
+                if to != (z * 4 + x) * 2 + c:
+                    route.append(((z * 4 + x) * 2 + c, to))
+    return lax.ppermute(block, ("zh", "x", "c"), route)
+
+
+def mirror(block, z, y):
+    route = [(i, (i // 2 ^ z) * 2 + (i % 2 ^ y)) for i in range(4)]
+    return lax.ppermute(block, ("zh", "yh"), route)
+
+
 def shards(hidden_in, norm_gain, snap_qkv, snap_out, owner_index, block_order):
     rows, width = hidden_in.shape
-    zh, y, x, c = (lax.axis_index(name) for name in ("zh", "y", "x", "c"))
+    zh, yh, yl, x, c = (lax.axis_index(name) for name in ("zh", "yh", "yl", "x", "c"))
     ny, nx = 8, 4
+    ys = ("yh", "yl")
     half = rows // 2
     core = c.reshape(1)
     owner = owner_index[0]
@@ -257,50 +278,50 @@
         mine * lax.rsqrt(jnp.mean(mine * mine, axis=-1, keepdims=True) + 1e-06) * norm_gain
     ).astype(jnp.bfloat16)
 
+    order = block_order.reshape(2, 2, ny // 2, nx) * rows
+    offsets = jnp.arange(half, dtype=jnp.int32)
+    kpos = (pick(pick(order, zh), yh)[:, :, None] + offsets).reshape(-1)
+    kpos = jnp.concatenate([kpos + c * half, kpos + (1 - c) * half]).reshape(1, -1)
+    start = lax.dynamic_index_in_dim(order, yl, 2, keepdims=False).reshape(-1) + c * half
+
     part = width // (2 * ny)
-    w = exchange(fold(snap_qkv[0], ny), "c").reshape(nx, ny, part, 3 * HD)
-    wo = snap_out[0].reshape(ny, -1, snap_out.shape[2])
+    w = fold(snap_qkv[0], snap_out[0], ny)
     w = pick(exchange(w, "x"), x0)
-    wo = scatter_by_shifts(wo, "y", y0)
-    w, wo, normed = lax.optimization_barrier((w, wo, normed))
-    w = pick(exchange(w, "y"), y0)
+    w, normed, kpos, start = lax.optimization_barrier((w, normed, kpos, start))
+    w = pick(exchange(w, ys), y0)
     normed = gather_by_shifts(normed, "x").reshape(-1, width)
-    wo = jnp.transpose(wo.reshape(wo.shape[0], nx, -1), (1, 0, 2))
-    wo = scatter_by_shifts(wo, "x", x0)
-    wo = jnp.transpose(wo.reshape(wo.shape[0], nx, HD), (1, 0, 2)).reshape(part, HD)
-    w = jnp.concatenate([w, wo], axis=1)
     w, normed = lax.optimization_barrier((w, normed))
-    w = jnp.where(zh == zh0, w, swap(w, "zh"))
-    w = spread(w, "y").reshape(ny * part, 4 * HD)
+    w = jnp.where(zh == zh0, jnp.where(x % 2 == c, w, trade(w, 0)), trade(w, 1))
+    w = spread(w, ys).reshape(ny * part, 4 * HD)
     q, kv = project(core, normed, w, swap(w, "c"))
     wo = w[:, 3 * HD :].reshape(ny, nx, part // nx, HD)
     wo = jnp.transpose(wo, (0, 2, 1, 3)).reshape(ny * part // nx, nx * HD)
     q, kv, wo = lax.optimization_barrier((q, kv, wo))
 
-    near = spread(kv, "y").reshape(-1, 2 * HD)
-    q_other = swap(q, "zh")
-    q_all = jnp.concatenate([jnp.where(zh == 0, q, q_other), jnp.where(zh == 0, q_other, q)])
+    near = spread(kv, "yl").reshape(-1, 2 * HD)
+    other = {(0, 0): q}
+    for z, y in ((1, 1), (1, 0), (0, 1)):
+        other[z, y] = mirror(q, z, y)
+    q_all = []
+    for z in range(2):
+        for y in range(2):
+            same = [jnp.where(yh == y, other[k, 0], other[k, 1]) for k in range(2)]
+            q_all.append(jnp.where(zh == z, same[0], same[1]))
+    q_all = jnp.concatenate(q_all)
     wo = gather_by_shifts(wo, "x")
     near, q_all, wo = lax.optimization_barrier((near, q_all, wo))
     far = swap(near, "c")
     wo_far = swap(wo, "c")
 
-    order = block_order.reshape(2, ny, nx) * rows
-    offsets = jnp.arange(half, dtype=jnp.int32)
-    kpos = (pick(order, zh)[:, :, None] + offsets).reshape(-1)
-    kpos = jnp.concatenate([kpos + c * half, kpos + (1 - c) * half])
-    here = lax.dynamic_index_in_dim(order, y, 1, keepdims=False)
-    qpos = here[:, :, None] + c * half + offsets
-
-    parts = attend(q_all, near, far, qpos.reshape(-1, 1), kpos.reshape(1, -1), half)
-    parts = exchange(parts, ("zh", "x")).reshape((2, nx) + parts.shape[1:])
+    parts = attend(start, q_all, near, far, kpos, half)
+    parts = exchange(parts, ("zh", "yh", "x")).reshape((4, nx) + parts.shape[1:])
     terms = finish(core, parts, wo, wo_far)
     terms = exchange(terms, ("zl", "c")).reshape(-1, rows, terms.shape[2])
     return jnp.sum(terms.astype(jnp.float32), axis=0).astype(jnp.bfloat16)
 
 
 def solution(mesh):
-    fine = Mesh(mesh.devices.reshape(2, 8, 4, 4, 2), ("zh", "y", "x", "zl", "c"))
-    ctx, tp = ("zh", "y", "x"), ("zl", "c")
+    fine = Mesh(mesh.devices.reshape(2, 2, 4, 4, 4, 2), ("zh", "yh", "yl", "x", "zl", "c"))
+    ctx, tp = ("zh", "yh", "yl", "x"), ("zl", "c")
     in_specs = (P(ctx, None), P(), P(ctx, None, None, tp), P(ctx, tp, None), P(), P())
     return jax.shard_map(shards, mesh=fine, in_specs=in_specs, out_specs=P(ctx, tp), check_vma=False)

time: 243 us -> 255 us (1.049); the launches traced: 242 us -> 251 us
  waiting for transfers between devices: 42.5 us -> 95.9 us
  starting transfers between devices: 106 us -> 81.1 us
  blocking collectives: 60.7 us -> 47.8 us
  other arithmetic: 6.15 us -> 1.8 us
    all_to_all x4, waiting for transfers between devices: 13.3 us -> 64.9 us  [exchange(): return lax.all_to_all(block, axis, 0, 0, tiled=True)]
    ppermute x16 -> x6, starting transfers between devices: 51.9 us -> 16 us  [shift(): lax.ppermute(block, axis, [(i, (i + distance) % count) for i in range(cou...]
    ppermute x0 -> x5, starting transfers between devices: none -> 30.2 us  [the longest x3 16.2 us: mirror(): return lax.ppermute(block, ('zh', 'yh'), route)]
    ppermute x5 -> x3, starting transfers between devices: 28.6 us -> 6.68 us  [swap(): return lax.ppermute(block, axis, [(0, 1), (1, 0)])]
    all_to_all x3 -> x2, blocking collectives: 60.7 us -> 47.8 us  [exchange(): return lax.all_to_all(block, axis, 0, 0, tiled=True)]
    ppermute x0 -> x5, waiting for transfers between devices: none -> 3.26 us  [the longest x2 3.25 us: trade(): return lax.ppermute(block, ('zh', 'x', 'c'), route)]
    all_to_all x4, starting transfers between devices: 25.7 us -> 28.3 us  [exchange(): return lax.all_to_all(block, axis, 0, 0, tiled=True)]
    ppermute x16 -> x6, waiting for transfers between devices: 25.3 us -> 26.1 us  [shift(): lax.ppermute(block, axis, [(i, (i + distance) % count) for i in range(cou...]
  transfers between devices with their start and end apart: 25 -> 18, of which waited for: 9 -> 12; matrix products, arithmetic and copies ran while one was open for 4% -> 1% of each run, Pallas kernels for 4% -> 4%
where the time goes in v4:
time: 255 us; the launch traced here: 251 us
  waiting for transfers between devices  95.9 us (38%)
  starting transfers between devices  81.1 us (32%)
  blocking collectives  47.8 us (19%)
  Pallas kernels  16.2 us (6%)
  local copies, waits for them, and re-layouts  7.19 us (3%)
    all_to_all x4, waiting for transfers between devices, exchange(): return lax.all_to_all(block, axis, 0, 0, tiled=True)  64.9 us
    all_to_all x2, blocking collectives, exchange(): return lax.all_to_all(block, axis, 0, 0, tiled=True)  47.8 us
    all_to_all x4, starting transfers between devices, exchange(): return lax.all_to_all(block, axis, 0, 0, tiled=True)  28.3 us
    ppermute x6, waiting for transfers between devices, shift(): lax.ppermute(block, axis, [(i, (i + distance) % count) for i in range(cou...  26.1 us
    ppermute x3, starting transfers between devices, mirror(): return lax.ppermute(block, ('zh', 'yh'), route)  16.2 us
    ppermute x6, starting transfers between devices, shift(): lax.ppermute(block, axis, [(i, (i + distance) % count) for i in range(cou...  16 us
    ppermute x2, starting transfers between devices, trade(): return lax.ppermute(block, ('zh', 'x', 'c'), route)  14 us
    pallas_call x1, Pallas kernels, attend(): pl.pallas_call(attend_kernel, grid=(nq // tile,), in_specs=[pl.BlockSpec(...  9.81 us
  transfers between devices with their start and end apart: 18, of which 12 were waited for; matrix products, arithmetic and copies ran while one was open for 1% of the time, Pallas kernels for 4%

profile of v4, /device:TPU:1, one launch (start us, length us, event | category | flops | bytes accessed | tf_op | source)
XLA Modules:
  0.0 251.2 jit_solution(16163979559775555035)
XLA Ops:
  0.0 1.9 copy-done
  1.9 1.2 copy-done.1
  3.1 4.0 %shard_map.64 = bf16[4,8,128,512]{3,2,1,0:T(8,128)(2,1)} custom-call(bf16[3,2,1024,256]{3,2,1,0:T(8,128)(2,1)S(1)} %bitcast.41, bf16[256,2048]{1,0:T(8,128)(2,1)S(1)} %bitcast.43), custom_call_target="tpu_custom_call" | custom-call | bytes 8388608 | tf_op jit(solution)/shard_map/pallas_call | solution.py:31
  7.1 5.0 %all-to-all-start = ((bf16[4,8,128,512]{3,2,1,0:T(8,128)(2,1)}), bf16[4,8,128,512]{3,2,1,0:T(8,128)(2,1)}, u32[]{:S(2)}, u32[]{:S(2)}) async-start(bf16[4,8,128,512]{3,2,1,0:T(8,128)(2,1)} %shard_map.64), calls=%async_computation | async-start | bytes 8388608 | tf_op jit(solution)/shard_map/all_to_all | solution.py:219
  13.3 0.2 fusion
  13.5 0.1 fusion.2
  13.6 41.7 %all-to-all-done = bf16[4,8,128,512]{3,2,1,0:T(8,128)(2,1)} async-done(((bf16[4,8,128,512]{3,2,1,0:T(8,128)(2,1)}), bf16[4,8,128,512]{3,2,1,0:T(8,128)(2,1)}, u32[]{:S(2)}, u32[]{:S(2)}) %all-to-all-start) | async-done | bytes 4194336 | tf_op jit(solution)/shard_map/all_to_all | solution.py:219
  55.3 2.3 dynamic-slice_bitcast_fusion
  57.6 12.7 %all-to-all-start.1 = ((bf16[8,128,512]{2,1,0:T(8,128)(2,1)}), bf16[8,128,512]{2,1,0:T(8,128)(2,1)S(1)}, u32[]{:S(2)}, u32[]{:S(2)}) async-start(bf16[8,128,512]{2,1,0:T(8,128)(2,1)} %dynamic-slice_bitcast_fusion), calls=%async_computation.1 | async-start | bytes 2097152 | tf_op jit(solution)/shard_map/all_to_all | solution.py:219
  70.3 2.8 %collective-permute-start.2 = (bf16[80,2048]{1,0:T(8,128)(2,1)S(1)}, bf16[80,2048]{1,0:T(8,128)(2,1)S(1)}, u32[]{:S(2)}, u32[]{:S(2)}) collective-permute-start(bf16[80,2048]{1,0:T(8,128)(2,1)S(1)} %fusion.2), channel_id=1, source_target_pairs={{0,24},{8,0},{16,8},{24,16},{1,25},{9,1},{17,9},{25,17},{2,26},{10... | collective-permute-start | bytes 983048 | tf_op jit(solution)/shard_map/ppermute | solution.py:233
  73.1 3.1 %collective-permute-start.1 = (bf16[80,2048]{1,0:T(8,128)(2,1)S(1)}, bf16[80,2048]{1,0:T(8,128)(2,1)S(1)}, u32[]{:S(2)}, u32[]{:S(2)}) collective-permute-start(bf16[80,2048]{1,0:T(8,128)(2,1)S(1)} %fusion.2), channel_id=1, source_target_pairs={{0,16},{8,24},{16,0},{24,8},{1,17},{9,25},{17,1},{25,9},{2,18},{10... | collective-permute-start | bytes 983048 | tf_op jit(solution)/shard_map/ppermute | solution.py:233
  76.2 1.9 collective-permute-start
  78.2 1.3 collective-permute-done.2
  79.5 4.0 %collective-permute-done.1 = bf16[80,2048]{1,0:T(8,128)(2,1)S(1)} collective-permute-done((bf16[80,2048]{1,0:T(8,128)(2,1)S(1)}, bf16[80,2048]{1,0:T(8,128)(2,1)S(1)}, u32[]{:S(2)}, u32[]{:S(2)}) %collective-permute-start.1) | collective-permute-done | bytes 327712 | tf_op jit(solution)/shard_map/ppermute | solution.py:233
  83.6 8.9 %collective-permute-done = bf16[80,2048]{1,0:T(8,128)(2,1)S(1)} collective-permute-done((bf16[80,2048]{1,0:T(8,128)(2,1)S(1)}, bf16[80,2048]{1,0:T(8,128)(2,1)S(1)}, u32[]{:S(2)}, u32[]{:S(2)}) %collective-permute-start) | collective-permute-done | bytes 327712 | tf_op jit(solution)/shard_map/ppermute | solution.py:233
  92.5 0.2 pad_maximum_fusion
  92.7 0.1 constant_dynamic-slice_fusion.7
  92.8 0.2 pad_maximum_fusion.1
  93.0 6.5 %all-to-all-done.1 = bf16[8,128,512]{2,1,0:T(8,128)(2,1)S(1)} async-done(((bf16[8,128,512]{2,1,0:T(8,128)(2,1)}), bf16[8,128,512]{2,1,0:T(8,128)(2,1)S(1)}, u32[]{:S(2)}, u32[]{:S(2)}) %all-to-all-start.1) | async-done | bytes 1048608 | tf_op jit(solution)/shard_map/all_to_all | solution.py:219
  99.5 11.0 %collective-permute-start.4 = (bf16[128,512]{1,0:T(8,128)(2,1)S(1)}, bf16[128,512]{1,0:T(8,128)(2,1)S(1)}, u32[]{:S(2)}, u32[]{:S(2)}) collective-permute-start(bf16[128,512]{1,0:T(8,128)(2,1)S(1)} %dynamic-slice_bitcast_fusion.1), channel_id=1, source_target_pairs={{0,256},{1,264},{8,257},{9,265},{16,272},{17,280},{24,273},{25,281... | collective-permute-start | bytes 393224 | tf_op jit(solution)/shard_map/ppermute | solution.py:258
  110.5 3.0 %collective-permute-start.3 = (bf16[128,512]{1,0:T(8,128)(2,1)S(1)}, bf16[128,512]{1,0:T(8,128)(2,1)S(1)}, u32[]{:S(2)}, u32[]{:S(2)}) collective-permute-start(bf16[128,512]{1,0:T(8,128)(2,1)S(1)} %dynamic-slice_bitcast_fusion.1), channel_id=1, source_target_pairs={{1,8},{8,1},{17,24},{24,17},{257,264},{264,257},{273,280},{280,273... | collective-permute-start | bytes 393224 | tf_op jit(solution)/shard_map/ppermute | solution.py:258
  113.6 0.4 collective-permute-done.4
  114.0 2.8 %collective-permute-done.3 = bf16[128,512]{1,0:T(8,128)(2,1)S(1)} collective-permute-done((bf16[128,512]{1,0:T(8,128)(2,1)S(1)}, bf16[128,512]{1,0:T(8,128)(2,1)S(1)}, u32[]{:S(2)}, u32[]{:S(2)}) %collective-permute-start.3) | collective-permute-done | bytes 131104 | tf_op jit(solution)/shard_map/ppermute | solution.py:258
  116.9 31.6 %all_to_all.30 = bf16[8,128,512]{2,1,0:T(8,128)(2,1)S(1)} all-to-all(bf16[8,128,512]{2,1,0:T(8,128)(2,1)S(1)} %broadcast_in_dim.4), channel_id=1, replica_groups=mesh['zh'=2,'yh'=2,'yl'=4,'x'=4,'zl'=4,'c'=2] {'yh','yl'}, dimensions={0} | all-to-all | bytes 2097152 | tf_op jit(solution)/shard_map/all_to_all | solution.py:219
  148.6 2.4 collective-permute-start.5
  151.0 0.1 copy.7
  151.2 0.5 shard_map.65.sum_ref
  151.7 1.5 collective-permute-done.5.w_ref
  153.2 0.5 shard_map.66
  153.7 0.9 broadcast_in_dim.5
  154.6 3.5 %all-to-all-start.3 = ((bf16[4,320,256]{2,1,0:T(8,128)(2,1)}), bf16[4,320,256]{2,1,0:T(8,128)(2,1)S(1)}, u32[]{:S(2)}, u32[]{:S(2)}) async-start(bf16[4,320,256]{2,1,0:T(8,128)(2,1)} %broadcast_in_dim.5), calls=%async_computation.3 | async-start | bytes 1310720 | tf_op jit(solution)/shard_map/all_to_all | solution.py:219
  158.1 2.2 collective-permute-start.6
  160.3 7.2 %collective-permute-start.7 = (bf16[320,128]{1,0:T(8,128)(2,1)S(1)}, bf16[320,128]{1,0:T(8,128)(2,1)S(1)}, u32[]{:S(2)}, u32[]{:S(2)}) collective-permute-start(bf16[320,128]{1,0:T(8,128)(2,1)S(1)} %get-tuple-element.27), channel_id=1, source_target_pairs={{0,256},{128,384},{256,0},{384,128},{1,257},{129,385},{257,1},{385... | collective-permute-start | bytes 245768 | tf_op jit(solution)/shard_map/ppermute | solution.py:263
  167.5 6.8 %collective-permute-start.8 = (bf16[320,128]{1,0:T(8,128)(2,1)S(1)}, bf16[320,128]{1,0:T(8,128)(2,1)S(1)}, u32[]{:S(2)}, u32[]{:S(2)}) collective-permute-start(bf16[320,128]{1,0:T(8,128)(2,1)S(1)} %get-tuple-element.27), channel_id=1, source_target_pairs={{0,384},{128,256},{256,128},{384,0},{1,385},{129,257},{257,129},{3... | collective-permute-start | bytes 245768 | tf_op jit(solution)/shard_map/ppermute | solution.py:263
  174.3 2.9 %collective-permute-start.11 = (bf16[256,512]{1,0:T(8,128)(2,1)S(1)}, bf16[256,512]{1,0:T(8,128)(2,1)S(1)}, u32[]{:S(2)}, u32[]{:S(2)}) collective-permute-start(bf16[256,512]{1,0:T(8,128)(2,1)S(1)} %bitcast.50), channel_id=1, source_target_pairs={{0,24},{8,0},{16,8},{24,16},{1,25},{9,1},{17,9},{25,17},{2,26},{10... | collective-permute-start | bytes 786440 | tf_op jit(solution)/shard_map/ppermute | solution.py:233
  177.2 2.5 %collective-permute-start.10 = (bf16[256,512]{1,0:T(8,128)(2,1)S(1)}, bf16[256,512]{1,0:T(8,128)(2,1)S(1)}, u32[]{:S(2)}, u32[]{:S(2)}) collective-permute-start(bf16[256,512]{1,0:T(8,128)(2,1)S(1)} %bitcast.51), channel_id=1, source_target_pairs={{0,16},{8,24},{16,0},{24,8},{1,17},{9,25},{17,1},{25,9},{2,18},{10... | collective-permute-start | bytes 786440 | tf_op jit(solution)/shard_map/ppermute | solution.py:233
  179.8 2.8 %collective-permute-start.9 = (bf16[256,512]{1,0:T(8,128)(2,1)S(1)}, bf16[256,512]{1,0:T(8,128)(2,1)S(1)}, u32[]{:S(2)}, u32[]{:S(2)}) collective-permute-start(bf16[256,512]{1,0:T(8,128)(2,1)S(1)} %bitcast.52), channel_id=1, source_target_pairs={{0,8},{8,16},{16,24},{24,0},{1,9},{9,17},{17,25},{25,1},{2,10},{10... | collective-permute-start | bytes 786440 | tf_op jit(solution)/shard_map/ppermute | solution.py:233
  182.6 0.2 collective-permute-done.11
  182.8 4.4 %collective-permute-done.10 = bf16[256,512]{1,0:T(8,128)(2,1)S(1)} collective-permute-done((bf16[256,512]{1,0:T(8,128)(2,1)S(1)}, bf16[256,512]{1,0:T(8,128)(2,1)S(1)}, u32[]{:S(2)}, u32[]{:S(2)}) %collective-permute-start.10) | collective-permute-done | bytes 262176 | tf_op jit(solution)/shard_map/ppermute | solution.py:233
  187.2 7.2 %collective-permute-done.9 = bf16[256,512]{1,0:T(8,128)(2,1)S(1)} collective-permute-done((bf16[256,512]{1,0:T(8,128)(2,1)S(1)}, bf16[256,512]{1,0:T(8,128)(2,1)S(1)}, u32[]{:S(2)}, u32[]{:S(2)}) %collective-permute-start.9) | collective-permute-done | bytes 262176 | tf_op jit(solution)/shard_map/ppermute | solution.py:233
  194.8 2.4 collective-permute-start.12
  197.3 1.9 collective-permute-start.13
  199.2 9.8 %shard_map.67 = bf16[16,96,128]{2,1,0:T(8,128)(2,1)} custom-call(s32[16]{0:T(128)S(1)} %add.151.start_ref, bf16[1280,128]{1,0:T(8,128)(2,1)S(1)} %pad_maximum_fusion.4.q_ref, bf16[1280,256]{1,0:T(8,128)(2,1)S(1)} %bitcast.45, bf16[1280,256]{1,0:T(8,128)(2,1)S(1)} %collective-permute-done.12.far_ref, s32[1,2560]{1,0:T(1,128)S(1)} %reshape.58.kpos_ref), custom_call_target="tpu_custom_call" | custom-call | flops 1677721600 | bytes 1310720 | tf_op jit(solution)/shard_map/pallas_call | solution.py:149
  209.0 7.1 %all-to-all-start.4 = ((bf16[16,96,128]{2,1,0:T(8,128)(2,1)}), bf16[16,96,128]{2,1,0:T(8,128)(2,1)S(1)}, u32[]{:S(2)}, u32[]{:S(2)}) async-start(bf16[16,96,128]{2,1,0:T(8,128)(2,1)} %shard_map.67), calls=%async_computation.4 | async-start | bytes 786432 | tf_op jit(solution)/shard_map/all_to_all | solution.py:219
  216.1 16.8 %all-to-all-done.4 = bf16[16,96,128]{2,1,0:T(8,128)(2,1)S(1)} async-done(((bf16[16,96,128]{2,1,0:T(8,128)(2,1)}), bf16[16,96,128]{2,1,0:T(8,128)(2,1)S(1)}, u32[]{:S(2)}, u32[]{:S(2)}) %all-to-all-start.4) | async-done | bytes 393248 | tf_op jit(solution)/shard_map/all_to_all | solution.py:219
  232.9 1.4 shard_map.68
  234.3 16.2 %all_to_all.31 = bf16[8,80,256]{2,1,0:T(8,128)(2,1)S(1)} all-to-all(bf16[8,80,256]{2,1,0:T(8,128)(2,1)S(1)} %shard_map.68), channel_id=1, replica_groups=mesh['zh'=2,'yh'=2,'yl'=4,'x'=4,'zl'=4,'c'=2] {'zl','c'}, dimensions={0} | all-to-all | bytes 655360 | tf_op jit(solution)/shard_map/all_to_all | solution.py:219
  250.5 0.7 bitcast_reduce_fusion
  (35 shorter events, 1.1 us)
Async XLA Ops:
  0.0 1.9 copy-start
  1.9 1.2 copy-start.1
  7.1 5.7 %copy-start.4 = (s32[64]{0:T(128)S(1)}, s32[64]{0:T(128)}, u32[]{:S(2)}) copy-start(s32[64]{0:T(128)} %param.11) | copy-start | bytes 772
  7.1 6.2 %copy-start.2 = (bf16[160,2048]{1,0:T(8,128)(2,1)S(1)}, bf16[160,2048]{1,0:T(8,128)(2,1)}, u32[]{:S(2)}) copy-start(bf16[160,2048]{1,0:T(8,128)(2,1)} %param.6) | copy-start | bytes 1966084
  7.1 6.4 %copy-start.3 = (f32[2048]{0:T(1024)S(1)}, f32[2048]{0:T(1024)}, u32[]{:S(2)}) copy-start(f32[2048]{0:T(1024)} %param.7) | copy-start | bytes 24580
  7.1 48.2 %all-to-all-start = ((bf16[4,8,128,512]{3,2,1,0:T(8,128)(2,1)}), bf16[4,8,128,512]{3,2,1,0:T(8,128)(2,1)}, u32[]{:S(2)}, u32[]{:S(2)}) async-start(bf16[4,8,128,512]{3,2,1,0:T(8,128)(2,1)} %shard_map.64), calls=%async_computation | async-start | bytes 8388608 | tf_op jit(solution)/shard_map/all_to_all | solution.py:219
  57.6 41.9 %all-to-all-start.1 = ((bf16[8,128,512]{2,1,0:T(8,128)(2,1)}), bf16[8,128,512]{2,1,0:T(8,128)(2,1)S(1)}, u32[]{:S(2)}, u32[]{:S(2)}) async-start(bf16[8,128,512]{2,1,0:T(8,128)(2,1)} %dynamic-slice_bitcast_fusion), calls=%async_computation.1 | async-start | bytes 2097152 | tf_op jit(solution)/shard_map/all_to_all | solution.py:219
  70.3 9.3 %collective-permute-start.2 = (bf16[80,2048]{1,0:T(8,128)(2,1)S(1)}, bf16[80,2048]{1,0:T(8,128)(2,1)S(1)}, u32[]{:S(2)}, u32[]{:S(2)}) collective-permute-start(bf16[80,2048]{1,0:T(8,128)(2,1)S(1)} %fusion.2), channel_id=1, source_target_pairs={{0,24},{8,0},{16,8},{24,16},{1,25},{9,1},{17,9},{25,17},{2,26},{10... | collective-permute-start | bytes 983048 | tf_op jit(solution)/shard_map/ppermute | solution.py:233
  73.1 10.5 %collective-permute-start.1 = (bf16[80,2048]{1,0:T(8,128)(2,1)S(1)}, bf16[80,2048]{1,0:T(8,128)(2,1)S(1)}, u32[]{:S(2)}, u32[]{:S(2)}) collective-permute-start(bf16[80,2048]{1,0:T(8,128)(2,1)S(1)} %fusion.2), channel_id=1, source_target_pairs={{0,16},{8,24},{16,0},{24,8},{1,17},{9,25},{17,1},{25,9},{2,18},{10... | collective-permute-start | bytes 983048 | tf_op jit(solution)/shard_map/ppermute | solution.py:233
  76.2 16.3 %collective-permute-start = (bf16[80,2048]{1,0:T(8,128)(2,1)S(1)}, bf16[80,2048]{1,0:T(8,128)(2,1)S(1)}, u32[]{:S(2)}, u32[]{:S(2)}) collective-permute-start(bf16[80,2048]{1,0:T(8,128)(2,1)S(1)} %fusion.2), channel_id=1, source_target_pairs={{0,8},{8,16},{16,24},{24,0},{1,9},{9,17},{17,25},{25,1},{2,10},{10... | collective-permute-start | bytes 983048 | tf_op jit(solution)/shard_map/ppermute | solution.py:233
  99.5 14.5 %collective-permute-start.4 = (bf16[128,512]{1,0:T(8,128)(2,1)S(1)}, bf16[128,512]{1,0:T(8,128)(2,1)S(1)}, u32[]{:S(2)}, u32[]{:S(2)}) collective-permute-start(bf16[128,512]{1,0:T(8,128)(2,1)S(1)} %dynamic-slice_bitcast_fusion.1), channel_id=1, source_target_pairs={{0,256},{1,264},{8,257},{9,265},{16,272},{17,280},{24,273},{25,281... | collective-permute-start | bytes 393224 | tf_op jit(solution)/shard_map/ppermute | solution.py:258
  110.5 6.3 %collective-permute-start.3 = (bf16[128,512]{1,0:T(8,128)(2,1)S(1)}, bf16[128,512]{1,0:T(8,128)(2,1)S(1)}, u32[]{:S(2)}, u32[]{:S(2)}) collective-permute-start(bf16[128,512]{1,0:T(8,128)(2,1)S(1)} %dynamic-slice_bitcast_fusion.1), channel_id=1, source_target_pairs={{1,8},{8,1},{17,24},{24,17},{257,264},{264,257},{273,280},{280,273... | collective-permute-start | bytes 393224 | tf_op jit(solution)/shard_map/ppermute | solution.py:258
  148.6 4.6 %collective-permute-start.5 = (bf16[1024,512]{1,0:T(8,128)(2,1)S(1)}, bf16[1024,512]{1,0:T(8,128)(2,1)S(1)}, u32[]{:S(2)}, u32[]{:S(2)}) collective-permute-start(bf16[1024,512]{1,0:T(8,128)(2,1)S(1)} %bitcast.38), channel_id=1, source_target_pairs={{0,1},{1,0},{2,3},{3,2},{4,5},{5,4},{6,7},{7,6},{8,9},{9,8},{10,11... | collective-permute-start | bytes 3145736 | tf_op jit(solution)/shard_map/ppermute | solution.py:215
  154.6 40.2 %all-to-all-start.3 = ((bf16[4,320,256]{2,1,0:T(8,128)(2,1)}), bf16[4,320,256]{2,1,0:T(8,128)(2,1)S(1)}, u32[]{:S(2)}, u32[]{:S(2)}) async-start(bf16[4,320,256]{2,1,0:T(8,128)(2,1)} %broadcast_in_dim.5), calls=%async_computation.3 | async-start | bytes 1310720 | tf_op jit(solution)/shard_map/all_to_all | solution.py:219
  158.1 21.6 %collective-permute-start.6 = (bf16[320,128]{1,0:T(8,128)(2,1)S(1)}, bf16[320,128]{1,0:T(8,128)(2,1)S(1)}, u32[]{:S(2)}, u32[]{:S(2)}) collective-permute-start(bf16[320,128]{1,0:T(8,128)(2,1)S(1)} %get-tuple-element.27), channel_id=1, source_target_pairs={{0,128},{128,0},{256,384},{384,256},{1,129},{129,1},{257,385},{385... | collective-permute-start | bytes 245768 | tf_op jit(solution)/shard_map/ppermute | solution.py:263
  160.3 22.2 %collective-permute-start.7 = (bf16[320,128]{1,0:T(8,128)(2,1)S(1)}, bf16[320,128]{1,0:T(8,128)(2,1)S(1)}, u32[]{:S(2)}, u32[]{:S(2)}) collective-permute-start(bf16[320,128]{1,0:T(8,128)(2,1)S(1)} %get-tuple-element.27), channel_id=1, source_target_pairs={{0,256},{128,384},{256,0},{384,128},{1,257},{129,385},{257,1},{385... | collective-permute-start | bytes 245768 | tf_op jit(solution)/shard_map/ppermute | solution.py:263
  167.5 15.1 %collective-permute-start.8 = (bf16[320,128]{1,0:T(8,128)(2,1)S(1)}, bf16[320,128]{1,0:T(8,128)(2,1)S(1)}, u32[]{:S(2)}, u32[]{:S(2)}) collective-permute-start(bf16[320,128]{1,0:T(8,128)(2,1)S(1)} %get-tuple-element.27), channel_id=1, source_target_pairs={{0,384},{128,256},{256,128},{384,0},{1,385},{129,257},{257,129},{3... | collective-permute-start | bytes 245768 | tf_op jit(solution)/shard_map/ppermute | solution.py:263
  174.3 8.5 %collective-permute-start.11 = (bf16[256,512]{1,0:T(8,128)(2,1)S(1)}, bf16[256,512]{1,0:T(8,128)(2,1)S(1)}, u32[]{:S(2)}, u32[]{:S(2)}) collective-permute-start(bf16[256,512]{1,0:T(8,128)(2,1)S(1)} %bitcast.50), channel_id=1, source_target_pairs={{0,24},{8,0},{16,8},{24,16},{1,25},{9,1},{17,9},{25,17},{2,26},{10... | collective-permute-start | bytes 786440 | tf_op jit(solution)/shard_map/ppermute | solution.py:233
  177.2 10.0 %collective-permute-start.10 = (bf16[256,512]{1,0:T(8,128)(2,1)S(1)}, bf16[256,512]{1,0:T(8,128)(2,1)S(1)}, u32[]{:S(2)}, u32[]{:S(2)}) collective-permute-start(bf16[256,512]{1,0:T(8,128)(2,1)S(1)} %bitcast.51), channel_id=1, source_target_pairs={{0,16},{8,24},{16,0},{24,8},{1,17},{9,25},{17,1},{25,9},{2,18},{10... | collective-permute-start | bytes 786440 | tf_op jit(solution)/shard_map/ppermute | solution.py:233
  179.8 14.7 %collective-permute-start.9 = (bf16[256,512]{1,0:T(8,128)(2,1)S(1)}, bf16[256,512]{1,0:T(8,128)(2,1)S(1)}, u32[]{:S(2)}, u32[]{:S(2)}) collective-permute-start(bf16[256,512]{1,0:T(8,128)(2,1)S(1)} %bitcast.52), channel_id=1, source_target_pairs={{0,8},{8,16},{16,24},{24,0},{1,9},{9,17},{17,25},{25,1},{2,10},{10... | collective-permute-start | bytes 786440 | tf_op jit(solution)/shard_map/ppermute | solution.py:233
  194.8 4.3 %collective-permute-start.12 = (bf16[1280,256]{1,0:T(8,128)(2,1)S(1)}, bf16[1280,256]{1,0:T(8,128)(2,1)S(1)}, u32[]{:S(2)}, u32[]{:S(2)}) collective-permute-start(bf16[1280,256]{1,0:T(8,128)(2,1)S(1)} %bitcast.44), channel_id=1, source_target_pairs={{0,1},{1,0},{2,3},{3,2},{4,5},{5,4},{6,7},{7,6},{8,9},{9,8},{10,11... | collective-permute-start | bytes 1966088 | tf_op jit(solution)/shard_map/ppermute | solution.py:215
  197.3 18.8 %collective-permute-start.13 = (bf16[4,256,512]{2,1,0:T(8,128)(2,1)S(1)}, bf16[4,256,512]{2,1,0:T(8,128)(2,1)S(1)}, u32[]{:S(2)}, u32[]{:S(2)}) collective-permute-start(bf16[4,256,512]{2,1,0:T(8,128)(2,1)S(1)} %pad_maximum_fusion.3.near_ref), channel_id=1, source_target_pairs={{0,1},{1,0},{2,3},{3,2},{4,5},{5,4},{6,7},{7,6},{8,9},{9,8},{10,11... | collective-permute-start | bytes 3145736 | tf_op jit(solution)/shard_map/ppermute | solution.py:215
  209.0 23.9 %all-to-all-start.4 = ((bf16[16,96,128]{2,1,0:T(8,128)(2,1)}), bf16[16,96,128]{2,1,0:T(8,128)(2,1)S(1)}, u32[]{:S(2)}, u32[]{:S(2)}) async-start(bf16[16,96,128]{2,1,0:T(8,128)(2,1)} %shard_map.67), calls=%async_computation.4 | async-start | bytes 786432 | tf_op jit(solution)/shard_map/all_to_all | solution.py:219

commit v5 on v4

--- a/solution.py
+++ b/solution.py
@@ -14,20 +14,22 @@
 LIMIT = pltpu.CompilerParams(vmem_limit_bytes=48 * 1024 * 1024)
 
 
-def fold_kernel(w_ref, wo_ref, out_ref):
+def fold_kernel(w_ref, wo_ref, kv_ref, rest_ref):
     span, cols = wo_ref.shape[0], wo_ref.shape[1] // 4
     for h in range(2):
         for r in range(2):
-            for j in range(3):
-                out_ref[2 * h + r, 0, :, j * HD : (j + 1) * HD] = w_ref[j, r, :, h * HD : (h + 1) * HD]
+            for ref, at, j in ((rest_ref, 0, 0), (kv_ref, 0, 1), (kv_ref, HD, 2)):
+                ref[2 * h + r, 0, :, at : at + HD] = w_ref[j, r, :, h * HD : (h + 1) * HD]
     for x in range(4):
         for k in range(4):
             at = x * cols + k * HD
-            out_ref[x, 0, k * span : (k + 1) * span, 3 * HD :] = wo_ref[:, at : at + HD]
+            rest_ref[x, 0, k * span : (k + 1) * span, HD:] = wo_ref[:, at : at + HD]
 
 
 def fold(w, wo, ny):
     part = w.shape[1] // (2 * ny)
+    spec = pl.BlockSpec((4, 1, part, 2 * HD), lambda i: (0, i, 0, 0))
+    shape = jax.ShapeDtypeStruct((4, ny, part, 2 * HD), w.dtype)
     return pl.pallas_call(
         fold_kernel,
         grid=(ny,),
@@ -35,8 +37,8 @@
             pl.BlockSpec((3, 2, part, 2 * HD), lambda i: (0, 0, i, 0)),
             pl.BlockSpec((wo.shape[0] // ny, wo.shape[1]), lambda i: (i, 0)),
         ],
-        out_specs=pl.BlockSpec((4, 1, part, 4 * HD), lambda i: (0, i, 0, 0)),
-        out_shape=jax.ShapeDtypeStruct((4, ny, part, 4 * HD), w.dtype),
+        out_specs=[spec, spec],
+        out_shape=[shape, shape],
         compiler_params=LIMIT,
         cost_estimate=pl.CostEstimate(flops=0, bytes_accessed=4 * (w.size + wo.size), transcendentals=0),
     )(w.reshape(3, 2, ny * part, 2 * HD), wo)
@@ -49,17 +51,16 @@
     out_ref[...] = jnp.dot(x_ref[:, span], w, preferred_element_type=jnp.float32)
 
 
-def far_kernel(c_ref, x_ref, w_ref, sum_ref, q_ref, kv_ref):
+def far_kernel(c_ref, x_ref, w_ref, sum_ref, out_ref):
     depth = w_ref.shape[0]
     span = pl.ds(pl.multiple_of((1 - c_ref[0]) * depth, depth), depth)
-    w = w_ref[:, : sum_ref.shape[1]]
+    w = w_ref[:, : out_ref.shape[1]]
     out = sum_ref[...] + jnp.dot(x_ref[:, span], w, preferred_element_type=jnp.float32)
-    q_ref[...] = out[:, :HD].astype(q_ref.dtype)
-    kv_ref[...] = out[:, HD:].astype(kv_ref.dtype)
-
-
-def project(core, x, near, far):
-    n, cols = x.shape[0], 3 * HD
+    out_ref[...] = out.astype(out_ref.dtype)
+
+
+def project(core, x, near, far, cols):
+    n = x.shape[0]
     smem, vmem = pl.BlockSpec(memory_space=pltpu.SMEM), pl.BlockSpec(memory_space=pltpu.VMEM)
     cost = pl.CostEstimate(
         flops=2 * n * near.shape[0] * cols, bytes_accessed=2 * (x.size + near.size), transcendentals=0
@@ -75,11 +76,8 @@
     return pl.pallas_call(
         far_kernel,
         in_specs=[smem, vmem, vmem, vmem],
-        out_specs=[vmem, vmem],
-        out_shape=[
-            jax.ShapeDtypeStruct((n, HD), jnp.bfloat16),
-            jax.ShapeDtypeStruct((n, 2 * HD), jnp.bfloat16),
-        ],
+        out_specs=vmem,
+        out_shape=jax.ShapeDtypeStruct((n, cols), jnp.bfloat16),
         compiler_params=LIMIT,
         cost_estimate=cost,
     )(core, x, far, total)
@@ -223,9 +221,8 @@
     return lax.dynamic_index_in_dim(blocks, index, 0, keepdims=False)
 
 
-def spread(block, axis):
-    count = lax.axis_size(axis)
-    return exchange(jnp.broadcast_to(block[None], (count,) + block.shape), axis)
+def copies(block, axis):
+    return jnp.broadcast_to(block[None], (lax.axis_size(axis),) + block.shape)
 
 
 def shift(block, axis, distance):
@@ -238,13 +235,24 @@
     return sorted(range(1, count), key=lambda s: -min(s, count - s))
 
 
+def scatter_by_shifts(blocks, axis, source):
+    here, count = lax.axis_index(axis), blocks.shape[0]
+    result = pick(blocks, here)
+    for s in distances(axis):
+        got = shift(pick(blocks, (here + s) % count), axis, s)
+        result = jnp.where((here - source) % count == s, got, result)
+    return result
+
+
+def in_order(got, axis):
+    here, count = lax.axis_index(axis), len(got)
+    got = jnp.stack(got)
+    return jnp.stack([pick(got, (here - i) % count) for i in range(count)])
+
+
 def gather_by_shifts(block, axis):
-    here, count = lax.axis_index(axis), lax.axis_size(axis)
-    got = {0: block}
-    for s in distances(axis):
-        got[s] = shift(block, axis, s)
-    got = jnp.stack([got[s] for s in range(count)])
-    return jnp.stack([pick(got, (here - i) % count) for i in range(count)])
+    got = {s: shift(block, axis, s) for s in distances(axis)}
+    return in_order([block] + [got[s + 1] for s in range(len(got))], axis)
 
 
 def trade(block, across):
@@ -258,70 +266,69 @@
     return lax.ppermute(block, ("zh", "x", "c"), route)
 
 
-def mirror(block, z, y):
-    route = [(i, (i // 2 ^ z) * 2 + (i % 2 ^ y)) for i in range(4)]
-    return lax.ppermute(block, ("zh", "yh"), route)
-
-
 def shards(hidden_in, norm_gain, snap_qkv, snap_out, owner_index, block_order):
     rows, width = hidden_in.shape
-    zh, yh, yl, x, c = (lax.axis_index(name) for name in ("zh", "yh", "yl", "x", "c"))
+    zh, y, x, c = (lax.axis_index(name) for name in ("zh", "y", "x", "c"))
     ny, nx = 8, 4
-    ys = ("yh", "yl")
     half = rows // 2
     core = c.reshape(1)
     owner = owner_index[0]
     zh0, y0, x0 = owner // (ny * nx), (owner // nx) % ny, owner % nx
 
+    def across(block):
+        return jnp.where(zh == zh0, jnp.where(x % 2 == c, block, trade(block, 0)), trade(block, 1))
+
     mine = lax.dynamic_slice_in_dim(hidden_in, c * half, half, 0).astype(jnp.float32)
     normed = (
         mine * lax.rsqrt(jnp.mean(mine * mine, axis=-1, keepdims=True) + 1e-06) * norm_gain
     ).astype(jnp.bfloat16)
 
-    order = block_order.reshape(2, 2, ny // 2, nx) * rows
+    order = block_order.reshape(2, ny, nx) * rows
     offsets = jnp.arange(half, dtype=jnp.int32)
-    kpos = (pick(pick(order, zh), yh)[:, :, None] + offsets).reshape(-1)
+    kpos = (pick(order, zh)[:, :, None] + offsets).reshape(-1)
     kpos = jnp.concatenate([kpos + c * half, kpos + (1 - c) * half]).reshape(1, -1)
-    start = lax.dynamic_index_in_dim(order, yl, 2, keepdims=False).reshape(-1) + c * half
+    start = lax.dynamic_index_in_dim(order, y, 1, keepdims=False).reshape(-1) + c * half
 
     part = width // (2 * ny)
-    w = fold(snap_qkv[0], snap_out[0], ny)
-    w = pick(exchange(w, "x"), x0)
-    w, normed, kpos, start = lax.optimization_barrier((w, normed, kpos, start))
-    w = pick(exchange(w, ys), y0)
-    normed = gather_by_shifts(normed, "x").reshape(-1, width)
-    w, normed = lax.optimization_barrier((w, normed))
-    w = jnp.where(zh == zh0, jnp.where(x % 2 == c, w, trade(w, 0)), trade(w, 1))
-    w = spread(w, ys).reshape(ny * part, 4 * HD)
-    q, kv = project(core, normed, w, swap(w, "c"))
-    wo = w[:, 3 * HD :].reshape(ny, nx, part // nx, HD)
+    a, b = fold(snap_qkv[0], snap_out[0], ny)
+    a = pick(exchange(a, "x"), x0)
+    third = shift(normed, "x", 3)
+    a, b, normed, third, kpos, start = lax.optimization_barrier((a, b, normed, third, kpos, start))
+    a = pick(exchange(a, "y"), y0)
+    b = scatter_by_shifts(b, "x", x0)
+    a, b, normed = lax.optimization_barrier((a, b, normed))
+    a = copies(across(a), "y")
+    b = pick(exchange(b, "y"), y0)
+    first, second = shift(normed, "x", 1), shift(normed, "x", 2)
+    a, b, normed, first, second = lax.optimization_barrier((a, b, normed, first, second))
+    a = exchange(a, "y").reshape(ny * part, 2 * HD)
+    b = copies(across(b), "y")
+    normed = in_order([normed, first, second, third], "x").reshape(-1, width)
+    a, b, normed = lax.optimization_barrier((a, b, normed))
+    kv = copies(project(core, normed, a, swap(a, "c"), 2 * HD), "y")
+    b = exchange(b, "y").reshape(ny * part, 2 * HD)
+    kv, b = lax.optimization_barrier((kv, b))
+
+    near = exchange(kv, "y").reshape(-1, 2 * HD)
+    q = project(core, normed, b, swap(b, "c"), HD)
+    q_other = swap(q, "zh")
+    q_all = jnp.concatenate([jnp.where(zh == 0, q, q_other), jnp.where(zh == 0, q_other, q)])
+    wo = b[:, HD:].reshape(ny, nx, part // nx, HD)
     wo = jnp.transpose(wo, (0, 2, 1, 3)).reshape(ny * part // nx, nx * HD)
-    q, kv, wo = lax.optimization_barrier((q, kv, wo))
-
-    near = spread(kv, "yl").reshape(-1, 2 * HD)
-    other = {(0, 0): q}
-    for z, y in ((1, 1), (1, 0), (0, 1)):
-        other[z, y] = mirror(q, z, y)
-    q_all = []
-    for z in range(2):
-        for y in range(2):
-            same = [jnp.where(yh == y, other[k, 0], other[k, 1]) for k in range(2)]
-            q_all.append(jnp.where(zh == z, same[0], same[1]))
-    q_all = jnp.concatenate(q_all)
     wo = gather_by_shifts(wo, "x")
     near, q_all, wo = lax.optimization_barrier((near, q_all, wo))
     far = swap(near, "c")
     wo_far = swap(wo, "c")
 
     parts = attend(start, q_all, near, far, kpos, half)
-    parts = exchange(parts, ("zh", "yh", "x")).reshape((4, nx) + parts.shape[1:])
+    parts = exchange(parts, ("zh", "x")).reshape((2, nx) + parts.shape[1:])
     terms = finish(core, parts, wo, wo_far)
     terms = exchange(terms, ("zl", "c")).reshape(-1, rows, terms.shape[2])
     return jnp.sum(terms.astype(jnp.float32), axis=0).astype(jnp.bfloat16)
 
 
 def solution(mesh):
-    fine = Mesh(mesh.devices.reshape(2, 2, 4, 4, 4, 2), ("zh", "yh", "yl", "x", "zl", "c"))
-    ctx, tp = ("zh", "yh", "yl", "x"), ("zl", "c")
+    fine = Mesh(mesh.devices.reshape(2, 8, 4, 4, 2), ("zh", "y", "x", "zl", "c"))
+    ctx, tp = ("zh", "y", "x"), ("zl", "c")
     in_specs = (P(ctx, None), P(), P(ctx, None, None, tp), P(ctx, tp, None), P(), P())
     return jax.shard_map(shards, mesh=fine, in_specs=in_specs, out_specs=P(ctx, tp), check_vma=False)

time: 255 us -> 268 us (1.051)
  blocking collectives: 47.8 us -> 17.4 us
  starting transfers between devices: 81.1 us -> 110 us
  waiting for transfers between devices: 95.9 us -> 105 us
  local copies, waits for them, and re-layouts: 7.19 us -> 11.3 us
    all_to_all x2 -> x1, blocking collectives: 47.8 us -> 17.4 us  [exchange(): return lax.all_to_all(block, axis, 0, 0, tiled=True)]
    ppermute x6 -> x9, waiting for transfers between devices: 26.1 us -> 42.5 us  [shift(): lax.ppermute(block, axis, [(i, (i + distance) % count) for i in range(cou...]
    ppermute x3 -> x0, starting transfers between devices: 16.2 us -> none  [mirror(): return lax.ppermute(block, ('zh', 'yh'), route)]
    all_to_all x4 -> x7, starting transfers between devices: 28.3 us -> 43.9 us  [exchange(): return lax.all_to_all(block, axis, 0, 0, tiled=True)]
    ppermute x6 -> x9, starting transfers between devices: 16 us -> 28.8 us  [shift(): lax.ppermute(block, axis, [(i, (i + distance) % count) for i in range(cou...]
    all_to_all x4 -> x7, waiting for transfers between devices: 64.9 us -> 56 us  [exchange(): return lax.all_to_all(block, axis, 0, 0, tiled=True)]
    ppermute x2 -> x4, starting transfers between devices: 14 us -> 22.4 us  [trade(): return lax.ppermute(block, ('zh', 'x', 'c'), route)]
    ppermute x3 -> x5, starting transfers between devices: 6.68 us -> 14.7 us  [swap(): return lax.ppermute(block, axis, [(0, 1), (1, 0)])]
  transfers between devices with their start and end apart: 18 -> 25, of which waited for: 12 -> 16; matrix products, arithmetic and copies ran while one was open for 1% -> 3% of each run, Pallas kernels for 4% -> 4%
where the time goes in v5:
time: 268 us; the launch traced here: 267 us
  starting transfers between devices  110 us (41%)
  waiting for transfers between devices  105 us (39%)
  Pallas kernels  18.3 us (7%)
  blocking collectives  17.4 us (6%)
  local copies, waits for them, and re-layouts  11.3 us (4%)
  other arithmetic  3.83 us (1%)
    all_to_all x7, waiting for transfers between devices, exchange(): return lax.all_to_all(block, axis, 0, 0, tiled=True)  56 us
    all_to_all x7, starting transfers between devices, exchange(): return lax.all_to_all(block, axis, 0, 0, tiled=True)  43.9 us
    ppermute x9, waiting for transfers between devices, shift(): lax.ppermute(block, axis, [(i, (i + distance) % count) for i in range(cou...  42.5 us
    ppermute x9, starting transfers between devices, shift(): lax.ppermute(block, axis, [(i, (i + distance) % count) for i in range(cou...  28.8 us
    ppermute x4, starting transfers between devices, trade(): return lax.ppermute(block, ('zh', 'x', 'c'), route)  22.4 us
    all_to_all x1, blocking collectives, exchange(): return lax.all_to_all(block, axis, 0, 0, tiled=True)  17.4 us
    ppermute x5, starting transfers between devices, swap(): return lax.ppermute(block, axis, [(0, 1), (1, 0)])  14.7 us
    pallas_call x1, Pallas kernels, attend(): pl.pallas_call(attend_kernel, grid=(nq // tile,), in_specs=[pl.BlockSpec(...  8.95 us
  transfers between devices with their start and end apart: 25, of which 16 were waited for; matrix products, arithmetic and copies ran while one was open for 3% of the time, Pallas kernels for 4%

profile of v5, /device:TPU:1, one launch (start us, length us, event | category | flops | bytes accessed | tf_op | source)
XLA Modules:
  0.0 266.6 jit_solution(8716242801632776032)
XLA Ops:
  0.0 1.2 copy-done.1
  1.2 4.8 %shard_map.64 = (bf16[4,8,128,256]{3,2,1,0:T(8,128)(2,1)S(1)}, bf16[4,8,128,256]{3,2,1,0:T(8,128)(2,1)S(1)}) custom-call(bf16[3,2,1024,256]{3,2,1,0:T(8,128)(2,1)} %bitcast.67, bf16[256,2048]{1,0:T(8,128)(2,1)S(1)} %bitcast.64), custom_call_target="tpu_custom_call" | custom-call | bytes 8388608 | tf_op jit(solution)/shard_map/pallas_call | solution.py:33
  6.0 1.3 copy-done
  7.4 5.0 %all-to-all-start = ((bf16[4,8,128,256]{3,2,1,0:T(8,128)(2,1)}), bf16[4,8,128,256]{3,2,1,0:T(8,128)(2,1)}, u32[]{:S(2)}, u32[]{:S(2)}) async-start(bf16[4,8,128,256]{3,2,1,0:T(8,128)(2,1)} %copy-done), calls=%async_computation | async-start | bytes 4194304 | tf_op jit(solution)/shard_map/all_to_all | solution.py:217
  12.7 4.8 %collective-permute-start = (bf16[80,2048]{1,0:T(8,128)(2,1)S(1)}, bf16[80,2048]{1,0:T(8,128)(2,1)S(1)}, u32[]{:S(2)}, u32[]{:S(2)}) collective-permute-start(bf16[80,2048]{1,0:T(8,128)(2,1)S(1)} %fusion.2), channel_id=1, source_target_pairs={{0,24},{8,0},{16,8},{24,16},{1,25},{9,1},{17,9},{25,17},{2,26},{10... | collective-permute-start | bytes 983048 | tf_op jit(solution)/shard_map/ppermute | solution.py:230
  18.7 13.7 %all-to-all-done = bf16[4,8,128,256]{3,2,1,0:T(8,128)(2,1)} async-done(((bf16[4,8,128,256]{3,2,1,0:T(8,128)(2,1)}), bf16[4,8,128,256]{3,2,1,0:T(8,128)(2,1)}, u32[]{:S(2)}, u32[]{:S(2)}) %all-to-all-start) | async-done | bytes 2097184 | tf_op jit(solution)/shard_map/all_to_all | solution.py:217
  32.4 1.9 dynamic-slice_bitcast_fusion.3
  34.3 4.0 %collective-permute-done = bf16[80,2048]{1,0:T(8,128)(2,1)S(1)} collective-permute-done((bf16[80,2048]{1,0:T(8,128)(2,1)S(1)}, bf16[80,2048]{1,0:T(8,128)(2,1)S(1)}, u32[]{:S(2)}, u32[]{:S(2)}) %collective-permute-start) | collective-permute-done | bytes 327712 | tf_op jit(solution)/shard_map/ppermute | solution.py:230
  39.0 12.5 %all-to-all-start.1 = ((bf16[8,128,256]{2,1,0:T(8,128)(2,1)}), bf16[8,128,256]{2,1,0:T(8,128)(2,1)S(1)}, u32[]{:S(2)}, u32[]{:S(2)}) async-start(bf16[8,128,256]{2,1,0:T(8,128)(2,1)} %dynamic-slice_bitcast_fusion.3), calls=%async_computation.1 | async-start | bytes 1048576 | tf_op jit(solution)/shard_map/all_to_all | solution.py:217
  52.7 3.4 %collective-permute-start.1 = (bf16[8,128,256]{2,1,0:T(8,128)(2,1)}, bf16[8,128,256]{2,1,0:T(8,128)(2,1)}, u32[]{:S(2)}, u32[]{:S(2)}) collective-permute-start(bf16[8,128,256]{2,1,0:T(8,128)(2,1)} %get-tuple-element.55), channel_id=1, source_target_pairs={{0,24},{8,0},{16,8},{24,16},{1,25},{9,1},{17,9},{25,17},{2,26},{10... | collective-permute-start | bytes 1572872 | tf_op jit(solution)/shard_map/ppermute | solution.py:230
  56.1 1.9 collective-permute-start.2
  58.0 4.2 %collective-permute-start.3 = (bf16[8,128,256]{2,1,0:T(8,128)(2,1)S(1)}, bf16[8,128,256]{2,1,0:T(8,128)(2,1)}, u32[]{:S(2)}, u32[]{:S(2)}) collective-permute-start(bf16[8,128,256]{2,1,0:T(8,128)(2,1)S(1)} %get-tuple-element.53), channel_id=1, source_target_pairs={{0,16},{8,24},{16,0},{24,8},{1,17},{9,25},{17,1},{25,9},{2,18},{10... | collective-permute-start | bytes 1572872 | tf_op jit(solution)/shard_map/ppermute | solution.py:230
  62.3 4.1 %collective-permute-done.1 = bf16[8,128,256]{2,1,0:T(8,128)(2,1)} collective-permute-done((bf16[8,128,256]{2,1,0:T(8,128)(2,1)}, bf16[8,128,256]{2,1,0:T(8,128)(2,1)}, u32[]{:S(2)}, u32[]{:S(2)}) %collective-permute-start.1) | collective-permute-done | bytes 524320 | tf_op jit(solution)/shard_map/ppermute | solution.py:230
  66.5 5.3 %collective-permute-done.2 = bf16[8,128,256]{2,1,0:T(8,128)(2,1)} collective-permute-done((bf16[8,128,256]{2,1,0:T(8,128)(2,1)}, bf16[8,128,256]{2,1,0:T(8,128)(2,1)}, u32[]{:S(2)}, u32[]{:S(2)}) %collective-permute-start.2) | collective-permute-done | bytes 524320 | tf_op jit(solution)/shard_map/ppermute | solution.py:230
  71.8 10.0 %collective-permute-done.3 = bf16[8,128,256]{2,1,0:T(8,128)(2,1)} collective-permute-done((bf16[8,128,256]{2,1,0:T(8,128)(2,1)S(1)}, bf16[8,128,256]{2,1,0:T(8,128)(2,1)}, u32[]{:S(2)}, u32[]{:S(2)}) %collective-permute-start.3) | collective-permute-done | bytes 524320 | tf_op jit(solution)/shard_map/ppermute | solution.py:230
  82.7 6.4 %all-to-all-start.2 = ((bf16[8,128,256]{2,1,0:T(8,128)(2,1)}), bf16[8,128,256]{2,1,0:T(8,128)(2,1)S(1)}, u32[]{:S(2)}, u32[]{:S(2)}) async-start(bf16[8,128,256]{2,1,0:T(8,128)(2,1)} %fusion.4), calls=%async_computation.2 | async-start | bytes 1048576 | tf_op jit(solution)/shard_map/all_to_all | solution.py:217
  89.1 12.4 %collective-permute-start.5 = (bf16[128,256]{1,0:T(8,128)(2,1)S(1)}, bf16[128,256]{1,0:T(8,128)(2,1)S(1)}, u32[]{:S(2)}, u32[]{:S(2)}) collective-permute-start(bf16[128,256]{1,0:T(8,128)(2,1)S(1)} %dynamic-slice_bitcast_fusion.5), channel_id=1, source_target_pairs={{0,256},{1,264},{8,257},{9,265},{16,272},{17,280},{24,273},{25,281... | collective-permute-start | bytes 196616 | tf_op jit(solution)/shard_map/ppermute | solution.py:266
  101.6 1.9 collective-permute-start.4
  103.6 1.9 collective-permute-start.6
  105.5 5.2 %collective-permute-start.7 = (bf16[80,2048]{1,0:T(8,128)(2,1)S(1)}, bf16[80,2048]{1,0:T(8,128)(2,1)S(1)}, u32[]{:S(2)}, u32[]{:S(2)}) collective-permute-start(bf16[80,2048]{1,0:T(8,128)(2,1)S(1)} %fusion.2), channel_id=1, source_target_pairs={{0,16},{8,24},{16,0},{24,8},{1,17},{9,25},{17,1},{25,9},{2,18},{10... | collective-permute-start | bytes 983048 | tf_op jit(solution)/shard_map/ppermute | solution.py:230
  110.9 3.8 %collective-permute-done.6 = bf16[80,2048]{1,0:T(8,128)(2,1)S(1)} collective-permute-done((bf16[80,2048]{1,0:T(8,128)(2,1)S(1)}, bf16[80,2048]{1,0:T(8,128)(2,1)S(1)}, u32[]{:S(2)}, u32[]{:S(2)}) %collective-permute-start.6) | collective-permute-done | bytes 327712 | tf_op jit(solution)/shard_map/ppermute | solution.py:230
  114.7 7.1 %collective-permute-done.7 = bf16[80,2048]{1,0:T(8,128)(2,1)S(1)} collective-permute-done((bf16[80,2048]{1,0:T(8,128)(2,1)S(1)}, bf16[80,2048]{1,0:T(8,128)(2,1)S(1)}, u32[]{:S(2)}, u32[]{:S(2)}) %collective-permute-start.7) | collective-permute-done | bytes 327712 | tf_op jit(solution)/shard_map/ppermute | solution.py:230
  122.6 1.9 collective-permute-start.9
  124.5 6.2 %collective-permute-start.8 = (bf16[128,256]{1,0:T(8,128)(2,1)S(1)}, bf16[128,256]{1,0:T(8,128)(2,1)S(1)}, u32[]{:S(2)}, u32[]{:S(2)}) collective-permute-start(bf16[128,256]{1,0:T(8,128)(2,1)S(1)} %dynamic-slice_bitcast_fusion.4), channel_id=1, source_target_pairs={{1,8},{8,1},{17,24},{24,17},{257,264},{264,257},{273,280},{280,273... | collective-permute-start | bytes 196616 | tf_op jit(solution)/shard_map/ppermute | solution.py:266
  130.7 6.9 %all-to-all-start.3 = ((bf16[8,128,256]{2,1,0:T(8,128)(2,1)}), bf16[8,128,256]{2,1,0:T(8,128)(2,1)S(1)}, u32[]{:S(2)}, u32[]{:S(2)}) async-start(bf16[8,128,256]{2,1,0:T(8,128)(2,1)} %broadcast_in_dim.6), calls=%async_computation.3 | async-start | bytes 1048576 | tf_op jit(solution)/shard_map/all_to_all | solution.py:217
  138.2 16.6 %all-to-all-done.3 = bf16[8,128,256]{2,1,0:T(8,128)(2,1)S(1)} async-done(((bf16[8,128,256]{2,1,0:T(8,128)(2,1)}), bf16[8,128,256]{2,1,0:T(8,128)(2,1)S(1)}, u32[]{:S(2)}, u32[]{:S(2)}) %all-to-all-start.3) | async-done | bytes 524320 | tf_op jit(solution)/shard_map/all_to_all | solution.py:217
  155.7 3.5 %all-to-all-start.4 = ((bf16[8,128,256]{2,1,0:T(8,128)(2,1)}), bf16[8,128,256]{2,1,0:T(8,128)(2,1)S(1)}, u32[]{:S(2)}, u32[]{:S(2)}) async-start(bf16[8,128,256]{2,1,0:T(8,128)(2,1)} %broadcast_in_dim.7), calls=%async_computation.4 | async-start | bytes 1048576 | tf_op jit(solution)/shard_map/all_to_all | solution.py:217
  159.2 2.3 collective-permute-start.10
  163.3 13.8 %all-to-all-done.4 = bf16[8,128,256]{2,1,0:T(8,128)(2,1)S(1)} async-done(((bf16[8,128,256]{2,1,0:T(8,128)(2,1)}), bf16[8,128,256]{2,1,0:T(8,128)(2,1)S(1)}, u32[]{:S(2)}, u32[]{:S(2)}) %all-to-all-start.4) | async-done | bytes 524320 | tf_op jit(solution)/shard_map/all_to_all | solution.py:217
  178.3 3.6 %all-to-all-start.5 = ((bf16[8,320,256]{2,1,0:T(8,128)(2,1)}), bf16[8,320,256]{2,1,0:T(8,128)(2,1)S(1)}, u32[]{:S(2)}, u32[]{:S(2)}) async-start(bf16[8,320,256]{2,1,0:T(8,128)(2,1)} %broadcast_in_dim.8), calls=%async_computation.5 | async-start | bytes 2621440 | tf_op jit(solution)/shard_map/all_to_all | solution.py:217
  182.7 1.9 collective-permute-start.15
  184.7 1.9 collective-permute-start.14
  186.6 3.4 %collective-permute-start.13 = (bf16[256,512]{1,0:T(8,128)(2,1)}, bf16[256,512]{1,0:T(8,128)(2,1)}, u32[]{:S(2)}, u32[]{:S(2)}) collective-permute-start(bf16[256,512]{1,0:T(8,128)(2,1)} %bitcast.46), channel_id=1, source_target_pairs={{0,8},{8,16},{16,24},{24,0},{1,9},{9,17},{17,25},{25,1},{2,10},{10... | collective-permute-start | bytes 786440 | tf_op jit(solution)/shard_map/ppermute | solution.py:230
  190.0 2.9 %collective-permute-start.11 = (bf16[1024,256]{1,0:T(8,128)(2,1)S(1)}, bf16[1024,256]{1,0:T(8,128)(2,1)}, u32[]{:S(2)}, u32[]{:S(2)}) collective-permute-start(bf16[1024,256]{1,0:T(8,128)(2,1)S(1)} %bitcast.58), channel_id=1, source_target_pairs={{0,1},{1,0},{2,3},{3,2},{4,5},{5,4},{6,7},{7,6},{8,9},{9,8},{10,11... | collective-permute-start | bytes 1572872 | tf_op jit(solution)/shard_map/ppermute | solution.py:213
  194.1 1.8 collective-permute-done.14
  195.8 6.4 %collective-permute-done.13 = bf16[256,512]{1,0:T(8,128)(2,1)} collective-permute-done((bf16[256,512]{1,0:T(8,128)(2,1)}, bf16[256,512]{1,0:T(8,128)(2,1)}, u32[]{:S(2)}, u32[]{:S(2)}) %collective-permute-start.13) | collective-permute-done | bytes 262176 | tf_op jit(solution)/shard_map/ppermute | solution.py:230
  202.2 1.2 pad_maximum_fusion.2
  203.6 1.4 shard_map.68
  204.9 5.1 %collective-permute-start.12 = (bf16[320,128]{1,0:T(8,128)(2,1)S(1)}, bf16[320,128]{1,0:T(8,128)(2,1)S(1)}, u32[]{:S(2)}, u32[]{:S(2)}) collective-permute-start(bf16[320,128]{1,0:T(8,128)(2,1)S(1)} %shard_map.68), channel_id=1, source_target_pairs={{0,256},{256,0},{1,257},{257,1},{2,258},{258,2},{3,259},{259,3},{4... | collective-permute-start | bytes 245768 | tf_op jit(solution)/shard_map/ppermute | solution.py:213
  210.2 4.1 %collective-permute-done.12 = bf16[320,128]{1,0:T(8,128)(2,1)S(1)} collective-permute-done((bf16[320,128]{1,0:T(8,128)(2,1)S(1)}, bf16[320,128]{1,0:T(8,128)(2,1)S(1)}, u32[]{:S(2)}, u32[]{:S(2)}) %collective-permute-start.12) | collective-permute-done | bytes 81952 | tf_op jit(solution)/shard_map/ppermute | solution.py:213
  214.4 2.2 all-to-all-done.5
  216.6 2.4 collective-permute-start.16
  219.0 1.9 collective-permute-start.17
  221.6 9.0 %shard_map.69 = bf16[8,96,128]{2,1,0:T(8,128)(2,1)} custom-call(s32[8]{0:T(128)S(1)} %add.179.start_ref, bf16[640,128]{1,0:T(8,128)(2,1)S(1)} %pad_maximum_fusion.4.q_ref, bf16[2560,256]{1,0:T(8,128)(2,1)S(1)} %bitcast.63, bf16[2560,256]{1,0:T(8,128)(2,1)S(1)} %collective-permute-done.16.far_ref, s32[1,5120]{1,0:T(1,128)S(1)} %bitcast.66), custom_call_target="tpu_custom_call" | custom-call | flops 1677721600 | bytes 2621440 | tf_op jit(solution)/shard_map/pallas_call | solution.py:147
  230.5 6.0 %all-to-all-start.6 = ((bf16[8,96,128]{2,1,0:T(8,128)(2,1)}), bf16[8,96,128]{2,1,0:T(8,128)(2,1)S(1)}, u32[]{:S(2)}, u32[]{:S(2)}) async-start(bf16[8,96,128]{2,1,0:T(8,128)(2,1)} %shard_map.69), calls=%async_computation.6 | async-start | bytes 393216 | tf_op jit(solution)/shard_map/all_to_all | solution.py:217
  236.6 9.7 %all-to-all-done.6 = bf16[8,96,128]{2,1,0:T(8,128)(2,1)S(1)} async-done(((bf16[8,96,128]{2,1,0:T(8,128)(2,1)}), bf16[8,96,128]{2,1,0:T(8,128)(2,1)S(1)}, u32[]{:S(2)}, u32[]{:S(2)}) %all-to-all-start.6) | async-done | bytes 196640 | tf_op jit(solution)/shard_map/all_to_all | solution.py:217
  246.3 2.2 shard_map.70
  248.5 17.4 %all_to_all.40 = bf16[8,80,256]{2,1,0:T(8,128)(2,1)S(1)} all-to-all(bf16[8,80,256]{2,1,0:T(8,128)(2,1)S(1)} %shard_map.70), channel_id=1, replica_groups=mesh['zh'=2,'y'=8,'x'=4,'zl'=4,'c'=2] {'zl','c'}, dimensions={0} | all-to-all | bytes 655360 | tf_op jit(solution)/shard_map/all_to_all | solution.py:217
  (61 shorter events, 12.4 us)
Async XLA Ops:
  0.0 1.2 copy-start.1
  6.0 1.3 copy-start
  7.4 5.0 %copy-start.3 = (bf16[160,2048]{1,0:T(8,128)(2,1)S(1)}, bf16[160,2048]{1,0:T(8,128)(2,1)}, u32[]{:S(2)}) copy-start(bf16[160,2048]{1,0:T(8,128)(2,1)} %param.6) | copy-start | bytes 1966084
  7.4 5.2 %copy-start.6 = (f32[2048]{0:T(1024)S(1)}, f32[2048]{0:T(1024)}, u32[]{:S(2)}) copy-start(f32[2048]{0:T(1024)} %param.7) | copy-start | bytes 24580
  7.4 10.2 %copy-start.7 = (s32[64]{0:T(128)S(1)}, s32[64]{0:T(128)}, u32[]{:S(2)}) copy-start(s32[64]{0:T(128)} %param.11) | copy-start | bytes 772
  7.4 25.0 %all-to-all-start = ((bf16[4,8,128,256]{3,2,1,0:T(8,128)(2,1)}), bf16[4,8,128,256]{3,2,1,0:T(8,128)(2,1)}, u32[]{:S(2)}, u32[]{:S(2)}) async-start(bf16[4,8,128,256]{3,2,1,0:T(8,128)(2,1)} %copy-done), calls=%async_computation | async-start | bytes 4194304 | tf_op jit(solution)/shard_map/all_to_all | solution.py:217
  12.7 25.6 %collective-permute-start = (bf16[80,2048]{1,0:T(8,128)(2,1)S(1)}, bf16[80,2048]{1,0:T(8,128)(2,1)S(1)}, u32[]{:S(2)}, u32[]{:S(2)}) collective-permute-start(bf16[80,2048]{1,0:T(8,128)(2,1)S(1)} %fusion.2), channel_id=1, source_target_pairs={{0,24},{8,0},{16,8},{24,16},{1,25},{9,1},{17,9},{25,17},{2,26},{10... | collective-permute-start | bytes 983048 | tf_op jit(solution)/shard_map/ppermute | solution.py:230
  38.3 0.7 copy-start.4
  39.0 43.7 %all-to-all-start.1 = ((bf16[8,128,256]{2,1,0:T(8,128)(2,1)}), bf16[8,128,256]{2,1,0:T(8,128)(2,1)S(1)}, u32[]{:S(2)}, u32[]{:S(2)}) async-start(bf16[8,128,256]{2,1,0:T(8,128)(2,1)} %dynamic-slice_bitcast_fusion.3), calls=%async_computation.1 | async-start | bytes 1048576 | tf_op jit(solution)/shard_map/all_to_all | solution.py:217
  52.7 13.8 %collective-permute-start.1 = (bf16[8,128,256]{2,1,0:T(8,128)(2,1)}, bf16[8,128,256]{2,1,0:T(8,128)(2,1)}, u32[]{:S(2)}, u32[]{:S(2)}) collective-permute-start(bf16[8,128,256]{2,1,0:T(8,128)(2,1)} %get-tuple-element.55), channel_id=1, source_target_pairs={{0,24},{8,0},{16,8},{24,16},{1,25},{9,1},{17,9},{25,17},{2,26},{10... | collective-permute-start | bytes 1572872 | tf_op jit(solution)/shard_map/ppermute | solution.py:230
  56.1 15.7 %collective-permute-start.2 = (bf16[8,128,256]{2,1,0:T(8,128)(2,1)}, bf16[8,128,256]{2,1,0:T(8,128)(2,1)}, u32[]{:S(2)}, u32[]{:S(2)}) collective-permute-start(bf16[8,128,256]{2,1,0:T(8,128)(2,1)} %get-tuple-element.54), channel_id=1, source_target_pairs={{0,8},{8,16},{16,24},{24,0},{1,9},{9,17},{17,25},{25,1},{2,10},{10... | collective-permute-start | bytes 1572872 | tf_op jit(solution)/shard_map/ppermute | solution.py:230
  58.0 23.8 %collective-permute-start.3 = (bf16[8,128,256]{2,1,0:T(8,128)(2,1)S(1)}, bf16[8,128,256]{2,1,0:T(8,128)(2,1)}, u32[]{:S(2)}, u32[]{:S(2)}) collective-permute-start(bf16[8,128,256]{2,1,0:T(8,128)(2,1)S(1)} %get-tuple-element.53), channel_id=1, source_target_pairs={{0,16},{8,24},{16,0},{24,8},{1,17},{9,25},{17,1},{25,9},{2,18},{10... | collective-permute-start | bytes 1572872 | tf_op jit(solution)/shard_map/ppermute | solution.py:230
  82.7 28.1 %all-to-all-start.2 = ((bf16[8,128,256]{2,1,0:T(8,128)(2,1)}), bf16[8,128,256]{2,1,0:T(8,128)(2,1)S(1)}, u32[]{:S(2)}, u32[]{:S(2)}) async-start(bf16[8,128,256]{2,1,0:T(8,128)(2,1)} %fusion.4), calls=%async_computation.2 | async-start | bytes 1048576 | tf_op jit(solution)/shard_map/all_to_all | solution.py:217
  89.1 48.5 %copy-start.5 = (bf16[80,2048]{1,0:T(8,128)(2,1)S(1)}, bf16[80,2048]{1,0:T(8,128)(2,1)}, u32[]{:S(2)}) copy-start(bf16[80,2048]{1,0:T(8,128)(2,1)} %copy-done.4) | copy-start | bytes 983044
  89.1 21.7 %collective-permute-start.5 = (bf16[128,256]{1,0:T(8,128)(2,1)S(1)}, bf16[128,256]{1,0:T(8,128)(2,1)S(1)}, u32[]{:S(2)}, u32[]{:S(2)}) collective-permute-start(bf16[128,256]{1,0:T(8,128)(2,1)S(1)} %dynamic-slice_bitcast_fusion.5), channel_id=1, source_target_pairs={{0,256},{1,264},{8,257},{9,265},{16,272},{17,280},{24,273},{25,281... | collective-permute-start | bytes 196616 | tf_op jit(solution)/shard_map/ppermute | solution.py:266
  101.6 9.2 %collective-permute-start.4 = (bf16[128,256]{1,0:T(8,128)(2,1)S(1)}, bf16[128,256]{1,0:T(8,128)(2,1)S(1)}, u32[]{:S(2)}, u32[]{:S(2)}) collective-permute-start(bf16[128,256]{1,0:T(8,128)(2,1)S(1)} %dynamic-slice_bitcast_fusion.5), channel_id=1, source_target_pairs={{1,8},{8,1},{17,24},{24,17},{257,264},{264,257},{273,280},{280,273... | collective-permute-start | bytes 196616 | tf_op jit(solution)/shard_map/ppermute | solution.py:266
  103.6 11.1 %collective-permute-start.6 = (bf16[80,2048]{1,0:T(8,128)(2,1)S(1)}, bf16[80,2048]{1,0:T(8,128)(2,1)S(1)}, u32[]{:S(2)}, u32[]{:S(2)}) collective-permute-start(bf16[80,2048]{1,0:T(8,128)(2,1)S(1)} %fusion.2), channel_id=1, source_target_pairs={{0,8},{8,16},{16,24},{24,0},{1,9},{9,17},{17,25},{25,1},{2,10},{10... | collective-permute-start | bytes 983048 | tf_op jit(solution)/shard_map/ppermute | solution.py:230
  105.5 16.2 %collective-permute-start.7 = (bf16[80,2048]{1,0:T(8,128)(2,1)S(1)}, bf16[80,2048]{1,0:T(8,128)(2,1)S(1)}, u32[]{:S(2)}, u32[]{:S(2)}) collective-permute-start(bf16[80,2048]{1,0:T(8,128)(2,1)S(1)} %fusion.2), channel_id=1, source_target_pairs={{0,16},{8,24},{16,0},{24,8},{1,17},{9,25},{17,1},{25,9},{2,18},{10... | collective-permute-start | bytes 983048 | tf_op jit(solution)/shard_map/ppermute | solution.py:230
  122.6 15.6 %collective-permute-start.9 = (bf16[128,256]{1,0:T(8,128)(2,1)S(1)}, bf16[128,256]{1,0:T(8,128)(2,1)S(1)}, u32[]{:S(2)}, u32[]{:S(2)}) collective-permute-start(bf16[128,256]{1,0:T(8,128)(2,1)S(1)} %dynamic-slice_bitcast_fusion.4), channel_id=1, source_target_pairs={{0,256},{1,264},{8,257},{9,265},{16,272},{17,280},{24,273},{25,281... | collective-permute-start | bytes 196616 | tf_op jit(solution)/shard_map/ppermute | solution.py:266
  124.5 13.6 %collective-permute-start.8 = (bf16[128,256]{1,0:T(8,128)(2,1)S(1)}, bf16[128,256]{1,0:T(8,128)(2,1)S(1)}, u32[]{:S(2)}, u32[]{:S(2)}) collective-permute-start(bf16[128,256]{1,0:T(8,128)(2,1)S(1)} %dynamic-slice_bitcast_fusion.4), channel_id=1, source_target_pairs={{1,8},{8,1},{17,24},{24,17},{257,264},{264,257},{273,280},{280,273... | collective-permute-start | bytes 196616 | tf_op jit(solution)/shard_map/ppermute | solution.py:266
  130.7 24.1 %all-to-all-start.3 = ((bf16[8,128,256]{2,1,0:T(8,128)(2,1)}), bf16[8,128,256]{2,1,0:T(8,128)(2,1)S(1)}, u32[]{:S(2)}, u32[]{:S(2)}) async-start(bf16[8,128,256]{2,1,0:T(8,128)(2,1)} %broadcast_in_dim.6), calls=%async_computation.3 | async-start | bytes 1048576 | tf_op jit(solution)/shard_map/all_to_all | solution.py:217
  155.7 21.4 %all-to-all-start.4 = ((bf16[8,128,256]{2,1,0:T(8,128)(2,1)}), bf16[8,128,256]{2,1,0:T(8,128)(2,1)S(1)}, u32[]{:S(2)}, u32[]{:S(2)}) async-start(bf16[8,128,256]{2,1,0:T(8,128)(2,1)} %broadcast_in_dim.7), calls=%async_computation.4 | async-start | bytes 1048576 | tf_op jit(solution)/shard_map/all_to_all | solution.py:217
  159.2 3.8 %collective-permute-start.10 = (bf16[1024,256]{1,0:T(8,128)(2,1)S(1)}, bf16[1024,256]{1,0:T(8,128)(2,1)S(1)}, u32[]{:S(2)}, u32[]{:S(2)}) collective-permute-start(bf16[1024,256]{1,0:T(8,128)(2,1)S(1)} %bitcast.60), channel_id=1, source_target_pairs={{0,1},{1,0},{2,3},{3,2},{4,5},{5,4},{6,7},{7,6},{8,9},{9,8},{10,11... | collective-permute-start | bytes 1572872 | tf_op jit(solution)/shard_map/ppermute | solution.py:213
  178.3 38.3 %all-to-all-start.5 = ((bf16[8,320,256]{2,1,0:T(8,128)(2,1)}), bf16[8,320,256]{2,1,0:T(8,128)(2,1)S(1)}, u32[]{:S(2)}, u32[]{:S(2)}) async-start(bf16[8,320,256]{2,1,0:T(8,128)(2,1)} %broadcast_in_dim.8), calls=%async_computation.5 | async-start | bytes 2621440 | tf_op jit(solution)/shard_map/all_to_all | solution.py:217
  182.7 11.3 %collective-permute-start.15 = (bf16[256,512]{1,0:T(8,128)(2,1)}, bf16[256,512]{1,0:T(8,128)(2,1)}, u32[]{:S(2)}, u32[]{:S(2)}) collective-permute-start(bf16[256,512]{1,0:T(8,128)(2,1)} %bitcast.46), channel_id=1, source_target_pairs={{0,24},{8,0},{16,8},{24,16},{1,25},{9,1},{17,9},{25,17},{2,26},{10... | collective-permute-start | bytes 786440 | tf_op jit(solution)/shard_map/ppermute | solution.py:230
  184.7 11.2 %collective-permute-start.14 = (bf16[256,512]{1,0:T(8,128)(2,1)}, bf16[256,512]{1,0:T(8,128)(2,1)}, u32[]{:S(2)}, u32[]{:S(2)}) collective-permute-start(bf16[256,512]{1,0:T(8,128)(2,1)} %bitcast.46), channel_id=1, source_target_pairs={{0,16},{8,24},{16,0},{24,8},{1,17},{9,25},{17,1},{25,9},{2,18},{10... | collective-permute-start | bytes 786440 | tf_op jit(solution)/shard_map/ppermute | solution.py:230
  186.6 15.6 %collective-permute-start.13 = (bf16[256,512]{1,0:T(8,128)(2,1)}, bf16[256,512]{1,0:T(8,128)(2,1)}, u32[]{:S(2)}, u32[]{:S(2)}) collective-permute-start(bf16[256,512]{1,0:T(8,128)(2,1)} %bitcast.46), channel_id=1, source_target_pairs={{0,8},{8,16},{16,24},{24,0},{1,9},{9,17},{17,25},{25,1},{2,10},{10... | collective-permute-start | bytes 786440 | tf_op jit(solution)/shard_map/ppermute | solution.py:230
  190.0 13.6 %collective-permute-start.11 = (bf16[1024,256]{1,0:T(8,128)(2,1)S(1)}, bf16[1024,256]{1,0:T(8,128)(2,1)}, u32[]{:S(2)}, u32[]{:S(2)}) collective-permute-start(bf16[1024,256]{1,0:T(8,128)(2,1)S(1)} %bitcast.58), channel_id=1, source_target_pairs={{0,1},{1,0},{2,3},{3,2},{4,5},{5,4},{6,7},{7,6},{8,9},{9,8},{10,11... | collective-permute-start | bytes 1572872 | tf_op jit(solution)/shard_map/ppermute | solution.py:213
  193.7 8.5 %copy-start.2 = (bf16[1,256,512]{2,1,0:T(8,128)(2,1)S(1)}, bf16[1,256,512]{2,1,0:T(8,128)(2,1)}, u32[]{:S(2)}) copy-start(bf16[1,256,512]{2,1,0:T(8,128)(2,1)} %stack_reshape.3) | copy-start | bytes 786436
  204.9 9.4 %collective-permute-start.12 = (bf16[320,128]{1,0:T(8,128)(2,1)S(1)}, bf16[320,128]{1,0:T(8,128)(2,1)S(1)}, u32[]{:S(2)}, u32[]{:S(2)}) collective-permute-start(bf16[320,128]{1,0:T(8,128)(2,1)S(1)} %shard_map.68), channel_id=1, source_target_pairs={{0,256},{256,0},{1,257},{257,1},{2,258},{258,2},{3,259},{259,3},{4... | collective-permute-start | bytes 245768 | tf_op jit(solution)/shard_map/ppermute | solution.py:213
  216.6 5.0 %collective-permute-start.16 = (bf16[2560,256]{1,0:T(8,128)(2,1)S(1)}, bf16[2560,256]{1,0:T(8,128)(2,1)S(1)}, u32[]{:S(2)}, u32[]{:S(2)}) collective-permute-start(bf16[2560,256]{1,0:T(8,128)(2,1)S(1)} %bitcast.62), channel_id=1, source_target_pairs={{0,1},{1,0},{2,3},{3,2},{4,5},{5,4},{6,7},{7,6},{8,9},{9,8},{10,11... | collective-permute-start | bytes 3932168 | tf_op jit(solution)/shard_map/ppermute | solution.py:213
  219.0 17.6 %collective-permute-start.17 = (bf16[4,256,512]{2,1,0:T(8,128)(2,1)S(1)}, bf16[4,256,512]{2,1,0:T(8,128)(2,1)}, u32[]{:S(2)}, u32[]{:S(2)}) collective-permute-start(bf16[4,256,512]{2,1,0:T(8,128)(2,1)S(1)} %pad_maximum_fusion.3.near_ref), channel_id=1, source_target_pairs={{0,1},{1,0},{2,3},{3,2},{4,5},{5,4},{6,7},{7,6},{8,9},{9,8},{10,11... | collective-permute-start | bytes 3145736 | tf_op jit(solution)/shard_map/ppermute | solution.py:213
  230.5 15.7 %all-to-all-start.6 = ((bf16[8,96,128]{2,1,0:T(8,128)(2,1)}), bf16[8,96,128]{2,1,0:T(8,128)(2,1)S(1)}, u32[]{:S(2)}, u32[]{:S(2)}) async-start(bf16[8,96,128]{2,1,0:T(8,128)(2,1)} %shard_map.69), calls=%async_computation.6 | async-start | bytes 393216 | tf_op jit(solution)/shard_map/all_to_all | solution.py:217

commit v6 on v4

--- a/solution.py
+++ b/solution.py
@@ -14,32 +14,24 @@
 LIMIT = pltpu.CompilerParams(vmem_limit_bytes=48 * 1024 * 1024)
 
 
-def fold_kernel(w_ref, wo_ref, out_ref):
-    span, cols = wo_ref.shape[0], wo_ref.shape[1] // 4
+def fold_kernel(w_ref, out_ref):
     for h in range(2):
         for r in range(2):
             for j in range(3):
                 out_ref[2 * h + r, 0, :, j * HD : (j + 1) * HD] = w_ref[j, r, :, h * HD : (h + 1) * HD]
-    for x in range(4):
-        for k in range(4):
-            at = x * cols + k * HD
-            out_ref[x, 0, k * span : (k + 1) * span, 3 * HD :] = wo_ref[:, at : at + HD]
-
-
-def fold(w, wo, ny):
+
+
+def fold(w, ny):
     part = w.shape[1] // (2 * ny)
     return pl.pallas_call(
         fold_kernel,
         grid=(ny,),
-        in_specs=[
-            pl.BlockSpec((3, 2, part, 2 * HD), lambda i: (0, 0, i, 0)),
-            pl.BlockSpec((wo.shape[0] // ny, wo.shape[1]), lambda i: (i, 0)),
-        ],
-        out_specs=pl.BlockSpec((4, 1, part, 4 * HD), lambda i: (0, i, 0, 0)),
-        out_shape=jax.ShapeDtypeStruct((4, ny, part, 4 * HD), w.dtype),
-        compiler_params=LIMIT,
-        cost_estimate=pl.CostEstimate(flops=0, bytes_accessed=4 * (w.size + wo.size), transcendentals=0),
-    )(w.reshape(3, 2, ny * part, 2 * HD), wo)
+        in_specs=[pl.BlockSpec((3, 2, part, 2 * HD), lambda i: (0, 0, i, 0))],
+        out_specs=pl.BlockSpec((4, 1, part, 3 * HD), lambda i: (0, i, 0, 0)),
+        out_shape=jax.ShapeDtypeStruct((4, ny, part, 3 * HD), w.dtype),
+        compiler_params=LIMIT,
+        cost_estimate=pl.CostEstimate(flops=0, bytes_accessed=4 * w.size, transcendentals=0),
+    )(w.reshape(3, 2, ny * part, 2 * HD))
 
 
 def near_kernel(c_ref, x_ref, w_ref, out_ref):
@@ -166,24 +158,38 @@
     )(start, q, near, far, kpos)
 
 
-def finish_kernel(c_ref, part_ref, near_ref, far_ref, out_ref):
-    count, nx, half = part_ref.shape[0], part_ref.shape[1], part_ref.shape[2] - EXTRA
-    context = []
+def merge_kernel(near_ref, far_ref, out_ref):
+    nx, half = out_ref.shape[0], out_ref.shape[1]
     for x in range(nx):
         tops, totals = [], []
-        for k in range(count):
-            stat = part_ref[k, x, half:, :].astype(jnp.float32)
+        for ref in (near_ref, far_ref):
+            stat = ref[x, half:, :].astype(jnp.float32)
             stat = jnp.concatenate([stat, jnp.zeros((HD - EXTRA, HD), jnp.float32)]).T[:half]
             tops.append(stat[:, 0:1] + stat[:, 1:2] + stat[:, 2:3])
             totals.append(stat[:, 3:4] + stat[:, 4:5] + stat[:, 5:6])
-        top = tops[0]
-        for k in range(1, count):
-            top = jnp.maximum(top, tops[k])
-        weights = [totals[k] * jnp.exp2(tops[k] - top) for k in range(count)]
-        mixed = sum(part_ref[k, x, :half, :].astype(jnp.float32) * weights[k] for k in range(count))
-        context.append((mixed / sum(weights)).astype(jnp.bfloat16))
-    low = jnp.concatenate([context[0], context[2]], axis=1)
-    high = jnp.concatenate([context[1], context[3]], axis=1)
+        top = jnp.maximum(tops[0], tops[1])
+        a = totals[0] * jnp.exp2(tops[0] - top)
+        b = totals[1] * jnp.exp2(tops[1] - top)
+        mixed = near_ref[x, :half, :].astype(jnp.float32) * a + far_ref[x, :half, :].astype(jnp.float32) * b
+        out_ref[x] = (mixed / (a + b)).astype(out_ref.dtype)
+
+
+def merge(near, far):
+    nx, rows = near.shape[0], near.shape[1] - EXTRA
+    vmem = pl.BlockSpec(memory_space=pltpu.VMEM)
+    return pl.pallas_call(
+        merge_kernel,
+        in_specs=[vmem, vmem],
+        out_specs=vmem,
+        out_shape=jax.ShapeDtypeStruct((nx, rows, HD), jnp.bfloat16),
+        compiler_params=LIMIT,
+        cost_estimate=pl.CostEstimate(flops=8 * near.size, bytes_accessed=6 * near.size, transcendentals=0),
+    )(near, far)
+
+
+def finish_kernel(c_ref, context_ref, near_ref, far_ref, out_ref):
+    low = jnp.concatenate([context_ref[0], context_ref[2]], axis=1)
+    high = jnp.concatenate([context_ref[1], context_ref[3]], axis=1)
     width = out_ref.shape[2]
     for ref, odd in ((near_ref, c_ref[0]), (far_ref, 1 - c_ref[0])):
         for h in range(2):
@@ -195,9 +201,9 @@
             out_ref[at + 1] = terms[:, width:]
 
 
-def finish(core, parts, mine, other):
-    half = parts.shape[2] - EXTRA
-    blocks, _, cols = mine.shape
+def finish(core, context, near, far):
+    half = context.shape[1]
+    blocks, _, cols = near.shape
     vmem = pl.BlockSpec(memory_space=pltpu.VMEM)
     return pl.pallas_call(
         finish_kernel,
@@ -206,9 +212,9 @@
         out_shape=jax.ShapeDtypeStruct((2 * blocks, half, cols // 2), jnp.bfloat16),
         compiler_params=LIMIT,
         cost_estimate=pl.CostEstimate(
-            flops=4 * half * mine.size, bytes_accessed=4 * mine.size, transcendentals=0
+            flops=4 * half * near.size, bytes_accessed=4 * near.size, transcendentals=0
         ),
-    )(core, parts, mine, other)
+    )(core, context, near, far)
 
 
 def swap(block, axis):
@@ -236,6 +242,15 @@
 def distances(axis):
     count = lax.axis_size(axis)
     return sorted(range(1, count), key=lambda s: -min(s, count - s))
+
+
+def scatter_by_shifts(blocks, axis, source):
+    here, count = lax.axis_index(axis), blocks.shape[0]
+    result = pick(blocks, here)
+    for s in distances(axis):
+        got = shift(pick(blocks, (here + s) % count), axis, s)
+        result = jnp.where((here - source) % count == s, got, result)
+    return result
 
 
 def gather_by_shifts(block, axis):
@@ -251,23 +266,24 @@
     route = []
     for z in range(2):
         for x in range(4):
-            for c in range(2):
-                to = ((z ^ across) * 4 + x - x % 2 + c) * 2 + x % 2
-                if to != (z * 4 + x) * 2 + c:
-                    route.append(((z * 4 + x) * 2 + c, to))
-    return lax.ppermute(block, ("zh", "x", "c"), route)
-
-
-def mirror(block, z, y):
-    route = [(i, (i // 2 ^ z) * 2 + (i % 2 ^ y)) for i in range(4)]
-    return lax.ppermute(block, ("zh", "yh"), route)
+            for low in range(4):
+                for c in range(2):
+                    to_low = 3 - low if across else low
+                    to = (((z ^ across) * 4 + x - x % 2 + c) * 4 + to_low) * 2 + x % 2
+                    here = ((z * 4 + x) * 4 + low) * 2 + c
+                    if to != here:
+                        route.append((here, to))
+    return lax.ppermute(block, ("zh", "x", "zl", "c"), route)
+
+
+def mirror(block):
+    return lax.ppermute(block, ("zh", "zl"), [(i, 7 - i) for i in range(8)])
 
 
 def shards(hidden_in, norm_gain, snap_qkv, snap_out, owner_index, block_order):
     rows, width = hidden_in.shape
-    zh, yh, yl, x, c = (lax.axis_index(name) for name in ("zh", "yh", "yl", "x", "c"))
+    zh, y, x, c = (lax.axis_index(name) for name in ("zh", "y", "x", "c"))
     ny, nx = 8, 4
-    ys = ("yh", "yl")
     half = rows // 2
     core = c.reshape(1)
     owner = owner_index[0]
@@ -278,50 +294,49 @@
         mine * lax.rsqrt(jnp.mean(mine * mine, axis=-1, keepdims=True) + 1e-06) * norm_gain
     ).astype(jnp.bfloat16)
 
-    order = block_order.reshape(2, 2, ny // 2, nx) * rows
+    order = block_order.reshape(2, ny, nx) * rows
     offsets = jnp.arange(half, dtype=jnp.int32)
-    kpos = (pick(pick(order, zh), yh)[:, :, None] + offsets).reshape(-1)
+    kpos = (pick(order, zh)[:, :, None] + offsets).reshape(-1)
     kpos = jnp.concatenate([kpos + c * half, kpos + (1 - c) * half]).reshape(1, -1)
-    start = lax.dynamic_index_in_dim(order, yl, 2, keepdims=False).reshape(-1) + c * half
+    here = lax.dynamic_index_in_dim(order, y, 1, keepdims=False)
+    start = jnp.stack([pick(here, zh), pick(here, 1 - zh)]).reshape(-1) + c * half
 
     part = width // (2 * ny)
-    w = fold(snap_qkv[0], snap_out[0], ny)
+    w = fold(snap_qkv[0], ny)
     w = pick(exchange(w, "x"), x0)
-    w, normed, kpos, start = lax.optimization_barrier((w, normed, kpos, start))
-    w = pick(exchange(w, ys), y0)
-    normed = gather_by_shifts(normed, "x").reshape(-1, width)
+    wo = scatter_by_shifts(snap_out[0].reshape(ny, -1, snap_out.shape[2]), "y", y0)
+    w, wo, normed, kpos, start = lax.optimization_barrier((w, wo, normed, kpos, start))
+    w = pick(exchange(w, "y"), y0)
+    wo = jnp.transpose(wo.reshape(wo.shape[0], nx, -1), (1, 0, 2))
+    wo = scatter_by_shifts(wo, "x", x0)
+    wo = jnp.transpose(wo.reshape(wo.shape[0], nx, HD), (1, 0, 2)).reshape(part, HD)
+    w = jnp.concatenate([w, wo], axis=1)
     w, normed = lax.optimization_barrier((w, normed))
     w = jnp.where(zh == zh0, jnp.where(x % 2 == c, w, trade(w, 0)), trade(w, 1))
-    w = spread(w, ys).reshape(ny * part, 4 * HD)
+    w = spread(w, "y").reshape(ny * part, 4 * HD)
+    normed = gather_by_shifts(normed, "x").reshape(-1, width)
     q, kv = project(core, normed, w, swap(w, "c"))
     wo = w[:, 3 * HD :].reshape(ny, nx, part // nx, HD)
     wo = jnp.transpose(wo, (0, 2, 1, 3)).reshape(ny * part // nx, nx * HD)
     q, kv, wo = lax.optimization_barrier((q, kv, wo))
 
-    near = spread(kv, "yl").reshape(-1, 2 * HD)
-    other = {(0, 0): q}
-    for z, y in ((1, 1), (1, 0), (0, 1)):
-        other[z, y] = mirror(q, z, y)
-    q_all = []
-    for z in range(2):
-        for y in range(2):
-            same = [jnp.where(yh == y, other[k, 0], other[k, 1]) for k in range(2)]
-            q_all.append(jnp.where(zh == z, same[0], same[1]))
-    q_all = jnp.concatenate(q_all)
+    near = spread(kv, "y").reshape(-1, 2 * HD)
+    q_all = jnp.concatenate([q, mirror(q)])
     wo = gather_by_shifts(wo, "x")
     near, q_all, wo = lax.optimization_barrier((near, q_all, wo))
     far = swap(near, "c")
     wo_far = swap(wo, "c")
 
     parts = attend(start, q_all, near, far, kpos, half)
-    parts = exchange(parts, ("zh", "yh", "x")).reshape((4, nx) + parts.shape[1:])
-    terms = finish(core, parts, wo, wo_far)
+    context = merge(parts[:nx], mirror(parts[nx:]))
+    context = exchange(context, "x")
+    terms = finish(core, context, wo, wo_far)
     terms = exchange(terms, ("zl", "c")).reshape(-1, rows, terms.shape[2])
     return jnp.sum(terms.astype(jnp.float32), axis=0).astype(jnp.bfloat16)
 
 
 def solution(mesh):
-    fine = Mesh(mesh.devices.reshape(2, 2, 4, 4, 4, 2), ("zh", "yh", "yl", "x", "zl", "c"))
-    ctx, tp = ("zh", "yh", "yl", "x"), ("zl", "c")
+    fine = Mesh(mesh.devices.reshape(2, 8, 4, 4, 2), ("zh", "y", "x", "zl", "c"))
+    ctx, tp = ("zh", "y", "x"), ("zl", "c")
     in_specs = (P(ctx, None), P(), P(ctx, None, None, tp), P(ctx, tp, None), P(), P())
     return jax.shard_map(shards, mesh=fine, in_specs=in_specs, out_specs=P(ctx, tp), check_vma=False)

time: 255 us -> 233 us (0.914)
  blocking collectives: 47.8 us -> 14.7 us
  starting transfers between devices: 81.1 us -> 107 us
  waiting for transfers between devices: 95.9 us -> 77.4 us
  other arithmetic: 1.8 us -> 6.04 us
    ppermute x6 -> x16, starting transfers between devices: 16 us -> 54.7 us  [shift(): lax.ppermute(block, axis, [(i, (i + distance) % count) for i in range(cou...]
    all_to_all x2 -> x1, blocking collectives: 47.8 us -> 14.7 us  [exchange(): return lax.all_to_all(block, axis, 0, 0, tiled=True)]
    ppermute x6 -> x16, waiting for transfers between devices: 26.1 us -> 10.5 us  [shift(): lax.ppermute(block, axis, [(i, (i + distance) % count) for i in range(cou...]
    all_to_all x4 -> x5, waiting for transfers between devices: 64.9 us -> 50 us  [exchange(): return lax.all_to_all(block, axis, 0, 0, tiled=True)]
    ppermute x5 -> x4, waiting for transfers between devices: 3.26 us -> 15.2 us  [the longest x2 10.9 us: mirror(): return lax.ppermute(block, ('zh', 'zl'), [(i, 7 - i) for i in range(8)])]
    ppermute x5 -> x4, starting transfers between devices: 30.2 us -> 18.8 us  [the longest x2 12.9 us: trade(): return lax.ppermute(block, ('zh', 'x', 'zl', 'c'), route)]
    all_to_all x4 -> x5, starting transfers between devices: 28.3 us -> 27.1 us  [exchange(): return lax.all_to_all(block, axis, 0, 0, tiled=True)]
  transfers between devices with their start and end apart: 18 -> 28, of which waited for: 12 -> 15; matrix products, arithmetic and copies ran while one was open for 1% -> 4% of each run, Pallas kernels for 4% -> 4%
where the time goes in v6:
time: 233 us; the launch traced here: 232 us
  starting transfers between devices  107 us (46%)
  waiting for transfers between devices  77.4 us (33%)
  Pallas kernels  17.4 us (7%)
  blocking collectives  14.7 us (6%)
  local copies, waits for them, and re-layouts  7.55 us (3%)
  other arithmetic  6.04 us (3%)
    ppermute x16, starting transfers between devices, shift(): lax.ppermute(block, axis, [(i, (i + distance) % count) for i in range(cou...  54.7 us
    all_to_all x5, waiting for transfers between devices, exchange(): return lax.all_to_all(block, axis, 0, 0, tiled=True)  50 us
    all_to_all x5, starting transfers between devices, exchange(): return lax.all_to_all(block, axis, 0, 0, tiled=True)  27.1 us
    all_to_all x1, blocking collectives, exchange(): return lax.all_to_all(block, axis, 0, 0, tiled=True)  14.7 us
    ppermute x2, starting transfers between devices, trade(): return lax.ppermute(block, ('zh', 'x', 'zl', 'c'), route)  12.9 us
    ppermute x2, waiting for transfers between devices, mirror(): return lax.ppermute(block, ('zh', 'zl'), [(i, 7 - i) for i in range(8)])  10.9 us
    ppermute x16, waiting for transfers between devices, shift(): lax.ppermute(block, axis, [(i, (i + distance) % count) for i in range(cou...  10.5 us
    pallas_call x1, Pallas kernels, attend(): pl.pallas_call(attend_kernel, grid=(nq // tile,), in_specs=[pl.BlockSpec(...  8.11 us
  transfers between devices with their start and end apart: 28, of which 15 were waited for; matrix products, arithmetic and copies ran while one was open for 4% of the time, Pallas kernels for 4%

profile of v6, /device:TPU:1, one launch (start us, length us, event | category | flops | bytes accessed | tf_op | source)
XLA Modules:
  0.0 231.6 jit_solution(17188079213587949059)
XLA Ops:
  0.0 6.3 %shard_map.64 = bf16[4,8,128,384]{3,2,1,0:T(8,128)(2,1)} custom-call(bf16[3,2,1024,256]{3,2,1,0:T(8,128)(2,1)} %bitcast.93), custom_call_target="tpu_custom_call" | custom-call | bytes 6291456 | tf_op jit(solution)/shard_map/pallas_call | solution.py:26
  6.3 4.8 %all-to-all-start = ((bf16[4,8,128,384]{3,2,1,0:T(8,128)(2,1)}), bf16[4,8,128,384]{3,2,1,0:T(8,128)(2,1)S(1)}, u32[]{:S(2)}, u32[]{:S(2)}) async-start(bf16[4,8,128,384]{3,2,1,0:T(8,128)(2,1)} %shard_map.64), calls=%async_computation | async-start | bytes 6291456 | tf_op jit(solution)/shard_map/all_to_all | solution.py:225
  11.1 2.2 dynamic-slice_bitcast_fusion.1
  13.3 5.1 %collective-permute-start = (bf16[32,2048]{1,0:T(8,128)(2,1)}, bf16[32,2048]{1,0:T(8,128)(2,1)}, u32[]{:S(2)}, u32[]{:S(2)}) collective-permute-start(bf16[32,2048]{1,0:T(8,128)(2,1)} %get-tuple-element.49), channel_id=1, source_target_pairs={{0,224},{32,0},{64,32},{96,64},{128,96},{160,128},{192,160},{224,1... | collective-permute-start | bytes 393224 | tf_op jit(solution)/shard_map/ppermute | solution.py:239
  18.4 1.9 collective-permute-start.1
  20.4 4.1 %collective-permute-start.2 = (bf16[32,2048]{1,0:T(8,128)(2,1)}, bf16[32,2048]{1,0:T(8,128)(2,1)}, u32[]{:S(2)}, u32[]{:S(2)}) collective-permute-start(bf16[32,2048]{1,0:T(8,128)(2,1)} %get-tuple-element.47), channel_id=1, source_target_pairs={{0,192},{32,224},{64,0},{96,32},{128,64},{160,96},{192,128},{224,1... | collective-permute-start | bytes 393224 | tf_op jit(solution)/shard_map/ppermute | solution.py:239
  24.5 2.0 collective-permute-start.3
  26.6 4.9 %collective-permute-start.4 = (bf16[32,2048]{1,0:T(8,128)(2,1)}, bf16[32,2048]{1,0:T(8,128)(2,1)}, u32[]{:S(2)}, u32[]{:S(2)}) collective-permute-start(bf16[32,2048]{1,0:T(8,128)(2,1)} %get-tuple-element.45), channel_id=1, source_target_pairs={{0,160},{32,192},{64,224},{96,0},{128,32},{160,64},{192,96},{224,1... | collective-permute-start | bytes 393224 | tf_op jit(solution)/shard_map/ppermute | solution.py:239
  31.6 1.1 fusion
  32.8 1.1 fusion.2
  34.0 2.9 %collective-permute-start.5 = (bf16[32,2048]{1,0:T(8,128)(2,1)}, bf16[32,2048]{1,0:T(8,128)(2,1)}, u32[]{:S(2)}, u32[]{:S(2)}) collective-permute-start(bf16[32,2048]{1,0:T(8,128)(2,1)} %get-tuple-element.44), channel_id=1, source_target_pairs={{0,96},{32,128},{64,160},{96,192},{128,224},{160,0},{192,32},{224,... | collective-permute-start | bytes 393224 | tf_op jit(solution)/shard_map/ppermute | solution.py:239
  37.0 5.0 %collective-permute-start.6 = (bf16[32,2048]{1,0:T(8,128)(2,1)}, bf16[32,2048]{1,0:T(8,128)(2,1)}, u32[]{:S(2)}, u32[]{:S(2)}) collective-permute-start(bf16[32,2048]{1,0:T(8,128)(2,1)} %get-tuple-element.43), channel_id=1, source_target_pairs={{0,128},{32,160},{64,192},{96,224},{128,0},{160,32},{192,64},{224,... | collective-permute-start | bytes 393224 | tf_op jit(solution)/shard_map/ppermute | solution.py:239
  43.0 1.2 collective-permute-done.5
  44.2 6.0 %collective-permute-done.6 = bf16[32,2048]{1,0:T(8,128)(2,1)} collective-permute-done((bf16[32,2048]{1,0:T(8,128)(2,1)}, bf16[32,2048]{1,0:T(8,128)(2,1)}, u32[]{:S(2)}, u32[]{:S(2)}) %collective-permute-start.6) | collective-permute-done | bytes 131104 | tf_op jit(solution)/shard_map/ppermute | solution.py:239
  50.2 1.7 fusion.8
  52.9 10.2 %all-to-all-start.1 = ((bf16[8,128,384]{2,1,0:T(8,128)(2,1)}), bf16[8,128,384]{2,1,0:T(8,128)(2,1)S(1)}, u32[]{:S(2)}, u32[]{:S(2)}) async-start(bf16[8,128,384]{2,1,0:T(8,128)(2,1)} %dynamic-slice_bitcast_fusion), calls=%async_computation.1 | async-start | bytes 1572864 | tf_op jit(solution)/shard_map/all_to_all | solution.py:225
  63.5 4.6 %collective-permute-start.7 = (bf16[32,512]{1,0:T(8,128)(2,1)S(1)}, bf16[32,512]{1,0:T(8,128)(2,1)S(1)}, u32[]{:S(2)}, u32[]{:S(2)}) collective-permute-start(bf16[32,512]{1,0:T(8,128)(2,1)S(1)} %bitcast.112), channel_id=1, source_target_pairs={{0,24},{8,0},{16,8},{24,16},{1,25},{9,1},{17,9},{25,17},{2,26},{10... | collective-permute-start | bytes 98312 | tf_op jit(solution)/shard_map/ppermute | solution.py:239
  68.1 1.9 collective-permute-start.8
  70.0 3.7 %collective-permute-start.9 = (bf16[32,512]{1,0:T(8,128)(2,1)S(1)}, bf16[32,512]{1,0:T(8,128)(2,1)S(1)}, u32[]{:S(2)}, u32[]{:S(2)}) collective-permute-start(bf16[32,512]{1,0:T(8,128)(2,1)S(1)} %bitcast.114), channel_id=1, source_target_pairs={{0,16},{8,24},{16,0},{24,8},{1,17},{9,25},{17,1},{25,9},{2,18},{10... | collective-permute-start | bytes 98312 | tf_op jit(solution)/shard_map/ppermute | solution.py:239
  74.2 2.1 collective-permute-done.9
  76.4 10.3 %all-to-all-done.1 = bf16[8,128,384]{2,1,0:T(8,128)(2,1)S(1)} async-done(((bf16[8,128,384]{2,1,0:T(8,128)(2,1)}), bf16[8,128,384]{2,1,0:T(8,128)(2,1)S(1)}, u32[]{:S(2)}, u32[]{:S(2)}) %all-to-all-start.1) | async-done | bytes 786464 | tf_op jit(solution)/shard_map/all_to_all | solution.py:225
  86.7 11.0 %collective-permute-start.14 = (bf16[128,512]{1,0:T(8,128)(2,1)S(1)}, bf16[128,512]{1,0:T(8,128)(2,1)S(1)}, u32[]{:S(2)}, u32[]{:S(2)}) collective-permute-start(bf16[128,512]{1,0:T(8,128)(2,1)S(1)} %pad_maximum_fusion.5), channel_id=1, source_target_pairs={{0,262},{1,270},{2,260},{3,268},{4,258},{5,266},{6,256},{7,264},{8... | collective-permute-start | bytes 393224 | tf_op jit(solution)/shard_map/ppermute | solution.py:276
  97.7 1.9 collective-permute-start.13
  99.7 3.6 %collective-permute-done.14 = bf16[128,512]{1,0:T(8,128)(2,1)S(1)} collective-permute-done((bf16[128,512]{1,0:T(8,128)(2,1)S(1)}, bf16[128,512]{1,0:T(8,128)(2,1)S(1)}, u32[]{:S(2)}, u32[]{:S(2)}) %collective-permute-start.14) | collective-permute-done | bytes 131104 | tf_op jit(solution)/shard_map/ppermute | solution.py:276
  104.0 1.1 broadcast_in_dim.4
  105.1 3.6 %all-to-all-start.2 = ((bf16[8,128,512]{2,1,0:T(8,128)(2,1)}), bf16[8,128,512]{2,1,0:T(8,128)(2,1)S(1)}, u32[]{:S(2)}, u32[]{:S(2)}) async-start(bf16[8,128,512]{2,1,0:T(8,128)(2,1)} %broadcast_in_dim.4), calls=%async_computation.2 | async-start | bytes 2097152 | tf_op jit(solution)/shard_map/all_to_all | solution.py:225
  108.7 1.9 collective-permute-start.12
  110.6 4.3 %collective-permute-start.11 = (bf16[80,2048]{1,0:T(8,128)(2,1)S(1)}, bf16[80,2048]{1,0:T(8,128)(2,1)S(1)}, u32[]{:S(2)}, u32[]{:S(2)}) collective-permute-start(bf16[80,2048]{1,0:T(8,128)(2,1)S(1)} %fusion.2), channel_id=1, source_target_pairs={{0,16},{8,24},{16,0},{24,8},{1,17},{9,25},{17,1},{25,9},{2,18},{10... | collective-permute-start | bytes 983048 | tf_op jit(solution)/shard_map/ppermute | solution.py:239
  114.9 2.8 %collective-permute-start.10 = (bf16[80,2048]{1,0:T(8,128)(2,1)S(1)}, bf16[80,2048]{1,0:T(8,128)(2,1)S(1)}, u32[]{:S(2)}, u32[]{:S(2)}) collective-permute-start(bf16[80,2048]{1,0:T(8,128)(2,1)S(1)} %fusion.2), channel_id=1, source_target_pairs={{0,8},{8,16},{16,24},{24,0},{1,9},{9,17},{17,25},{25,1},{2,10},{10... | collective-permute-start | bytes 983048 | tf_op jit(solution)/shard_map/ppermute | solution.py:239
  117.7 19.7 %all-to-all-done.2 = bf16[8,128,512]{2,1,0:T(8,128)(2,1)S(1)} async-done(((bf16[8,128,512]{2,1,0:T(8,128)(2,1)}), bf16[8,128,512]{2,1,0:T(8,128)(2,1)S(1)}, u32[]{:S(2)}, u32[]{:S(2)}) %all-to-all-start.2) | async-done | bytes 1048608 | tf_op jit(solution)/shard_map/all_to_all | solution.py:225
  137.3 2.3 collective-permute-start.15
  142.4 1.2 broadcast_in_dim.5
  143.6 3.6 %all-to-all-start.3 = ((bf16[8,320,256]{2,1,0:T(8,128)(2,1)}), bf16[8,320,256]{2,1,0:T(8,128)(2,1)S(1)}, u32[]{:S(2)}, u32[]{:S(2)}) async-start(bf16[8,320,256]{2,1,0:T(8,128)(2,1)} %broadcast_in_dim.5), calls=%async_computation.3 | async-start | bytes 2621440 | tf_op jit(solution)/shard_map/all_to_all | solution.py:225
  147.1 1.9 collective-permute-start.19
  149.1 4.9 %collective-permute-start.18 = (bf16[256,512]{1,0:T(8,128)(2,1)S(1)}, bf16[256,512]{1,0:T(8,128)(2,1)S(1)}, u32[]{:S(2)}, u32[]{:S(2)}) collective-permute-start(bf16[256,512]{1,0:T(8,128)(2,1)S(1)} %bitcast.101), channel_id=1, source_target_pairs={{0,16},{8,24},{16,0},{24,8},{1,17},{9,25},{17,1},{25,9},{2,18},{10... | collective-permute-start | bytes 786440 | tf_op jit(solution)/shard_map/ppermute | solution.py:239
  154.0 2.8 %collective-permute-start.17 = (bf16[256,512]{1,0:T(8,128)(2,1)S(1)}, bf16[256,512]{1,0:T(8,128)(2,1)S(1)}, u32[]{:S(2)}, u32[]{:S(2)}) collective-permute-start(bf16[256,512]{1,0:T(8,128)(2,1)S(1)} %bitcast.102), channel_id=1, source_target_pairs={{0,8},{8,16},{16,24},{24,0},{1,9},{9,17},{17,25},{25,1},{2,10},{10... | collective-permute-start | bytes 786440 | tf_op jit(solution)/shard_map/ppermute | solution.py:239
  156.7 2.6 %collective-permute-start.16 = (bf16[320,128]{1,0:T(8,128)(2,1)S(1)}, bf16[320,128]{1,0:T(8,128)(2,1)S(1)}, u32[]{:S(2)}, u32[]{:S(2)}) collective-permute-start(bf16[320,128]{1,0:T(8,128)(2,1)S(1)} %get-tuple-element.29), channel_id=1, source_target_pairs={{0,262},{2,260},{4,258},{6,256},{256,6},{258,4},{260,2},{262,0},{1... | collective-permute-start | bytes 245768 | tf_op jit(solution)/shard_map/ppermute | solution.py:280
  159.4 5.3 %collective-permute-done.16 = bf16[320,128]{1,0:T(8,128)(2,1)S(1)} collective-permute-done((bf16[320,128]{1,0:T(8,128)(2,1)S(1)}, bf16[320,128]{1,0:T(8,128)(2,1)S(1)}, u32[]{:S(2)}, u32[]{:S(2)}) %collective-permute-start.16) | collective-permute-done | bytes 81952 | tf_op jit(solution)/shard_map/ppermute | solution.py:280
  166.4 15.5 %all-to-all-done.3 = bf16[8,320,256]{2,1,0:T(8,128)(2,1)S(1)} async-done(((bf16[8,320,256]{2,1,0:T(8,128)(2,1)}), bf16[8,320,256]{2,1,0:T(8,128)(2,1)S(1)}, u32[]{:S(2)}, u32[]{:S(2)}) %all-to-all-start.3) | async-done | bytes 1310752 | tf_op jit(solution)/shard_map/all_to_all | solution.py:225
  181.9 2.4 %collective-permute-start.20 = (bf16[2560,256]{1,0:T(8,128)(2,1)S(1)}, bf16[2560,256]{1,0:T(8,128)(2,1)S(1)}, u32[]{:S(2)}, u32[]{:S(2)}) collective-permute-start(bf16[2560,256]{1,0:T(8,128)(2,1)S(1)} %bitcast.90), channel_id=1, source_target_pairs={{0,1},{1,0},{2,3},{3,2},{4,5},{5,4},{6,7},{7,6},{8,9},{9,8},{10,11... | collective-permute-start | bytes 3932168 | tf_op jit(solution)/shard_map/ppermute | solution.py:221
  184.3 1.9 collective-permute-start.22
  187.8 8.1 %shard_map.67 = bf16[8,96,128]{2,1,0:T(8,128)(2,1)S(1)} custom-call(s32[8]{0:T(128)S(1)} %add.288.start_ref, bf16[640,128]{1,0:T(8,128)(2,1)S(1)} %copy-done, bf16[2560,256]{1,0:T(8,128)(2,1)S(1)} %bitcast.91, bf16[2560,256]{1,0:T(8,128)(2,1)S(1)} %collective-permute-done.20.far_ref, s32[1,5120]{1,0:T(1,128)S(1)} %bitcast.92), custom_call_target="tpu_custom_call" | custom-call | flops 1677721600 | bytes 2621440 | tf_op jit(solution)/shard_map/pallas_call | solution.py:141
  196.0 3.2 %collective-permute-start.21 = (bf16[4,96,128]{2,1,0:T(8,128)(2,1)S(1)}, bf16[4,96,128]{2,1,0:T(8,128)(2,1)S(1)}, u32[]{:S(2)}, u32[]{:S(2)}) collective-permute-start(bf16[4,96,128]{2,1,0:T(8,128)(2,1)S(1)} %get-tuple-element.50), channel_id=1, source_target_pairs={{0,262},{2,260},{4,258},{6,256},{256,6},{258,4},{260,2},{262,0},{1... | collective-permute-start | bytes 294920 | tf_op jit(solution)/shard_map/ppermute | solution.py:280
  199.2 5.6 %collective-permute-done.21.far_ref = bf16[4,96,128]{2,1,0:T(8,128)(2,1)S(1)} collective-permute-done((bf16[4,96,128]{2,1,0:T(8,128)(2,1)S(1)}, bf16[4,96,128]{2,1,0:T(8,128)(2,1)S(1)}, u32[]{:S(2)}, u32[]{:S(2)}) %collective-permute-start.21) | collective-permute-done | bytes 98336 | tf_op jit(solution)/shard_map/ppermute | solution.py:280
  204.8 1.5 shard_map.68
  206.3 4.9 %all-to-all-start.4 = ((bf16[4,80,128]{2,1,0:T(8,128)(2,1)}), bf16[4,80,128]{2,1,0:T(8,128)(2,1)S(1)}, u32[]{:S(2)}, u32[]{:S(2)}) async-start(bf16[4,80,128]{2,1,0:T(8,128)(2,1)} %shard_map.68), calls=%async_computation.4 | async-start | bytes 163840 | tf_op jit(solution)/shard_map/all_to_all | solution.py:225
  211.2 4.6 %all-to-all-done.4.context_ref = bf16[4,80,128]{2,1,0:T(8,128)(2,1)S(1)} async-done(((bf16[4,80,128]{2,1,0:T(8,128)(2,1)}), bf16[4,80,128]{2,1,0:T(8,128)(2,1)S(1)}, u32[]{:S(2)}, u32[]{:S(2)}) %all-to-all-start.4) | async-done | bytes 81952 | tf_op jit(solution)/shard_map/all_to_all | solution.py:225
  216.2 14.7 %all_to_all.30 = bf16[8,80,256]{2,1,0:T(8,128)(2,1)S(1)} all-to-all(bf16[8,80,256]{2,1,0:T(8,128)(2,1)S(1)} %shard_map.69), channel_id=1, replica_groups=mesh['zh'=2,'y'=8,'x'=4,'zl'=4,'c'=2] {'zl','c'}, dimensions={0} | all-to-all | bytes 655360 | tf_op jit(solution)/shard_map/all_to_all | solution.py:225
  (64 shorter events, 10.2 us)
Async XLA Ops:
  6.3 45.6 %all-to-all-start = ((bf16[4,8,128,384]{3,2,1,0:T(8,128)(2,1)}), bf16[4,8,128,384]{3,2,1,0:T(8,128)(2,1)S(1)}, u32[]{:S(2)}, u32[]{:S(2)}) async-start(bf16[4,8,128,384]{3,2,1,0:T(8,128)(2,1)} %shard_map.64), calls=%async_computation | async-start | bytes 6291456 | tf_op jit(solution)/shard_map/all_to_all | solution.py:225
  11.1 20.4 %copy-start.3 = (s32[64]{0:T(128)S(1)}, s32[64]{0:T(128)}, u32[]{:S(2)}) copy-start(s32[64]{0:T(128)} %param.11) | copy-start | bytes 772
  11.1 21.7 %copy-start.2 = (f32[2048]{0:T(1024)S(1)}, f32[2048]{0:T(1024)}, u32[]{:S(2)}) copy-start(f32[2048]{0:T(1024)} %param.7) | copy-start | bytes 24580
  13.3 20.7 %collective-permute-start = (bf16[32,2048]{1,0:T(8,128)(2,1)}, bf16[32,2048]{1,0:T(8,128)(2,1)}, u32[]{:S(2)}, u32[]{:S(2)}) collective-permute-start(bf16[32,2048]{1,0:T(8,128)(2,1)} %get-tuple-element.49), channel_id=1, source_target_pairs={{0,224},{32,0},{64,32},{96,64},{128,96},{160,128},{192,160},{224,1... | collective-permute-start | bytes 393224 | tf_op jit(solution)/shard_map/ppermute | solution.py:239
  18.4 18.5 %collective-permute-start.1 = (bf16[32,2048]{1,0:T(8,128)(2,1)}, bf16[32,2048]{1,0:T(8,128)(2,1)}, u32[]{:S(2)}, u32[]{:S(2)}) collective-permute-start(bf16[32,2048]{1,0:T(8,128)(2,1)} %get-tuple-element.48), channel_id=1, source_target_pairs={{0,32},{32,64},{64,96},{96,128},{128,160},{160,192},{192,224},{224... | collective-permute-start | bytes 393224 | tf_op jit(solution)/shard_map/ppermute | solution.py:239
  20.4 22.6 %collective-permute-start.2 = (bf16[32,2048]{1,0:T(8,128)(2,1)}, bf16[32,2048]{1,0:T(8,128)(2,1)}, u32[]{:S(2)}, u32[]{:S(2)}) collective-permute-start(bf16[32,2048]{1,0:T(8,128)(2,1)} %get-tuple-element.47), channel_id=1, source_target_pairs={{0,192},{32,224},{64,0},{96,32},{128,64},{160,96},{192,128},{224,1... | collective-permute-start | bytes 393224 | tf_op jit(solution)/shard_map/ppermute | solution.py:239
  24.5 18.4 %collective-permute-start.3 = (bf16[32,2048]{1,0:T(8,128)(2,1)}, bf16[32,2048]{1,0:T(8,128)(2,1)}, u32[]{:S(2)}, u32[]{:S(2)}) collective-permute-start(bf16[32,2048]{1,0:T(8,128)(2,1)} %get-tuple-element.46), channel_id=1, source_target_pairs={{0,64},{32,96},{64,128},{96,160},{128,192},{160,224},{192,0},{224,... | collective-permute-start | bytes 393224 | tf_op jit(solution)/shard_map/ppermute | solution.py:239
  26.6 16.4 %collective-permute-start.4 = (bf16[32,2048]{1,0:T(8,128)(2,1)}, bf16[32,2048]{1,0:T(8,128)(2,1)}, u32[]{:S(2)}, u32[]{:S(2)}) collective-permute-start(bf16[32,2048]{1,0:T(8,128)(2,1)} %get-tuple-element.45), channel_id=1, source_target_pairs={{0,160},{32,192},{64,224},{96,0},{128,32},{160,64},{192,96},{224,1... | collective-permute-start | bytes 393224 | tf_op jit(solution)/shard_map/ppermute | solution.py:239
  34.0 10.1 %collective-permute-start.5 = (bf16[32,2048]{1,0:T(8,128)(2,1)}, bf16[32,2048]{1,0:T(8,128)(2,1)}, u32[]{:S(2)}, u32[]{:S(2)}) collective-permute-start(bf16[32,2048]{1,0:T(8,128)(2,1)} %get-tuple-element.44), channel_id=1, source_target_pairs={{0,96},{32,128},{64,160},{96,192},{128,224},{160,0},{192,32},{224,... | collective-permute-start | bytes 393224 | tf_op jit(solution)/shard_map/ppermute | solution.py:239
  37.0 13.2 %collective-permute-start.6 = (bf16[32,2048]{1,0:T(8,128)(2,1)}, bf16[32,2048]{1,0:T(8,128)(2,1)}, u32[]{:S(2)}, u32[]{:S(2)}) collective-permute-start(bf16[32,2048]{1,0:T(8,128)(2,1)} %get-tuple-element.43), channel_id=1, source_target_pairs={{0,128},{32,160},{64,192},{96,224},{128,0},{160,32},{192,64},{224,... | collective-permute-start | bytes 393224 | tf_op jit(solution)/shard_map/ppermute | solution.py:239
  52.9 10.2 %copy-start.1 = (bf16[32,2048]{1,0:T(8,128)(2,1)S(1)}, bf16[32,2048]{1,0:T(8,128)(2,1)}, u32[]{:S(2)}) copy-start(bf16[32,2048]{1,0:T(8,128)(2,1)} %fusion.8) | copy-start | bytes 393220
  52.9 33.8 %all-to-all-start.1 = ((bf16[8,128,384]{2,1,0:T(8,128)(2,1)}), bf16[8,128,384]{2,1,0:T(8,128)(2,1)S(1)}, u32[]{:S(2)}, u32[]{:S(2)}) async-start(bf16[8,128,384]{2,1,0:T(8,128)(2,1)} %dynamic-slice_bitcast_fusion), calls=%async_computation.1 | async-start | bytes 1572864 | tf_op jit(solution)/shard_map/all_to_all | solution.py:225
  63.5 10.2 %collective-permute-start.7 = (bf16[32,512]{1,0:T(8,128)(2,1)S(1)}, bf16[32,512]{1,0:T(8,128)(2,1)S(1)}, u32[]{:S(2)}, u32[]{:S(2)}) collective-permute-start(bf16[32,512]{1,0:T(8,128)(2,1)S(1)} %bitcast.112), channel_id=1, source_target_pairs={{0,24},{8,0},{16,8},{24,16},{1,25},{9,1},{17,9},{25,17},{2,26},{10... | collective-permute-start | bytes 98312 | tf_op jit(solution)/shard_map/ppermute | solution.py:239
  68.1 6.2 %collective-permute-start.8 = (bf16[32,512]{1,0:T(8,128)(2,1)S(1)}, bf16[32,512]{1,0:T(8,128)(2,1)S(1)}, u32[]{:S(2)}, u32[]{:S(2)}) collective-permute-start(bf16[32,512]{1,0:T(8,128)(2,1)S(1)} %bitcast.113), channel_id=1, source_target_pairs={{0,8},{8,16},{16,24},{24,0},{1,9},{9,17},{17,25},{25,1},{2,10},{10... | collective-permute-start | bytes 98312 | tf_op jit(solution)/shard_map/ppermute | solution.py:239
  70.0 6.3 %collective-permute-start.9 = (bf16[32,512]{1,0:T(8,128)(2,1)S(1)}, bf16[32,512]{1,0:T(8,128)(2,1)S(1)}, u32[]{:S(2)}, u32[]{:S(2)}) collective-permute-start(bf16[32,512]{1,0:T(8,128)(2,1)S(1)} %bitcast.114), channel_id=1, source_target_pairs={{0,16},{8,24},{16,0},{24,8},{1,17},{9,25},{17,1},{25,9},{2,18},{10... | collective-permute-start | bytes 98312 | tf_op jit(solution)/shard_map/ppermute | solution.py:239
  86.7 16.6 %collective-permute-start.14 = (bf16[128,512]{1,0:T(8,128)(2,1)S(1)}, bf16[128,512]{1,0:T(8,128)(2,1)S(1)}, u32[]{:S(2)}, u32[]{:S(2)}) collective-permute-start(bf16[128,512]{1,0:T(8,128)(2,1)S(1)} %pad_maximum_fusion.5), channel_id=1, source_target_pairs={{0,262},{1,270},{2,260},{3,268},{4,258},{5,266},{6,256},{7,264},{8... | collective-permute-start | bytes 393224 | tf_op jit(solution)/shard_map/ppermute | solution.py:276
  97.7 6.3 %collective-permute-start.13 = (bf16[128,512]{1,0:T(8,128)(2,1)S(1)}, bf16[128,512]{1,0:T(8,128)(2,1)S(1)}, u32[]{:S(2)}, u32[]{:S(2)}) collective-permute-start(bf16[128,512]{1,0:T(8,128)(2,1)S(1)} %pad_maximum_fusion.5), channel_id=1, source_target_pairs={{1,8},{3,10},{5,12},{7,14},{8,1},{10,3},{12,5},{14,7},{17,24},{19,... | collective-permute-start | bytes 393224 | tf_op jit(solution)/shard_map/ppermute | solution.py:276
  105.1 32.2 %all-to-all-start.2 = ((bf16[8,128,512]{2,1,0:T(8,128)(2,1)}), bf16[8,128,512]{2,1,0:T(8,128)(2,1)S(1)}, u32[]{:S(2)}, u32[]{:S(2)}) async-start(bf16[8,128,512]{2,1,0:T(8,128)(2,1)} %broadcast_in_dim.4), calls=%async_computation.2 | async-start | bytes 2097152 | tf_op jit(solution)/shard_map/all_to_all | solution.py:225
  108.7 31.0 %collective-permute-start.12 = (bf16[80,2048]{1,0:T(8,128)(2,1)S(1)}, bf16[80,2048]{1,0:T(8,128)(2,1)S(1)}, u32[]{:S(2)}, u32[]{:S(2)}) collective-permute-start(bf16[80,2048]{1,0:T(8,128)(2,1)S(1)} %fusion.2), channel_id=1, source_target_pairs={{0,24},{8,0},{16,8},{24,16},{1,25},{9,1},{17,9},{25,17},{2,26},{10... | collective-permute-start | bytes 983048 | tf_op jit(solution)/shard_map/ppermute | solution.py:239
  110.6 29.1 %collective-permute-start.11 = (bf16[80,2048]{1,0:T(8,128)(2,1)S(1)}, bf16[80,2048]{1,0:T(8,128)(2,1)S(1)}, u32[]{:S(2)}, u32[]{:S(2)}) collective-permute-start(bf16[80,2048]{1,0:T(8,128)(2,1)S(1)} %fusion.2), channel_id=1, source_target_pairs={{0,16},{8,24},{16,0},{24,8},{1,17},{9,25},{17,1},{25,9},{2,18},{10... | collective-permute-start | bytes 983048 | tf_op jit(solution)/shard_map/ppermute | solution.py:239
  114.9 24.8 %collective-permute-start.10 = (bf16[80,2048]{1,0:T(8,128)(2,1)S(1)}, bf16[80,2048]{1,0:T(8,128)(2,1)S(1)}, u32[]{:S(2)}, u32[]{:S(2)}) collective-permute-start(bf16[80,2048]{1,0:T(8,128)(2,1)S(1)} %fusion.2), channel_id=1, source_target_pairs={{0,8},{8,16},{16,24},{24,0},{1,9},{9,17},{17,25},{25,1},{2,10},{10... | collective-permute-start | bytes 983048 | tf_op jit(solution)/shard_map/ppermute | solution.py:239
  137.3 4.6 %collective-permute-start.15 = (bf16[1024,512]{1,0:T(8,128)(2,1)S(1)}, bf16[1024,512]{1,0:T(8,128)(2,1)S(1)}, u32[]{:S(2)}, u32[]{:S(2)}) collective-permute-start(bf16[1024,512]{1,0:T(8,128)(2,1)S(1)} %bitcast.87), channel_id=1, source_target_pairs={{0,1},{1,0},{2,3},{3,2},{4,5},{5,4},{6,7},{7,6},{8,9},{9,8},{10,11... | collective-permute-start | bytes 3145736 | tf_op jit(solution)/shard_map/ppermute | solution.py:221
  143.6 38.3 %all-to-all-start.3 = ((bf16[8,320,256]{2,1,0:T(8,128)(2,1)}), bf16[8,320,256]{2,1,0:T(8,128)(2,1)S(1)}, u32[]{:S(2)}, u32[]{:S(2)}) async-start(bf16[8,320,256]{2,1,0:T(8,128)(2,1)} %broadcast_in_dim.5), calls=%async_computation.3 | async-start | bytes 2621440 | tf_op jit(solution)/shard_map/all_to_all | solution.py:225
  147.1 18.2 %collective-permute-start.19 = (bf16[256,512]{1,0:T(8,128)(2,1)S(1)}, bf16[256,512]{1,0:T(8,128)(2,1)S(1)}, u32[]{:S(2)}, u32[]{:S(2)}) collective-permute-start(bf16[256,512]{1,0:T(8,128)(2,1)S(1)} %bitcast.100), channel_id=1, source_target_pairs={{0,24},{8,0},{16,8},{24,16},{1,25},{9,1},{17,9},{25,17},{2,26},{10... | collective-permute-start | bytes 786440 | tf_op jit(solution)/shard_map/ppermute | solution.py:239
  149.1 16.3 %collective-permute-start.18 = (bf16[256,512]{1,0:T(8,128)(2,1)S(1)}, bf16[256,512]{1,0:T(8,128)(2,1)S(1)}, u32[]{:S(2)}, u32[]{:S(2)}) collective-permute-start(bf16[256,512]{1,0:T(8,128)(2,1)S(1)} %bitcast.101), channel_id=1, source_target_pairs={{0,16},{8,24},{16,0},{24,8},{1,17},{9,25},{17,1},{25,9},{2,18},{10... | collective-permute-start | bytes 786440 | tf_op jit(solution)/shard_map/ppermute | solution.py:239
  154.0 12.0 %collective-permute-start.17 = (bf16[256,512]{1,0:T(8,128)(2,1)S(1)}, bf16[256,512]{1,0:T(8,128)(2,1)S(1)}, u32[]{:S(2)}, u32[]{:S(2)}) collective-permute-start(bf16[256,512]{1,0:T(8,128)(2,1)S(1)} %bitcast.102), channel_id=1, source_target_pairs={{0,8},{8,16},{16,24},{24,0},{1,9},{9,17},{17,25},{25,1},{2,10},{10... | collective-permute-start | bytes 786440 | tf_op jit(solution)/shard_map/ppermute | solution.py:239
  156.7 7.9 %collective-permute-start.16 = (bf16[320,128]{1,0:T(8,128)(2,1)S(1)}, bf16[320,128]{1,0:T(8,128)(2,1)S(1)}, u32[]{:S(2)}, u32[]{:S(2)}) collective-permute-start(bf16[320,128]{1,0:T(8,128)(2,1)S(1)} %get-tuple-element.29), channel_id=1, source_target_pairs={{0,262},{2,260},{4,258},{6,256},{256,6},{258,4},{260,2},{262,0},{1... | collective-permute-start | bytes 245768 | tf_op jit(solution)/shard_map/ppermute | solution.py:280
  181.9 5.0 %collective-permute-start.20 = (bf16[2560,256]{1,0:T(8,128)(2,1)S(1)}, bf16[2560,256]{1,0:T(8,128)(2,1)S(1)}, u32[]{:S(2)}, u32[]{:S(2)}) collective-permute-start(bf16[2560,256]{1,0:T(8,128)(2,1)S(1)} %bitcast.90), channel_id=1, source_target_pairs={{0,1},{1,0},{2,3},{3,2},{4,5},{5,4},{6,7},{7,6},{8,9},{9,8},{10,11... | collective-permute-start | bytes 3932168 | tf_op jit(solution)/shard_map/ppermute | solution.py:221
  184.3 26.9 %collective-permute-start.22 = (bf16[4,256,512]{2,1,0:T(8,128)(2,1)S(1)}, bf16[4,256,512]{2,1,0:T(8,128)(2,1)S(1)}, u32[]{:S(2)}, u32[]{:S(2)}) collective-permute-start(bf16[4,256,512]{2,1,0:T(8,128)(2,1)S(1)} %pad_maximum_fusion.3.near_ref), channel_id=1, source_target_pairs={{0,1},{1,0},{2,3},{3,2},{4,5},{5,4},{6,7},{7,6},{8,9},{9,8},{10,11... | collective-permute-start | bytes 3145736 | tf_op jit(solution)/shard_map/ppermute | solution.py:221
  186.9 0.9 copy-start
  196.0 8.8 %collective-permute-start.21 = (bf16[4,96,128]{2,1,0:T(8,128)(2,1)S(1)}, bf16[4,96,128]{2,1,0:T(8,128)(2,1)S(1)}, u32[]{:S(2)}, u32[]{:S(2)}) collective-permute-start(bf16[4,96,128]{2,1,0:T(8,128)(2,1)S(1)} %get-tuple-element.50), channel_id=1, source_target_pairs={{0,262},{2,260},{4,258},{6,256},{256,6},{258,4},{260,2},{262,0},{1... | collective-permute-start | bytes 294920 | tf_op jit(solution)/shard_map/ppermute | solution.py:280
  206.3 9.4 %all-to-all-start.4 = ((bf16[4,80,128]{2,1,0:T(8,128)(2,1)}), bf16[4,80,128]{2,1,0:T(8,128)(2,1)S(1)}, u32[]{:S(2)}, u32[]{:S(2)}) async-start(bf16[4,80,128]{2,1,0:T(8,128)(2,1)} %shard_map.68), calls=%async_computation.4 | async-start | bytes 163840 | tf_op jit(solution)/shard_map/all_to_all | solution.py:225

commit v7 on v6

--- a/solution.py
+++ b/solution.py
@@ -1,3 +1,5 @@
+import functools
+
 import jax
 import jax.numpy as jnp
 import numpy as np
@@ -14,24 +16,34 @@
 LIMIT = pltpu.CompilerParams(vmem_limit_bytes=48 * 1024 * 1024)
 
 
-def fold_kernel(w_ref, out_ref):
+def fold_kernel(w_ref, out_ref, done):
+    copies = []
     for h in range(2):
         for r in range(2):
             for j in range(3):
-                out_ref[2 * h + r, 0, :, j * HD : (j + 1) * HD] = w_ref[j, r, :, h * HD : (h + 1) * HD]
+                copies.append(
+                    pltpu.make_async_copy(
+                        w_ref.at[j, r, :, :, pl.ds(h * HD, HD)],
+                        out_ref.at[2 * h + r, :, :, pl.ds(j * HD, HD)],
+                        done.at[len(copies)],
+                    )
+                )
+    for copy in copies:
+        copy.start()
+    for copy in copies:
+        copy.wait()
 
 
 def fold(w, ny):
     part = w.shape[1] // (2 * ny)
     return pl.pallas_call(
         fold_kernel,
-        grid=(ny,),
-        in_specs=[pl.BlockSpec((3, 2, part, 2 * HD), lambda i: (0, 0, i, 0))],
-        out_specs=pl.BlockSpec((4, 1, part, 3 * HD), lambda i: (0, i, 0, 0)),
+        in_specs=[pl.BlockSpec(memory_space=pl.ANY)],
+        out_specs=pl.BlockSpec(memory_space=pl.ANY),
         out_shape=jax.ShapeDtypeStruct((4, ny, part, 3 * HD), w.dtype),
-        compiler_params=LIMIT,
+        scratch_shapes=[pltpu.SemaphoreType.DMA((12,))],
         cost_estimate=pl.CostEstimate(flops=0, bytes_accessed=4 * w.size, transcendentals=0),
-    )(w.reshape(3, 2, ny * part, 2 * HD))
+    )(w.reshape(3, 2, ny, part, 2 * HD))
 
 
 def near_kernel(c_ref, x_ref, w_ref, out_ref):
@@ -84,50 +96,70 @@
     return first, second, rest - second
 
 
-def attend_kernel(start_ref, q_ref, near_ref, far_ref, kpos_ref, o_ref, s_ref):
-    factor = float(np.log2(np.e) / HD**0.5)
-    rows = q_ref.shape[0]
-    blocks, half = o_ref.shape[0], o_ref.shape[1] - EXTRA
+def positions(start_ref, rows, half):
+    blocks = rows // half
     row = lax.broadcasted_iota(jnp.int32, (rows, 1), 0)
     first = blocks * pl.program_id(0)
     qpos = row + start_ref[first]
     for b in range(1, blocks):
         qpos = jnp.where(row < b * half, qpos, row - b * half + start_ref[first + b])
-    pieces = [
-        (ref, j * CHUNK, i * ref.shape[0] + j * CHUNK)
-        for i, ref in enumerate((near_ref, far_ref))
-        for j in range(ref.shape[0] // CHUNK)
-    ]
-    q = q_ref[...]
-    high = jnp.full((rows, HD), HIDE, jnp.float32)
-    for ref, at, column in pieces:
-        span = pl.ds(column, CHUNK)
+    return qpos
+
+
+def score(q, qpos, kv_ref, kpos_ref, s_ref):
+    factor = float(np.log2(np.e) / HD**0.5)
+    high = jnp.full((q.shape[0], HD), HIDE, jnp.float32)
+    for j in range(kv_ref.shape[0] // CHUNK):
+        span = pl.ds(j * CHUNK, CHUNK)
         s = lax.dot_general(
-            q, ref[pl.ds(at, CHUNK), :HD], (((1,), (1,)), ((), ())), preferred_element_type=jnp.float32
+            q, kv_ref[span, :HD], (((1,), (1,)), ((), ())), preferred_element_type=jnp.float32
         )
         s = jnp.where(kpos_ref[:, span] <= qpos, s * factor, HIDE)
         s_ref[:, span] = s
         for t in range(CHUNK // HD):
             high = jnp.maximum(high, s[:, t * HD : (t + 1) * HD])
-    top = jnp.max(high, axis=1, keepdims=True)
+    return jnp.max(high, axis=1, keepdims=True)
+
+
+def weigh(top, kv_ref, s_ref):
+    rows = s_ref.shape[0]
     base = jnp.where(top <= 0.5 * HIDE, 0.0, top)
     total = jnp.zeros((rows, HD), jnp.float32)
     acc = jnp.zeros((rows, HD), jnp.float32)
-    for ref, at, column in pieces:
-        span = pl.ds(column, CHUNK)
+    for j in range(kv_ref.shape[0] // CHUNK):
+        span = pl.ds(j * CHUNK, CHUNK)
         p = jnp.exp2(s_ref[:, span] - base)
         for t in range(CHUNK // HD):
             total = total + p[:, t * HD : (t + 1) * HD]
         acc = acc + jnp.dot(
-            p.astype(jnp.bfloat16), ref[pl.ds(at, CHUNK), HD:], preferred_element_type=jnp.float32
+            p.astype(jnp.bfloat16), kv_ref[span, HD:], preferred_element_type=jnp.float32
         )
-    total = jnp.sum(total, axis=1, keepdims=True)
+    return jnp.sum(total, axis=1, keepdims=True), acc
+
+
+def attend_near_kernel(half, start_ref, q_ref, kv_ref, kpos_ref, acc_ref, stat_ref, s_ref):
+    rows = q_ref.shape[0]
+    top = score(q_ref[...], positions(start_ref, rows, half), kv_ref, kpos_ref, s_ref)
+    total, acc_ref[...] = weigh(top, kv_ref, s_ref)
+    lane = lax.broadcasted_iota(jnp.int32, (rows, HD), 1)
+    stat_ref[...] = jnp.where(lane == 0, top, total)
+
+
+def attend_far_kernel(half, start_ref, q_ref, kv_ref, kpos_ref, acc_ref, stat_ref, o_ref, s_ref):
+    rows = q_ref.shape[0]
+    top = score(q_ref[...], positions(start_ref, rows, half), kv_ref, kpos_ref, s_ref)
+    before = stat_ref[:, 0:1]
+    top = jnp.maximum(top, before)
+    total, acc = weigh(top, kv_ref, s_ref)
+    keep = jnp.exp2(before - top)
+    total = total + stat_ref[:, 1:2] * keep
+    acc = acc + acc_ref[...] * keep
     o = acc / jnp.where(total == 0.0, 1.0, total)
     lane = lax.broadcasted_iota(jnp.int32, (rows, HD), 1)
     stat = jnp.zeros((rows, HD), jnp.float32)
     for k, piece in enumerate(three_parts(top) + three_parts(total)):
         stat = jnp.where(lane == k, piece, stat)
-    for b in range(blocks):
+    for b in range(o_ref.shape[0]):
         o_ref[b, :half, :] = o[b * half : (b + 1) * half].astype(o_ref.dtype)
         block = jnp.concatenate(
             [stat[b * half : (b + 1) * half], jnp.zeros((HD - half, HD), jnp.float32)]
@@ -135,27 +167,35 @@
         o_ref[b, half:, :] = block.T[:EXTRA].astype(o_ref.dtype)
 
 
-def attend(start, q, near, far, kpos, half):
-    nq, nk = q.shape[0], 2 * near.shape[0]
+def attend(start, q, kv, kpos, half, state=None):
+    nq, nk = q.shape[0], kv.shape[0]
     tile = 2 * half
-    return pl.pallas_call(
-        attend_kernel,
+    row = pl.BlockSpec((tile, HD), lambda i: (i, 0))
+    in_specs = [
+        pl.BlockSpec(memory_space=pltpu.SMEM),
+        row,
+        pl.BlockSpec((nk, 2 * HD), lambda i: (0, 0)),
+        pl.BlockSpec((1, nk), lambda i: (0, 0)),
+    ]
+    if state is None:
+        body, state = attend_near_kernel, ()
+        out_specs, out_shape = [row, row], [jax.ShapeDtypeStruct((nq, HD), jnp.float32)] * 2
+    else:
+        body = attend_far_kernel
+        out_specs = pl.BlockSpec((2, half + EXTRA, HD), lambda i: (i, 0, 0))
+        out_shape = jax.ShapeDtypeStruct((nq // half, half + EXTRA, HD), jnp.bfloat16)
+    return pl.pallas_call(
+        functools.partial(body, half),
         grid=(nq // tile,),
-        in_specs=[
-            pl.BlockSpec(memory_space=pltpu.SMEM),
-            pl.BlockSpec((tile, HD), lambda i: (i, 0)),
-            pl.BlockSpec((nk // 2, 2 * HD), lambda i: (0, 0)),
-            pl.BlockSpec((nk // 2, 2 * HD), lambda i: (0, 0)),
-            pl.BlockSpec((1, nk), lambda i: (0, 0)),
-        ],
-        out_specs=pl.BlockSpec((2, half + EXTRA, HD), lambda i: (i, 0, 0)),
-        out_shape=jax.ShapeDtypeStruct((nq // half, half + EXTRA, HD), jnp.bfloat16),
+        in_specs=in_specs + [row] * len(state),
+        out_specs=out_specs,
+        out_shape=out_shape,
         scratch_shapes=[pltpu.VMEM((tile, nk), jnp.float32)],
         compiler_params=LIMIT,
         cost_estimate=pl.CostEstimate(
             flops=4 * nq * nk * HD, bytes_accessed=nk * HD * 4, transcendentals=nq * nk
         ),
-    )(start, q, near, far, kpos)
+    )(start, q, kv, kpos, *state)
 
 
 def merge_kernel(near_ref, far_ref, out_ref):
@@ -297,7 +337,7 @@
     order = block_order.reshape(2, ny, nx) * rows
     offsets = jnp.arange(half, dtype=jnp.int32)
     kpos = (pick(order, zh)[:, :, None] + offsets).reshape(-1)
-    kpos = jnp.concatenate([kpos + c * half, kpos + (1 - c) * half]).reshape(1, -1)
+    kpos = jnp.stack([kpos + c * half, kpos + (1 - c) * half])
     here = lax.dynamic_index_in_dim(order, y, 1, keepdims=False)
     start = jnp.stack([pick(here, zh), pick(here, 1 - zh)]).reshape(-1) + c * half
 
@@ -327,7 +367,8 @@
     far = swap(near, "c")
     wo_far = swap(wo, "c")
 
-    parts = attend(start, q_all, near, far, kpos, half)
+    state = attend(start, q_all, near, kpos[:1], half)
+    parts = attend(start, q_all, far, kpos[1:], half, state)
     context = merge(parts[:nx], mirror(parts[nx:]))
     context = exchange(context, "x")
     terms = finish(core, context, wo, wo_far)

time: 233 us -> 325 us (1.39)
  Pallas kernels: 17.4 us -> 110 us
    pallas_call x2 -> x3, Pallas kernels: 14.4 us -> 107 us  [the longest x1 96.5 us: fold(): pl.pallas_call(fold_kernel, in_specs=[pl.BlockSpec(memory_space=pl.ANY)],...]
  transfers between devices with their start and end apart: 28 -> 28, of which waited for: 15 -> 14; matrix products, arithmetic and copies ran while one was open for 4% -> 3% of each run, Pallas kernels for 4% -> 4%
where the time goes in v7:
time: 325 us; the launch traced here: 324 us
  Pallas kernels  110 us (34%)
  starting transfers between devices  107 us (33%)
  waiting for transfers between devices  76.9 us (24%)
  blocking collectives  14.7 us (5%)
  local copies, waits for them, and re-layouts  7.61 us (2%)
  other arithmetic  6.05 us (2%)
    pallas_call x1, Pallas kernels, fold(): pl.pallas_call(fold_kernel, in_specs=[pl.BlockSpec(memory_space=pl.ANY)],...  96.5 us
    ppermute x16, starting transfers between devices, shift(): lax.ppermute(block, axis, [(i, (i + distance) % count) for i in range(cou...  54.7 us
    all_to_all x5, waiting for transfers between devices, exchange(): return lax.all_to_all(block, axis, 0, 0, tiled=True)  50 us
    all_to_all x5, starting transfers between devices, exchange(): return lax.all_to_all(block, axis, 0, 0, tiled=True)  27.1 us
    all_to_all x1, blocking collectives, exchange(): return lax.all_to_all(block, axis, 0, 0, tiled=True)  14.7 us
    ppermute x2, starting transfers between devices, trade(): return lax.ppermute(block, ('zh', 'x', 'zl', 'c'), route)  12.9 us
    ppermute x2, waiting for transfers between devices, mirror(): return lax.ppermute(block, ('zh', 'zl'), [(i, 7 - i) for i in range(8)])  10.9 us
    ppermute x16, waiting for transfers between devices, shift(): lax.ppermute(block, axis, [(i, (i + distance) % count) for i in range(cou...  10.7 us
  transfers between devices with their start and end apart: 28, of which 14 were waited for; matrix products, arithmetic and copies ran while one was open for 3% of the time, Pallas kernels for 4%

profile of v7, /device:TPU:1, one launch (start us, length us, event | category | flops | bytes accessed | tf_op | source)
XLA Modules:
  0.0 323.6 jit_solution(13162040812004838351)
XLA Ops:
  0.0 96.5 %shard_map.64 = bf16[4,8,128,384]{3,2,1,0:T(8,128)(2,1)} custom-call(bf16[3,2,8,128,256]{4,3,2,1,0:T(8,128)(2,1)} %bitcast.91), custom_call_target="tpu_custom_call" | custom-call | bytes 6291456 | tf_op jit(solution)/shard_map/pallas_call | solution.py:39
  96.5 4.9 %all-to-all-start = ((bf16[4,8,128,384]{3,2,1,0:T(8,128)(2,1)}), bf16[4,8,128,384]{3,2,1,0:T(8,128)(2,1)S(1)}, u32[]{:S(2)}, u32[]{:S(2)}) async-start(bf16[4,8,128,384]{3,2,1,0:T(8,128)(2,1)} %shard_map.64), calls=%async_computation | async-start | bytes 6291456 | tf_op jit(solution)/shard_map/all_to_all | solution.py:265
  101.4 2.2 dynamic-slice_bitcast_fusion.1
  103.6 5.1 %collective-permute-start = (bf16[32,2048]{1,0:T(8,128)(2,1)}, bf16[32,2048]{1,0:T(8,128)(2,1)}, u32[]{:S(2)}, u32[]{:S(2)}) collective-permute-start(bf16[32,2048]{1,0:T(8,128)(2,1)} %get-tuple-element.53), channel_id=1, source_target_pairs={{0,224},{32,0},{64,32},{96,64},{128,96},{160,128},{192,160},{224,1... | collective-permute-start | bytes 393224 | tf_op jit(solution)/shard_map/ppermute | solution.py:279
  108.7 1.9 collective-permute-start.1
  110.6 4.1 %collective-permute-start.2 = (bf16[32,2048]{1,0:T(8,128)(2,1)}, bf16[32,2048]{1,0:T(8,128)(2,1)}, u32[]{:S(2)}, u32[]{:S(2)}) collective-permute-start(bf16[32,2048]{1,0:T(8,128)(2,1)} %get-tuple-element.51), channel_id=1, source_target_pairs={{0,192},{32,224},{64,0},{96,32},{128,64},{160,96},{192,128},{224,1... | collective-permute-start | bytes 393224 | tf_op jit(solution)/shard_map/ppermute | solution.py:279
  114.8 2.0 collective-permute-start.3
  116.8 4.9 %collective-permute-start.4 = (bf16[32,2048]{1,0:T(8,128)(2,1)}, bf16[32,2048]{1,0:T(8,128)(2,1)}, u32[]{:S(2)}, u32[]{:S(2)}) collective-permute-start(bf16[32,2048]{1,0:T(8,128)(2,1)} %get-tuple-element.49), channel_id=1, source_target_pairs={{0,160},{32,192},{64,224},{96,0},{128,32},{160,64},{192,96},{224,1... | collective-permute-start | bytes 393224 | tf_op jit(solution)/shard_map/ppermute | solution.py:279
  122.1 1.1 fusion
  123.3 1.1 fusion.2
  124.5 2.9 collective-permute-start.5
  127.4 5.0 %collective-permute-start.6 = (bf16[32,2048]{1,0:T(8,128)(2,1)}, bf16[32,2048]{1,0:T(8,128)(2,1)}, u32[]{:S(2)}, u32[]{:S(2)}) collective-permute-start(bf16[32,2048]{1,0:T(8,128)(2,1)} %get-tuple-element.47), channel_id=1, source_target_pairs={{0,128},{32,160},{64,192},{96,224},{128,0},{160,32},{192,64},{224,... | collective-permute-start | bytes 393224 | tf_op jit(solution)/shard_map/ppermute | solution.py:279
  133.2 1.4 collective-permute-done.5
  134.6 6.0 %collective-permute-done.6 = bf16[32,2048]{1,0:T(8,128)(2,1)} collective-permute-done((bf16[32,2048]{1,0:T(8,128)(2,1)}, bf16[32,2048]{1,0:T(8,128)(2,1)}, u32[]{:S(2)}, u32[]{:S(2)}) %collective-permute-start.6) | collective-permute-done | bytes 131104 | tf_op jit(solution)/shard_map/ppermute | solution.py:279
  140.6 1.7 fusion.8
  143.3 10.3 %all-to-all-start.1 = ((bf16[8,128,384]{2,1,0:T(8,128)(2,1)}), bf16[8,128,384]{2,1,0:T(8,128)(2,1)S(1)}, u32[]{:S(2)}, u32[]{:S(2)}) async-start(bf16[8,128,384]{2,1,0:T(8,128)(2,1)} %dynamic-slice_bitcast_fusion), calls=%async_computation.1 | async-start | bytes 1572864 | tf_op jit(solution)/shard_map/all_to_all | solution.py:265
  154.0 4.6 %collective-permute-start.7 = (bf16[32,512]{1,0:T(8,128)(2,1)S(1)}, bf16[32,512]{1,0:T(8,128)(2,1)S(1)}, u32[]{:S(2)}, u32[]{:S(2)}) collective-permute-start(bf16[32,512]{1,0:T(8,128)(2,1)S(1)} %bitcast.110), channel_id=1, source_target_pairs={{0,24},{8,0},{16,8},{24,16},{1,25},{9,1},{17,9},{25,17},{2,26},{10... | collective-permute-start | bytes 98312 | tf_op jit(solution)/shard_map/ppermute | solution.py:279
  158.6 1.9 collective-permute-start.8
  160.5 3.7 %collective-permute-start.9 = (bf16[32,512]{1,0:T(8,128)(2,1)S(1)}, bf16[32,512]{1,0:T(8,128)(2,1)S(1)}, u32[]{:S(2)}, u32[]{:S(2)}) collective-permute-start(bf16[32,512]{1,0:T(8,128)(2,1)S(1)} %bitcast.112), channel_id=1, source_target_pairs={{0,16},{8,24},{16,0},{24,8},{1,17},{9,25},{17,1},{25,9},{2,18},{10... | collective-permute-start | bytes 98312 | tf_op jit(solution)/shard_map/ppermute | solution.py:279
  164.8 2.1 collective-permute-done.9
  166.9 10.3 %all-to-all-done.1 = bf16[8,128,384]{2,1,0:T(8,128)(2,1)S(1)} async-done(((bf16[8,128,384]{2,1,0:T(8,128)(2,1)}), bf16[8,128,384]{2,1,0:T(8,128)(2,1)S(1)}, u32[]{:S(2)}, u32[]{:S(2)}) %all-to-all-start.1) | async-done | bytes 786464 | tf_op jit(solution)/shard_map/all_to_all | solution.py:265
  177.2 11.0 %collective-permute-start.14 = (bf16[128,512]{1,0:T(8,128)(2,1)S(1)}, bf16[128,512]{1,0:T(8,128)(2,1)S(1)}, u32[]{:S(2)}, u32[]{:S(2)}) collective-permute-start(bf16[128,512]{1,0:T(8,128)(2,1)S(1)} %pad_maximum_fusion.5), channel_id=1, source_target_pairs={{0,262},{1,270},{2,260},{3,268},{4,258},{5,266},{6,256},{7,264},{8... | collective-permute-start | bytes 393224 | tf_op jit(solution)/shard_map/ppermute | solution.py:316
  188.2 1.9 collective-permute-start.13
  190.2 3.6 %collective-permute-done.14 = bf16[128,512]{1,0:T(8,128)(2,1)S(1)} collective-permute-done((bf16[128,512]{1,0:T(8,128)(2,1)S(1)}, bf16[128,512]{1,0:T(8,128)(2,1)S(1)}, u32[]{:S(2)}, u32[]{:S(2)}) %collective-permute-start.14) | collective-permute-done | bytes 131104 | tf_op jit(solution)/shard_map/ppermute | solution.py:316
  195.6 3.6 %all-to-all-start.2 = ((bf16[8,128,512]{2,1,0:T(8,128)(2,1)}), bf16[8,128,512]{2,1,0:T(8,128)(2,1)S(1)}, u32[]{:S(2)}, u32[]{:S(2)}) async-start(bf16[8,128,512]{2,1,0:T(8,128)(2,1)} %broadcast_in_dim.4), calls=%async_computation.2 | async-start | bytes 2097152 | tf_op jit(solution)/shard_map/all_to_all | solution.py:265
  199.2 1.9 collective-permute-start.12
  201.1 4.3 %collective-permute-start.11 = (bf16[80,2048]{1,0:T(8,128)(2,1)S(1)}, bf16[80,2048]{1,0:T(8,128)(2,1)S(1)}, u32[]{:S(2)}, u32[]{:S(2)}) collective-permute-start(bf16[80,2048]{1,0:T(8,128)(2,1)S(1)} %fusion.2), channel_id=1, source_target_pairs={{0,16},{8,24},{16,0},{24,8},{1,17},{9,25},{17,1},{25,9},{2,18},{10... | collective-permute-start | bytes 983048 | tf_op jit(solution)/shard_map/ppermute | solution.py:279
  205.4 2.8 collective-permute-start.10
  208.2 19.7 %all-to-all-done.2 = bf16[8,128,512]{2,1,0:T(8,128)(2,1)S(1)} async-done(((bf16[8,128,512]{2,1,0:T(8,128)(2,1)}), bf16[8,128,512]{2,1,0:T(8,128)(2,1)S(1)}, u32[]{:S(2)}, u32[]{:S(2)}) %all-to-all-start.2) | async-done | bytes 1048608 | tf_op jit(solution)/shard_map/all_to_all | solution.py:265
  227.8 2.3 collective-permute-start.15
  232.9 1.2 broadcast_in_dim.5
  234.1 3.6 %all-to-all-start.3 = ((bf16[8,320,256]{2,1,0:T(8,128)(2,1)}), bf16[8,320,256]{2,1,0:T(8,128)(2,1)S(1)}, u32[]{:S(2)}, u32[]{:S(2)}) async-start(bf16[8,320,256]{2,1,0:T(8,128)(2,1)} %broadcast_in_dim.5), calls=%async_computation.3 | async-start | bytes 2621440 | tf_op jit(solution)/shard_map/all_to_all | solution.py:265
  237.7 1.9 collective-permute-start.19
  239.6 4.9 %collective-permute-start.18 = (bf16[256,512]{1,0:T(8,128)(2,1)S(1)}, bf16[256,512]{1,0:T(8,128)(2,1)S(1)}, u32[]{:S(2)}, u32[]{:S(2)}) collective-permute-start(bf16[256,512]{1,0:T(8,128)(2,1)S(1)} %bitcast.99), channel_id=1, source_target_pairs={{0,16},{8,24},{16,0},{24,8},{1,17},{9,25},{17,1},{25,9},{2,18},{10... | collective-permute-start | bytes 786440 | tf_op jit(solution)/shard_map/ppermute | solution.py:279
  244.5 2.8 collective-permute-start.17
  247.3 2.6 collective-permute-start.16
  249.9 5.3 %collective-permute-done.16 = bf16[320,128]{1,0:T(8,128)(2,1)S(1)} collective-permute-done((bf16[320,128]{1,0:T(8,128)(2,1)S(1)}, bf16[320,128]{1,0:T(8,128)(2,1)S(1)}, u32[]{:S(2)}, u32[]{:S(2)}) %collective-permute-start.16) | collective-permute-done | bytes 81952 | tf_op jit(solution)/shard_map/ppermute | solution.py:320
  256.9 15.5 %all-to-all-done.3 = bf16[8,320,256]{2,1,0:T(8,128)(2,1)S(1)} async-done(((bf16[8,320,256]{2,1,0:T(8,128)(2,1)}), bf16[8,320,256]{2,1,0:T(8,128)(2,1)S(1)}, u32[]{:S(2)}, u32[]{:S(2)}) %all-to-all-start.3) | async-done | bytes 1310752 | tf_op jit(solution)/shard_map/all_to_all | solution.py:265
  272.4 2.4 collective-permute-start.20
  274.8 1.9 collective-permute-start.22
  277.7 4.8 %shard_map.67 = (f32[640,128]{1,0:T(8,128)S(1)}, f32[640,128]{1,0:T(8,128)S(1)}) custom-call(s32[8]{0:T(128)S(1)} %add.313.start_ref, bf16[640,128]{1,0:T(8,128)(2,1)S(1)} %copy-done, bf16[2560,256]{1,0:T(8,128)(2,1)S(1)} %bitcast.90, s32[1,2560]{1,0:T(1,128)S(1)} %get-tuple-element.60.kpos_ref), custom_call_target="tpu_custom_call" | custom-call | flops 838860800 | bytes 1310720 | tf_op jit(solution)/shard_map/pallas_call | solution.py:187
  282.5 5.4 %shard_map.68 = bf16[8,96,128]{2,1,0:T(8,128)(2,1)S(1)} custom-call(s32[8]{0:T(128)S(1)} %add.313.start_ref, bf16[640,128]{1,0:T(8,128)(2,1)S(1)} %copy-done, bf16[2560,256]{1,0:T(8,128)(2,1)S(1)} %collective-permute-done.20.kv_ref, s32[1,2560]{1,0:T(1,128)S(1)} %get-tuple-element.61.kpos_ref, f32[640,128]{1,0:T(8,128)S(1)} %get-tuple-element.36.acc_ref, ...), custom_call_target="tpu_custom_call" | custom-call | flops 838860800 | bytes 1310720 | tf_op jit(solution)/shard_map/pallas_call | solution.py:187
  288.0 3.2 collective-permute-start.21
  291.2 5.6 %collective-permute-done.21.far_ref = bf16[4,96,128]{2,1,0:T(8,128)(2,1)S(1)} collective-permute-done((bf16[4,96,128]{2,1,0:T(8,128)(2,1)S(1)}, bf16[4,96,128]{2,1,0:T(8,128)(2,1)S(1)}, u32[]{:S(2)}, u32[]{:S(2)}) %collective-permute-start.21) | collective-permute-done | bytes 98336 | tf_op jit(solution)/shard_map/ppermute | solution.py:320
  296.8 1.5 shard_map.69
  298.3 4.9 %all-to-all-start.4 = ((bf16[4,80,128]{2,1,0:T(8,128)(2,1)}), bf16[4,80,128]{2,1,0:T(8,128)(2,1)S(1)}, u32[]{:S(2)}, u32[]{:S(2)}) async-start(bf16[4,80,128]{2,1,0:T(8,128)(2,1)} %shard_map.69), calls=%async_computation.4 | async-start | bytes 163840 | tf_op jit(solution)/shard_map/all_to_all | solution.py:265
  303.1 4.6 %all-to-all-done.4.context_ref = bf16[4,80,128]{2,1,0:T(8,128)(2,1)S(1)} async-done(((bf16[4,80,128]{2,1,0:T(8,128)(2,1)}), bf16[4,80,128]{2,1,0:T(8,128)(2,1)S(1)}, u32[]{:S(2)}, u32[]{:S(2)}) %all-to-all-start.4) | async-done | bytes 81952 | tf_op jit(solution)/shard_map/all_to_all | solution.py:265
  308.2 14.7 %all_to_all.30 = bf16[8,80,256]{2,1,0:T(8,128)(2,1)S(1)} all-to-all(bf16[8,80,256]{2,1,0:T(8,128)(2,1)S(1)} %shard_map.70), channel_id=1, replica_groups=mesh['zh'=2,'y'=8,'x'=4,'zl'=4,'c'=2] {'zl','c'}, dimensions={0} | all-to-all | bytes 655360 | tf_op jit(solution)/shard_map/all_to_all | solution.py:265
  (66 shorter events, 10.7 us)
Async XLA Ops:
  96.5 45.8 %all-to-all-start = ((bf16[4,8,128,384]{3,2,1,0:T(8,128)(2,1)}), bf16[4,8,128,384]{3,2,1,0:T(8,128)(2,1)S(1)}, u32[]{:S(2)}, u32[]{:S(2)}) async-start(bf16[4,8,128,384]{3,2,1,0:T(8,128)(2,1)} %shard_map.64), calls=%async_computation | async-start | bytes 6291456 | tf_op jit(solution)/shard_map/all_to_all | solution.py:265
  101.4 20.4 %copy-start.3 = (s32[64]{0:T(128)S(1)}, s32[64]{0:T(128)}, u32[]{:S(2)}) copy-start(s32[64]{0:T(128)} %param.11) | copy-start | bytes 772
  101.4 21.9 %copy-start.2 = (f32[2048]{0:T(1024)S(1)}, f32[2048]{0:T(1024)}, u32[]{:S(2)}) copy-start(f32[2048]{0:T(1024)} %param.7) | copy-start | bytes 24580
  103.6 20.9 %collective-permute-start = (bf16[32,2048]{1,0:T(8,128)(2,1)}, bf16[32,2048]{1,0:T(8,128)(2,1)}, u32[]{:S(2)}, u32[]{:S(2)}) collective-permute-start(bf16[32,2048]{1,0:T(8,128)(2,1)} %get-tuple-element.53), channel_id=1, source_target_pairs={{0,224},{32,0},{64,32},{96,64},{128,96},{160,128},{192,160},{224,1... | collective-permute-start | bytes 393224 | tf_op jit(solution)/shard_map/ppermute | solution.py:279
  108.7 18.7 %collective-permute-start.1 = (bf16[32,2048]{1,0:T(8,128)(2,1)}, bf16[32,2048]{1,0:T(8,128)(2,1)}, u32[]{:S(2)}, u32[]{:S(2)}) collective-permute-start(bf16[32,2048]{1,0:T(8,128)(2,1)} %get-tuple-element.52), channel_id=1, source_target_pairs={{0,32},{32,64},{64,96},{96,128},{128,160},{160,192},{192,224},{224... | collective-permute-start | bytes 393224 | tf_op jit(solution)/shard_map/ppermute | solution.py:279
  110.6 22.6 %collective-permute-start.2 = (bf16[32,2048]{1,0:T(8,128)(2,1)}, bf16[32,2048]{1,0:T(8,128)(2,1)}, u32[]{:S(2)}, u32[]{:S(2)}) collective-permute-start(bf16[32,2048]{1,0:T(8,128)(2,1)} %get-tuple-element.51), channel_id=1, source_target_pairs={{0,192},{32,224},{64,0},{96,32},{128,64},{160,96},{192,128},{224,1... | collective-permute-start | bytes 393224 | tf_op jit(solution)/shard_map/ppermute | solution.py:279
  114.8 18.5 %collective-permute-start.3 = (bf16[32,2048]{1,0:T(8,128)(2,1)}, bf16[32,2048]{1,0:T(8,128)(2,1)}, u32[]{:S(2)}, u32[]{:S(2)}) collective-permute-start(bf16[32,2048]{1,0:T(8,128)(2,1)} %get-tuple-element.50), channel_id=1, source_target_pairs={{0,64},{32,96},{64,128},{96,160},{128,192},{160,224},{192,0},{224,... | collective-permute-start | bytes 393224 | tf_op jit(solution)/shard_map/ppermute | solution.py:279
  116.8 16.4 %collective-permute-start.4 = (bf16[32,2048]{1,0:T(8,128)(2,1)}, bf16[32,2048]{1,0:T(8,128)(2,1)}, u32[]{:S(2)}, u32[]{:S(2)}) collective-permute-start(bf16[32,2048]{1,0:T(8,128)(2,1)} %get-tuple-element.49), channel_id=1, source_target_pairs={{0,160},{32,192},{64,224},{96,0},{128,32},{160,64},{192,96},{224,1... | collective-permute-start | bytes 393224 | tf_op jit(solution)/shard_map/ppermute | solution.py:279
  124.5 10.1 %collective-permute-start.5 = (bf16[32,2048]{1,0:T(8,128)(2,1)}, bf16[32,2048]{1,0:T(8,128)(2,1)}, u32[]{:S(2)}, u32[]{:S(2)}) collective-permute-start(bf16[32,2048]{1,0:T(8,128)(2,1)} %get-tuple-element.48), channel_id=1, source_target_pairs={{0,96},{32,128},{64,160},{96,192},{128,224},{160,0},{192,32},{224,... | collective-permute-start | bytes 393224 | tf_op jit(solution)/shard_map/ppermute | solution.py:279
  127.4 13.2 %collective-permute-start.6 = (bf16[32,2048]{1,0:T(8,128)(2,1)}, bf16[32,2048]{1,0:T(8,128)(2,1)}, u32[]{:S(2)}, u32[]{:S(2)}) collective-permute-start(bf16[32,2048]{1,0:T(8,128)(2,1)} %get-tuple-element.47), channel_id=1, source_target_pairs={{0,128},{32,160},{64,192},{96,224},{128,0},{160,32},{192,64},{224,... | collective-permute-start | bytes 393224 | tf_op jit(solution)/shard_map/ppermute | solution.py:279
  143.3 10.3 %copy-start.1 = (bf16[32,2048]{1,0:T(8,128)(2,1)S(1)}, bf16[32,2048]{1,0:T(8,128)(2,1)}, u32[]{:S(2)}) copy-start(bf16[32,2048]{1,0:T(8,128)(2,1)} %fusion.8) | copy-start | bytes 393220
  143.3 33.9 %all-to-all-start.1 = ((bf16[8,128,384]{2,1,0:T(8,128)(2,1)}), bf16[8,128,384]{2,1,0:T(8,128)(2,1)S(1)}, u32[]{:S(2)}, u32[]{:S(2)}) async-start(bf16[8,128,384]{2,1,0:T(8,128)(2,1)} %dynamic-slice_bitcast_fusion), calls=%async_computation.1 | async-start | bytes 1572864 | tf_op jit(solution)/shard_map/all_to_all | solution.py:265
  154.0 10.2 %collective-permute-start.7 = (bf16[32,512]{1,0:T(8,128)(2,1)S(1)}, bf16[32,512]{1,0:T(8,128)(2,1)S(1)}, u32[]{:S(2)}, u32[]{:S(2)}) collective-permute-start(bf16[32,512]{1,0:T(8,128)(2,1)S(1)} %bitcast.110), channel_id=1, source_target_pairs={{0,24},{8,0},{16,8},{24,16},{1,25},{9,1},{17,9},{25,17},{2,26},{10... | collective-permute-start | bytes 98312 | tf_op jit(solution)/shard_map/ppermute | solution.py:279
  158.6 6.2 %collective-permute-start.8 = (bf16[32,512]{1,0:T(8,128)(2,1)S(1)}, bf16[32,512]{1,0:T(8,128)(2,1)S(1)}, u32[]{:S(2)}, u32[]{:S(2)}) collective-permute-start(bf16[32,512]{1,0:T(8,128)(2,1)S(1)} %bitcast.111), channel_id=1, source_target_pairs={{0,8},{8,16},{16,24},{24,0},{1,9},{9,17},{17,25},{25,1},{2,10},{10... | collective-permute-start | bytes 98312 | tf_op jit(solution)/shard_map/ppermute | solution.py:279
  160.5 6.3 %collective-permute-start.9 = (bf16[32,512]{1,0:T(8,128)(2,1)S(1)}, bf16[32,512]{1,0:T(8,128)(2,1)S(1)}, u32[]{:S(2)}, u32[]{:S(2)}) collective-permute-start(bf16[32,512]{1,0:T(8,128)(2,1)S(1)} %bitcast.112), channel_id=1, source_target_pairs={{0,16},{8,24},{16,0},{24,8},{1,17},{9,25},{17,1},{25,9},{2,18},{10... | collective-permute-start | bytes 98312 | tf_op jit(solution)/shard_map/ppermute | solution.py:279
  177.2 16.6 %collective-permute-start.14 = (bf16[128,512]{1,0:T(8,128)(2,1)S(1)}, bf16[128,512]{1,0:T(8,128)(2,1)S(1)}, u32[]{:S(2)}, u32[]{:S(2)}) collective-permute-start(bf16[128,512]{1,0:T(8,128)(2,1)S(1)} %pad_maximum_fusion.5), channel_id=1, source_target_pairs={{0,262},{1,270},{2,260},{3,268},{4,258},{5,266},{6,256},{7,264},{8... | collective-permute-start | bytes 393224 | tf_op jit(solution)/shard_map/ppermute | solution.py:316
  188.2 6.3 %collective-permute-start.13 = (bf16[128,512]{1,0:T(8,128)(2,1)S(1)}, bf16[128,512]{1,0:T(8,128)(2,1)S(1)}, u32[]{:S(2)}, u32[]{:S(2)}) collective-permute-start(bf16[128,512]{1,0:T(8,128)(2,1)S(1)} %pad_maximum_fusion.5), channel_id=1, source_target_pairs={{1,8},{3,10},{5,12},{7,14},{8,1},{10,3},{12,5},{14,7},{17,24},{19,... | collective-permute-start | bytes 393224 | tf_op jit(solution)/shard_map/ppermute | solution.py:316
  195.6 32.2 %all-to-all-start.2 = ((bf16[8,128,512]{2,1,0:T(8,128)(2,1)}), bf16[8,128,512]{2,1,0:T(8,128)(2,1)S(1)}, u32[]{:S(2)}, u32[]{:S(2)}) async-start(bf16[8,128,512]{2,1,0:T(8,128)(2,1)} %broadcast_in_dim.4), calls=%async_computation.2 | async-start | bytes 2097152 | tf_op jit(solution)/shard_map/all_to_all | solution.py:265
  199.2 31.0 %collective-permute-start.12 = (bf16[80,2048]{1,0:T(8,128)(2,1)S(1)}, bf16[80,2048]{1,0:T(8,128)(2,1)S(1)}, u32[]{:S(2)}, u32[]{:S(2)}) collective-permute-start(bf16[80,2048]{1,0:T(8,128)(2,1)S(1)} %fusion.2), channel_id=1, source_target_pairs={{0,24},{8,0},{16,8},{24,16},{1,25},{9,1},{17,9},{25,17},{2,26},{10... | collective-permute-start | bytes 983048 | tf_op jit(solution)/shard_map/ppermute | solution.py:279
  201.1 29.1 %collective-permute-start.11 = (bf16[80,2048]{1,0:T(8,128)(2,1)S(1)}, bf16[80,2048]{1,0:T(8,128)(2,1)S(1)}, u32[]{:S(2)}, u32[]{:S(2)}) collective-permute-start(bf16[80,2048]{1,0:T(8,128)(2,1)S(1)} %fusion.2), channel_id=1, source_target_pairs={{0,16},{8,24},{16,0},{24,8},{1,17},{9,25},{17,1},{25,9},{2,18},{10... | collective-permute-start | bytes 983048 | tf_op jit(solution)/shard_map/ppermute | solution.py:279
  205.4 24.8 %collective-permute-start.10 = (bf16[80,2048]{1,0:T(8,128)(2,1)S(1)}, bf16[80,2048]{1,0:T(8,128)(2,1)S(1)}, u32[]{:S(2)}, u32[]{:S(2)}) collective-permute-start(bf16[80,2048]{1,0:T(8,128)(2,1)S(1)} %fusion.2), channel_id=1, source_target_pairs={{0,8},{8,16},{16,24},{24,0},{1,9},{9,17},{17,25},{25,1},{2,10},{10... | collective-permute-start | bytes 983048 | tf_op jit(solution)/shard_map/ppermute | solution.py:279
  227.8 4.6 %collective-permute-start.15 = (bf16[1024,512]{1,0:T(8,128)(2,1)S(1)}, bf16[1024,512]{1,0:T(8,128)(2,1)S(1)}, u32[]{:S(2)}, u32[]{:S(2)}) collective-permute-start(bf16[1024,512]{1,0:T(8,128)(2,1)S(1)} %bitcast.86), channel_id=1, source_target_pairs={{0,1},{1,0},{2,3},{3,2},{4,5},{5,4},{6,7},{7,6},{8,9},{9,8},{10,11... | collective-permute-start | bytes 3145736 | tf_op jit(solution)/shard_map/ppermute | solution.py:261
  234.1 38.3 %all-to-all-start.3 = ((bf16[8,320,256]{2,1,0:T(8,128)(2,1)}), bf16[8,320,256]{2,1,0:T(8,128)(2,1)S(1)}, u32[]{:S(2)}, u32[]{:S(2)}) async-start(bf16[8,320,256]{2,1,0:T(8,128)(2,1)} %broadcast_in_dim.5), calls=%async_computation.3 | async-start | bytes 2621440 | tf_op jit(solution)/shard_map/all_to_all | solution.py:265
  237.7 18.2 %collective-permute-start.19 = (bf16[256,512]{1,0:T(8,128)(2,1)S(1)}, bf16[256,512]{1,0:T(8,128)(2,1)S(1)}, u32[]{:S(2)}, u32[]{:S(2)}) collective-permute-start(bf16[256,512]{1,0:T(8,128)(2,1)S(1)} %bitcast.98), channel_id=1, source_target_pairs={{0,24},{8,0},{16,8},{24,16},{1,25},{9,1},{17,9},{25,17},{2,26},{10... | collective-permute-start | bytes 786440 | tf_op jit(solution)/shard_map/ppermute | solution.py:279
  239.6 16.3 %collective-permute-start.18 = (bf16[256,512]{1,0:T(8,128)(2,1)S(1)}, bf16[256,512]{1,0:T(8,128)(2,1)S(1)}, u32[]{:S(2)}, u32[]{:S(2)}) collective-permute-start(bf16[256,512]{1,0:T(8,128)(2,1)S(1)} %bitcast.99), channel_id=1, source_target_pairs={{0,16},{8,24},{16,0},{24,8},{1,17},{9,25},{17,1},{25,9},{2,18},{10... | collective-permute-start | bytes 786440 | tf_op jit(solution)/shard_map/ppermute | solution.py:279
  244.5 12.0 %collective-permute-start.17 = (bf16[256,512]{1,0:T(8,128)(2,1)S(1)}, bf16[256,512]{1,0:T(8,128)(2,1)S(1)}, u32[]{:S(2)}, u32[]{:S(2)}) collective-permute-start(bf16[256,512]{1,0:T(8,128)(2,1)S(1)} %bitcast.100), channel_id=1, source_target_pairs={{0,8},{8,16},{16,24},{24,0},{1,9},{9,17},{17,25},{25,1},{2,10},{10... | collective-permute-start | bytes 786440 | tf_op jit(solution)/shard_map/ppermute | solution.py:279
  247.3 7.9 %collective-permute-start.16 = (bf16[320,128]{1,0:T(8,128)(2,1)S(1)}, bf16[320,128]{1,0:T(8,128)(2,1)S(1)}, u32[]{:S(2)}, u32[]{:S(2)}) collective-permute-start(bf16[320,128]{1,0:T(8,128)(2,1)S(1)} %get-tuple-element.31), channel_id=1, source_target_pairs={{0,262},{2,260},{4,258},{6,256},{256,6},{258,4},{260,2},{262,0},{1... | collective-permute-start | bytes 245768 | tf_op jit(solution)/shard_map/ppermute | solution.py:320
  272.4 10.1 %collective-permute-start.20 = (bf16[2560,256]{1,0:T(8,128)(2,1)S(1)}, bf16[2560,256]{1,0:T(8,128)(2,1)S(1)}, u32[]{:S(2)}, u32[]{:S(2)}) collective-permute-start(bf16[2560,256]{1,0:T(8,128)(2,1)S(1)} %bitcast.89), channel_id=1, source_target_pairs={{0,1},{1,0},{2,3},{3,2},{4,5},{5,4},{6,7},{7,6},{8,9},{9,8},{10,11... | collective-permute-start | bytes 3932168 | tf_op jit(solution)/shard_map/ppermute | solution.py:261
  274.8 28.3 %collective-permute-start.22 = (bf16[4,256,512]{2,1,0:T(8,128)(2,1)S(1)}, bf16[4,256,512]{2,1,0:T(8,128)(2,1)S(1)}, u32[]{:S(2)}, u32[]{:S(2)}) collective-permute-start(bf16[4,256,512]{2,1,0:T(8,128)(2,1)S(1)} %pad_maximum_fusion.3.near_ref), channel_id=1, source_target_pairs={{0,1},{1,0},{2,3},{3,2},{4,5},{5,4},{6,7},{7,6},{8,9},{9,8},{10,11... | collective-permute-start | bytes 3145736 | tf_op jit(solution)/shard_map/ppermute | solution.py:261
  276.8 0.9 copy-start
  288.0 8.8 %collective-permute-start.21 = (bf16[4,96,128]{2,1,0:T(8,128)(2,1)S(1)}, bf16[4,96,128]{2,1,0:T(8,128)(2,1)S(1)}, u32[]{:S(2)}, u32[]{:S(2)}) collective-permute-start(bf16[4,96,128]{2,1,0:T(8,128)(2,1)S(1)} %get-tuple-element.54), channel_id=1, source_target_pairs={{0,262},{2,260},{4,258},{6,256},{256,6},{258,4},{260,2},{262,0},{1... | collective-permute-start | bytes 294920 | tf_op jit(solution)/shard_map/ppermute | solution.py:320
  298.3 9.4 %all-to-all-start.4 = ((bf16[4,80,128]{2,1,0:T(8,128)(2,1)}), bf16[4,80,128]{2,1,0:T(8,128)(2,1)S(1)}, u32[]{:S(2)}, u32[]{:S(2)}) async-start(bf16[4,80,128]{2,1,0:T(8,128)(2,1)} %shard_map.69), calls=%async_computation.4 | async-start | bytes 163840 | tf_op jit(solution)/shard_map/all_to_all | solution.py:265

commit v8 on v6

--- a/solution.py
+++ b/solution.py
@@ -47,10 +47,12 @@
     w = w_ref[:, : sum_ref.shape[1]]
     out = sum_ref[...] + jnp.dot(x_ref[:, span], w, preferred_element_type=jnp.float32)
     q_ref[...] = out[:, :HD].astype(q_ref.dtype)
-    kv_ref[...] = out[:, HD:].astype(kv_ref.dtype)
-
-
-def project(core, x, near, far):
+    kv = out[:, HD:].astype(kv_ref.dtype)
+    for i in range(kv_ref.shape[0]):
+        kv_ref[i] = kv
+
+
+def project(core, x, near, far, count):
     n, cols = x.shape[0], 3 * HD
     smem, vmem = pl.BlockSpec(memory_space=pltpu.SMEM), pl.BlockSpec(memory_space=pltpu.VMEM)
     cost = pl.CostEstimate(
@@ -70,7 +72,7 @@
         out_specs=[vmem, vmem],
         out_shape=[
             jax.ShapeDtypeStruct((n, HD), jnp.bfloat16),
-            jax.ShapeDtypeStruct((n, 2 * HD), jnp.bfloat16),
+            jax.ShapeDtypeStruct((count, n, 2 * HD), jnp.bfloat16),
         ],
         compiler_params=LIMIT,
         cost_estimate=cost,
@@ -253,6 +255,15 @@
     return result
 
 
+def scatter_along_y(blocks, y0):
+    yh = lax.axis_index("yh")
+    blocks = blocks.reshape((2, 4) + blocks.shape[1:])
+    got = lax.ppermute(pick(blocks, 1 - yh), ("yh", "yl"), [(i, 7 - i) for i in range(8)])
+    home = yh == y0 // 4
+    blocks = jnp.where(home, pick(blocks, yh), got)
+    return scatter_by_shifts(blocks, "yl", jnp.where(home, y0 % 4, 3 - y0 % 4))
+
+
 def gather_by_shifts(block, axis):
     here, count = lax.axis_index(axis), lax.axis_size(axis)
     got = {0: block}
@@ -282,7 +293,8 @@
 
 def shards(hidden_in, norm_gain, snap_qkv, snap_out, owner_index, block_order):
     rows, width = hidden_in.shape
-    zh, y, x, c = (lax.axis_index(name) for name in ("zh", "y", "x", "c"))
+    ys = ("yh", "yl")
+    zh, y, x, c = (lax.axis_index(name) for name in ("zh", ys, "x", "c"))
     ny, nx = 8, 4
     half = rows // 2
     core = c.reshape(1)
@@ -299,36 +311,37 @@
     kpos = (pick(order, zh)[:, :, None] + offsets).reshape(-1)
     kpos = jnp.concatenate([kpos + c * half, kpos + (1 - c) * half]).reshape(1, -1)
     here = lax.dynamic_index_in_dim(order, y, 1, keepdims=False)
-    start = jnp.stack([pick(here, zh), pick(here, 1 - zh)]).reshape(-1) + c * half
+    start = pick(here, zh) + c * half
+    start_other = pick(here, 1 - zh) + c * half
 
     part = width // (2 * ny)
     w = fold(snap_qkv[0], ny)
     w = pick(exchange(w, "x"), x0)
-    wo = scatter_by_shifts(snap_out[0].reshape(ny, -1, snap_out.shape[2]), "y", y0)
-    w, wo, normed, kpos, start = lax.optimization_barrier((w, wo, normed, kpos, start))
-    w = pick(exchange(w, "y"), y0)
+    wo = scatter_along_y(snap_out[0].reshape(ny, -1, snap_out.shape[2]), y0)
+    w, wo, normed, kpos, start, start_other = lax.optimization_barrier((w, wo, normed, kpos, start, start_other))
+    w = pick(exchange(w, ys), y0)
     wo = jnp.transpose(wo.reshape(wo.shape[0], nx, -1), (1, 0, 2))
     wo = scatter_by_shifts(wo, "x", x0)
     wo = jnp.transpose(wo.reshape(wo.shape[0], nx, HD), (1, 0, 2)).reshape(part, HD)
     w = jnp.concatenate([w, wo], axis=1)
     w, normed = lax.optimization_barrier((w, normed))
     w = jnp.where(zh == zh0, jnp.where(x % 2 == c, w, trade(w, 0)), trade(w, 1))
-    w = spread(w, "y").reshape(ny * part, 4 * HD)
+    w = spread(w, ys).reshape(ny * part, 4 * HD)
     normed = gather_by_shifts(normed, "x").reshape(-1, width)
-    q, kv = project(core, normed, w, swap(w, "c"))
+    q, kv = project(core, normed, w, swap(w, "c"), ny)
     wo = w[:, 3 * HD :].reshape(ny, nx, part // nx, HD)
     wo = jnp.transpose(wo, (0, 2, 1, 3)).reshape(ny * part // nx, nx * HD)
     q, kv, wo = lax.optimization_barrier((q, kv, wo))
 
-    near = spread(kv, "y").reshape(-1, 2 * HD)
-    q_all = jnp.concatenate([q, mirror(q)])
+    near = exchange(kv, ys).reshape(-1, 2 * HD)
+    q_other = mirror(q)
     wo = gather_by_shifts(wo, "x")
-    near, q_all, wo = lax.optimization_barrier((near, q_all, wo))
+    near, q_other, wo = lax.optimization_barrier((near, q_other, wo))
     far = swap(near, "c")
     wo_far = swap(wo, "c")
 
-    parts = attend(start, q_all, near, far, kpos, half)
-    context = merge(parts[:nx], mirror(parts[nx:]))
+    others = mirror(attend(start_other, q_other, near, far, kpos, half))
+    context = merge(attend(start, q, near, far, kpos, half), others)
     context = exchange(context, "x")
     terms = finish(core, context, wo, wo_far)
     terms = exchange(terms, ("zl", "c")).reshape(-1, rows, terms.shape[2])
@@ -336,7 +349,7 @@
 
 
 def solution(mesh):
-    fine = Mesh(mesh.devices.reshape(2, 8, 4, 4, 2), ("zh", "y", "x", "zl", "c"))
-    ctx, tp = ("zh", "y", "x"), ("zl", "c")
+    fine = Mesh(mesh.devices.reshape(2, 2, 4, 4, 4, 2), ("zh", "yh", "yl", "x", "zl", "c"))
+    ctx, tp = ("zh", "yh", "yl", "x"), ("zl", "c")
     in_specs = (P(ctx, None), P(), P(ctx, None, None, tp), P(ctx, tp, None), P(), P())
     return jax.shard_map(shards, mesh=fine, in_specs=in_specs, out_specs=P(ctx, tp), check_vma=False)

time: 233 us -> 237 us (1.017)
  waiting for transfers between devices: 77.4 us -> 92.9 us
  starting transfers between devices: 107 us -> 93.5 us
    ppermute x0 -> x1, waiting for transfers between devices: none -> 19.2 us  [scatter_along_y(): lax.ppermute(pick(blocks, 1 - yh), ('yh', 'yl'), [(i, 7 - i) for i in ran...]
    ppermute x16 -> x12, starting transfers between devices: 54.7 us -> 38.4 us  [shift(): lax.ppermute(block, axis, [(i, (i + distance) % count) for i in range(cou...]
    ppermute x2, waiting for transfers between devices: 10.9 us -> 0.22 us  [mirror(): return lax.ppermute(block, ('zh', 'zl'), [(i, 7 - i) for i in range(8)])]
    ppermute x16 -> x12, waiting for transfers between devices: 10.5 us -> 19.9 us  [shift(): lax.ppermute(block, axis, [(i, (i + distance) % count) for i in range(cou...]
    all_to_all x5, starting transfers between devices: 27.1 us -> 20.8 us  [exchange(): return lax.all_to_all(block, axis, 0, 0, tiled=True)]
    ppermute x0 -> x1, starting transfers between devices: none -> 5.09 us  [scatter_along_y(): lax.ppermute(pick(blocks, 1 - yh), ('yh', 'yl'), [(i, 7 - i) for i in ran...]
    all_to_all x5, waiting for transfers between devices: 50 us -> 47 us  [exchange(): return lax.all_to_all(block, axis, 0, 0, tiled=True)]
    ppermute x2, starting transfers between devices: 5.84 us -> 8.4 us  [mirror(): return lax.ppermute(block, ('zh', 'zl'), [(i, 7 - i) for i in range(8)])]
  transfers between devices with their start and end apart: 28 -> 25, of which waited for: 15 -> 16; matrix products, arithmetic and copies ran while one was open for 4% -> 4% of each run, Pallas kernels for 4% -> 5%
where the time goes in v8:
time: 237 us; the launch traced here: 236 us
  starting transfers between devices  93.5 us (39%)
  waiting for transfers between devices  92.9 us (39%)
  Pallas kernels  19.1 us (8%)
  blocking collectives  14.8 us (6%)
  local copies, waits for them, and re-layouts  7.39 us (3%)
  other arithmetic  6.61 us (3%)
    all_to_all x5, waiting for transfers between devices, exchange(): return lax.all_to_all(block, axis, 0, 0, tiled=True)  47 us
    ppermute x12, starting transfers between devices, shift(): lax.ppermute(block, axis, [(i, (i + distance) % count) for i in range(cou...  38.4 us
    all_to_all x5, starting transfers between devices, exchange(): return lax.all_to_all(block, axis, 0, 0, tiled=True)  20.8 us
    ppermute x12, waiting for transfers between devices, shift(): lax.ppermute(block, axis, [(i, (i + distance) % count) for i in range(cou...  19.9 us
    ppermute x1, waiting for transfers between devices, scatter_along_y(): lax.ppermute(pick(blocks, 1 - yh), ('yh', 'yl'), [(i, 7 - i) for i in ran...  19.2 us
    all_to_all x1, blocking collectives, exchange(): return lax.all_to_all(block, axis, 0, 0, tiled=True)  14.8 us
    ppermute x2, starting transfers between devices, trade(): return lax.ppermute(block, ('zh', 'x', 'zl', 'c'), route)  14.1 us
    pallas_call x2, Pallas kernels, attend(): pl.pallas_call(attend_kernel, grid=(nq // tile,), in_specs=[pl.BlockSpec(...  8.76 us
  transfers between devices with their start and end apart: 25, of which 16 were waited for; matrix products, arithmetic and copies ran while one was open for 4% of the time, Pallas kernels for 5%

profile of v8, /device:TPU:1, one launch (start us, length us, event | category | flops | bytes accessed | tf_op | source)
XLA Modules:
  0.0 235.8 jit_solution(14109390510413761325)
XLA Ops:
  0.0 6.3 %shard_map.64 = bf16[4,8,128,384]{3,2,1,0:T(8,128)(2,1)} custom-call(bf16[3,2,1024,256]{3,2,1,0:T(8,128)(2,1)} %bitcast.83), custom_call_target="tpu_custom_call" | custom-call | bytes 6291456 | tf_op jit(solution)/shard_map/pallas_call | solution.py:26
  6.3 5.0 %all-to-all-start = ((bf16[4,8,128,384]{3,2,1,0:T(8,128)(2,1)}), bf16[4,8,128,384]{3,2,1,0:T(8,128)(2,1)S(1)}, u32[]{:S(2)}, u32[]{:S(2)}) async-start(bf16[4,8,128,384]{3,2,1,0:T(8,128)(2,1)} %shard_map.64), calls=%async_computation | async-start | bytes 6291456 | tf_op jit(solution)/shard_map/all_to_all | solution.py:227
  11.3 1.9 dynamic-slice_bitcast_fusion.1
  13.2 5.1 %collective-permute-start = (bf16[4,32,2048]{2,1,0:T(8,128)(2,1)}, bf16[4,32,2048]{2,1,0:T(8,128)(2,1)}, u32[]{:S(2)}, u32[]{:S(2)}) collective-permute-start(bf16[4,32,2048]{2,1,0:T(8,128)(2,1)} %dynamic-slice_bitcast_fusion.1), channel_id=1, source_target_pairs={{0,224},{32,192},{64,160},{96,128},{128,96},{160,64},{192,32},{224... | collective-permute-start | bytes 1572872 | tf_op jit(solution)/shard_map/ppermute | solution.py:261
  18.4 1.1 fusion
  20.4 1.1 fusion.2
  21.5 19.2 %collective-permute-done = bf16[4,32,2048]{2,1,0:T(8,128)(2,1)} collective-permute-done((bf16[4,32,2048]{2,1,0:T(8,128)(2,1)}, bf16[4,32,2048]{2,1,0:T(8,128)(2,1)}, u32[]{:S(2)}, u32[]{:S(2)}) %collective-permute-start) | collective-permute-done | bytes 524320 | tf_op jit(solution)/shard_map/ppermute | solution.py:261
  40.7 1.3 bitcast_select_fusion
  42.8 5.3 %collective-permute-start.1 = (bf16[32,2048]{1,0:T(8,128)(2,1)}, bf16[32,2048]{1,0:T(8,128)(2,1)}, u32[]{:S(2)}, u32[]{:S(2)}) collective-permute-start(bf16[32,2048]{1,0:T(8,128)(2,1)} %get-tuple-element.47), channel_id=1, source_target_pairs={{0,96},{32,0},{64,32},{96,64},{1,97},{33,1},{65,33},{97,65},{2,98}... | collective-permute-start | bytes 393224 | tf_op jit(solution)/shard_map/ppermute | solution.py:241
  48.1 1.9 collective-permute-start.2
  50.1 2.2 collective-permute-start.3
  52.5 3.5 %collective-permute-done.2 = bf16[32,2048]{1,0:T(8,128)(2,1)} collective-permute-done((bf16[32,2048]{1,0:T(8,128)(2,1)}, bf16[32,2048]{1,0:T(8,128)(2,1)}, u32[]{:S(2)}, u32[]{:S(2)}) %collective-permute-start.2) | collective-permute-done | bytes 131104 | tf_op jit(solution)/shard_map/ppermute | solution.py:241
  56.0 6.6 %collective-permute-done.3 = bf16[32,2048]{1,0:T(8,128)(2,1)} collective-permute-done((bf16[32,2048]{1,0:T(8,128)(2,1)}, bf16[32,2048]{1,0:T(8,128)(2,1)}, u32[]{:S(2)}, u32[]{:S(2)}) %collective-permute-start.3) | collective-permute-done | bytes 131104 | tf_op jit(solution)/shard_map/ppermute | solution.py:241
  62.6 1.6 fusion.4
  64.2 1.0 dynamic-slice_bitcast_fusion
  65.2 4.7 %all-to-all-start.1 = ((bf16[8,128,384]{2,1,0:T(8,128)(2,1)}), bf16[8,128,384]{2,1,0:T(8,128)(2,1)S(1)}, u32[]{:S(2)}, u32[]{:S(2)}) async-start(bf16[8,128,384]{2,1,0:T(8,128)(2,1)} %dynamic-slice_bitcast_fusion), calls=%async_computation.1 | async-start | bytes 1572864 | tf_op jit(solution)/shard_map/all_to_all | solution.py:227
  70.3 4.6 %collective-permute-start.4 = (bf16[32,512]{1,0:T(8,128)(2,1)S(1)}, bf16[32,512]{1,0:T(8,128)(2,1)S(1)}, u32[]{:S(2)}, u32[]{:S(2)}) collective-permute-start(bf16[32,512]{1,0:T(8,128)(2,1)S(1)} %bitcast.102), channel_id=1, source_target_pairs={{0,24},{8,0},{16,8},{24,16},{1,25},{9,1},{17,9},{25,17},{2,26},{10... | collective-permute-start | bytes 98312 | tf_op jit(solution)/shard_map/ppermute | solution.py:241
  74.9 1.9 collective-permute-start.5
  76.8 3.7 %collective-permute-start.6 = (bf16[32,512]{1,0:T(8,128)(2,1)S(1)}, bf16[32,512]{1,0:T(8,128)(2,1)S(1)}, u32[]{:S(2)}, u32[]{:S(2)}) collective-permute-start(bf16[32,512]{1,0:T(8,128)(2,1)S(1)} %bitcast.104), channel_id=1, source_target_pairs={{0,16},{8,24},{16,0},{24,8},{1,17},{9,25},{17,1},{25,9},{2,18},{10... | collective-permute-start | bytes 98312 | tf_op jit(solution)/shard_map/ppermute | solution.py:241
  81.0 2.1 collective-permute-done.6
  83.2 10.3 %all-to-all-done.1 = bf16[8,128,384]{2,1,0:T(8,128)(2,1)S(1)} async-done(((bf16[8,128,384]{2,1,0:T(8,128)(2,1)}), bf16[8,128,384]{2,1,0:T(8,128)(2,1)S(1)}, u32[]{:S(2)}, u32[]{:S(2)}) %all-to-all-start.1) | async-done | bytes 786464 | tf_op jit(solution)/shard_map/all_to_all | solution.py:227
  93.5 12.2 %collective-permute-start.11 = (bf16[128,512]{1,0:T(8,128)(2,1)S(1)}, bf16[128,512]{1,0:T(8,128)(2,1)S(1)}, u32[]{:S(2)}, u32[]{:S(2)}) collective-permute-start(bf16[128,512]{1,0:T(8,128)(2,1)S(1)} %pad_maximum_fusion.4), channel_id=1, source_target_pairs={{0,262},{1,270},{2,260},{3,268},{4,258},{5,266},{6,256},{7,264},{8... | collective-permute-start | bytes 393224 | tf_op jit(solution)/shard_map/ppermute | solution.py:287
  105.7 1.9 collective-permute-start.10
  107.7 4.3 %collective-permute-done.11 = bf16[128,512]{1,0:T(8,128)(2,1)S(1)} collective-permute-done((bf16[128,512]{1,0:T(8,128)(2,1)S(1)}, bf16[128,512]{1,0:T(8,128)(2,1)S(1)}, u32[]{:S(2)}, u32[]{:S(2)}) %collective-permute-start.11) | collective-permute-done | bytes 131104 | tf_op jit(solution)/shard_map/ppermute | solution.py:287
  112.7 1.1 broadcast_in_dim.2
  113.7 3.6 %all-to-all-start.2 = ((bf16[8,128,512]{2,1,0:T(8,128)(2,1)}), bf16[8,128,512]{2,1,0:T(8,128)(2,1)S(1)}, u32[]{:S(2)}, u32[]{:S(2)}) async-start(bf16[8,128,512]{2,1,0:T(8,128)(2,1)} %broadcast_in_dim.2), calls=%async_computation.2 | async-start | bytes 2097152 | tf_op jit(solution)/shard_map/all_to_all | solution.py:227
  117.3 2.8 %collective-permute-start.9 = (bf16[80,2048]{1,0:T(8,128)(2,1)S(1)}, bf16[80,2048]{1,0:T(8,128)(2,1)S(1)}, u32[]{:S(2)}, u32[]{:S(2)}) collective-permute-start(bf16[80,2048]{1,0:T(8,128)(2,1)S(1)} %fusion.2), channel_id=1, source_target_pairs={{0,24},{8,0},{16,8},{24,16},{1,25},{9,1},{17,9},{25,17},{2,26},{10... | collective-permute-start | bytes 983048 | tf_op jit(solution)/shard_map/ppermute | solution.py:241
  120.2 3.4 %collective-permute-start.8 = (bf16[80,2048]{1,0:T(8,128)(2,1)S(1)}, bf16[80,2048]{1,0:T(8,128)(2,1)S(1)}, u32[]{:S(2)}, u32[]{:S(2)}) collective-permute-start(bf16[80,2048]{1,0:T(8,128)(2,1)S(1)} %fusion.2), channel_id=1, source_target_pairs={{0,16},{8,24},{16,0},{24,8},{1,17},{9,25},{17,1},{25,9},{2,18},{10... | collective-permute-start | bytes 983048 | tf_op jit(solution)/shard_map/ppermute | solution.py:241
  123.6 2.8 %collective-permute-start.7 = (bf16[80,2048]{1,0:T(8,128)(2,1)S(1)}, bf16[80,2048]{1,0:T(8,128)(2,1)S(1)}, u32[]{:S(2)}, u32[]{:S(2)}) collective-permute-start(bf16[80,2048]{1,0:T(8,128)(2,1)S(1)} %fusion.2), channel_id=1, source_target_pairs={{0,8},{8,16},{16,24},{24,0},{1,9},{9,17},{17,25},{25,1},{2,10},{10... | collective-permute-start | bytes 983048 | tf_op jit(solution)/shard_map/ppermute | solution.py:241
  126.3 19.4 %all-to-all-done.2 = bf16[8,128,512]{2,1,0:T(8,128)(2,1)S(1)} async-done(((bf16[8,128,512]{2,1,0:T(8,128)(2,1)}), bf16[8,128,512]{2,1,0:T(8,128)(2,1)S(1)}, u32[]{:S(2)}, u32[]{:S(2)}) %all-to-all-start.2) | async-done | bytes 1048608 | tf_op jit(solution)/shard_map/all_to_all | solution.py:227
  145.7 2.3 collective-permute-start.12
  150.2 1.6 shard_map.66
  151.8 3.6 %all-to-all-start.3 = ((bf16[8,320,256]{2,1,0:T(8,128)(2,1)}), bf16[8,320,256]{2,1,0:T(8,128)(2,1)S(1)}, u32[]{:S(2)}, u32[]{:S(2)}) async-start(bf16[8,320,256]{2,1,0:T(8,128)(2,1)} %get-tuple-element.30), calls=%async_computation.3 | async-start | bytes 2621440 | tf_op jit(solution)/shard_map/all_to_all | solution.py:227
  155.4 3.7 %collective-permute-start.16 = (bf16[256,512]{1,0:T(8,128)(2,1)S(1)}, bf16[256,512]{1,0:T(8,128)(2,1)S(1)}, u32[]{:S(2)}, u32[]{:S(2)}) collective-permute-start(bf16[256,512]{1,0:T(8,128)(2,1)S(1)} %bitcast.90), channel_id=1, source_target_pairs={{0,24},{8,0},{16,8},{24,16},{1,25},{9,1},{17,9},{25,17},{2,26},{10... | collective-permute-start | bytes 786440 | tf_op jit(solution)/shard_map/ppermute | solution.py:241
  159.1 3.4 %collective-permute-start.15 = (bf16[256,512]{1,0:T(8,128)(2,1)S(1)}, bf16[256,512]{1,0:T(8,128)(2,1)S(1)}, u32[]{:S(2)}, u32[]{:S(2)}) collective-permute-start(bf16[256,512]{1,0:T(8,128)(2,1)S(1)} %bitcast.91), channel_id=1, source_target_pairs={{0,16},{8,24},{16,0},{24,8},{1,17},{9,25},{17,1},{25,9},{2,18},{10... | collective-permute-start | bytes 786440 | tf_op jit(solution)/shard_map/ppermute | solution.py:241
  162.6 2.8 %collective-permute-start.14 = (bf16[256,512]{1,0:T(8,128)(2,1)S(1)}, bf16[256,512]{1,0:T(8,128)(2,1)S(1)}, u32[]{:S(2)}, u32[]{:S(2)}) collective-permute-start(bf16[256,512]{1,0:T(8,128)(2,1)S(1)} %bitcast.92), channel_id=1, source_target_pairs={{0,8},{8,16},{16,24},{24,0},{1,9},{9,17},{17,25},{25,1},{2,10},{10... | collective-permute-start | bytes 786440 | tf_op jit(solution)/shard_map/ppermute | solution.py:241
  165.3 3.7 %collective-permute-start.13 = (bf16[320,128]{1,0:T(8,128)(2,1)S(1)}, bf16[320,128]{1,0:T(8,128)(2,1)S(1)}, u32[]{:S(2)}, u32[]{:S(2)}) collective-permute-start(bf16[320,128]{1,0:T(8,128)(2,1)S(1)} %get-tuple-element.29.q_ref), channel_id=1, source_target_pairs={{0,262},{2,260},{4,258},{6,256},{256,6},{258,4},{260,2},{262,0},{1... | collective-permute-start | bytes 245768 | tf_op jit(solution)/shard_map/ppermute | solution.py:291
  169.7 6.6 %collective-permute-done.14 = bf16[256,512]{1,0:T(8,128)(2,1)S(1)} collective-permute-done((bf16[256,512]{1,0:T(8,128)(2,1)S(1)}, bf16[256,512]{1,0:T(8,128)(2,1)S(1)}, u32[]{:S(2)}, u32[]{:S(2)}) %collective-permute-start.14) | collective-permute-done | bytes 262176 | tf_op jit(solution)/shard_map/ppermute | solution.py:241
  177.4 12.8 %all-to-all-done.3 = bf16[8,320,256]{2,1,0:T(8,128)(2,1)S(1)} async-done(((bf16[8,320,256]{2,1,0:T(8,128)(2,1)}), bf16[8,320,256]{2,1,0:T(8,128)(2,1)S(1)}, u32[]{:S(2)}, u32[]{:S(2)}) %all-to-all-start.3) | async-done | bytes 1310752 | tf_op jit(solution)/shard_map/all_to_all | solution.py:227
  190.2 2.4 %collective-permute-start.17 = (bf16[2560,256]{1,0:T(8,128)(2,1)S(1)}, bf16[2560,256]{1,0:T(8,128)(2,1)S(1)}, u32[]{:S(2)}, u32[]{:S(2)}) collective-permute-start(bf16[2560,256]{1,0:T(8,128)(2,1)S(1)} %bitcast.78), channel_id=1, source_target_pairs={{0,1},{1,0},{2,3},{3,2},{4,5},{5,4},{6,7},{7,6},{8,9},{9,8},{10,11... | collective-permute-start | bytes 3932168 | tf_op jit(solution)/shard_map/ppermute | solution.py:223
  192.5 1.9 collective-permute-start.19
  196.1 4.4 %shard_map.68 = bf16[4,96,128]{2,1,0:T(8,128)(2,1)S(1)} custom-call(s32[4]{0:T(128)S(1)} %get-tuple-element.34.start_ref, bf16[320,128]{1,0:T(8,128)(2,1)S(1)} %copy-done.1, bf16[2560,256]{1,0:T(8,128)(2,1)S(1)} %bitcast.79, bf16[2560,256]{1,0:T(8,128)(2,1)S(1)} %collective-permute-done.17.far_ref, s32[1,5120]{1,0:T(1,128)S(1)} %bitcast.81), custom_call_target="tpu_custom_call" | custom-call | flops 838860800 | bytes 2621440 | tf_op jit(solution)/shard_map/pallas_call | solution.py:143
  200.5 4.7 %collective-permute-start.18 = (bf16[4,96,128]{2,1,0:T(8,128)(2,1)S(1)}, bf16[4,96,128]{2,1,0:T(8,128)(2,1)S(1)}, u32[]{:S(2)}, u32[]{:S(2)}) collective-permute-start(bf16[4,96,128]{2,1,0:T(8,128)(2,1)S(1)} %shard_map.68), channel_id=1, source_target_pairs={{0,262},{2,260},{4,258},{6,256},{256,6},{258,4},{260,2},{262,0},{1... | collective-permute-start | bytes 294920 | tf_op jit(solution)/shard_map/ppermute | solution.py:291
  205.1 4.4 %shard_map.67.near_ref = bf16[4,96,128]{2,1,0:T(8,128)(2,1)S(1)} custom-call(s32[4]{0:T(128)S(1)} %get-tuple-element.21.start_ref, bf16[320,128]{1,0:T(8,128)(2,1)S(1)} %get-tuple-element.29.q_ref, bf16[2560,256]{1,0:T(8,128)(2,1)S(1)} %bitcast.80, bf16[2560,256]{1,0:T(8,128)(2,1)S(1)} %collective-permute-done.17.far_ref, s32[1,5120]{1,0:T(1,128)S(1)} %bitcast.82), custom_call_target="tpu_custom_call" | custom-call | flops 838860800 | bytes 2621440 | tf_op jit(solution)/shard_map/pallas_call | solution.py:143
  209.7 1.5 shard_map.69
  211.3 4.0 %all-to-all-start.4 = ((bf16[4,80,128]{2,1,0:T(8,128)(2,1)}), bf16[4,80,128]{2,1,0:T(8,128)(2,1)S(1)}, u32[]{:S(2)}, u32[]{:S(2)}) async-start(bf16[4,80,128]{2,1,0:T(8,128)(2,1)} %shard_map.69), calls=%async_computation.4 | async-start | bytes 163840 | tf_op jit(solution)/shard_map/all_to_all | solution.py:227
  215.3 4.6 %all-to-all-done.4.context_ref = bf16[4,80,128]{2,1,0:T(8,128)(2,1)S(1)} async-done(((bf16[4,80,128]{2,1,0:T(8,128)(2,1)}), bf16[4,80,128]{2,1,0:T(8,128)(2,1)S(1)}, u32[]{:S(2)}, u32[]{:S(2)}) %all-to-all-start.4) | async-done | bytes 81952 | tf_op jit(solution)/shard_map/all_to_all | solution.py:227
  220.3 14.8 %all_to_all.30 = bf16[8,80,256]{2,1,0:T(8,128)(2,1)S(1)} all-to-all(bf16[8,80,256]{2,1,0:T(8,128)(2,1)S(1)} %shard_map.70), channel_id=1, replica_groups=mesh['zh'=2,'yh'=2,'yl'=4,'x'=4,'zl'=4,'c'=2] {'zl','c'}, dimensions={0} | all-to-all | bytes 655360 | tf_op jit(solution)/shard_map/all_to_all | solution.py:227
  (60 shorter events, 9.5 us)
Async XLA Ops:
  6.3 12.0 %copy-start.5 = (s32[64]{0:T(128)S(1)}, s32[64]{0:T(128)}, u32[]{:S(2)}) copy-start(s32[64]{0:T(128)} %param.11) | copy-start | bytes 772
  6.3 57.9 %all-to-all-start = ((bf16[4,8,128,384]{3,2,1,0:T(8,128)(2,1)}), bf16[4,8,128,384]{3,2,1,0:T(8,128)(2,1)S(1)}, u32[]{:S(2)}, u32[]{:S(2)}) async-start(bf16[4,8,128,384]{3,2,1,0:T(8,128)(2,1)} %shard_map.64), calls=%async_computation | async-start | bytes 6291456 | tf_op jit(solution)/shard_map/all_to_all | solution.py:227
  11.2 9.1 %copy-start.4 = (f32[2048]{0:T(1024)S(1)}, f32[2048]{0:T(1024)}, u32[]{:S(2)}) copy-start(f32[2048]{0:T(1024)} %param.7) | copy-start | bytes 24580
  13.2 27.6 %collective-permute-start = (bf16[4,32,2048]{2,1,0:T(8,128)(2,1)}, bf16[4,32,2048]{2,1,0:T(8,128)(2,1)}, u32[]{:S(2)}, u32[]{:S(2)}) collective-permute-start(bf16[4,32,2048]{2,1,0:T(8,128)(2,1)} %dynamic-slice_bitcast_fusion.1), channel_id=1, source_target_pairs={{0,224},{32,192},{64,160},{96,128},{128,96},{160,64},{192,32},{224... | collective-permute-start | bytes 1572872 | tf_op jit(solution)/shard_map/ppermute | solution.py:261
  42.0 8.1 %copy-start.2 = (bf16[4,32,2048]{2,1,0:T(8,128)(2,1)}, bf16[4,32,2048]{2,1,0:T(8,128)(2,1)S(1)}, u32[]{:S(2)}) copy-start(bf16[4,32,2048]{2,1,0:T(8,128)(2,1)S(1)} %bitcast_select_fusion) | copy-start | bytes 1572868
  42.8 9.7 %collective-permute-start.1 = (bf16[32,2048]{1,0:T(8,128)(2,1)}, bf16[32,2048]{1,0:T(8,128)(2,1)}, u32[]{:S(2)}, u32[]{:S(2)}) collective-permute-start(bf16[32,2048]{1,0:T(8,128)(2,1)} %get-tuple-element.47), channel_id=1, source_target_pairs={{0,96},{32,0},{64,32},{96,64},{1,97},{33,1},{65,33},{97,65},{2,98}... | collective-permute-start | bytes 393224 | tf_op jit(solution)/shard_map/ppermute | solution.py:241
  48.1 7.9 %collective-permute-start.2 = (bf16[32,2048]{1,0:T(8,128)(2,1)}, bf16[32,2048]{1,0:T(8,128)(2,1)}, u32[]{:S(2)}, u32[]{:S(2)}) collective-permute-start(bf16[32,2048]{1,0:T(8,128)(2,1)} %get-tuple-element.46), channel_id=1, source_target_pairs={{0,32},{32,64},{64,96},{96,0},{1,33},{33,65},{65,97},{97,1},{2,34}... | collective-permute-start | bytes 393224 | tf_op jit(solution)/shard_map/ppermute | solution.py:241
  50.1 12.5 %collective-permute-start.3 = (bf16[32,2048]{1,0:T(8,128)(2,1)}, bf16[32,2048]{1,0:T(8,128)(2,1)}, u32[]{:S(2)}, u32[]{:S(2)}) collective-permute-start(bf16[32,2048]{1,0:T(8,128)(2,1)} %get-tuple-element.45), channel_id=1, source_target_pairs={{0,64},{32,96},{64,0},{96,32},{1,65},{33,97},{65,1},{97,33},{2,66}... | collective-permute-start | bytes 393224 | tf_op jit(solution)/shard_map/ppermute | solution.py:241
  65.2 4.7 %copy-start.3 = (bf16[32,2048]{1,0:T(8,128)(2,1)S(1)}, bf16[32,2048]{1,0:T(8,128)(2,1)}, u32[]{:S(2)}) copy-start(bf16[32,2048]{1,0:T(8,128)(2,1)} %fusion.4) | copy-start | bytes 393220
  65.2 28.2 %all-to-all-start.1 = ((bf16[8,128,384]{2,1,0:T(8,128)(2,1)}), bf16[8,128,384]{2,1,0:T(8,128)(2,1)S(1)}, u32[]{:S(2)}, u32[]{:S(2)}) async-start(bf16[8,128,384]{2,1,0:T(8,128)(2,1)} %dynamic-slice_bitcast_fusion), calls=%async_computation.1 | async-start | bytes 1572864 | tf_op jit(solution)/shard_map/all_to_all | solution.py:227
  70.3 10.2 %collective-permute-start.4 = (bf16[32,512]{1,0:T(8,128)(2,1)S(1)}, bf16[32,512]{1,0:T(8,128)(2,1)S(1)}, u32[]{:S(2)}, u32[]{:S(2)}) collective-permute-start(bf16[32,512]{1,0:T(8,128)(2,1)S(1)} %bitcast.102), channel_id=1, source_target_pairs={{0,24},{8,0},{16,8},{24,16},{1,25},{9,1},{17,9},{25,17},{2,26},{10... | collective-permute-start | bytes 98312 | tf_op jit(solution)/shard_map/ppermute | solution.py:241
  74.9 6.2 %collective-permute-start.5 = (bf16[32,512]{1,0:T(8,128)(2,1)S(1)}, bf16[32,512]{1,0:T(8,128)(2,1)S(1)}, u32[]{:S(2)}, u32[]{:S(2)}) collective-permute-start(bf16[32,512]{1,0:T(8,128)(2,1)S(1)} %bitcast.103), channel_id=1, source_target_pairs={{0,8},{8,16},{16,24},{24,0},{1,9},{9,17},{17,25},{25,1},{2,10},{10... | collective-permute-start | bytes 98312 | tf_op jit(solution)/shard_map/ppermute | solution.py:241
  76.8 6.3 %collective-permute-start.6 = (bf16[32,512]{1,0:T(8,128)(2,1)S(1)}, bf16[32,512]{1,0:T(8,128)(2,1)S(1)}, u32[]{:S(2)}, u32[]{:S(2)}) collective-permute-start(bf16[32,512]{1,0:T(8,128)(2,1)S(1)} %bitcast.104), channel_id=1, source_target_pairs={{0,16},{8,24},{16,0},{24,8},{1,17},{9,25},{17,1},{25,9},{2,18},{10... | collective-permute-start | bytes 98312 | tf_op jit(solution)/shard_map/ppermute | solution.py:241
  93.5 18.5 %collective-permute-start.11 = (bf16[128,512]{1,0:T(8,128)(2,1)S(1)}, bf16[128,512]{1,0:T(8,128)(2,1)S(1)}, u32[]{:S(2)}, u32[]{:S(2)}) collective-permute-start(bf16[128,512]{1,0:T(8,128)(2,1)S(1)} %pad_maximum_fusion.4), channel_id=1, source_target_pairs={{0,262},{1,270},{2,260},{3,268},{4,258},{5,266},{6,256},{7,264},{8... | collective-permute-start | bytes 393224 | tf_op jit(solution)/shard_map/ppermute | solution.py:287
  105.7 7.0 %collective-permute-start.10 = (bf16[128,512]{1,0:T(8,128)(2,1)S(1)}, bf16[128,512]{1,0:T(8,128)(2,1)S(1)}, u32[]{:S(2)}, u32[]{:S(2)}) collective-permute-start(bf16[128,512]{1,0:T(8,128)(2,1)S(1)} %pad_maximum_fusion.4), channel_id=1, source_target_pairs={{1,8},{3,10},{5,12},{7,14},{8,1},{10,3},{12,5},{14,7},{17,24},{19,... | collective-permute-start | bytes 393224 | tf_op jit(solution)/shard_map/ppermute | solution.py:287
  113.7 31.9 %all-to-all-start.2 = ((bf16[8,128,512]{2,1,0:T(8,128)(2,1)}), bf16[8,128,512]{2,1,0:T(8,128)(2,1)S(1)}, u32[]{:S(2)}, u32[]{:S(2)}) async-start(bf16[8,128,512]{2,1,0:T(8,128)(2,1)} %broadcast_in_dim.2), calls=%async_computation.2 | async-start | bytes 2097152 | tf_op jit(solution)/shard_map/all_to_all | solution.py:227
  117.3 30.7 %collective-permute-start.9 = (bf16[80,2048]{1,0:T(8,128)(2,1)S(1)}, bf16[80,2048]{1,0:T(8,128)(2,1)S(1)}, u32[]{:S(2)}, u32[]{:S(2)}) collective-permute-start(bf16[80,2048]{1,0:T(8,128)(2,1)S(1)} %fusion.2), channel_id=1, source_target_pairs={{0,24},{8,0},{16,8},{24,16},{1,25},{9,1},{17,9},{25,17},{2,26},{10... | collective-permute-start | bytes 983048 | tf_op jit(solution)/shard_map/ppermute | solution.py:241
  120.2 27.9 %collective-permute-start.8 = (bf16[80,2048]{1,0:T(8,128)(2,1)S(1)}, bf16[80,2048]{1,0:T(8,128)(2,1)S(1)}, u32[]{:S(2)}, u32[]{:S(2)}) collective-permute-start(bf16[80,2048]{1,0:T(8,128)(2,1)S(1)} %fusion.2), channel_id=1, source_target_pairs={{0,16},{8,24},{16,0},{24,8},{1,17},{9,25},{17,1},{25,9},{2,18},{10... | collective-permute-start | bytes 983048 | tf_op jit(solution)/shard_map/ppermute | solution.py:241
  123.6 24.5 %collective-permute-start.7 = (bf16[80,2048]{1,0:T(8,128)(2,1)S(1)}, bf16[80,2048]{1,0:T(8,128)(2,1)S(1)}, u32[]{:S(2)}, u32[]{:S(2)}) collective-permute-start(bf16[80,2048]{1,0:T(8,128)(2,1)S(1)} %fusion.2), channel_id=1, source_target_pairs={{0,8},{8,16},{16,24},{24,0},{1,9},{9,17},{17,25},{25,1},{2,10},{10... | collective-permute-start | bytes 983048 | tf_op jit(solution)/shard_map/ppermute | solution.py:241
  145.7 4.6 %collective-permute-start.12 = (bf16[1024,512]{1,0:T(8,128)(2,1)S(1)}, bf16[1024,512]{1,0:T(8,128)(2,1)S(1)}, u32[]{:S(2)}, u32[]{:S(2)}) collective-permute-start(bf16[1024,512]{1,0:T(8,128)(2,1)S(1)} %bitcast.75), channel_id=1, source_target_pairs={{0,1},{1,0},{2,3},{3,2},{4,5},{5,4},{6,7},{7,6},{8,9},{9,8},{10,11... | collective-permute-start | bytes 3145736 | tf_op jit(solution)/shard_map/ppermute | solution.py:223
  151.8 38.3 %all-to-all-start.3 = ((bf16[8,320,256]{2,1,0:T(8,128)(2,1)}), bf16[8,320,256]{2,1,0:T(8,128)(2,1)S(1)}, u32[]{:S(2)}, u32[]{:S(2)}) async-start(bf16[8,320,256]{2,1,0:T(8,128)(2,1)} %get-tuple-element.30), calls=%async_computation.3 | async-start | bytes 2621440 | tf_op jit(solution)/shard_map/all_to_all | solution.py:227
  155.4 13.7 %collective-permute-start.16 = (bf16[256,512]{1,0:T(8,128)(2,1)S(1)}, bf16[256,512]{1,0:T(8,128)(2,1)S(1)}, u32[]{:S(2)}, u32[]{:S(2)}) collective-permute-start(bf16[256,512]{1,0:T(8,128)(2,1)S(1)} %bitcast.90), channel_id=1, source_target_pairs={{0,24},{8,0},{16,8},{24,16},{1,25},{9,1},{17,9},{25,17},{2,26},{10... | collective-permute-start | bytes 786440 | tf_op jit(solution)/shard_map/ppermute | solution.py:241
  159.1 10.6 %collective-permute-start.15 = (bf16[256,512]{1,0:T(8,128)(2,1)S(1)}, bf16[256,512]{1,0:T(8,128)(2,1)S(1)}, u32[]{:S(2)}, u32[]{:S(2)}) collective-permute-start(bf16[256,512]{1,0:T(8,128)(2,1)S(1)} %bitcast.91), channel_id=1, source_target_pairs={{0,16},{8,24},{16,0},{24,8},{1,17},{9,25},{17,1},{25,9},{2,18},{10... | collective-permute-start | bytes 786440 | tf_op jit(solution)/shard_map/ppermute | solution.py:241
  162.6 13.8 %collective-permute-start.14 = (bf16[256,512]{1,0:T(8,128)(2,1)S(1)}, bf16[256,512]{1,0:T(8,128)(2,1)S(1)}, u32[]{:S(2)}, u32[]{:S(2)}) collective-permute-start(bf16[256,512]{1,0:T(8,128)(2,1)S(1)} %bitcast.92), channel_id=1, source_target_pairs={{0,8},{8,16},{16,24},{24,0},{1,9},{9,17},{17,25},{25,1},{2,10},{10... | collective-permute-start | bytes 786440 | tf_op jit(solution)/shard_map/ppermute | solution.py:241
  165.3 11.4 %collective-permute-start.13 = (bf16[320,128]{1,0:T(8,128)(2,1)S(1)}, bf16[320,128]{1,0:T(8,128)(2,1)S(1)}, u32[]{:S(2)}, u32[]{:S(2)}) collective-permute-start(bf16[320,128]{1,0:T(8,128)(2,1)S(1)} %get-tuple-element.29.q_ref), channel_id=1, source_target_pairs={{0,262},{2,260},{4,258},{6,256},{256,6},{258,4},{260,2},{262,0},{1... | collective-permute-start | bytes 245768 | tf_op jit(solution)/shard_map/ppermute | solution.py:291
  176.7 0.6 copy-start
  190.2 5.0 %collective-permute-start.17 = (bf16[2560,256]{1,0:T(8,128)(2,1)S(1)}, bf16[2560,256]{1,0:T(8,128)(2,1)S(1)}, u32[]{:S(2)}, u32[]{:S(2)}) collective-permute-start(bf16[2560,256]{1,0:T(8,128)(2,1)S(1)} %bitcast.78), channel_id=1, source_target_pairs={{0,1},{1,0},{2,3},{3,2},{4,5},{5,4},{6,7},{7,6},{8,9},{9,8},{10,11... | collective-permute-start | bytes 3932168 | tf_op jit(solution)/shard_map/ppermute | solution.py:223
  192.5 22.7 %collective-permute-start.19 = (bf16[4,256,512]{2,1,0:T(8,128)(2,1)S(1)}, bf16[4,256,512]{2,1,0:T(8,128)(2,1)S(1)}, u32[]{:S(2)}, u32[]{:S(2)}) collective-permute-start(bf16[4,256,512]{2,1,0:T(8,128)(2,1)S(1)} %pad_maximum_fusion.3.near_ref), channel_id=1, source_target_pairs={{0,1},{1,0},{2,3},{3,2},{4,5},{5,4},{6,7},{7,6},{8,9},{9,8},{10,11... | collective-permute-start | bytes 3145736 | tf_op jit(solution)/shard_map/ppermute | solution.py:223
  195.2 0.9 copy-start.1
  200.5 9.3 %collective-permute-start.18 = (bf16[4,96,128]{2,1,0:T(8,128)(2,1)S(1)}, bf16[4,96,128]{2,1,0:T(8,128)(2,1)S(1)}, u32[]{:S(2)}, u32[]{:S(2)}) collective-permute-start(bf16[4,96,128]{2,1,0:T(8,128)(2,1)S(1)} %shard_map.68), channel_id=1, source_target_pairs={{0,262},{2,260},{4,258},{6,256},{256,6},{258,4},{260,2},{262,0},{1... | collective-permute-start | bytes 294920 | tf_op jit(solution)/shard_map/ppermute | solution.py:291
  211.3 8.6 %all-to-all-start.4 = ((bf16[4,80,128]{2,1,0:T(8,128)(2,1)}), bf16[4,80,128]{2,1,0:T(8,128)(2,1)S(1)}, u32[]{:S(2)}, u32[]{:S(2)}) async-start(bf16[4,80,128]{2,1,0:T(8,128)(2,1)} %shard_map.69), calls=%async_computation.4 | async-start | bytes 163840 | tf_op jit(solution)/shard_map/all_to_all | solution.py:227

commit v9 on v8

--- a/solution.py
+++ b/solution.py
@@ -11,27 +11,27 @@
 HIDE = -1e30
 CHUNK = 640
 EXTRA = 16
-LIMIT = pltpu.CompilerParams(vmem_limit_bytes=48 * 1024 * 1024)
+LIMIT = pltpu.CompilerParams(vmem_limit_bytes=24 * 1024 * 1024)
 
 
 def fold_kernel(w_ref, out_ref):
     for h in range(2):
         for r in range(2):
             for j in range(3):
-                out_ref[2 * h + r, 0, :, j * HD : (j + 1) * HD] = w_ref[j, r, :, h * HD : (h + 1) * HD]
+                out_ref[2 * h + r, :, :, j * HD : (j + 1) * HD] = w_ref[j, r, :, :, h * HD : (h + 1) * HD]
 
 
 def fold(w, ny):
-    part = w.shape[1] // (2 * ny)
+    part, steps = w.shape[1] // (2 * ny), 2
     return pl.pallas_call(
         fold_kernel,
-        grid=(ny,),
-        in_specs=[pl.BlockSpec((3, 2, part, 2 * HD), lambda i: (0, 0, i, 0))],
-        out_specs=pl.BlockSpec((4, 1, part, 3 * HD), lambda i: (0, i, 0, 0)),
+        grid=(steps,),
+        in_specs=[pl.BlockSpec((3, 2, ny // steps, part, 2 * HD), lambda i: (0, 0, i, 0, 0))],
+        out_specs=pl.BlockSpec((4, ny // steps, part, 3 * HD), lambda i: (0, i, 0, 0)),
         out_shape=jax.ShapeDtypeStruct((4, ny, part, 3 * HD), w.dtype),
         compiler_params=LIMIT,
         cost_estimate=pl.CostEstimate(flops=0, bytes_accessed=4 * w.size, transcendentals=0),
-    )(w.reshape(3, 2, ny * part, 2 * HD))
+    )(w.reshape(3, 2, ny, part, 2 * HD))
 
 
 def near_kernel(c_ref, x_ref, w_ref, out_ref):
@@ -246,22 +246,16 @@
     return sorted(range(1, count), key=lambda s: -min(s, count - s))
 
 
-def scatter_by_shifts(blocks, axis, source):
+def take_shifts(result, blocks, axis, source):
+    behind = (lax.axis_index(axis) - source) % lax.axis_size(axis)
+    for s, block in blocks.items():
+        result = jnp.where(behind == s, shift(block, axis, s), result)
+    return result
+
+
+def ahead(blocks, axis):
     here, count = lax.axis_index(axis), blocks.shape[0]
-    result = pick(blocks, here)
-    for s in distances(axis):
-        got = shift(pick(blocks, (here + s) % count), axis, s)
-        result = jnp.where((here - source) % count == s, got, result)
-    return result
-
-
-def scatter_along_y(blocks, y0):
-    yh = lax.axis_index("yh")
-    blocks = blocks.reshape((2, 4) + blocks.shape[1:])
-    got = lax.ppermute(pick(blocks, 1 - yh), ("yh", "yl"), [(i, 7 - i) for i in range(8)])
-    home = yh == y0 // 4
-    blocks = jnp.where(home, pick(blocks, yh), got)
-    return scatter_by_shifts(blocks, "yl", jnp.where(home, y0 % 4, 3 - y0 % 4))
+    return {s: pick(blocks, (here + s) % count) for s in distances(axis)}
 
 
 def gather_by_shifts(block, axis):
@@ -317,11 +311,17 @@
     part = width // (2 * ny)
     w = fold(snap_qkv[0], ny)
     w = pick(exchange(w, "x"), x0)
-    wo = scatter_along_y(snap_out[0].reshape(ny, -1, snap_out.shape[2]), y0)
-    w, wo, normed, kpos, start, start_other = lax.optimization_barrier((w, wo, normed, kpos, start, start_other))
+    wo = snap_out[0].reshape(ny, -1, snap_out.shape[2])
+    blocks = ahead(wo, ys)
+    after = {s: blocks.pop(s) for s in (1, ny - 1)}
+    wo = take_shifts(pick(wo, y), blocks, ys, y0)
+    w, wo, after, normed, kpos, start, start_other = lax.optimization_barrier(
+        (w, wo, after, normed, kpos, start, start_other)
+    )
     w = pick(exchange(w, ys), y0)
+    wo = take_shifts(wo, after, ys, y0)
     wo = jnp.transpose(wo.reshape(wo.shape[0], nx, -1), (1, 0, 2))
-    wo = scatter_by_shifts(wo, "x", x0)
+    wo = take_shifts(pick(wo, x), ahead(wo, "x"), "x", x0)
     wo = jnp.transpose(wo.reshape(wo.shape[0], nx, HD), (1, 0, 2)).reshape(part, HD)
     w = jnp.concatenate([w, wo], axis=1)
     w, normed = lax.optimization_barrier((w, normed))

time: 237 us -> 234 us (0.987)
  starting transfers between devices: 93.5 us -> 110 us
  waiting for transfers between devices: 92.9 us -> 77.8 us
  Pallas kernels: 19.1 us -> 15 us
    ppermute x1 -> x0, waiting for transfers between devices: 19.2 us -> none  [scatter_along_y(): lax.ppermute(pick(blocks, 1 - yh), ('yh', 'yl'), [(i, 7 - i) for i in ran...]
    ppermute x12 -> x16, starting transfers between devices: 38.4 us -> 52 us  [shift(): lax.ppermute(block, axis, [(i, (i + distance) % count) for i in range(cou...]
    ppermute x12 -> x16, waiting for transfers between devices: 19.9 us -> 29.8 us  [shift(): lax.ppermute(block, axis, [(i, (i + distance) % count) for i in range(cou...]
    all_to_all x5, waiting for transfers between devices: 47 us -> 38.7 us  [exchange(): return lax.all_to_all(block, axis, 0, 0, tiled=True)]
    all_to_all x5, starting transfers between devices: 20.8 us -> 27.6 us  [exchange(): return lax.all_to_all(block, axis, 0, 0, tiled=True)]
    ppermute x1 -> x0, starting transfers between devices: 5.09 us -> none  [scatter_along_y(): lax.ppermute(pick(blocks, 1 - yh), ('yh', 'yl'), [(i, 7 - i) for i in ran...]
    pallas_call x1, Pallas kernels: 6.27 us -> 2.16 us  [fold(): pl.pallas_call(fold_kernel, grid=(steps,), in_specs=[pl.BlockSpec((3, 2,...]
    ppermute x2, starting transfers between devices: 14.1 us -> 17.6 us  [trade(): return lax.ppermute(block, ('zh', 'x', 'zl', 'c'), route)]
  transfers between devices with their start and end apart: 25 -> 28, of which waited for: 16 -> 16; matrix products, arithmetic and copies ran while one was open for 4% -> 3% of each run, Pallas kernels for 5% -> 5%
where the time goes in v9:
time: 234 us; the launch traced here: 232 us
  starting transfers between devices  110 us (47%)
  waiting for transfers between devices  77.8 us (33%)
  Pallas kernels  15 us (6%)
  blocking collectives  14.4 us (6%)
  local copies, waits for them, and re-layouts  8.82 us (4%)
  other arithmetic  5.4 us (2%)
    ppermute x16, starting transfers between devices, shift(): lax.ppermute(block, axis, [(i, (i + distance) % count) for i in range(cou...  52 us
    all_to_all x5, waiting for transfers between devices, exchange(): return lax.all_to_all(block, axis, 0, 0, tiled=True)  38.7 us
    ppermute x16, waiting for transfers between devices, shift(): lax.ppermute(block, axis, [(i, (i + distance) % count) for i in range(cou...  29.8 us
    all_to_all x5, starting transfers between devices, exchange(): return lax.all_to_all(block, axis, 0, 0, tiled=True)  27.6 us
    ppermute x2, starting transfers between devices, trade(): return lax.ppermute(block, ('zh', 'x', 'zl', 'c'), route)  17.6 us
    all_to_all x1, blocking collectives, exchange(): return lax.all_to_all(block, axis, 0, 0, tiled=True)  14.4 us
    pallas_call x2, Pallas kernels, attend(): pl.pallas_call(attend_kernel, grid=(nq // tile,), in_specs=[pl.BlockSpec(...  8.76 us
    ppermute x3, starting transfers between devices, swap(): return lax.ppermute(block, axis, [(0, 1), (1, 0)])  6.7 us
  transfers between devices with their start and end apart: 28, of which 16 were waited for; matrix products, arithmetic and copies ran while one was open for 3% of the time, Pallas kernels for 5%

profile of v9, /device:TPU:1, one launch (start us, length us, event | category | flops | bytes accessed | tf_op | source)
XLA Modules:
  0.0 232.5 jit_solution(10986326107867353886)
XLA Ops:
  0.0 1.9 copy-done
  1.9 2.2 shard_map.64
  4.0 4.8 %all-to-all-start = ((bf16[4,8,128,384]{3,2,1,0:T(8,128)(2,1)}), bf16[4,8,128,384]{3,2,1,0:T(8,128)(2,1)S(1)}, u32[]{:S(2)}, u32[]{:S(2)}) async-start(bf16[4,8,128,384]{3,2,1,0:T(8,128)(2,1)} %shard_map.64), calls=%async_computation | async-start | bytes 6291456 | tf_op jit(solution)/shard_map/all_to_all | solution.py:227
  8.9 2.2 dynamic-slice_bitcast_fusion.1
  11.1 5.9 %collective-permute-start = (bf16[32,2048]{1,0:T(8,128)(2,1)}, bf16[32,2048]{1,0:T(8,128)(2,1)}, u32[]{:S(2)}, u32[]{:S(2)}) collective-permute-start(bf16[32,2048]{1,0:T(8,128)(2,1)} %get-tuple-element.55), channel_id=1, source_target_pairs={{0,192},{32,224},{64,0},{96,32},{128,64},{160,96},{192,128},{224,1... | collective-permute-start | bytes 393224 | tf_op jit(solution)/shard_map/ppermute | solution.py:241
  17.0 1.9 collective-permute-start.1
  18.9 5.0 %collective-permute-start.2 = (bf16[32,2048]{1,0:T(8,128)(2,1)}, bf16[32,2048]{1,0:T(8,128)(2,1)}, u32[]{:S(2)}, u32[]{:S(2)}) collective-permute-start(bf16[32,2048]{1,0:T(8,128)(2,1)} %get-tuple-element.53), channel_id=1, source_target_pairs={{0,160},{32,192},{64,224},{96,0},{128,32},{160,64},{192,96},{224,1... | collective-permute-start | bytes 393224 | tf_op jit(solution)/shard_map/ppermute | solution.py:241
  24.0 2.0 collective-permute-start.3
  26.0 5.8 %collective-permute-start.4 = (bf16[32,2048]{1,0:T(8,128)(2,1)}, bf16[32,2048]{1,0:T(8,128)(2,1)}, u32[]{:S(2)}, u32[]{:S(2)}) collective-permute-start(bf16[32,2048]{1,0:T(8,128)(2,1)} %get-tuple-element.51), channel_id=1, source_target_pairs={{0,128},{32,160},{64,192},{96,224},{128,0},{160,32},{192,64},{224,... | collective-permute-start | bytes 393224 | tf_op jit(solution)/shard_map/ppermute | solution.py:241
  35.3 2.3 collective-permute-done.3
  37.6 1.7 collective-permute-done.4
  39.3 1.7 fusion.6
  42.0 11.5 %all-to-all-start.1 = ((bf16[8,128,384]{2,1,0:T(8,128)(2,1)}), bf16[8,128,384]{2,1,0:T(8,128)(2,1)S(1)}, u32[]{:S(2)}, u32[]{:S(2)}) async-start(bf16[8,128,384]{2,1,0:T(8,128)(2,1)} %dynamic-slice_bitcast_fusion), calls=%async_computation.1 | async-start | bytes 1572864 | tf_op jit(solution)/shard_map/all_to_all | solution.py:227
  53.5 4.6 %collective-permute-start.5 = (bf16[32,2048]{1,0:T(8,128)(2,1)S(1)}, bf16[32,2048]{1,0:T(8,128)(2,1)S(1)}, u32[]{:S(2)}, u32[]{:S(2)}) collective-permute-start(bf16[32,2048]{1,0:T(8,128)(2,1)S(1)} %copy-done.5), channel_id=1, source_target_pairs={{0,224},{32,0},{64,32},{96,64},{128,96},{160,128},{192,160},{224,1... | collective-permute-start | bytes 393224 | tf_op jit(solution)/shard_map/ppermute | solution.py:241
  58.1 1.9 collective-permute-start.6
  60.1 13.4 %collective-permute-done.5 = bf16[32,2048]{1,0:T(8,128)(2,1)S(1)} collective-permute-done((bf16[32,2048]{1,0:T(8,128)(2,1)S(1)}, bf16[32,2048]{1,0:T(8,128)(2,1)S(1)}, u32[]{:S(2)}, u32[]{:S(2)}) %collective-permute-start.5) | collective-permute-done | bytes 131104 | tf_op jit(solution)/shard_map/ppermute | solution.py:241
  74.2 2.8 %collective-permute-start.7 = (bf16[32,512]{1,0:T(8,128)(2,1)S(1)}, bf16[32,512]{1,0:T(8,128)(2,1)S(1)}, u32[]{:S(2)}, u32[]{:S(2)}) collective-permute-start(bf16[32,512]{1,0:T(8,128)(2,1)S(1)} %bitcast.110), channel_id=1, source_target_pairs={{0,24},{8,0},{16,8},{24,16},{1,25},{9,1},{17,9},{25,17},{2,26},{10... | collective-permute-start | bytes 98312 | tf_op jit(solution)/shard_map/ppermute | solution.py:241
  77.0 2.5 %collective-permute-start.8 = (bf16[32,512]{1,0:T(8,128)(2,1)S(1)}, bf16[32,512]{1,0:T(8,128)(2,1)S(1)}, u32[]{:S(2)}, u32[]{:S(2)}) collective-permute-start(bf16[32,512]{1,0:T(8,128)(2,1)S(1)} %bitcast.111), channel_id=1, source_target_pairs={{0,8},{8,16},{16,24},{24,0},{1,9},{9,17},{17,25},{25,1},{2,10},{10... | collective-permute-start | bytes 98312 | tf_op jit(solution)/shard_map/ppermute | solution.py:241
  79.5 2.5 %collective-permute-start.9 = (bf16[32,512]{1,0:T(8,128)(2,1)S(1)}, bf16[32,512]{1,0:T(8,128)(2,1)S(1)}, u32[]{:S(2)}, u32[]{:S(2)}) collective-permute-start(bf16[32,512]{1,0:T(8,128)(2,1)S(1)} %bitcast.112), channel_id=1, source_target_pairs={{0,16},{8,24},{16,0},{24,8},{1,17},{9,25},{17,1},{25,9},{2,18},{10... | collective-permute-start | bytes 98312 | tf_op jit(solution)/shard_map/ppermute | solution.py:241
  82.9 3.1 %collective-permute-done.9 = bf16[32,512]{1,0:T(8,128)(2,1)S(1)} collective-permute-done((bf16[32,512]{1,0:T(8,128)(2,1)S(1)}, bf16[32,512]{1,0:T(8,128)(2,1)S(1)}, u32[]{:S(2)}, u32[]{:S(2)}) %collective-permute-start.9) | collective-permute-done | bytes 32800 | tf_op jit(solution)/shard_map/ppermute | solution.py:241
  86.1 15.7 %collective-permute-start.14 = (bf16[128,512]{1,0:T(8,128)(2,1)S(1)}, bf16[128,512]{1,0:T(8,128)(2,1)S(1)}, u32[]{:S(2)}, u32[]{:S(2)}) collective-permute-start(bf16[128,512]{1,0:T(8,128)(2,1)S(1)} %pad_maximum_fusion.4), channel_id=1, source_target_pairs={{0,262},{1,270},{2,260},{3,268},{4,258},{5,266},{6,256},{7,264},{8... | collective-permute-start | bytes 393224 | tf_op jit(solution)/shard_map/ppermute | solution.py:281
  101.8 1.9 collective-permute-start.13
  103.8 3.5 %collective-permute-done.14 = bf16[128,512]{1,0:T(8,128)(2,1)S(1)} collective-permute-done((bf16[128,512]{1,0:T(8,128)(2,1)S(1)}, bf16[128,512]{1,0:T(8,128)(2,1)S(1)}, u32[]{:S(2)}, u32[]{:S(2)}) %collective-permute-start.14) | collective-permute-done | bytes 131104 | tf_op jit(solution)/shard_map/ppermute | solution.py:281
  109.2 4.4 %all-to-all-start.2 = ((bf16[8,128,512]{2,1,0:T(8,128)(2,1)}), bf16[8,128,512]{2,1,0:T(8,128)(2,1)S(1)}, u32[]{:S(2)}, u32[]{:S(2)}) async-start(bf16[8,128,512]{2,1,0:T(8,128)(2,1)} %broadcast_in_dim.2), calls=%async_computation.2 | async-start | bytes 2097152 | tf_op jit(solution)/shard_map/all_to_all | solution.py:227
  113.6 1.9 collective-permute-start.12
  115.6 4.9 %collective-permute-start.11 = (bf16[80,2048]{1,0:T(8,128)(2,1)S(1)}, bf16[80,2048]{1,0:T(8,128)(2,1)S(1)}, u32[]{:S(2)}, u32[]{:S(2)}) collective-permute-start(bf16[80,2048]{1,0:T(8,128)(2,1)S(1)} %fusion.2), channel_id=1, source_target_pairs={{0,16},{8,24},{16,0},{24,8},{1,17},{9,25},{17,1},{25,9},{2,18},{10... | collective-permute-start | bytes 983048 | tf_op jit(solution)/shard_map/ppermute | solution.py:241
  120.5 2.8 %collective-permute-start.10 = (bf16[80,2048]{1,0:T(8,128)(2,1)S(1)}, bf16[80,2048]{1,0:T(8,128)(2,1)S(1)}, u32[]{:S(2)}, u32[]{:S(2)}) collective-permute-start(bf16[80,2048]{1,0:T(8,128)(2,1)S(1)} %fusion.2), channel_id=1, source_target_pairs={{0,8},{8,16},{16,24},{24,0},{1,9},{9,17},{17,25},{25,1},{2,10},{10... | collective-permute-start | bytes 983048 | tf_op jit(solution)/shard_map/ppermute | solution.py:241
  123.2 19.6 %all-to-all-done.2 = bf16[8,128,512]{2,1,0:T(8,128)(2,1)S(1)} async-done(((bf16[8,128,512]{2,1,0:T(8,128)(2,1)}), bf16[8,128,512]{2,1,0:T(8,128)(2,1)S(1)}, u32[]{:S(2)}, u32[]{:S(2)}) %all-to-all-start.2) | async-done | bytes 1048608 | tf_op jit(solution)/shard_map/all_to_all | solution.py:227
  142.9 2.4 %collective-permute-start.15 = (bf16[1024,512]{1,0:T(8,128)(2,1)S(1)}, bf16[1024,512]{1,0:T(8,128)(2,1)S(1)}, u32[]{:S(2)}, u32[]{:S(2)}) collective-permute-start(bf16[1024,512]{1,0:T(8,128)(2,1)S(1)} %bitcast.83), channel_id=1, source_target_pairs={{0,1},{1,0},{2,3},{3,2},{4,5},{5,4},{6,7},{7,6},{8,9},{9,8},{10,11... | collective-permute-start | bytes 3145736 | tf_op jit(solution)/shard_map/ppermute | solution.py:223
  147.5 1.6 shard_map.66
  149.2 3.6 %all-to-all-start.3 = ((bf16[8,320,256]{2,1,0:T(8,128)(2,1)}), bf16[8,320,256]{2,1,0:T(8,128)(2,1)S(1)}, u32[]{:S(2)}, u32[]{:S(2)}) async-start(bf16[8,320,256]{2,1,0:T(8,128)(2,1)} %get-tuple-element.34), calls=%async_computation.3 | async-start | bytes 2621440 | tf_op jit(solution)/shard_map/all_to_all | solution.py:227
  152.8 1.9 collective-permute-start.19
  154.7 2.8 %collective-permute-start.18 = (bf16[256,512]{1,0:T(8,128)(2,1)S(1)}, bf16[256,512]{1,0:T(8,128)(2,1)S(1)}, u32[]{:S(2)}, u32[]{:S(2)}) collective-permute-start(bf16[256,512]{1,0:T(8,128)(2,1)S(1)} %bitcast.99), channel_id=1, source_target_pairs={{0,16},{8,24},{16,0},{24,8},{1,17},{9,25},{17,1},{25,9},{2,18},{10... | collective-permute-start | bytes 786440 | tf_op jit(solution)/shard_map/ppermute | solution.py:241
  157.5 2.8 %collective-permute-start.17 = (bf16[256,512]{1,0:T(8,128)(2,1)S(1)}, bf16[256,512]{1,0:T(8,128)(2,1)S(1)}, u32[]{:S(2)}, u32[]{:S(2)}) collective-permute-start(bf16[256,512]{1,0:T(8,128)(2,1)S(1)} %bitcast.100), channel_id=1, source_target_pairs={{0,8},{8,16},{16,24},{24,0},{1,9},{9,17},{17,25},{25,1},{2,10},{10... | collective-permute-start | bytes 786440 | tf_op jit(solution)/shard_map/ppermute | solution.py:241
  160.2 3.5 %collective-permute-start.16 = (bf16[320,128]{1,0:T(8,128)(2,1)S(1)}, bf16[320,128]{1,0:T(8,128)(2,1)S(1)}, u32[]{:S(2)}, u32[]{:S(2)}) collective-permute-start(bf16[320,128]{1,0:T(8,128)(2,1)S(1)} %get-tuple-element.33.q_ref), channel_id=1, source_target_pairs={{0,262},{2,260},{4,258},{6,256},{256,6},{258,4},{260,2},{262,0},{1... | collective-permute-start | bytes 245768 | tf_op jit(solution)/shard_map/ppermute | solution.py:285
  163.7 1.9 collective-permute-done.18
  165.6 6.3 %collective-permute-done.17 = bf16[256,512]{1,0:T(8,128)(2,1)S(1)} collective-permute-done((bf16[256,512]{1,0:T(8,128)(2,1)S(1)}, bf16[256,512]{1,0:T(8,128)(2,1)S(1)}, u32[]{:S(2)}, u32[]{:S(2)}) %collective-permute-start.17) | collective-permute-done | bytes 262176 | tf_op jit(solution)/shard_map/ppermute | solution.py:241
  172.9 14.6 %all-to-all-done.3 = bf16[8,320,256]{2,1,0:T(8,128)(2,1)S(1)} async-done(((bf16[8,320,256]{2,1,0:T(8,128)(2,1)}), bf16[8,320,256]{2,1,0:T(8,128)(2,1)S(1)}, u32[]{:S(2)}, u32[]{:S(2)}) %all-to-all-start.3) | async-done | bytes 1310752 | tf_op jit(solution)/shard_map/all_to_all | solution.py:227
  187.5 2.4 %collective-permute-start.20 = (bf16[2560,256]{1,0:T(8,128)(2,1)S(1)}, bf16[2560,256]{1,0:T(8,128)(2,1)S(1)}, u32[]{:S(2)}, u32[]{:S(2)}) collective-permute-start(bf16[2560,256]{1,0:T(8,128)(2,1)S(1)} %bitcast.87), channel_id=1, source_target_pairs={{0,1},{1,0},{2,3},{3,2},{4,5},{5,4},{6,7},{7,6},{8,9},{9,8},{10,11... | collective-permute-start | bytes 3932168 | tf_op jit(solution)/shard_map/ppermute | solution.py:223
  189.9 1.9 collective-permute-start.22
  193.4 4.4 %shard_map.68 = bf16[4,96,128]{2,1,0:T(8,128)(2,1)S(1)} custom-call(s32[4]{0:T(128)S(1)} %get-tuple-element.38.start_ref, bf16[320,128]{1,0:T(8,128)(2,1)S(1)} %copy-done.2, bf16[2560,256]{1,0:T(8,128)(2,1)S(1)} %bitcast.88, bf16[2560,256]{1,0:T(8,128)(2,1)S(1)} %collective-permute-done.20.far_ref, s32[1,5120]{1,0:T(1,128)S(1)} %bitcast.90), custom_call_target="tpu_custom_call" | custom-call | flops 838860800 | bytes 2621440 | tf_op jit(solution)/shard_map/pallas_call | solution.py:143
  197.8 2.1 collective-permute-start.21
  199.9 4.4 %shard_map.67.near_ref = bf16[4,96,128]{2,1,0:T(8,128)(2,1)S(1)} custom-call(s32[4]{0:T(128)S(1)} %get-tuple-element.23.start_ref, bf16[320,128]{1,0:T(8,128)(2,1)S(1)} %get-tuple-element.33.q_ref, bf16[2560,256]{1,0:T(8,128)(2,1)S(1)} %bitcast.89, bf16[2560,256]{1,0:T(8,128)(2,1)S(1)} %collective-permute-done.20.far_ref, s32[1,5120]{1,0:T(1,128)S(1)} %bitcast.91), custom_call_target="tpu_custom_call" | custom-call | flops 838860800 | bytes 2621440 | tf_op jit(solution)/shard_map/pallas_call | solution.py:143
  204.3 3.3 %collective-permute-done.21.far_ref = bf16[4,96,128]{2,1,0:T(8,128)(2,1)S(1)} collective-permute-done((bf16[4,96,128]{2,1,0:T(8,128)(2,1)S(1)}, bf16[4,96,128]{2,1,0:T(8,128)(2,1)S(1)}, u32[]{:S(2)}, u32[]{:S(2)}) %collective-permute-start.21) | collective-permute-done | bytes 98336 | tf_op jit(solution)/shard_map/ppermute | solution.py:285
  207.6 1.5 shard_map.69
  209.1 3.3 %all-to-all-start.4 = ((bf16[4,80,128]{2,1,0:T(8,128)(2,1)}), bf16[4,80,128]{2,1,0:T(8,128)(2,1)S(1)}, u32[]{:S(2)}, u32[]{:S(2)}) async-start(bf16[4,80,128]{2,1,0:T(8,128)(2,1)} %shard_map.69), calls=%async_computation.4 | async-start | bytes 163840 | tf_op jit(solution)/shard_map/all_to_all | solution.py:227
  212.4 4.5 %all-to-all-done.4.context_ref = bf16[4,80,128]{2,1,0:T(8,128)(2,1)S(1)} async-done(((bf16[4,80,128]{2,1,0:T(8,128)(2,1)}), bf16[4,80,128]{2,1,0:T(8,128)(2,1)S(1)}, u32[]{:S(2)}, u32[]{:S(2)}) %all-to-all-start.4) | async-done | bytes 81952 | tf_op jit(solution)/shard_map/all_to_all | solution.py:227
  217.4 14.4 %all_to_all.30 = bf16[8,80,256]{2,1,0:T(8,128)(2,1)S(1)} all-to-all(bf16[8,80,256]{2,1,0:T(8,128)(2,1)S(1)} %shard_map.70), channel_id=1, replica_groups=mesh['zh'=2,'yh'=2,'yl'=4,'x'=4,'zl'=4,'c'=2] {'zl','c'}, dimensions={0} | all-to-all | bytes 655360 | tf_op jit(solution)/shard_map/all_to_all | solution.py:227
  (69 shorter events, 13.0 us)
Async XLA Ops:
  0.0 1.9 copy-start
  4.0 37.0 %all-to-all-start = ((bf16[4,8,128,384]{3,2,1,0:T(8,128)(2,1)}), bf16[4,8,128,384]{3,2,1,0:T(8,128)(2,1)S(1)}, u32[]{:S(2)}, u32[]{:S(2)}) async-start(bf16[4,8,128,384]{3,2,1,0:T(8,128)(2,1)} %shard_map.64), calls=%async_computation | async-start | bytes 6291456 | tf_op jit(solution)/shard_map/all_to_all | solution.py:227
  8.9 23.0 %copy-start.7 = (s32[64]{0:T(128)S(1)}, s32[64]{0:T(128)}, u32[]{:S(2)}) copy-start(s32[64]{0:T(128)} %param.11) | copy-start | bytes 772
  8.9 24.3 %copy-start.6 = (f32[2048]{0:T(1024)S(1)}, f32[2048]{0:T(1024)}, u32[]{:S(2)}) copy-start(f32[2048]{0:T(1024)} %param.7) | copy-start | bytes 24580
  11.1 24.2 %collective-permute-start = (bf16[32,2048]{1,0:T(8,128)(2,1)}, bf16[32,2048]{1,0:T(8,128)(2,1)}, u32[]{:S(2)}, u32[]{:S(2)}) collective-permute-start(bf16[32,2048]{1,0:T(8,128)(2,1)} %get-tuple-element.55), channel_id=1, source_target_pairs={{0,192},{32,224},{64,0},{96,32},{128,64},{160,96},{192,128},{224,1... | collective-permute-start | bytes 393224 | tf_op jit(solution)/shard_map/ppermute | solution.py:241
  17.0 18.3 %collective-permute-start.1 = (bf16[32,2048]{1,0:T(8,128)(2,1)}, bf16[32,2048]{1,0:T(8,128)(2,1)}, u32[]{:S(2)}, u32[]{:S(2)}) collective-permute-start(bf16[32,2048]{1,0:T(8,128)(2,1)} %get-tuple-element.54), channel_id=1, source_target_pairs={{0,64},{32,96},{64,128},{96,160},{128,192},{160,224},{192,0},{224,... | collective-permute-start | bytes 393224 | tf_op jit(solution)/shard_map/ppermute | solution.py:241
  18.9 16.4 %collective-permute-start.2 = (bf16[32,2048]{1,0:T(8,128)(2,1)}, bf16[32,2048]{1,0:T(8,128)(2,1)}, u32[]{:S(2)}, u32[]{:S(2)}) collective-permute-start(bf16[32,2048]{1,0:T(8,128)(2,1)} %get-tuple-element.53), channel_id=1, source_target_pairs={{0,160},{32,192},{64,224},{96,0},{128,32},{160,64},{192,96},{224,1... | collective-permute-start | bytes 393224 | tf_op jit(solution)/shard_map/ppermute | solution.py:241
  24.0 13.6 %collective-permute-start.3 = (bf16[32,2048]{1,0:T(8,128)(2,1)}, bf16[32,2048]{1,0:T(8,128)(2,1)}, u32[]{:S(2)}, u32[]{:S(2)}) collective-permute-start(bf16[32,2048]{1,0:T(8,128)(2,1)} %get-tuple-element.52), channel_id=1, source_target_pairs={{0,96},{32,128},{64,160},{96,192},{128,224},{160,0},{192,32},{224,... | collective-permute-start | bytes 393224 | tf_op jit(solution)/shard_map/ppermute | solution.py:241
  26.0 13.3 %collective-permute-start.4 = (bf16[32,2048]{1,0:T(8,128)(2,1)}, bf16[32,2048]{1,0:T(8,128)(2,1)}, u32[]{:S(2)}, u32[]{:S(2)}) collective-permute-start(bf16[32,2048]{1,0:T(8,128)(2,1)} %get-tuple-element.51), channel_id=1, source_target_pairs={{0,128},{32,160},{64,192},{96,224},{128,0},{160,32},{192,64},{224,... | collective-permute-start | bytes 393224 | tf_op jit(solution)/shard_map/ppermute | solution.py:241
  42.0 11.5 %copy-start.5 = (bf16[32,2048]{1,0:T(8,128)(2,1)S(1)}, bf16[32,2048]{1,0:T(8,128)(2,1)}, u32[]{:S(2)}) copy-start(bf16[32,2048]{1,0:T(8,128)(2,1)} %get-tuple-element.25) | copy-start | bytes 393220
  42.0 16.1 %copy-start.4 = (bf16[32,2048]{1,0:T(8,128)(2,1)S(1)}, bf16[32,2048]{1,0:T(8,128)(2,1)}, u32[]{:S(2)}) copy-start(bf16[32,2048]{1,0:T(8,128)(2,1)} %get-tuple-element.26) | copy-start | bytes 393220
  42.0 31.8 %copy-start.3 = (bf16[32,2048]{1,0:T(8,128)(2,1)S(1)}, bf16[32,2048]{1,0:T(8,128)(2,1)}, u32[]{:S(2)}) copy-start(bf16[32,2048]{1,0:T(8,128)(2,1)} %fusion.6) | copy-start | bytes 393220
  42.0 44.1 %all-to-all-start.1 = ((bf16[8,128,384]{2,1,0:T(8,128)(2,1)}), bf16[8,128,384]{2,1,0:T(8,128)(2,1)S(1)}, u32[]{:S(2)}, u32[]{:S(2)}) async-start(bf16[8,128,384]{2,1,0:T(8,128)(2,1)} %dynamic-slice_bitcast_fusion), calls=%async_computation.1 | async-start | bytes 1572864 | tf_op jit(solution)/shard_map/all_to_all | solution.py:227
  53.5 20.0 %collective-permute-start.5 = (bf16[32,2048]{1,0:T(8,128)(2,1)S(1)}, bf16[32,2048]{1,0:T(8,128)(2,1)S(1)}, u32[]{:S(2)}, u32[]{:S(2)}) collective-permute-start(bf16[32,2048]{1,0:T(8,128)(2,1)S(1)} %copy-done.5), channel_id=1, source_target_pairs={{0,224},{32,0},{64,32},{96,64},{128,96},{160,128},{192,160},{224,1... | collective-permute-start | bytes 393224 | tf_op jit(solution)/shard_map/ppermute | solution.py:241
  58.1 15.7 %collective-permute-start.6 = (bf16[32,2048]{1,0:T(8,128)(2,1)S(1)}, bf16[32,2048]{1,0:T(8,128)(2,1)S(1)}, u32[]{:S(2)}, u32[]{:S(2)}) collective-permute-start(bf16[32,2048]{1,0:T(8,128)(2,1)S(1)} %copy-done.4), channel_id=1, source_target_pairs={{0,32},{32,64},{64,96},{96,128},{128,160},{160,192},{192,224},{224... | collective-permute-start | bytes 393224 | tf_op jit(solution)/shard_map/ppermute | solution.py:241
  74.2 7.9 %collective-permute-start.7 = (bf16[32,512]{1,0:T(8,128)(2,1)S(1)}, bf16[32,512]{1,0:T(8,128)(2,1)S(1)}, u32[]{:S(2)}, u32[]{:S(2)}) collective-permute-start(bf16[32,512]{1,0:T(8,128)(2,1)S(1)} %bitcast.110), channel_id=1, source_target_pairs={{0,24},{8,0},{16,8},{24,16},{1,25},{9,1},{17,9},{25,17},{2,26},{10... | collective-permute-start | bytes 98312 | tf_op jit(solution)/shard_map/ppermute | solution.py:241
  77.0 5.9 %collective-permute-start.8 = (bf16[32,512]{1,0:T(8,128)(2,1)S(1)}, bf16[32,512]{1,0:T(8,128)(2,1)S(1)}, u32[]{:S(2)}, u32[]{:S(2)}) collective-permute-start(bf16[32,512]{1,0:T(8,128)(2,1)S(1)} %bitcast.111), channel_id=1, source_target_pairs={{0,8},{8,16},{16,24},{24,0},{1,9},{9,17},{17,25},{25,1},{2,10},{10... | collective-permute-start | bytes 98312 | tf_op jit(solution)/shard_map/ppermute | solution.py:241
  79.5 6.5 %collective-permute-start.9 = (bf16[32,512]{1,0:T(8,128)(2,1)S(1)}, bf16[32,512]{1,0:T(8,128)(2,1)S(1)}, u32[]{:S(2)}, u32[]{:S(2)}) collective-permute-start(bf16[32,512]{1,0:T(8,128)(2,1)S(1)} %bitcast.112), channel_id=1, source_target_pairs={{0,16},{8,24},{16,0},{24,8},{1,17},{9,25},{17,1},{25,9},{2,18},{10... | collective-permute-start | bytes 98312 | tf_op jit(solution)/shard_map/ppermute | solution.py:241
  86.1 21.2 %collective-permute-start.14 = (bf16[128,512]{1,0:T(8,128)(2,1)S(1)}, bf16[128,512]{1,0:T(8,128)(2,1)S(1)}, u32[]{:S(2)}, u32[]{:S(2)}) collective-permute-start(bf16[128,512]{1,0:T(8,128)(2,1)S(1)} %pad_maximum_fusion.4), channel_id=1, source_target_pairs={{0,262},{1,270},{2,260},{3,268},{4,258},{5,266},{6,256},{7,264},{8... | collective-permute-start | bytes 393224 | tf_op jit(solution)/shard_map/ppermute | solution.py:281
  101.8 6.3 %collective-permute-start.13 = (bf16[128,512]{1,0:T(8,128)(2,1)S(1)}, bf16[128,512]{1,0:T(8,128)(2,1)S(1)}, u32[]{:S(2)}, u32[]{:S(2)}) collective-permute-start(bf16[128,512]{1,0:T(8,128)(2,1)S(1)} %pad_maximum_fusion.4), channel_id=1, source_target_pairs={{1,8},{3,10},{5,12},{7,14},{8,1},{10,3},{12,5},{14,7},{17,24},{19,... | collective-permute-start | bytes 393224 | tf_op jit(solution)/shard_map/ppermute | solution.py:281
  109.2 33.6 %all-to-all-start.2 = ((bf16[8,128,512]{2,1,0:T(8,128)(2,1)}), bf16[8,128,512]{2,1,0:T(8,128)(2,1)S(1)}, u32[]{:S(2)}, u32[]{:S(2)}) async-start(bf16[8,128,512]{2,1,0:T(8,128)(2,1)} %broadcast_in_dim.2), calls=%async_computation.2 | async-start | bytes 2097152 | tf_op jit(solution)/shard_map/all_to_all | solution.py:227
  113.6 31.7 %collective-permute-start.12 = (bf16[80,2048]{1,0:T(8,128)(2,1)S(1)}, bf16[80,2048]{1,0:T(8,128)(2,1)S(1)}, u32[]{:S(2)}, u32[]{:S(2)}) collective-permute-start(bf16[80,2048]{1,0:T(8,128)(2,1)S(1)} %fusion.2), channel_id=1, source_target_pairs={{0,24},{8,0},{16,8},{24,16},{1,25},{9,1},{17,9},{25,17},{2,26},{10... | collective-permute-start | bytes 983048 | tf_op jit(solution)/shard_map/ppermute | solution.py:241
  115.6 29.8 %collective-permute-start.11 = (bf16[80,2048]{1,0:T(8,128)(2,1)S(1)}, bf16[80,2048]{1,0:T(8,128)(2,1)S(1)}, u32[]{:S(2)}, u32[]{:S(2)}) collective-permute-start(bf16[80,2048]{1,0:T(8,128)(2,1)S(1)} %fusion.2), channel_id=1, source_target_pairs={{0,16},{8,24},{16,0},{24,8},{1,17},{9,25},{17,1},{25,9},{2,18},{10... | collective-permute-start | bytes 983048 | tf_op jit(solution)/shard_map/ppermute | solution.py:241
  120.5 24.9 %collective-permute-start.10 = (bf16[80,2048]{1,0:T(8,128)(2,1)S(1)}, bf16[80,2048]{1,0:T(8,128)(2,1)S(1)}, u32[]{:S(2)}, u32[]{:S(2)}) collective-permute-start(bf16[80,2048]{1,0:T(8,128)(2,1)S(1)} %fusion.2), channel_id=1, source_target_pairs={{0,8},{8,16},{16,24},{24,0},{1,9},{9,17},{17,25},{25,1},{2,10},{10... | collective-permute-start | bytes 983048 | tf_op jit(solution)/shard_map/ppermute | solution.py:241
  142.9 4.7 %collective-permute-start.15 = (bf16[1024,512]{1,0:T(8,128)(2,1)S(1)}, bf16[1024,512]{1,0:T(8,128)(2,1)S(1)}, u32[]{:S(2)}, u32[]{:S(2)}) collective-permute-start(bf16[1024,512]{1,0:T(8,128)(2,1)S(1)} %bitcast.83), channel_id=1, source_target_pairs={{0,1},{1,0},{2,3},{3,2},{4,5},{5,4},{6,7},{7,6},{8,9},{9,8},{10,11... | collective-permute-start | bytes 3145736 | tf_op jit(solution)/shard_map/ppermute | solution.py:223
  149.2 38.3 %all-to-all-start.3 = ((bf16[8,320,256]{2,1,0:T(8,128)(2,1)}), bf16[8,320,256]{2,1,0:T(8,128)(2,1)S(1)}, u32[]{:S(2)}, u32[]{:S(2)}) async-start(bf16[8,320,256]{2,1,0:T(8,128)(2,1)} %get-tuple-element.34), calls=%async_computation.3 | async-start | bytes 2621440 | tf_op jit(solution)/shard_map/all_to_all | solution.py:227
  152.8 11.0 %collective-permute-start.19 = (bf16[256,512]{1,0:T(8,128)(2,1)S(1)}, bf16[256,512]{1,0:T(8,128)(2,1)S(1)}, u32[]{:S(2)}, u32[]{:S(2)}) collective-permute-start(bf16[256,512]{1,0:T(8,128)(2,1)S(1)} %bitcast.98), channel_id=1, source_target_pairs={{0,24},{8,0},{16,8},{24,16},{1,25},{9,1},{17,9},{25,17},{2,26},{10... | collective-permute-start | bytes 786440 | tf_op jit(solution)/shard_map/ppermute | solution.py:241
  154.7 11.0 %collective-permute-start.18 = (bf16[256,512]{1,0:T(8,128)(2,1)S(1)}, bf16[256,512]{1,0:T(8,128)(2,1)S(1)}, u32[]{:S(2)}, u32[]{:S(2)}) collective-permute-start(bf16[256,512]{1,0:T(8,128)(2,1)S(1)} %bitcast.99), channel_id=1, source_target_pairs={{0,16},{8,24},{16,0},{24,8},{1,17},{9,25},{17,1},{25,9},{2,18},{10... | collective-permute-start | bytes 786440 | tf_op jit(solution)/shard_map/ppermute | solution.py:241
  157.5 14.5 %collective-permute-start.17 = (bf16[256,512]{1,0:T(8,128)(2,1)S(1)}, bf16[256,512]{1,0:T(8,128)(2,1)S(1)}, u32[]{:S(2)}, u32[]{:S(2)}) collective-permute-start(bf16[256,512]{1,0:T(8,128)(2,1)S(1)} %bitcast.100), channel_id=1, source_target_pairs={{0,8},{8,16},{16,24},{24,0},{1,9},{9,17},{17,25},{25,1},{2,10},{10... | collective-permute-start | bytes 786440 | tf_op jit(solution)/shard_map/ppermute | solution.py:241
  160.2 12.1 %collective-permute-start.16 = (bf16[320,128]{1,0:T(8,128)(2,1)S(1)}, bf16[320,128]{1,0:T(8,128)(2,1)S(1)}, u32[]{:S(2)}, u32[]{:S(2)}) collective-permute-start(bf16[320,128]{1,0:T(8,128)(2,1)S(1)} %get-tuple-element.33.q_ref), channel_id=1, source_target_pairs={{0,262},{2,260},{4,258},{6,256},{256,6},{258,4},{260,2},{262,0},{1... | collective-permute-start | bytes 245768 | tf_op jit(solution)/shard_map/ppermute | solution.py:285
  172.3 0.6 copy-start.1
  187.5 5.0 %collective-permute-start.20 = (bf16[2560,256]{1,0:T(8,128)(2,1)S(1)}, bf16[2560,256]{1,0:T(8,128)(2,1)S(1)}, u32[]{:S(2)}, u32[]{:S(2)}) collective-permute-start(bf16[2560,256]{1,0:T(8,128)(2,1)S(1)} %bitcast.87), channel_id=1, source_target_pairs={{0,1},{1,0},{2,3},{3,2},{4,5},{5,4},{6,7},{7,6},{8,9},{9,8},{10,11... | collective-permute-start | bytes 3932168 | tf_op jit(solution)/shard_map/ppermute | solution.py:223
  189.9 22.5 %collective-permute-start.22 = (bf16[4,256,512]{2,1,0:T(8,128)(2,1)S(1)}, bf16[4,256,512]{2,1,0:T(8,128)(2,1)S(1)}, u32[]{:S(2)}, u32[]{:S(2)}) collective-permute-start(bf16[4,256,512]{2,1,0:T(8,128)(2,1)S(1)} %pad_maximum_fusion.3.near_ref), channel_id=1, source_target_pairs={{0,1},{1,0},{2,3},{3,2},{4,5},{5,4},{6,7},{7,6},{8,9},{9,8},{10,11... | collective-permute-start | bytes 3145736 | tf_op jit(solution)/shard_map/ppermute | solution.py:223
  192.5 0.9 copy-start.2
  197.8 9.8 %collective-permute-start.21 = (bf16[4,96,128]{2,1,0:T(8,128)(2,1)S(1)}, bf16[4,96,128]{2,1,0:T(8,128)(2,1)S(1)}, u32[]{:S(2)}, u32[]{:S(2)}) collective-permute-start(bf16[4,96,128]{2,1,0:T(8,128)(2,1)S(1)} %shard_map.68), channel_id=1, source_target_pairs={{0,262},{2,260},{4,258},{6,256},{256,6},{258,4},{260,2},{262,0},{1... | collective-permute-start | bytes 294920 | tf_op jit(solution)/shard_map/ppermute | solution.py:285
  209.1 7.8 %all-to-all-start.4 = ((bf16[4,80,128]{2,1,0:T(8,128)(2,1)}), bf16[4,80,128]{2,1,0:T(8,128)(2,1)S(1)}, u32[]{:S(2)}, u32[]{:S(2)}) async-start(bf16[4,80,128]{2,1,0:T(8,128)(2,1)} %shard_map.69), calls=%async_computation.4 | async-start | bytes 163840 | tf_op jit(solution)/shard_map/all_to_all | solution.py:227

commit v10 on v9

--- a/solution.py
+++ b/solution.py
@@ -288,7 +288,8 @@
 def shards(hidden_in, norm_gain, snap_qkv, snap_out, owner_index, block_order):
     rows, width = hidden_in.shape
     ys = ("yh", "yl")
-    zh, y, x, c = (lax.axis_index(name) for name in ("zh", ys, "x", "c"))
+    zh, yh, yl, x, c = (lax.axis_index(name) for name in ("zh", "yh", "yl", "x", "c"))
+    y = lax.axis_index(ys)
     ny, nx = 8, 4
     half = rows // 2
     core = c.reshape(1)
@@ -311,17 +312,16 @@
     part = width // (2 * ny)
     w = fold(snap_qkv[0], ny)
     w = pick(exchange(w, "x"), x0)
-    wo = snap_out[0].reshape(ny, -1, snap_out.shape[2])
-    blocks = ahead(wo, ys)
-    after = {s: blocks.pop(s) for s in (1, ny - 1)}
-    wo = take_shifts(pick(wo, y), blocks, ys, y0)
-    w, wo, after, normed, kpos, start, start_other = lax.optimization_barrier(
-        (w, wo, after, normed, kpos, start, start_other)
+    wo = snap_out[0].reshape(2, ny // 2, -1, snap_out.shape[2])
+    wo = jnp.stack([pick(wo, yh), jnp.flip(pick(wo, 1 - yh), 0)], axis=1)
+    wo = take_shifts(pick(wo, yl), ahead(wo, "yl"), "yl", y0 % (ny // 2))
+    w, wo, normed, kpos, start, start_other = lax.optimization_barrier(
+        (w, wo, normed, kpos, start, start_other)
     )
     w = pick(exchange(w, ys), y0)
-    wo = take_shifts(wo, after, ys, y0)
-    wo = jnp.transpose(wo.reshape(wo.shape[0], nx, -1), (1, 0, 2))
+    wo = jnp.transpose(wo.reshape(2, -1, nx, snap_out.shape[2] // nx), (2, 0, 1, 3))
     wo = take_shifts(pick(wo, x), ahead(wo, "x"), "x", x0)
+    wo = jnp.where(yh == y0 // (ny // 2), wo[0], lax.ppermute(wo[1], ys, [(i, 7 - i) for i in range(8)]))
     wo = jnp.transpose(wo.reshape(wo.shape[0], nx, HD), (1, 0, 2)).reshape(part, HD)
     w = jnp.concatenate([w, wo], axis=1)
     w, normed = lax.optimization_barrier((w, normed))

time: 234 us -> 223 us (0.953)
  starting transfers between devices: 110 us -> 93.6 us
  waiting for transfers between devices: 77.8 us -> 81.6 us
    ppermute x16 -> x12, starting transfers between devices: 52 us -> 34.1 us  [shift(): lax.ppermute(block, axis, [(i, (i + distance) % count) for i in range(cou...]
    ppermute x0 -> x1, starting transfers between devices: none -> 4.58 us  [shards(): lax.ppermute(wo[1], ys, [(i, 7 - i) for i in range(8)])]
    ppermute x2, starting transfers between devices: 17.6 us -> 14.8 us  [trade(): return lax.ppermute(block, ('zh', 'x', 'zl', 'c'), route)]
    ppermute x0 -> x1, waiting for transfers between devices: none -> 2.74 us  [shards(): lax.ppermute(wo[1], ys, [(i, 7 - i) for i in range(8)])]
    ppermute x16 -> x12, waiting for transfers between devices: 29.8 us -> 29.3 us  [shift(): lax.ppermute(block, axis, [(i, (i + distance) % count) for i in range(cou...]
  transfers between devices with their start and end apart: 28 -> 25, of which waited for: 16 -> 16; matrix products, arithmetic and copies ran while one was open for 3% -> 4% of each run, Pallas kernels for 5% -> 5%
where the time goes in v10:
time: 223 us; the launch traced here: 222 us
  starting transfers between devices  93.6 us (42%)
  waiting for transfers between devices  81.6 us (37%)
  Pallas kernels  15 us (7%)
  blocking collectives  14.4 us (6%)
  local copies, waits for them, and re-layouts  9.16 us (4%)
  other arithmetic  6.46 us (3%)
    all_to_all x5, waiting for transfers between devices, exchange(): return lax.all_to_all(block, axis, 0, 0, tiled=True)  40.1 us
    ppermute x12, starting transfers between devices, shift(): lax.ppermute(block, axis, [(i, (i + distance) % count) for i in range(cou...  34.1 us
    ppermute x12, waiting for transfers between devices, shift(): lax.ppermute(block, axis, [(i, (i + distance) % count) for i in range(cou...  29.3 us
    all_to_all x5, starting transfers between devices, exchange(): return lax.all_to_all(block, axis, 0, 0, tiled=True)  28.4 us
    ppermute x2, starting transfers between devices, trade(): return lax.ppermute(block, ('zh', 'x', 'zl', 'c'), route)  14.8 us
    all_to_all x1, blocking collectives, exchange(): return lax.all_to_all(block, axis, 0, 0, tiled=True)  14.4 us
    pallas_call x2, Pallas kernels, attend(): pl.pallas_call(attend_kernel, grid=(nq // tile,), in_specs=[pl.BlockSpec(...  8.74 us
    ppermute x3, starting transfers between devices, swap(): return lax.ppermute(block, axis, [(0, 1), (1, 0)])  6.7 us
  transfers between devices with their start and end apart: 25, of which 16 were waited for; matrix products, arithmetic and copies ran while one was open for 4% of the time, Pallas kernels for 5%

profile of v10, /device:TPU:1, one launch (start us, length us, event | category | flops | bytes accessed | tf_op | source)
XLA Modules:
  0.0 221.6 jit_solution(17264299994458689814)
XLA Ops:
  0.0 1.9 copy-done
  1.9 2.1 shard_map.64
  4.0 4.8 %all-to-all-start = ((bf16[4,8,128,384]{3,2,1,0:T(8,128)(2,1)}), bf16[4,8,128,384]{3,2,1,0:T(8,128)(2,1)S(1)}, u32[]{:S(2)}, u32[]{:S(2)}) async-start(bf16[4,8,128,384]{3,2,1,0:T(8,128)(2,1)} %shard_map.64), calls=%async_computation | async-start | bytes 6291456 | tf_op jit(solution)/shard_map/all_to_all | solution.py:227
  8.9 1.3 dynamic-slice_bitcast_fusion.1
  12.0 5.2 %collective-permute-start = (bf16[2,32,2048]{2,1,0:T(8,128)(2,1)}, bf16[2,32,2048]{2,1,0:T(8,128)(2,1)}, u32[]{:S(2)}, u32[]{:S(2)}) collective-permute-start(bf16[2,32,2048]{2,1,0:T(8,128)(2,1)} %get-tuple-element.46), channel_id=1, source_target_pairs={{0,96},{32,0},{64,32},{96,64},{1,97},{33,1},{65,33},{97,65},{2,98}... | collective-permute-start | bytes 786440 | tf_op jit(solution)/shard_map/ppermute | solution.py:241
  17.3 1.9 collective-permute-start.1
  19.2 2.4 %collective-permute-start.2 = (bf16[2,32,2048]{2,1,0:T(8,128)(2,1)}, bf16[2,32,2048]{2,1,0:T(8,128)(2,1)}, u32[]{:S(2)}, u32[]{:S(2)}) collective-permute-start(bf16[2,32,2048]{2,1,0:T(8,128)(2,1)} %get-tuple-element.45), channel_id=1, source_target_pairs={{0,64},{32,96},{64,0},{96,32},{1,65},{33,97},{65,1},{97,33},{2,66}... | collective-permute-start | bytes 786440 | tf_op jit(solution)/shard_map/ppermute | solution.py:241
  21.7 1.1 fusion
  25.0 3.0 %collective-permute-done.1 = bf16[2,32,2048]{2,1,0:T(8,128)(2,1)} collective-permute-done((bf16[2,32,2048]{2,1,0:T(8,128)(2,1)}, bf16[2,32,2048]{2,1,0:T(8,128)(2,1)}, u32[]{:S(2)}, u32[]{:S(2)}) %collective-permute-start.1) | collective-permute-done | bytes 262176 | tf_op jit(solution)/shard_map/ppermute | solution.py:241
  28.0 13.3 %collective-permute-done.2 = bf16[2,32,2048]{2,1,0:T(8,128)(2,1)} collective-permute-done((bf16[2,32,2048]{2,1,0:T(8,128)(2,1)}, bf16[2,32,2048]{2,1,0:T(8,128)(2,1)}, u32[]{:S(2)}, u32[]{:S(2)}) %collective-permute-start.2) | collective-permute-done | bytes 262176 | tf_op jit(solution)/shard_map/ppermute | solution.py:241
  41.3 1.8 fusion.7
  44.1 9.4 %all-to-all-start.1 = ((bf16[8,128,384]{2,1,0:T(8,128)(2,1)}), bf16[8,128,384]{2,1,0:T(8,128)(2,1)S(1)}, u32[]{:S(2)}, u32[]{:S(2)}) async-start(bf16[8,128,384]{2,1,0:T(8,128)(2,1)} %dynamic-slice_bitcast_fusion), calls=%async_computation.1 | async-start | bytes 1572864 | tf_op jit(solution)/shard_map/all_to_all | solution.py:227
  54.2 2.8 %collective-permute-start.3 = (bf16[2,32,512]{2,1,0:T(8,128)(2,1)S(1)}, bf16[2,32,512]{2,1,0:T(8,128)(2,1)S(1)}, u32[]{:S(2)}, u32[]{:S(2)}) collective-permute-start(bf16[2,32,512]{2,1,0:T(8,128)(2,1)S(1)} %bitcast.111), channel_id=1, source_target_pairs={{0,24},{8,0},{16,8},{24,16},{1,25},{9,1},{17,9},{25,17},{2,26},{10... | collective-permute-start | bytes 196616 | tf_op jit(solution)/shard_map/ppermute | solution.py:241
  57.0 2.5 %collective-permute-start.4 = (bf16[2,32,512]{2,1,0:T(8,128)(2,1)S(1)}, bf16[2,32,512]{2,1,0:T(8,128)(2,1)S(1)}, u32[]{:S(2)}, u32[]{:S(2)}) collective-permute-start(bf16[2,32,512]{2,1,0:T(8,128)(2,1)S(1)} %bitcast.112), channel_id=1, source_target_pairs={{0,8},{8,16},{16,24},{24,0},{1,9},{9,17},{17,25},{25,1},{2,10},{10... | collective-permute-start | bytes 196616 | tf_op jit(solution)/shard_map/ppermute | solution.py:241
  59.6 2.5 %collective-permute-start.5 = (bf16[2,32,512]{2,1,0:T(8,128)(2,1)S(1)}, bf16[2,32,512]{2,1,0:T(8,128)(2,1)S(1)}, u32[]{:S(2)}, u32[]{:S(2)}) collective-permute-start(bf16[2,32,512]{2,1,0:T(8,128)(2,1)S(1)} %bitcast.113), channel_id=1, source_target_pairs={{0,16},{8,24},{16,0},{24,8},{1,17},{9,25},{17,1},{25,9},{2,18},{10... | collective-permute-start | bytes 196616 | tf_op jit(solution)/shard_map/ppermute | solution.py:241
  62.1 1.4 collective-permute-done.4
  63.6 2.8 %collective-permute-done.5 = bf16[2,32,512]{2,1,0:T(8,128)(2,1)S(1)} collective-permute-done((bf16[2,32,512]{2,1,0:T(8,128)(2,1)S(1)}, bf16[2,32,512]{2,1,0:T(8,128)(2,1)S(1)}, u32[]{:S(2)}, u32[]{:S(2)}) %collective-permute-start.5) | collective-permute-done | bytes 65568 | tf_op jit(solution)/shard_map/ppermute | solution.py:241
  66.4 4.6 %collective-permute-start.6 = (bf16[32,512]{1,0:T(8,128)(2,1)S(1)}, bf16[32,512]{1,0:T(8,128)(2,1)S(1)}, u32[]{:S(2)}, u32[]{:S(2)}) collective-permute-start(bf16[32,512]{1,0:T(8,128)(2,1)S(1)} %slice_bitcast_fusion), channel_id=1, source_target_pairs={{0,224},{32,192},{64,160},{96,128},{128,96},{160,64},{192,32},{224... | collective-permute-start | bytes 98312 | tf_op jit(solution)/shard_map/ppermute | solution.py:324
  71.0 2.7 %collective-permute-done.6 = bf16[32,512]{1,0:T(8,128)(2,1)S(1)} collective-permute-done((bf16[32,512]{1,0:T(8,128)(2,1)S(1)}, bf16[32,512]{1,0:T(8,128)(2,1)S(1)}, u32[]{:S(2)}, u32[]{:S(2)}) %collective-permute-start.6) | collective-permute-done | bytes 32800 | tf_op jit(solution)/shard_map/ppermute | solution.py:324
  73.8 1.4 all-to-all-done.1
  75.3 12.8 %collective-permute-start.11 = (bf16[128,512]{1,0:T(8,128)(2,1)S(1)}, bf16[128,512]{1,0:T(8,128)(2,1)S(1)}, u32[]{:S(2)}, u32[]{:S(2)}) collective-permute-start(bf16[128,512]{1,0:T(8,128)(2,1)S(1)} %pad_maximum_fusion.4), channel_id=1, source_target_pairs={{0,262},{1,270},{2,260},{3,268},{4,258},{5,266},{6,256},{7,264},{8... | collective-permute-start | bytes 393224 | tf_op jit(solution)/shard_map/ppermute | solution.py:281
  88.1 1.9 collective-permute-start.10
  90.1 3.5 %collective-permute-done.11 = bf16[128,512]{1,0:T(8,128)(2,1)S(1)} collective-permute-done((bf16[128,512]{1,0:T(8,128)(2,1)S(1)}, bf16[128,512]{1,0:T(8,128)(2,1)S(1)}, u32[]{:S(2)}, u32[]{:S(2)}) %collective-permute-start.11) | collective-permute-done | bytes 131104 | tf_op jit(solution)/shard_map/ppermute | solution.py:281
  95.5 7.4 %all-to-all-start.2 = ((bf16[8,128,512]{2,1,0:T(8,128)(2,1)}), bf16[8,128,512]{2,1,0:T(8,128)(2,1)S(1)}, u32[]{:S(2)}, u32[]{:S(2)}) async-start(bf16[8,128,512]{2,1,0:T(8,128)(2,1)} %broadcast_in_dim.2), calls=%async_computation.2 | async-start | bytes 2097152 | tf_op jit(solution)/shard_map/all_to_all | solution.py:227
  102.8 1.9 collective-permute-start.9
  104.8 4.9 %collective-permute-start.8 = (bf16[80,2048]{1,0:T(8,128)(2,1)S(1)}, bf16[80,2048]{1,0:T(8,128)(2,1)S(1)}, u32[]{:S(2)}, u32[]{:S(2)}) collective-permute-start(bf16[80,2048]{1,0:T(8,128)(2,1)S(1)} %fusion.2), channel_id=1, source_target_pairs={{0,16},{8,24},{16,0},{24,8},{1,17},{9,25},{17,1},{25,9},{2,18},{10... | collective-permute-start | bytes 983048 | tf_op jit(solution)/shard_map/ppermute | solution.py:241
  109.7 2.8 %collective-permute-start.7 = (bf16[80,2048]{1,0:T(8,128)(2,1)S(1)}, bf16[80,2048]{1,0:T(8,128)(2,1)S(1)}, u32[]{:S(2)}, u32[]{:S(2)}) collective-permute-start(bf16[80,2048]{1,0:T(8,128)(2,1)S(1)} %fusion.2), channel_id=1, source_target_pairs={{0,8},{8,16},{16,24},{24,0},{1,9},{9,17},{17,25},{25,1},{2,10},{10... | collective-permute-start | bytes 983048 | tf_op jit(solution)/shard_map/ppermute | solution.py:241
  112.4 19.6 %all-to-all-done.2 = bf16[8,128,512]{2,1,0:T(8,128)(2,1)S(1)} async-done(((bf16[8,128,512]{2,1,0:T(8,128)(2,1)}), bf16[8,128,512]{2,1,0:T(8,128)(2,1)S(1)}, u32[]{:S(2)}, u32[]{:S(2)}) %all-to-all-start.2) | async-done | bytes 1048608 | tf_op jit(solution)/shard_map/all_to_all | solution.py:227
  132.1 2.4 %collective-permute-start.12 = (bf16[1024,512]{1,0:T(8,128)(2,1)S(1)}, bf16[1024,512]{1,0:T(8,128)(2,1)S(1)}, u32[]{:S(2)}, u32[]{:S(2)}) collective-permute-start(bf16[1024,512]{1,0:T(8,128)(2,1)S(1)} %bitcast.85), channel_id=1, source_target_pairs={{0,1},{1,0},{2,3},{3,2},{4,5},{5,4},{6,7},{7,6},{8,9},{9,8},{10,11... | collective-permute-start | bytes 3145736 | tf_op jit(solution)/shard_map/ppermute | solution.py:223
  136.7 1.6 shard_map.66
  138.4 3.6 %all-to-all-start.3 = ((bf16[8,320,256]{2,1,0:T(8,128)(2,1)}), bf16[8,320,256]{2,1,0:T(8,128)(2,1)S(1)}, u32[]{:S(2)}, u32[]{:S(2)}) async-start(bf16[8,320,256]{2,1,0:T(8,128)(2,1)} %get-tuple-element.30), calls=%async_computation.3 | async-start | bytes 2621440 | tf_op jit(solution)/shard_map/all_to_all | solution.py:227
  141.9 1.9 collective-permute-start.16
  143.9 1.9 collective-permute-start.15
  145.8 3.4 %collective-permute-start.14 = (bf16[256,512]{1,0:T(8,128)(2,1)S(1)}, bf16[256,512]{1,0:T(8,128)(2,1)S(1)}, u32[]{:S(2)}, u32[]{:S(2)}) collective-permute-start(bf16[256,512]{1,0:T(8,128)(2,1)S(1)} %bitcast.101), channel_id=1, source_target_pairs={{0,8},{8,16},{16,24},{24,0},{1,9},{9,17},{17,25},{25,1},{2,10},{10... | collective-permute-start | bytes 786440 | tf_op jit(solution)/shard_map/ppermute | solution.py:241
  149.2 3.1 %collective-permute-start.13 = (bf16[320,128]{1,0:T(8,128)(2,1)S(1)}, bf16[320,128]{1,0:T(8,128)(2,1)S(1)}, u32[]{:S(2)}, u32[]{:S(2)}) collective-permute-start(bf16[320,128]{1,0:T(8,128)(2,1)S(1)} %get-tuple-element.29.q_ref), channel_id=1, source_target_pairs={{0,262},{2,260},{4,258},{6,256},{256,6},{258,4},{260,2},{262,0},{1... | collective-permute-start | bytes 245768 | tf_op jit(solution)/shard_map/ppermute | solution.py:285
  152.3 2.5 %collective-permute-done.15 = bf16[256,512]{1,0:T(8,128)(2,1)S(1)} collective-permute-done((bf16[256,512]{1,0:T(8,128)(2,1)S(1)}, bf16[256,512]{1,0:T(8,128)(2,1)S(1)}, u32[]{:S(2)}, u32[]{:S(2)}) %collective-permute-start.15) | collective-permute-done | bytes 262176 | tf_op jit(solution)/shard_map/ppermute | solution.py:241
  154.8 6.3 %collective-permute-done.14 = bf16[256,512]{1,0:T(8,128)(2,1)S(1)} collective-permute-done((bf16[256,512]{1,0:T(8,128)(2,1)S(1)}, bf16[256,512]{1,0:T(8,128)(2,1)S(1)}, u32[]{:S(2)}, u32[]{:S(2)}) %collective-permute-start.14) | collective-permute-done | bytes 262176 | tf_op jit(solution)/shard_map/ppermute | solution.py:241
  162.1 14.6 %all-to-all-done.3 = bf16[8,320,256]{2,1,0:T(8,128)(2,1)S(1)} async-done(((bf16[8,320,256]{2,1,0:T(8,128)(2,1)}), bf16[8,320,256]{2,1,0:T(8,128)(2,1)S(1)}, u32[]{:S(2)}, u32[]{:S(2)}) %all-to-all-start.3) | async-done | bytes 1310752 | tf_op jit(solution)/shard_map/all_to_all | solution.py:227
  176.7 2.4 %collective-permute-start.17 = (bf16[2560,256]{1,0:T(8,128)(2,1)S(1)}, bf16[2560,256]{1,0:T(8,128)(2,1)S(1)}, u32[]{:S(2)}, u32[]{:S(2)}) collective-permute-start(bf16[2560,256]{1,0:T(8,128)(2,1)S(1)} %bitcast.89), channel_id=1, source_target_pairs={{0,1},{1,0},{2,3},{3,2},{4,5},{5,4},{6,7},{7,6},{8,9},{9,8},{10,11... | collective-permute-start | bytes 3932168 | tf_op jit(solution)/shard_map/ppermute | solution.py:223
  179.1 1.9 collective-permute-start.19
  182.6 4.4 %shard_map.68 = bf16[4,96,128]{2,1,0:T(8,128)(2,1)S(1)} custom-call(s32[4]{0:T(128)S(1)} %get-tuple-element.34.start_ref, bf16[320,128]{1,0:T(8,128)(2,1)S(1)} %copy-done.2, bf16[2560,256]{1,0:T(8,128)(2,1)S(1)} %bitcast.90, bf16[2560,256]{1,0:T(8,128)(2,1)S(1)} %collective-permute-done.17.far_ref, s32[1,5120]{1,0:T(1,128)S(1)} %bitcast.92), custom_call_target="tpu_custom_call" | custom-call | flops 838860800 | bytes 2621440 | tf_op jit(solution)/shard_map/pallas_call | solution.py:143
  186.9 1.9 collective-permute-start.18
  188.9 4.4 %shard_map.67.near_ref = bf16[4,96,128]{2,1,0:T(8,128)(2,1)S(1)} custom-call(s32[4]{0:T(128)S(1)} %get-tuple-element.21.start_ref, bf16[320,128]{1,0:T(8,128)(2,1)S(1)} %get-tuple-element.29.q_ref, bf16[2560,256]{1,0:T(8,128)(2,1)S(1)} %bitcast.91, bf16[2560,256]{1,0:T(8,128)(2,1)S(1)} %collective-permute-done.17.far_ref, s32[1,5120]{1,0:T(1,128)S(1)} %bitcast.93), custom_call_target="tpu_custom_call" | custom-call | flops 838860800 | bytes 2621440 | tf_op jit(solution)/shard_map/pallas_call | solution.py:143
  193.3 3.5 %collective-permute-done.18.far_ref = bf16[4,96,128]{2,1,0:T(8,128)(2,1)S(1)} collective-permute-done((bf16[4,96,128]{2,1,0:T(8,128)(2,1)S(1)}, bf16[4,96,128]{2,1,0:T(8,128)(2,1)S(1)}, u32[]{:S(2)}, u32[]{:S(2)}) %collective-permute-start.18) | collective-permute-done | bytes 98336 | tf_op jit(solution)/shard_map/ppermute | solution.py:285
  196.7 1.5 shard_map.69
  198.2 3.3 %all-to-all-start.4 = ((bf16[4,80,128]{2,1,0:T(8,128)(2,1)}), bf16[4,80,128]{2,1,0:T(8,128)(2,1)S(1)}, u32[]{:S(2)}, u32[]{:S(2)}) async-start(bf16[4,80,128]{2,1,0:T(8,128)(2,1)} %shard_map.69), calls=%async_computation.4 | async-start | bytes 163840 | tf_op jit(solution)/shard_map/all_to_all | solution.py:227
  201.6 4.5 %all-to-all-done.4.context_ref = bf16[4,80,128]{2,1,0:T(8,128)(2,1)S(1)} async-done(((bf16[4,80,128]{2,1,0:T(8,128)(2,1)}), bf16[4,80,128]{2,1,0:T(8,128)(2,1)S(1)}, u32[]{:S(2)}, u32[]{:S(2)}) %all-to-all-start.4) | async-done | bytes 81952 | tf_op jit(solution)/shard_map/all_to_all | solution.py:227
  206.5 14.4 %all_to_all.30 = bf16[8,80,256]{2,1,0:T(8,128)(2,1)S(1)} all-to-all(bf16[8,80,256]{2,1,0:T(8,128)(2,1)S(1)} %shard_map.70), channel_id=1, replica_groups=mesh['zh'=2,'yh'=2,'yl'=4,'x'=4,'zl'=4,'c'=2] {'zl','c'}, dimensions={0} | all-to-all | bytes 655360 | tf_op jit(solution)/shard_map/all_to_all | solution.py:227
  (66 shorter events, 13.0 us)
Async XLA Ops:
  0.0 1.9 copy-start
  4.0 39.1 %all-to-all-start = ((bf16[4,8,128,384]{3,2,1,0:T(8,128)(2,1)}), bf16[4,8,128,384]{3,2,1,0:T(8,128)(2,1)S(1)}, u32[]{:S(2)}, u32[]{:S(2)}) async-start(bf16[4,8,128,384]{3,2,1,0:T(8,128)(2,1)} %shard_map.64), calls=%async_computation | async-start | bytes 6291456 | tf_op jit(solution)/shard_map/all_to_all | solution.py:227
  10.1 1.9 copy-start.4
  10.1 11.4 %copy-start.7 = (s32[64]{0:T(128)S(1)}, s32[64]{0:T(128)}, u32[]{:S(2)}) copy-start(s32[64]{0:T(128)} %param.11) | copy-start | bytes 772
  10.2 0.9 copy-start.3
  10.2 12.6 %copy-start.6 = (f32[2048]{0:T(1024)S(1)}, f32[2048]{0:T(1024)}, u32[]{:S(2)}) copy-start(f32[2048]{0:T(1024)} %param.7) | copy-start | bytes 24580
  12.0 13.0 %collective-permute-start = (bf16[2,32,2048]{2,1,0:T(8,128)(2,1)}, bf16[2,32,2048]{2,1,0:T(8,128)(2,1)}, u32[]{:S(2)}, u32[]{:S(2)}) collective-permute-start(bf16[2,32,2048]{2,1,0:T(8,128)(2,1)} %get-tuple-element.46), channel_id=1, source_target_pairs={{0,96},{32,0},{64,32},{96,64},{1,97},{33,1},{65,33},{97,65},{2,98}... | collective-permute-start | bytes 786440 | tf_op jit(solution)/shard_map/ppermute | solution.py:241
  17.3 10.7 %collective-permute-start.1 = (bf16[2,32,2048]{2,1,0:T(8,128)(2,1)}, bf16[2,32,2048]{2,1,0:T(8,128)(2,1)}, u32[]{:S(2)}, u32[]{:S(2)}) collective-permute-start(bf16[2,32,2048]{2,1,0:T(8,128)(2,1)} %get-tuple-element.47), channel_id=1, source_target_pairs={{0,32},{32,64},{64,96},{96,0},{1,33},{33,65},{65,97},{97,1},{2,34}... | collective-permute-start | bytes 786440 | tf_op jit(solution)/shard_map/ppermute | solution.py:241
  19.2 22.1 %collective-permute-start.2 = (bf16[2,32,2048]{2,1,0:T(8,128)(2,1)}, bf16[2,32,2048]{2,1,0:T(8,128)(2,1)}, u32[]{:S(2)}, u32[]{:S(2)}) collective-permute-start(bf16[2,32,2048]{2,1,0:T(8,128)(2,1)} %get-tuple-element.45), channel_id=1, source_target_pairs={{0,64},{32,96},{64,0},{96,32},{1,65},{33,97},{65,1},{97,33},{2,66}... | collective-permute-start | bytes 786440 | tf_op jit(solution)/shard_map/ppermute | solution.py:241
  44.1 9.4 %copy-start.5 = (bf16[2,32,2048]{2,1,0:T(8,128)(2,1)S(1)}, bf16[2,32,2048]{2,1,0:T(8,128)(2,1)}, u32[]{:S(2)}) copy-start(bf16[2,32,2048]{2,1,0:T(8,128)(2,1)} %fusion.7) | copy-start | bytes 786436
  44.1 31.2 %all-to-all-start.1 = ((bf16[8,128,384]{2,1,0:T(8,128)(2,1)}), bf16[8,128,384]{2,1,0:T(8,128)(2,1)S(1)}, u32[]{:S(2)}, u32[]{:S(2)}) async-start(bf16[8,128,384]{2,1,0:T(8,128)(2,1)} %dynamic-slice_bitcast_fusion), calls=%async_computation.1 | async-start | bytes 1572864 | tf_op jit(solution)/shard_map/all_to_all | solution.py:227
  54.2 7.9 %collective-permute-start.3 = (bf16[2,32,512]{2,1,0:T(8,128)(2,1)S(1)}, bf16[2,32,512]{2,1,0:T(8,128)(2,1)S(1)}, u32[]{:S(2)}, u32[]{:S(2)}) collective-permute-start(bf16[2,32,512]{2,1,0:T(8,128)(2,1)S(1)} %bitcast.111), channel_id=1, source_target_pairs={{0,24},{8,0},{16,8},{24,16},{1,25},{9,1},{17,9},{25,17},{2,26},{10... | collective-permute-start | bytes 196616 | tf_op jit(solution)/shard_map/ppermute | solution.py:241
  57.0 6.5 %collective-permute-start.4 = (bf16[2,32,512]{2,1,0:T(8,128)(2,1)S(1)}, bf16[2,32,512]{2,1,0:T(8,128)(2,1)S(1)}, u32[]{:S(2)}, u32[]{:S(2)}) collective-permute-start(bf16[2,32,512]{2,1,0:T(8,128)(2,1)S(1)} %bitcast.112), channel_id=1, source_target_pairs={{0,8},{8,16},{16,24},{24,0},{1,9},{9,17},{17,25},{25,1},{2,10},{10... | collective-permute-start | bytes 196616 | tf_op jit(solution)/shard_map/ppermute | solution.py:241
  59.6 6.8 %collective-permute-start.5 = (bf16[2,32,512]{2,1,0:T(8,128)(2,1)S(1)}, bf16[2,32,512]{2,1,0:T(8,128)(2,1)S(1)}, u32[]{:S(2)}, u32[]{:S(2)}) collective-permute-start(bf16[2,32,512]{2,1,0:T(8,128)(2,1)S(1)} %bitcast.113), channel_id=1, source_target_pairs={{0,16},{8,24},{16,0},{24,8},{1,17},{9,25},{17,1},{25,9},{2,18},{10... | collective-permute-start | bytes 196616 | tf_op jit(solution)/shard_map/ppermute | solution.py:241
  66.4 7.4 %collective-permute-start.6 = (bf16[32,512]{1,0:T(8,128)(2,1)S(1)}, bf16[32,512]{1,0:T(8,128)(2,1)S(1)}, u32[]{:S(2)}, u32[]{:S(2)}) collective-permute-start(bf16[32,512]{1,0:T(8,128)(2,1)S(1)} %slice_bitcast_fusion), channel_id=1, source_target_pairs={{0,224},{32,192},{64,160},{96,128},{128,96},{160,64},{192,32},{224... | collective-permute-start | bytes 98312 | tf_op jit(solution)/shard_map/ppermute | solution.py:324
  75.3 18.3 %collective-permute-start.11 = (bf16[128,512]{1,0:T(8,128)(2,1)S(1)}, bf16[128,512]{1,0:T(8,128)(2,1)S(1)}, u32[]{:S(2)}, u32[]{:S(2)}) collective-permute-start(bf16[128,512]{1,0:T(8,128)(2,1)S(1)} %pad_maximum_fusion.4), channel_id=1, source_target_pairs={{0,262},{1,270},{2,260},{3,268},{4,258},{5,266},{6,256},{7,264},{8... | collective-permute-start | bytes 393224 | tf_op jit(solution)/shard_map/ppermute | solution.py:281
  88.1 6.3 %collective-permute-start.10 = (bf16[128,512]{1,0:T(8,128)(2,1)S(1)}, bf16[128,512]{1,0:T(8,128)(2,1)S(1)}, u32[]{:S(2)}, u32[]{:S(2)}) collective-permute-start(bf16[128,512]{1,0:T(8,128)(2,1)S(1)} %pad_maximum_fusion.4), channel_id=1, source_target_pairs={{1,8},{3,10},{5,12},{7,14},{8,1},{10,3},{12,5},{14,7},{17,24},{19,... | collective-permute-start | bytes 393224 | tf_op jit(solution)/shard_map/ppermute | solution.py:281
  95.5 36.6 %all-to-all-start.2 = ((bf16[8,128,512]{2,1,0:T(8,128)(2,1)}), bf16[8,128,512]{2,1,0:T(8,128)(2,1)S(1)}, u32[]{:S(2)}, u32[]{:S(2)}) async-start(bf16[8,128,512]{2,1,0:T(8,128)(2,1)} %broadcast_in_dim.2), calls=%async_computation.2 | async-start | bytes 2097152 | tf_op jit(solution)/shard_map/all_to_all | solution.py:227
  102.8 31.7 %collective-permute-start.9 = (bf16[80,2048]{1,0:T(8,128)(2,1)S(1)}, bf16[80,2048]{1,0:T(8,128)(2,1)S(1)}, u32[]{:S(2)}, u32[]{:S(2)}) collective-permute-start(bf16[80,2048]{1,0:T(8,128)(2,1)S(1)} %fusion.2), channel_id=1, source_target_pairs={{0,24},{8,0},{16,8},{24,16},{1,25},{9,1},{17,9},{25,17},{2,26},{10... | collective-permute-start | bytes 983048 | tf_op jit(solution)/shard_map/ppermute | solution.py:241
  104.8 29.8 %collective-permute-start.8 = (bf16[80,2048]{1,0:T(8,128)(2,1)S(1)}, bf16[80,2048]{1,0:T(8,128)(2,1)S(1)}, u32[]{:S(2)}, u32[]{:S(2)}) collective-permute-start(bf16[80,2048]{1,0:T(8,128)(2,1)S(1)} %fusion.2), channel_id=1, source_target_pairs={{0,16},{8,24},{16,0},{24,8},{1,17},{9,25},{17,1},{25,9},{2,18},{10... | collective-permute-start | bytes 983048 | tf_op jit(solution)/shard_map/ppermute | solution.py:241
  109.7 24.9 %collective-permute-start.7 = (bf16[80,2048]{1,0:T(8,128)(2,1)S(1)}, bf16[80,2048]{1,0:T(8,128)(2,1)S(1)}, u32[]{:S(2)}, u32[]{:S(2)}) collective-permute-start(bf16[80,2048]{1,0:T(8,128)(2,1)S(1)} %fusion.2), channel_id=1, source_target_pairs={{0,8},{8,16},{16,24},{24,0},{1,9},{9,17},{17,25},{25,1},{2,10},{10... | collective-permute-start | bytes 983048 | tf_op jit(solution)/shard_map/ppermute | solution.py:241
  132.1 4.7 %collective-permute-start.12 = (bf16[1024,512]{1,0:T(8,128)(2,1)S(1)}, bf16[1024,512]{1,0:T(8,128)(2,1)S(1)}, u32[]{:S(2)}, u32[]{:S(2)}) collective-permute-start(bf16[1024,512]{1,0:T(8,128)(2,1)S(1)} %bitcast.85), channel_id=1, source_target_pairs={{0,1},{1,0},{2,3},{3,2},{4,5},{5,4},{6,7},{7,6},{8,9},{9,8},{10,11... | collective-permute-start | bytes 3145736 | tf_op jit(solution)/shard_map/ppermute | solution.py:223
  138.4 38.3 %all-to-all-start.3 = ((bf16[8,320,256]{2,1,0:T(8,128)(2,1)}), bf16[8,320,256]{2,1,0:T(8,128)(2,1)S(1)}, u32[]{:S(2)}, u32[]{:S(2)}) async-start(bf16[8,320,256]{2,1,0:T(8,128)(2,1)} %get-tuple-element.30), calls=%async_computation.3 | async-start | bytes 2621440 | tf_op jit(solution)/shard_map/all_to_all | solution.py:227
  141.9 10.3 %collective-permute-start.16 = (bf16[256,512]{1,0:T(8,128)(2,1)S(1)}, bf16[256,512]{1,0:T(8,128)(2,1)S(1)}, u32[]{:S(2)}, u32[]{:S(2)}) collective-permute-start(bf16[256,512]{1,0:T(8,128)(2,1)S(1)} %bitcast.99), channel_id=1, source_target_pairs={{0,24},{8,0},{16,8},{24,16},{1,25},{9,1},{17,9},{25,17},{2,26},{10... | collective-permute-start | bytes 786440 | tf_op jit(solution)/shard_map/ppermute | solution.py:241
  143.9 11.0 %collective-permute-start.15 = (bf16[256,512]{1,0:T(8,128)(2,1)S(1)}, bf16[256,512]{1,0:T(8,128)(2,1)S(1)}, u32[]{:S(2)}, u32[]{:S(2)}) collective-permute-start(bf16[256,512]{1,0:T(8,128)(2,1)S(1)} %bitcast.100), channel_id=1, source_target_pairs={{0,16},{8,24},{16,0},{24,8},{1,17},{9,25},{17,1},{25,9},{2,18},{10... | collective-permute-start | bytes 786440 | tf_op jit(solution)/shard_map/ppermute | solution.py:241
  145.8 15.3 %collective-permute-start.14 = (bf16[256,512]{1,0:T(8,128)(2,1)S(1)}, bf16[256,512]{1,0:T(8,128)(2,1)S(1)}, u32[]{:S(2)}, u32[]{:S(2)}) collective-permute-start(bf16[256,512]{1,0:T(8,128)(2,1)S(1)} %bitcast.101), channel_id=1, source_target_pairs={{0,8},{8,16},{16,24},{24,0},{1,9},{9,17},{17,25},{25,1},{2,10},{10... | collective-permute-start | bytes 786440 | tf_op jit(solution)/shard_map/ppermute | solution.py:241
  149.2 12.3 %collective-permute-start.13 = (bf16[320,128]{1,0:T(8,128)(2,1)S(1)}, bf16[320,128]{1,0:T(8,128)(2,1)S(1)}, u32[]{:S(2)}, u32[]{:S(2)}) collective-permute-start(bf16[320,128]{1,0:T(8,128)(2,1)S(1)} %get-tuple-element.29.q_ref), channel_id=1, source_target_pairs={{0,262},{2,260},{4,258},{6,256},{256,6},{258,4},{260,2},{262,0},{1... | collective-permute-start | bytes 245768 | tf_op jit(solution)/shard_map/ppermute | solution.py:285
  161.5 0.6 copy-start.1
  176.7 5.0 %collective-permute-start.17 = (bf16[2560,256]{1,0:T(8,128)(2,1)S(1)}, bf16[2560,256]{1,0:T(8,128)(2,1)S(1)}, u32[]{:S(2)}, u32[]{:S(2)}) collective-permute-start(bf16[2560,256]{1,0:T(8,128)(2,1)S(1)} %bitcast.89), channel_id=1, source_target_pairs={{0,1},{1,0},{2,3},{3,2},{4,5},{5,4},{6,7},{7,6},{8,9},{9,8},{10,11... | collective-permute-start | bytes 3932168 | tf_op jit(solution)/shard_map/ppermute | solution.py:223
  179.1 22.5 %collective-permute-start.19 = (bf16[4,256,512]{2,1,0:T(8,128)(2,1)S(1)}, bf16[4,256,512]{2,1,0:T(8,128)(2,1)S(1)}, u32[]{:S(2)}, u32[]{:S(2)}) collective-permute-start(bf16[4,256,512]{2,1,0:T(8,128)(2,1)S(1)} %pad_maximum_fusion.3.near_ref), channel_id=1, source_target_pairs={{0,1},{1,0},{2,3},{3,2},{4,5},{5,4},{6,7},{7,6},{8,9},{9,8},{10,11... | collective-permute-start | bytes 3145736 | tf_op jit(solution)/shard_map/ppermute | solution.py:223
  181.7 0.9 copy-start.2
  186.9 9.8 %collective-permute-start.18 = (bf16[4,96,128]{2,1,0:T(8,128)(2,1)S(1)}, bf16[4,96,128]{2,1,0:T(8,128)(2,1)S(1)}, u32[]{:S(2)}, u32[]{:S(2)}) collective-permute-start(bf16[4,96,128]{2,1,0:T(8,128)(2,1)S(1)} %shard_map.68), channel_id=1, source_target_pairs={{0,262},{2,260},{4,258},{6,256},{256,6},{258,4},{260,2},{262,0},{1... | collective-permute-start | bytes 294920 | tf_op jit(solution)/shard_map/ppermute | solution.py:285
  198.2 7.8 %all-to-all-start.4 = ((bf16[4,80,128]{2,1,0:T(8,128)(2,1)}), bf16[4,80,128]{2,1,0:T(8,128)(2,1)S(1)}, u32[]{:S(2)}, u32[]{:S(2)}) async-start(bf16[4,80,128]{2,1,0:T(8,128)(2,1)} %shard_map.69), calls=%async_computation.4 | async-start | bytes 163840 | tf_op jit(solution)/shard_map/all_to_all | solution.py:227

commit v11 on v10

--- a/solution.py
+++ b/solution.py
@@ -1,3 +1,5 @@
+import functools
+
 import jax
 import jax.numpy as jnp
 import numpy as np
@@ -15,23 +17,27 @@
 
 
 def fold_kernel(w_ref, out_ref):
+    part = w_ref.shape[4]
     for h in range(2):
-        for r in range(2):
+        for k in range(2):
             for j in range(3):
-                out_ref[2 * h + r, :, :, j * HD : (j + 1) * HD] = w_ref[j, r, :, :, h * HD : (h + 1) * HD]
-
-
-def fold(w, ny):
-    part, steps = w.shape[1] // (2 * ny), 2
+                for x in range(out_ref.shape[0]):
+                    out_ref[x, 4 * h : 4 * h + 4, k * part : (k + 1) * part, j * HD : (j + 1) * HD] = w_ref[
+                        j, k, :, x, :, h * HD : (h + 1) * HD
+                    ]
+
+
+def fold(w):
+    part, steps = w.shape[1] // 32, 2
     return pl.pallas_call(
         fold_kernel,
         grid=(steps,),
-        in_specs=[pl.BlockSpec((3, 2, ny // steps, part, 2 * HD), lambda i: (0, 0, i, 0, 0))],
-        out_specs=pl.BlockSpec((4, ny // steps, part, 3 * HD), lambda i: (0, i, 0, 0)),
-        out_shape=jax.ShapeDtypeStruct((4, ny, part, 3 * HD), w.dtype),
+        in_specs=[pl.BlockSpec((3, 2, 4, 4 // steps, part, 2 * HD), lambda i: (0, 0, 0, i, 0, 0))],
+        out_specs=pl.BlockSpec((4 // steps, 8, 2 * part, 3 * HD), lambda i: (i, 0, 0, 0)),
+        out_shape=jax.ShapeDtypeStruct((4, 8, 2 * part, 3 * HD), w.dtype),
         compiler_params=LIMIT,
         cost_estimate=pl.CostEstimate(flops=0, bytes_accessed=4 * w.size, transcendentals=0),
-    )(w.reshape(3, 2, ny, part, 2 * HD))
+    )(w.reshape(3, 2, 4, 4, part, 2 * HD))
 
 
 def near_kernel(c_ref, x_ref, w_ref, out_ref):
@@ -160,47 +166,49 @@
     )(start, q, near, far, kpos)
 
 
-def merge_kernel(near_ref, far_ref, out_ref):
-    nx, half = out_ref.shape[0], out_ref.shape[1]
-    for x in range(nx):
+def merge_kernel(*refs):
+    part_refs, out_ref = refs[:-1], refs[-1]
+    half = out_ref.shape[1]
+    for n in range(out_ref.shape[0]):
         tops, totals = [], []
-        for ref in (near_ref, far_ref):
-            stat = ref[x, half:, :].astype(jnp.float32)
+        for ref in part_refs:
+            stat = ref[n, half:, :].astype(jnp.float32)
             stat = jnp.concatenate([stat, jnp.zeros((HD - EXTRA, HD), jnp.float32)]).T[:half]
             tops.append(stat[:, 0:1] + stat[:, 1:2] + stat[:, 2:3])
             totals.append(stat[:, 3:4] + stat[:, 4:5] + stat[:, 5:6])
-        top = jnp.maximum(tops[0], tops[1])
-        a = totals[0] * jnp.exp2(tops[0] - top)
-        b = totals[1] * jnp.exp2(tops[1] - top)
-        mixed = near_ref[x, :half, :].astype(jnp.float32) * a + far_ref[x, :half, :].astype(jnp.float32) * b
-        out_ref[x] = (mixed / (a + b)).astype(out_ref.dtype)
-
-
-def merge(near, far):
-    nx, rows = near.shape[0], near.shape[1] - EXTRA
+        top = functools.reduce(jnp.maximum, tops)
+        weights = [total * jnp.exp2(mine - top) for mine, total in zip(tops, totals)]
+        mixed = sum(ref[n, :half, :].astype(jnp.float32) * weight for ref, weight in zip(part_refs, weights))
+        out_ref[n] = (mixed / sum(weights)).astype(out_ref.dtype)
+
+
+def merge(parts):
+    blocks, rows = parts[0].shape[0], parts[0].shape[1] - EXTRA
+    size = len(parts) * parts[0].size
     vmem = pl.BlockSpec(memory_space=pltpu.VMEM)
     return pl.pallas_call(
         merge_kernel,
-        in_specs=[vmem, vmem],
+        in_specs=[vmem] * len(parts),
         out_specs=vmem,
-        out_shape=jax.ShapeDtypeStruct((nx, rows, HD), jnp.bfloat16),
-        compiler_params=LIMIT,
-        cost_estimate=pl.CostEstimate(flops=8 * near.size, bytes_accessed=6 * near.size, transcendentals=0),
-    )(near, far)
+        out_shape=jax.ShapeDtypeStruct((blocks, rows, HD), jnp.bfloat16),
+        compiler_params=LIMIT,
+        cost_estimate=pl.CostEstimate(flops=4 * size, bytes_accessed=3 * size, transcendentals=0),
+    )(*parts)
 
 
 def finish_kernel(c_ref, context_ref, near_ref, far_ref, out_ref):
-    low = jnp.concatenate([context_ref[0], context_ref[2]], axis=1)
-    high = jnp.concatenate([context_ref[1], context_ref[3]], axis=1)
+    low = jnp.concatenate([context_ref[0], context_ref[1]], axis=1)
+    high = jnp.concatenate([context_ref[2], context_ref[3]], axis=1)
+    first = c_ref[0] == 0
+    near = jnp.where(first, low, high)
+    far = jnp.where(first, high, low)
     width = out_ref.shape[2]
-    for ref, odd in ((near_ref, c_ref[0]), (far_ref, 1 - c_ref[0])):
-        for h in range(2):
-            terms = jnp.dot(low, ref[2 * h], preferred_element_type=jnp.float32)
-            terms += jnp.dot(high, ref[2 * h + 1], preferred_element_type=jnp.float32)
-            terms = terms.astype(out_ref.dtype)
-            at = 2 * (2 * h + odd)
-            out_ref[at] = terms[:, :width]
-            out_ref[at + 1] = terms[:, width:]
+    for n in range(near_ref.shape[0]):
+        terms = jnp.dot(near, near_ref[n], preferred_element_type=jnp.float32)
+        terms += jnp.dot(far, far_ref[n], preferred_element_type=jnp.float32)
+        terms = terms.astype(out_ref.dtype)
+        out_ref[2 * n] = terms[:, :width]
+        out_ref[2 * n + 1] = terms[:, width:]
 
 
 def finish(core, context, near, far):
@@ -258,38 +266,18 @@
     return {s: pick(blocks, (here + s) % count) for s in distances(axis)}
 
 
-def gather_by_shifts(block, axis):
-    here, count = lax.axis_index(axis), lax.axis_size(axis)
-    got = {0: block}
-    for s in distances(axis):
-        got[s] = shift(block, axis, s)
-    got = jnp.stack([got[s] for s in range(count)])
-    return jnp.stack([pick(got, (here - i) % count) for i in range(count)])
-
-
-def trade(block, across):
-    route = []
-    for z in range(2):
-        for x in range(4):
-            for low in range(4):
-                for c in range(2):
-                    to_low = 3 - low if across else low
-                    to = (((z ^ across) * 4 + x - x % 2 + c) * 4 + to_low) * 2 + x % 2
-                    here = ((z * 4 + x) * 4 + low) * 2 + c
-                    if to != here:
-                        route.append((here, to))
-    return lax.ppermute(block, ("zh", "x", "zl", "c"), route)
-
-
-def mirror(block):
-    return lax.ppermute(block, ("zh", "zl"), [(i, 7 - i) for i in range(8)])
+def mirror(block, axes):
+    return lax.ppermute(block, axes, [(i, 7 - i) for i in range(8)])
+
+
+def by_index(mine, other, index):
+    return [jnp.where(index == 0, mine, other), jnp.where(index == 0, other, mine)]
 
 
 def shards(hidden_in, norm_gain, snap_qkv, snap_out, owner_index, block_order):
     rows, width = hidden_in.shape
     ys = ("yh", "yl")
     zh, yh, yl, x, c = (lax.axis_index(name) for name in ("zh", "yh", "yl", "x", "c"))
-    y = lax.axis_index(ys)
     ny, nx = 8, 4
     half = rows // 2
     core = c.reshape(1)
@@ -300,49 +288,61 @@
     normed = (
         mine * lax.rsqrt(jnp.mean(mine * mine, axis=-1, keepdims=True) + 1e-06) * norm_gain
     ).astype(jnp.bfloat16)
-
-    order = block_order.reshape(2, ny, nx) * rows
+    normed = jnp.concatenate(by_index(normed, swap(normed, "yh"), yh))
+
+    order = block_order.reshape(2, 2, ny // 2, nx) * rows
     offsets = jnp.arange(half, dtype=jnp.int32)
-    kpos = (pick(order, zh)[:, :, None] + offsets).reshape(-1)
+    kpos = jnp.transpose(lax.dynamic_index_in_dim(order, x, 3, keepdims=False), (2, 0, 1)).reshape(-1)
+    kpos = (kpos[:, None] + offsets).reshape(-1)
     kpos = jnp.concatenate([kpos + c * half, kpos + (1 - c) * half]).reshape(1, -1)
-    here = lax.dynamic_index_in_dim(order, y, 1, keepdims=False)
-    start = pick(here, zh) + c * half
-    start_other = pick(here, 1 - zh) + c * half
-
-    part = width // (2 * ny)
-    w = fold(snap_qkv[0], ny)
+    order = lax.dynamic_index_in_dim(order, yl, 2, keepdims=False).reshape(-1, nx) + c * half
+    start = {s: lax.dynamic_index_in_dim(order, (x - s) % nx, 1, keepdims=False) for s in range(nx)}
+
+    w = fold(snap_qkv[0])
     w = pick(exchange(w, "x"), x0)
     wo = snap_out[0].reshape(2, ny // 2, -1, snap_out.shape[2])
     wo = jnp.stack([pick(wo, yh), jnp.flip(pick(wo, 1 - yh), 0)], axis=1)
     wo = take_shifts(pick(wo, yl), ahead(wo, "yl"), "yl", y0 % (ny // 2))
-    w, wo, normed, kpos, start, start_other = lax.optimization_barrier(
-        (w, wo, normed, kpos, start, start_other)
-    )
+    w, wo, normed, kpos, start = lax.optimization_barrier((w, wo, normed, kpos, start))
     w = pick(exchange(w, ys), y0)
     wo = jnp.transpose(wo.reshape(2, -1, nx, snap_out.shape[2] // nx), (2, 0, 1, 3))
     wo = take_shifts(pick(wo, x), ahead(wo, "x"), "x", x0)
-    wo = jnp.where(yh == y0 // (ny // 2), wo[0], lax.ppermute(wo[1], ys, [(i, 7 - i) for i in range(8)]))
-    wo = jnp.transpose(wo.reshape(wo.shape[0], nx, HD), (1, 0, 2)).reshape(part, HD)
-    w = jnp.concatenate([w, wo], axis=1)
-    w, normed = lax.optimization_barrier((w, normed))
-    w = jnp.where(zh == zh0, jnp.where(x % 2 == c, w, trade(w, 0)), trade(w, 1))
-    w = spread(w, ys).reshape(ny * part, 4 * HD)
-    normed = gather_by_shifts(normed, "x").reshape(-1, width)
-    q, kv = project(core, normed, w, swap(w, "c"), ny)
-    wo = w[:, 3 * HD :].reshape(ny, nx, part // nx, HD)
-    wo = jnp.transpose(wo, (0, 2, 1, 3)).reshape(ny * part // nx, nx * HD)
+    wo = jnp.where(yh == y0 // (ny // 2), wo[0], mirror(wo[1], ys))
+    w, wo, normed = lax.optimization_barrier((w, wo, normed))
+
+    w = w.reshape(2, -1, 3 * HD)
+    same, cross = pick(w, c), pick(w, 1 - c)
+    part = same.shape[0]
+    there = jnp.where(
+        c == zh,
+        lax.ppermute(same, ("zh", "c"), [(2, 0), (1, 3)]),
+        lax.ppermute(cross, ("zh", "c"), [(2, 1), (1, 2)]),
+    )
+    here = jnp.where(c == zh, same, lax.ppermute(cross, ("zh", "c"), [(0, 1), (3, 2)]))
+    w = jnp.where(zh == zh0, here, there)
+    wo = jnp.where(zh == zh0, wo, swap(wo, "zh"))
+    wide = wo.shape[1] // 2
+    w = jnp.concatenate([w, jnp.concatenate([wo[:, :wide], wo[:, wide:]])], axis=1)
+    w = spread(w, ("yl", "x"))
+    normed = jnp.concatenate(by_index(normed, mirror(normed, ("zh", "zl")), zh))
+    wo = w[:, :, 3 * HD :].reshape(ny // 2, nx, 2, -1, wide)
+    wo = jnp.transpose(wo, (1, 0, 3, 2, 4)).reshape(nx, -1, 2 * wide)
+    w = w.reshape(nx * (ny // 2) * part, -1)
+    q, kv = project(core, normed, w, swap(w, "c"), ny // 2)
     q, kv, wo = lax.optimization_barrier((q, kv, wo))
 
-    near = exchange(kv, ys).reshape(-1, 2 * HD)
-    q_other = mirror(q)
-    wo = gather_by_shifts(wo, "x")
-    near, q_other, wo = lax.optimization_barrier((near, q_other, wo))
+    near = exchange(kv, "yl").reshape(-1, 2 * HD)
+    queries = {s: shift(q, "x", s) for s in distances("x")}
+    wo = jnp.concatenate(by_index(wo, mirror(wo, ys), yh), axis=1)
+    near, queries, wo = lax.optimization_barrier((near, queries, wo))
     far = swap(near, "c")
     wo_far = swap(wo, "c")
 
-    others = mirror(attend(start_other, q_other, near, far, kpos, half))
-    context = merge(attend(start, q, near, far, kpos, half), others)
-    context = exchange(context, "x")
+    parts = []
+    for s in distances("x"):
+        parts.append(shift(attend(start[s], queries[s], near, far, kpos, half), "x", nx - s))
+    context = merge([attend(start[0], q, near, far, kpos, half)] + parts)
+    context = exchange(context, ("zh", "yh"))
     terms = finish(core, context, wo, wo_far)
     terms = exchange(terms, ("zl", "c")).reshape(-1, rows, terms.shape[2])
     return jnp.sum(terms.astype(jnp.float32), axis=0).astype(jnp.bfloat16)

time: 223 us -> 258 us (1.16)
  starting transfers between devices: 93.6 us -> 118 us
  blocking collectives: 14.4 us -> 35.4 us
  waiting for transfers between devices: 81.6 us -> 71.2 us
  other arithmetic: 6.46 us -> 2.82 us
  Pallas kernels: 15 us -> 17.8 us
    ppermute x3 -> x5, starting transfers between devices: 6.7 us -> 30.5 us  [swap(): return lax.ppermute(block, axis, [(0, 1), (1, 0)])]
    all_to_all x5 -> x4, waiting for transfers between devices: 40.1 us -> 17.9 us  [exchange(): return lax.all_to_all(block, axis, 0, 0, tiled=True)]
    all_to_all x1 -> x2, blocking collectives: 14.4 us -> 35.4 us  [exchange(): return lax.all_to_all(block, axis, 0, 0, tiled=True)]
    ppermute x5 -> x6, waiting for transfers between devices: 10.5 us -> 21.3 us  [the longest x3 20.1 us: mirror(): return lax.ppermute(block, axes, [(i, 7 - i) for i in range(8)])]
    all_to_all x5 -> x4, starting transfers between devices: 28.4 us -> 19 us  [exchange(): return lax.all_to_all(block, axis, 0, 0, tiled=True)]
    ppermute x12, starting transfers between devices: 34.1 us -> 40.4 us  [shift(): lax.ppermute(block, axis, [(i, (i + distance) % count) for i in range(cou...]
    ppermute x5 -> x6, starting transfers between devices: 24.4 us -> 28.1 us  [the longest x3 16.7 us: mirror(): return lax.ppermute(block, axes, [(i, 7 - i) for i in range(8)])]
    pallas_call x2 -> x4, Pallas kernels: 8.74 us -> 10.8 us  [attend(): pl.pallas_call(attend_kernel, grid=(nq // tile,), in_specs=[pl.BlockSpec(...]
  transfers between devices with their start and end apart: 25 -> 27, of which waited for: 16 -> 11; matrix products, arithmetic and copies ran while one was open for 4% -> 3% of each run, Pallas kernels for 5% -> 5%
where the time goes in v11:
time: 258 us; the launch traced here: 257 us
  starting transfers between devices  118 us (46%)
  waiting for transfers between devices  71.2 us (28%)
  blocking collectives  35.4 us (14%)
  Pallas kernels  17.8 us (7%)
  local copies, waits for them, and re-layouts  9.83 us (4%)
  other arithmetic  2.82 us (1%)
    ppermute x12, starting transfers between devices, shift(): lax.ppermute(block, axis, [(i, (i + distance) % count) for i in range(cou...  40.4 us
    all_to_all x2, blocking collectives, exchange(): return lax.all_to_all(block, axis, 0, 0, tiled=True)  35.4 us
    ppermute x5, starting transfers between devices, swap(): return lax.ppermute(block, axis, [(0, 1), (1, 0)])  30.5 us
    ppermute x12, waiting for transfers between devices, shift(): lax.ppermute(block, axis, [(i, (i + distance) % count) for i in range(cou...  30 us
    ppermute x3, waiting for transfers between devices, mirror(): return lax.ppermute(block, axes, [(i, 7 - i) for i in range(8)])  20.1 us
    all_to_all x4, starting transfers between devices, exchange(): return lax.all_to_all(block, axis, 0, 0, tiled=True)  19 us
    all_to_all x4, waiting for transfers between devices, exchange(): return lax.all_to_all(block, axis, 0, 0, tiled=True)  17.9 us
    ppermute x3, starting transfers between devices, mirror(): return lax.ppermute(block, axes, [(i, 7 - i) for i in range(8)])  16.7 us
  transfers between devices with their start and end apart: 27, of which 11 were waited for; matrix products, arithmetic and copies ran while one was open for 3% of the time, Pallas kernels for 5%

profile of v11, /device:TPU:1, one launch (start us, length us, event | category | flops | bytes accessed | tf_op | source)
XLA Modules:
  0.0 256.7 jit_solution(17165265328141948137)
XLA Ops:
  0.0 1.9 copy-done
  1.9 2.2 shard_map.64
  4.1 5.0 %all-to-all-start = ((bf16[4,8,128,384]{3,2,1,0:T(8,128)(2,1)}), bf16[4,8,128,384]{3,2,1,0:T(8,128)(2,1)}, u32[]{:S(2)}, u32[]{:S(2)}) async-start(bf16[4,8,128,384]{3,2,1,0:T(8,128)(2,1)} %shard_map.64), calls=%async_computation | async-start | bytes 6291456 | tf_op jit(solution)/shard_map/all_to_all | solution.py:235
  10.1 5.9 %collective-permute-start = (bf16[2,32,2048]{2,1,0:T(8,128)(2,1)}, bf16[2,32,2048]{2,1,0:T(8,128)(2,1)S(1)}, u32[]{:S(2)}, u32[]{:S(2)}) collective-permute-start(bf16[2,32,2048]{2,1,0:T(8,128)(2,1)} %get-tuple-element.56), channel_id=1, source_target_pairs={{0,96},{32,0},{64,32},{96,64},{1,97},{33,1},{65,33},{97,65},{2,98}... | collective-permute-start | bytes 786440 | tf_op jit(solution)/shard_map/ppermute | solution.py:249
  16.1 1.9 collective-permute-start.1
  18.0 2.3 collective-permute-start.2
  20.7 5.7 %collective-permute-start.3 = (bf16[80,2048]{1,0:T(8,128)(2,1)S(1)}, bf16[80,2048]{1,0:T(8,128)(2,1)S(1)}, u32[]{:S(2)}, u32[]{:S(2)}) collective-permute-start(bf16[80,2048]{1,0:T(8,128)(2,1)S(1)} %fusion.2), channel_id=1, source_target_pairs={{0,128},{128,0},{1,129},{129,1},{2,130},{130,2},{3,131},{131,3},{4... | collective-permute-start | bytes 983048 | tf_op jit(solution)/shard_map/ppermute | solution.py:231
  28.3 25.5 %collective-permute-done.2 = bf16[2,32,2048]{2,1,0:T(8,128)(2,1)S(1)} collective-permute-done((bf16[2,32,2048]{2,1,0:T(8,128)(2,1)S(1)}, bf16[2,32,2048]{2,1,0:T(8,128)(2,1)S(1)}, u32[]{:S(2)}, u32[]{:S(2)}) %collective-permute-start.2) | collective-permute-done | bytes 262176 | tf_op jit(solution)/shard_map/ppermute | solution.py:249
  54.2 2.1 dynamic-slice_bitcast_fusion
  56.3 5.0 %all-to-all-start.1 = ((bf16[8,128,384]{2,1,0:T(8,128)(2,1)}), bf16[8,128,384]{2,1,0:T(8,128)(2,1)S(1)}, u32[]{:S(2)}, u32[]{:S(2)}) async-start(bf16[8,128,384]{2,1,0:T(8,128)(2,1)} %dynamic-slice_bitcast_fusion), calls=%async_computation.1 | async-start | bytes 1572864 | tf_op jit(solution)/shard_map/all_to_all | solution.py:235
  62.0 4.3 %collective-permute-start.4 = (bf16[2,32,512]{2,1,0:T(8,128)(2,1)S(1)}, bf16[2,32,512]{2,1,0:T(8,128)(2,1)S(1)}, u32[]{:S(2)}, u32[]{:S(2)}) collective-permute-start(bf16[2,32,512]{2,1,0:T(8,128)(2,1)S(1)} %bitcast.80), channel_id=1, source_target_pairs={{0,24},{8,0},{16,8},{24,16},{1,25},{9,1},{17,9},{25,17},{2,26},{10... | collective-permute-start | bytes 196616 | tf_op jit(solution)/shard_map/ppermute | solution.py:249
  66.3 1.9 collective-permute-start.5
  68.3 3.7 %collective-permute-start.6 = (bf16[2,32,512]{2,1,0:T(8,128)(2,1)S(1)}, bf16[2,32,512]{2,1,0:T(8,128)(2,1)S(1)}, u32[]{:S(2)}, u32[]{:S(2)}) collective-permute-start(bf16[2,32,512]{2,1,0:T(8,128)(2,1)S(1)} %bitcast.82), channel_id=1, source_target_pairs={{0,16},{8,24},{16,0},{24,8},{1,17},{9,25},{17,1},{25,9},{2,18},{10... | collective-permute-start | bytes 196616 | tf_op jit(solution)/shard_map/ppermute | solution.py:249
  72.9 2.2 collective-permute-done.6
  75.1 4.6 %collective-permute-start.7 = (bf16[32,512]{1,0:T(8,128)(2,1)S(1)}, bf16[32,512]{1,0:T(8,128)(2,1)S(1)}, u32[]{:S(2)}, u32[]{:S(2)}) collective-permute-start(bf16[32,512]{1,0:T(8,128)(2,1)S(1)} %slice_bitcast_fusion), channel_id=1, source_target_pairs={{0,224},{32,192},{64,160},{96,128},{128,96},{160,64},{192,32},{224... | collective-permute-start | bytes 98312 | tf_op jit(solution)/shard_map/ppermute | solution.py:270
  79.8 3.9 %collective-permute-done.7 = bf16[32,512]{1,0:T(8,128)(2,1)S(1)} collective-permute-done((bf16[32,512]{1,0:T(8,128)(2,1)S(1)}, bf16[32,512]{1,0:T(8,128)(2,1)S(1)}, u32[]{:S(2)}, u32[]{:S(2)}) %collective-permute-start.7) | collective-permute-done | bytes 32800 | tf_op jit(solution)/shard_map/ppermute | solution.py:270
  84.8 10.6 %collective-permute-start.12 = (bf16[32,512]{1,0:T(8,128)(2,1)S(1)}, bf16[32,512]{1,0:T(8,128)(2,1)S(1)}, u32[]{:S(2)}, u32[]{:S(2)}) collective-permute-start(bf16[32,512]{1,0:T(8,128)(2,1)S(1)} %fusion.16), channel_id=1, source_target_pairs={{0,256},{256,0},{1,257},{257,1},{2,258},{258,2},{3,259},{259,3},{4... | collective-permute-start | bytes 98312 | tf_op jit(solution)/shard_map/ppermute | solution.py:231
  95.5 2.3 collective-permute-start.11
  97.8 1.3 collective-permute-start.9
  99.1 7.9 %collective-permute-start.10 = (bf16[64,384]{1,0:T(8,128)(2,1)S(1)}, bf16[64,384]{1,0:T(8,128)(2,1)S(1)}, u32[]{:S(2)}, u32[]{:S(2)}) collective-permute-start(bf16[64,384]{1,0:T(8,128)(2,1)S(1)} %get-tuple-element.67), channel_id=1, source_target_pairs={{256,0},{1,257},{258,2},{3,259},{260,4},{5,261},{262,6},{7,263},{2... | collective-permute-start | bytes 147464 | tf_op jit(solution)/shard_map/ppermute | solution.py:318
  108.2 1.2 broadcast_in_dim.2
  109.5 4.6 %all-to-all-start.2 = ((bf16[16,64,640]{2,1,0:T(8,128)(2,1)}), bf16[16,64,640]{2,1,0:T(8,128)(2,1)S(1)}, u32[]{:S(2)}, u32[]{:S(2)}) async-start(bf16[16,64,640]{2,1,0:T(8,128)(2,1)} %broadcast_in_dim.2), calls=%async_computation.2 | async-start | bytes 2621440 | tf_op jit(solution)/shard_map/all_to_all | solution.py:235
  114.1 8.1 %collective-permute-start.8 = (bf16[160,2048]{1,0:T(8,128)(2,1)S(1)}, bf16[160,2048]{1,0:T(8,128)(2,1)S(1)}, u32[]{:S(2)}, u32[]{:S(2)}) collective-permute-start(bf16[160,2048]{1,0:T(8,128)(2,1)S(1)} %pad_maximum_fusion.2), channel_id=1, source_target_pairs={{0,262},{2,260},{4,258},{6,256},{256,6},{258,4},{260,2},{262,0},{1... | collective-permute-start | bytes 1966088 | tf_op jit(solution)/shard_map/ppermute | solution.py:270
  122.2 16.7 %all-to-all-done.2 = bf16[16,64,640]{2,1,0:T(8,128)(2,1)S(1)} async-done(((bf16[16,64,640]{2,1,0:T(8,128)(2,1)}), bf16[16,64,640]{2,1,0:T(8,128)(2,1)S(1)}, u32[]{:S(2)}, u32[]{:S(2)}) %all-to-all-start.2) | async-done | bytes 1310752 | tf_op jit(solution)/shard_map/all_to_all | solution.py:235
  139.0 8.7 %collective-permute-start.13 = (bf16[1024,640]{1,0:T(8,128)(2,1)S(1)}, bf16[1024,640]{1,0:T(8,128)(2,1)}, u32[]{:S(2)}, u32[]{:S(2)}) collective-permute-start(bf16[1024,640]{1,0:T(8,128)(2,1)S(1)} %bitcast.68), channel_id=1, source_target_pairs={{0,1},{1,0},{2,3},{3,2},{4,5},{5,4},{6,7},{7,6},{8,9},{9,8},{10,11... | collective-permute-start | bytes 3932168 | tf_op jit(solution)/shard_map/ppermute | solution.py:231
  147.7 3.7 %collective-permute-done.8 = bf16[160,2048]{1,0:T(8,128)(2,1)S(1)} collective-permute-done((bf16[160,2048]{1,0:T(8,128)(2,1)S(1)}, bf16[160,2048]{1,0:T(8,128)(2,1)S(1)}, u32[]{:S(2)}, u32[]{:S(2)}) %collective-permute-start.8) | collective-permute-done | bytes 655392 | tf_op jit(solution)/shard_map/ppermute | solution.py:270
  151.7 1.3 copy.11
  153.0 1.4 reshape.68
  154.9 2.7 %shard_map.66 = (bf16[320,128]{1,0:T(8,128)(2,1)S(1)}, bf16[4,320,256]{2,1,0:T(8,128)(2,1)}) custom-call(s32[1]{0:T(128)} %bitcast.c_ref, bf16[320,2048]{1,0:T(8,128)(2,1)S(1)} %pad_maximum_fusion.x_ref, bf16[1024,640]{1,0:T(8,128)(2,1)} %collective-permute-done.13.w_ref, f32[320,384]{1,0:T(8,128)S(1)} %shard_map.65.sum_ref), custom_call_target="tpu_custom_call" | custom-call | flops 251658240 | bytes 2621440 | tf_op jit(solution)/shard_map/pallas_call | solution.py:75
  157.6 4.4 %all-to-all-start.3 = ((bf16[4,320,256]{2,1,0:T(8,128)(2,1)}), bf16[4,320,256]{2,1,0:T(8,128)(2,1)S(1)}, u32[]{:S(2)}, u32[]{:S(2)}) async-start(bf16[4,320,256]{2,1,0:T(8,128)(2,1)} %get-tuple-element.36), calls=%async_computation.3 | async-start | bytes 1310720 | tf_op jit(solution)/shard_map/all_to_all | solution.py:235
  162.0 3.9 %collective-permute-start.17 = (bf16[4,128,512]{2,1,0:T(8,128)(2,1)S(1)}, bf16[4,128,512]{2,1,0:T(8,128)(2,1)S(1)}, u32[]{:S(2)}, u32[]{:S(2)}) collective-permute-start(bf16[4,128,512]{2,1,0:T(8,128)(2,1)S(1)} %reshape.68), channel_id=1, source_target_pairs={{0,224},{32,192},{64,160},{96,128},{128,96},{160,64},{192,32},{224... | collective-permute-start | bytes 1572872 | tf_op jit(solution)/shard_map/ppermute | solution.py:270
  166.0 3.1 %collective-permute-start.14 = (bf16[320,128]{1,0:T(8,128)(2,1)S(1)}, bf16[320,128]{1,0:T(8,128)(2,1)S(1)}, u32[]{:S(2)}, u32[]{:S(2)}) collective-permute-start(bf16[320,128]{1,0:T(8,128)(2,1)S(1)} %get-tuple-element.35.q_ref), channel_id=1, source_target_pairs={{0,8},{8,16},{16,24},{24,0},{1,9},{9,17},{17,25},{25,1},{2,10},{10... | collective-permute-start | bytes 245768 | tf_op jit(solution)/shard_map/ppermute | solution.py:249
  169.1 4.3 %collective-permute-start.15 = (bf16[320,128]{1,0:T(8,128)(2,1)S(1)}, bf16[320,128]{1,0:T(8,128)(2,1)S(1)}, u32[]{:S(2)}, u32[]{:S(2)}) collective-permute-start(bf16[320,128]{1,0:T(8,128)(2,1)S(1)} %get-tuple-element.35.q_ref), channel_id=1, source_target_pairs={{0,16},{8,24},{16,0},{24,8},{1,17},{9,25},{17,1},{25,9},{2,18},{10... | collective-permute-start | bytes 245768 | tf_op jit(solution)/shard_map/ppermute | solution.py:249
  173.4 3.1 %collective-permute-start.16 = (bf16[320,128]{1,0:T(8,128)(2,1)S(1)}, bf16[320,128]{1,0:T(8,128)(2,1)S(1)}, u32[]{:S(2)}, u32[]{:S(2)}) collective-permute-start(bf16[320,128]{1,0:T(8,128)(2,1)S(1)} %get-tuple-element.35.q_ref), channel_id=1, source_target_pairs={{0,24},{8,0},{16,8},{24,16},{1,25},{9,1},{17,9},{25,17},{2,26},{10... | collective-permute-start | bytes 245768 | tf_op jit(solution)/shard_map/ppermute | solution.py:249
  176.5 12.5 %collective-permute-done.17 = bf16[4,128,512]{2,1,0:T(8,128)(2,1)S(1)} collective-permute-done((bf16[4,128,512]{2,1,0:T(8,128)(2,1)S(1)}, bf16[4,128,512]{2,1,0:T(8,128)(2,1)S(1)}, u32[]{:S(2)}, u32[]{:S(2)}) %collective-permute-start.17) | collective-permute-done | bytes 524320 | tf_op jit(solution)/shard_map/ppermute | solution.py:270
  189.3 3.6 %collective-permute-start.22 = (bf16[4,256,512]{2,1,0:T(8,128)(2,1)S(1)}, bf16[4,256,512]{2,1,0:T(8,128)(2,1)S(1)}, u32[]{:S(2)}, u32[]{:S(2)}) collective-permute-start(bf16[4,256,512]{2,1,0:T(8,128)(2,1)S(1)} %pad_maximum_fusion.1.near_ref), channel_id=1, source_target_pairs={{0,1},{1,0},{2,3},{3,2},{4,5},{5,4},{6,7},{7,6},{8,9},{9,8},{10,11... | collective-permute-start | bytes 3145736 | tf_op jit(solution)/shard_map/ppermute | solution.py:231
  192.9 1.9 collective-permute-start.18
  194.8 2.1 collective-permute-done.18.far_ref
  196.9 2.7 %shard_map.68 = bf16[4,96,128]{2,1,0:T(8,128)(2,1)S(1)} custom-call(s32[4]{0:T(128)S(1)} %get-tuple-element.40.start_ref, bf16[320,128]{1,0:T(8,128)(2,1)S(1)} %collective-permute-done.15.q_ref, bf16[1280,256]{1,0:T(8,128)(2,1)S(1)} %bitcast.72, bf16[1280,256]{1,0:T(8,128)(2,1)S(1)} %collective-permute-done.18.far_ref, s32[1,2560]{1,0:T(1,128)S(1)} %reshape.63.kpos_ref), custom_call_target="tpu_custom_call" | custom-call | flops 419430400 | bytes 1310720 | tf_op jit(solution)/shard_map/pallas_call | solution.py:149
  199.6 4.6 %collective-permute-start.19 = (bf16[4,96,128]{2,1,0:T(8,128)(2,1)S(1)}, bf16[4,96,128]{2,1,0:T(8,128)(2,1)S(1)}, u32[]{:S(2)}, u32[]{:S(2)}) collective-permute-start(bf16[4,96,128]{2,1,0:T(8,128)(2,1)S(1)} %shard_map.68), channel_id=1, source_target_pairs={{0,16},{8,24},{16,0},{24,8},{1,17},{9,25},{17,1},{25,9},{2,18},{10... | collective-permute-start | bytes 294920 | tf_op jit(solution)/shard_map/ppermute | solution.py:249
  204.2 2.7 %shard_map.69 = bf16[4,96,128]{2,1,0:T(8,128)(2,1)S(1)} custom-call(s32[4]{0:T(128)S(1)} %get-tuple-element.42.start_ref, bf16[320,128]{1,0:T(8,128)(2,1)S(1)} %collective-permute-done.14.q_ref, bf16[1280,256]{1,0:T(8,128)(2,1)S(1)} %bitcast.73, bf16[1280,256]{1,0:T(8,128)(2,1)S(1)} %collective-permute-done.18.far_ref, s32[1,2560]{1,0:T(1,128)S(1)} %reshape.63.kpos_ref), custom_call_target="tpu_custom_call" | custom-call | flops 419430400 | bytes 1310720 | tf_op jit(solution)/shard_map/pallas_call | solution.py:149
  206.9 2.8 %collective-permute-start.20 = (bf16[4,96,128]{2,1,0:T(8,128)(2,1)S(1)}, bf16[4,96,128]{2,1,0:T(8,128)(2,1)S(1)}, u32[]{:S(2)}, u32[]{:S(2)}) collective-permute-start(bf16[4,96,128]{2,1,0:T(8,128)(2,1)S(1)} %shard_map.69), channel_id=1, source_target_pairs={{0,24},{8,0},{16,8},{24,16},{1,25},{9,1},{17,9},{25,17},{2,26},{10... | collective-permute-start | bytes 294920 | tf_op jit(solution)/shard_map/ppermute | solution.py:249
  209.7 2.7 %shard_map.70 = bf16[4,96,128]{2,1,0:T(8,128)(2,1)S(1)} custom-call(s32[4]{0:T(128)S(1)} %get-tuple-element.44.start_ref, bf16[320,128]{1,0:T(8,128)(2,1)S(1)} %collective-permute-done.16.q_ref, bf16[1280,256]{1,0:T(8,128)(2,1)S(1)} %bitcast.74, bf16[1280,256]{1,0:T(8,128)(2,1)S(1)} %collective-permute-done.18.far_ref, s32[1,2560]{1,0:T(1,128)S(1)} %reshape.63.kpos_ref), custom_call_target="tpu_custom_call" | custom-call | flops 419430400 | bytes 1310720 | tf_op jit(solution)/shard_map/pallas_call | solution.py:149
  212.4 2.5 collective-permute-start.21
  214.9 2.7 %shard_map.67.refs_0_ = bf16[4,96,128]{2,1,0:T(8,128)(2,1)S(1)} custom-call(s32[4]{0:T(128)S(1)} %get-tuple-element.26.start_ref, bf16[320,128]{1,0:T(8,128)(2,1)S(1)} %get-tuple-element.35.q_ref, bf16[1280,256]{1,0:T(8,128)(2,1)S(1)} %bitcast.75, bf16[1280,256]{1,0:T(8,128)(2,1)S(1)} %collective-permute-done.18.far_ref, s32[1,2560]{1,0:T(1,128)S(1)} %reshape.63.kpos_ref), custom_call_target="tpu_custom_call" | custom-call | flops 419430400 | bytes 1310720 | tf_op jit(solution)/shard_map/pallas_call | solution.py:149
  217.6 1.3 collective-permute-done.21.refs_3_
  220.1 16.1 %all_to_all.30.context_ref = bf16[4,80,128]{2,1,0:T(8,128)(2,1)S(1)} all-to-all(bf16[4,80,128]{2,1,0:T(8,128)(2,1)S(1)} %shard_map.71), channel_id=1, replica_groups=mesh['zh'=2,'yh'=2,'yl'=4,'x'=4,'zl'=4,'c'=2] {'zh','yh'}, dimensions={0} | all-to-all | bytes 163840 | tf_op jit(solution)/shard_map/all_to_all | solution.py:235
  236.7 19.3 %all_to_all.31 = bf16[8,80,256]{2,1,0:T(8,128)(2,1)S(1)} all-to-all(bf16[8,80,256]{2,1,0:T(8,128)(2,1)S(1)} %shard_map.72), channel_id=1, replica_groups=mesh['zh'=2,'yh'=2,'yl'=4,'x'=4,'zl'=4,'c'=2] {'zl','c'}, dimensions={0} | all-to-all | bytes 655360 | tf_op jit(solution)/shard_map/all_to_all | solution.py:235
  (72 shorter events, 10.0 us)
Async XLA Ops:
  0.0 1.9 copy-start
  4.1 5.0 %copy-start.2 = (bf16[1,256,2048]{2,1,0:T(8,128)(2,1)S(1)}, bf16[1,256,2048]{2,1,0:T(8,128)(2,1)}, u32[]{:S(2)}) copy-start(bf16[1,256,2048]{2,1,0:T(8,128)(2,1)} %param.9) | copy-start | bytes 3145732
  4.1 50.1 %all-to-all-start = ((bf16[4,8,128,384]{3,2,1,0:T(8,128)(2,1)}), bf16[4,8,128,384]{3,2,1,0:T(8,128)(2,1)}, u32[]{:S(2)}, u32[]{:S(2)}) async-start(bf16[4,8,128,384]{3,2,1,0:T(8,128)(2,1)} %shard_map.64), calls=%async_computation | async-start | bytes 6291456 | tf_op jit(solution)/shard_map/all_to_all | solution.py:235
  9.0 11.3 %copy-start.1 = (bf16[160,2048]{1,0:T(8,128)(2,1)S(1)}, bf16[160,2048]{1,0:T(8,128)(2,1)}, u32[]{:S(2)}) copy-start(bf16[160,2048]{1,0:T(8,128)(2,1)} %param.6) | copy-start | bytes 1966084
  9.1 11.4 %copy-start.3 = (f32[2048]{0:T(1024)S(1)}, f32[2048]{0:T(1024)}, u32[]{:S(2)}) copy-start(f32[2048]{0:T(1024)} %param.7) | copy-start | bytes 24580
  9.2 17.2 %copy-start.4 = (s32[64]{0:T(128)S(1)}, s32[64]{0:T(128)}, u32[]{:S(2)}) copy-start(s32[64]{0:T(128)} %param.11) | copy-start | bytes 772
  10.1 18.1 %collective-permute-start = (bf16[2,32,2048]{2,1,0:T(8,128)(2,1)}, bf16[2,32,2048]{2,1,0:T(8,128)(2,1)S(1)}, u32[]{:S(2)}, u32[]{:S(2)}) collective-permute-start(bf16[2,32,2048]{2,1,0:T(8,128)(2,1)} %get-tuple-element.56), channel_id=1, source_target_pairs={{0,96},{32,0},{64,32},{96,64},{1,97},{33,1},{65,33},{97,65},{2,98}... | collective-permute-start | bytes 786440 | tf_op jit(solution)/shard_map/ppermute | solution.py:249
  16.1 12.2 %collective-permute-start.1 = (bf16[2,32,2048]{2,1,0:T(8,128)(2,1)}, bf16[2,32,2048]{2,1,0:T(8,128)(2,1)S(1)}, u32[]{:S(2)}, u32[]{:S(2)}) collective-permute-start(bf16[2,32,2048]{2,1,0:T(8,128)(2,1)} %get-tuple-element.57), channel_id=1, source_target_pairs={{0,32},{32,64},{64,96},{96,0},{1,33},{33,65},{65,97},{97,1},{2,34}... | collective-permute-start | bytes 786440 | tf_op jit(solution)/shard_map/ppermute | solution.py:249
  18.0 35.8 %collective-permute-start.2 = (bf16[2,32,2048]{2,1,0:T(8,128)(2,1)S(1)}, bf16[2,32,2048]{2,1,0:T(8,128)(2,1)S(1)}, u32[]{:S(2)}, u32[]{:S(2)}) collective-permute-start(bf16[2,32,2048]{2,1,0:T(8,128)(2,1)S(1)} %get-tuple-element.55), channel_id=1, source_target_pairs={{0,64},{32,96},{64,0},{96,32},{1,65},{33,97},{65,1},{97,33},{2,66}... | collective-permute-start | bytes 786440 | tf_op jit(solution)/shard_map/ppermute | solution.py:249
  20.7 33.2 %collective-permute-start.3 = (bf16[80,2048]{1,0:T(8,128)(2,1)S(1)}, bf16[80,2048]{1,0:T(8,128)(2,1)S(1)}, u32[]{:S(2)}, u32[]{:S(2)}) collective-permute-start(bf16[80,2048]{1,0:T(8,128)(2,1)S(1)} %fusion.2), channel_id=1, source_target_pairs={{0,128},{128,0},{1,129},{129,1},{2,130},{130,2},{3,131},{131,3},{4... | collective-permute-start | bytes 983048 | tf_op jit(solution)/shard_map/ppermute | solution.py:231
  56.3 28.5 %all-to-all-start.1 = ((bf16[8,128,384]{2,1,0:T(8,128)(2,1)}), bf16[8,128,384]{2,1,0:T(8,128)(2,1)S(1)}, u32[]{:S(2)}, u32[]{:S(2)}) async-start(bf16[8,128,384]{2,1,0:T(8,128)(2,1)} %dynamic-slice_bitcast_fusion), calls=%async_computation.1 | async-start | bytes 1572864 | tf_op jit(solution)/shard_map/all_to_all | solution.py:235
  62.0 10.0 %collective-permute-start.4 = (bf16[2,32,512]{2,1,0:T(8,128)(2,1)S(1)}, bf16[2,32,512]{2,1,0:T(8,128)(2,1)S(1)}, u32[]{:S(2)}, u32[]{:S(2)}) collective-permute-start(bf16[2,32,512]{2,1,0:T(8,128)(2,1)S(1)} %bitcast.80), channel_id=1, source_target_pairs={{0,24},{8,0},{16,8},{24,16},{1,25},{9,1},{17,9},{25,17},{2,26},{10... | collective-permute-start | bytes 196616 | tf_op jit(solution)/shard_map/ppermute | solution.py:249
  66.3 6.5 %collective-permute-start.5 = (bf16[2,32,512]{2,1,0:T(8,128)(2,1)S(1)}, bf16[2,32,512]{2,1,0:T(8,128)(2,1)S(1)}, u32[]{:S(2)}, u32[]{:S(2)}) collective-permute-start(bf16[2,32,512]{2,1,0:T(8,128)(2,1)S(1)} %bitcast.81), channel_id=1, source_target_pairs={{0,8},{8,16},{16,24},{24,0},{1,9},{9,17},{17,25},{25,1},{2,10},{10... | collective-permute-start | bytes 196616 | tf_op jit(solution)/shard_map/ppermute | solution.py:249
  68.3 6.8 %collective-permute-start.6 = (bf16[2,32,512]{2,1,0:T(8,128)(2,1)S(1)}, bf16[2,32,512]{2,1,0:T(8,128)(2,1)S(1)}, u32[]{:S(2)}, u32[]{:S(2)}) collective-permute-start(bf16[2,32,512]{2,1,0:T(8,128)(2,1)S(1)} %bitcast.82), channel_id=1, source_target_pairs={{0,16},{8,24},{16,0},{24,8},{1,17},{9,25},{17,1},{25,9},{2,18},{10... | collective-permute-start | bytes 196616 | tf_op jit(solution)/shard_map/ppermute | solution.py:249
  75.1 8.6 %collective-permute-start.7 = (bf16[32,512]{1,0:T(8,128)(2,1)S(1)}, bf16[32,512]{1,0:T(8,128)(2,1)S(1)}, u32[]{:S(2)}, u32[]{:S(2)}) collective-permute-start(bf16[32,512]{1,0:T(8,128)(2,1)S(1)} %slice_bitcast_fusion), channel_id=1, source_target_pairs={{0,224},{32,192},{64,160},{96,128},{128,96},{160,64},{192,32},{224... | collective-permute-start | bytes 98312 | tf_op jit(solution)/shard_map/ppermute | solution.py:270
  84.8 22.2 %collective-permute-start.12 = (bf16[32,512]{1,0:T(8,128)(2,1)S(1)}, bf16[32,512]{1,0:T(8,128)(2,1)S(1)}, u32[]{:S(2)}, u32[]{:S(2)}) collective-permute-start(bf16[32,512]{1,0:T(8,128)(2,1)S(1)} %fusion.16), channel_id=1, source_target_pairs={{0,256},{256,0},{1,257},{257,1},{2,258},{258,2},{3,259},{259,3},{4... | collective-permute-start | bytes 98312 | tf_op jit(solution)/shard_map/ppermute | solution.py:231
  95.5 12.7 %collective-permute-start.11 = (bf16[64,384]{1,0:T(8,128)(2,1)S(1)}, bf16[64,384]{1,0:T(8,128)(2,1)S(1)}, u32[]{:S(2)}, u32[]{:S(2)}) collective-permute-start(bf16[64,384]{1,0:T(8,128)(2,1)S(1)} %get-tuple-element.66), channel_id=1, source_target_pairs={{256,1},{1,256},{258,3},{3,258},{260,5},{5,260},{262,7},{7,262},{2... | collective-permute-start | bytes 147464 | tf_op jit(solution)/shard_map/ppermute | solution.py:319
  97.8 10.4 %collective-permute-start.9 = (bf16[64,384]{1,0:T(8,128)(2,1)S(1)}, bf16[64,384]{1,0:T(8,128)(2,1)S(1)}, u32[]{:S(2)}, u32[]{:S(2)}) collective-permute-start(bf16[64,384]{1,0:T(8,128)(2,1)S(1)} %get-tuple-element.66), channel_id=1, source_target_pairs={{0,1},{257,256},{2,3},{259,258},{4,5},{261,260},{6,7},{263,262},{8... | collective-permute-start | bytes 147464 | tf_op jit(solution)/shard_map/ppermute | solution.py:321
  99.1 9.1 %collective-permute-start.10 = (bf16[64,384]{1,0:T(8,128)(2,1)S(1)}, bf16[64,384]{1,0:T(8,128)(2,1)S(1)}, u32[]{:S(2)}, u32[]{:S(2)}) collective-permute-start(bf16[64,384]{1,0:T(8,128)(2,1)S(1)} %get-tuple-element.67), channel_id=1, source_target_pairs={{256,0},{1,257},{258,2},{3,259},{260,4},{5,261},{262,6},{7,263},{2... | collective-permute-start | bytes 147464 | tf_op jit(solution)/shard_map/ppermute | solution.py:318
  109.5 29.5 %all-to-all-start.2 = ((bf16[16,64,640]{2,1,0:T(8,128)(2,1)}), bf16[16,64,640]{2,1,0:T(8,128)(2,1)S(1)}, u32[]{:S(2)}, u32[]{:S(2)}) async-start(bf16[16,64,640]{2,1,0:T(8,128)(2,1)} %broadcast_in_dim.2), calls=%async_computation.2 | async-start | bytes 2621440 | tf_op jit(solution)/shard_map/all_to_all | solution.py:235
  114.1 37.3 %collective-permute-start.8 = (bf16[160,2048]{1,0:T(8,128)(2,1)S(1)}, bf16[160,2048]{1,0:T(8,128)(2,1)S(1)}, u32[]{:S(2)}, u32[]{:S(2)}) collective-permute-start(bf16[160,2048]{1,0:T(8,128)(2,1)S(1)} %pad_maximum_fusion.2), channel_id=1, source_target_pairs={{0,262},{2,260},{4,258},{6,256},{256,6},{258,4},{260,2},{262,0},{1... | collective-permute-start | bytes 1966088 | tf_op jit(solution)/shard_map/ppermute | solution.py:270
  139.0 16.0 %collective-permute-start.13 = (bf16[1024,640]{1,0:T(8,128)(2,1)S(1)}, bf16[1024,640]{1,0:T(8,128)(2,1)}, u32[]{:S(2)}, u32[]{:S(2)}) collective-permute-start(bf16[1024,640]{1,0:T(8,128)(2,1)S(1)} %bitcast.68), channel_id=1, source_target_pairs={{0,1},{1,0},{2,3},{3,2},{4,5},{5,4},{6,7},{7,6},{8,9},{9,8},{10,11... | collective-permute-start | bytes 3932168 | tf_op jit(solution)/shard_map/ppermute | solution.py:231
  157.6 31.7 %all-to-all-start.3 = ((bf16[4,320,256]{2,1,0:T(8,128)(2,1)}), bf16[4,320,256]{2,1,0:T(8,128)(2,1)S(1)}, u32[]{:S(2)}, u32[]{:S(2)}) async-start(bf16[4,320,256]{2,1,0:T(8,128)(2,1)} %get-tuple-element.36), calls=%async_computation.3 | async-start | bytes 1310720 | tf_op jit(solution)/shard_map/all_to_all | solution.py:235
  162.0 27.0 %collective-permute-start.17 = (bf16[4,128,512]{2,1,0:T(8,128)(2,1)S(1)}, bf16[4,128,512]{2,1,0:T(8,128)(2,1)S(1)}, u32[]{:S(2)}, u32[]{:S(2)}) collective-permute-start(bf16[4,128,512]{2,1,0:T(8,128)(2,1)S(1)} %reshape.68), channel_id=1, source_target_pairs={{0,224},{32,192},{64,160},{96,128},{128,96},{160,64},{192,32},{224... | collective-permute-start | bytes 1572872 | tf_op jit(solution)/shard_map/ppermute | solution.py:270
  166.0 23.3 %collective-permute-start.14 = (bf16[320,128]{1,0:T(8,128)(2,1)S(1)}, bf16[320,128]{1,0:T(8,128)(2,1)S(1)}, u32[]{:S(2)}, u32[]{:S(2)}) collective-permute-start(bf16[320,128]{1,0:T(8,128)(2,1)S(1)} %get-tuple-element.35.q_ref), channel_id=1, source_target_pairs={{0,8},{8,16},{16,24},{24,0},{1,9},{9,17},{17,25},{25,1},{2,10},{10... | collective-permute-start | bytes 245768 | tf_op jit(solution)/shard_map/ppermute | solution.py:249
  169.1 20.2 %collective-permute-start.15 = (bf16[320,128]{1,0:T(8,128)(2,1)S(1)}, bf16[320,128]{1,0:T(8,128)(2,1)S(1)}, u32[]{:S(2)}, u32[]{:S(2)}) collective-permute-start(bf16[320,128]{1,0:T(8,128)(2,1)S(1)} %get-tuple-element.35.q_ref), channel_id=1, source_target_pairs={{0,16},{8,24},{16,0},{24,8},{1,17},{9,25},{17,1},{25,9},{2,18},{10... | collective-permute-start | bytes 245768 | tf_op jit(solution)/shard_map/ppermute | solution.py:249
  173.4 15.9 %collective-permute-start.16 = (bf16[320,128]{1,0:T(8,128)(2,1)S(1)}, bf16[320,128]{1,0:T(8,128)(2,1)S(1)}, u32[]{:S(2)}, u32[]{:S(2)}) collective-permute-start(bf16[320,128]{1,0:T(8,128)(2,1)S(1)} %get-tuple-element.35.q_ref), channel_id=1, source_target_pairs={{0,24},{8,0},{16,8},{24,16},{1,25},{9,1},{17,9},{25,17},{2,26},{10... | collective-permute-start | bytes 245768 | tf_op jit(solution)/shard_map/ppermute | solution.py:249
  189.3 46.9 %collective-permute-start.22 = (bf16[4,256,512]{2,1,0:T(8,128)(2,1)S(1)}, bf16[4,256,512]{2,1,0:T(8,128)(2,1)S(1)}, u32[]{:S(2)}, u32[]{:S(2)}) collective-permute-start(bf16[4,256,512]{2,1,0:T(8,128)(2,1)S(1)} %pad_maximum_fusion.1.near_ref), channel_id=1, source_target_pairs={{0,1},{1,0},{2,3},{3,2},{4,5},{5,4},{6,7},{7,6},{8,9},{9,8},{10,11... | collective-permute-start | bytes 3145736 | tf_op jit(solution)/shard_map/ppermute | solution.py:231
  192.9 4.0 %collective-permute-start.18 = (bf16[1280,256]{1,0:T(8,128)(2,1)S(1)}, bf16[1280,256]{1,0:T(8,128)(2,1)S(1)}, u32[]{:S(2)}, u32[]{:S(2)}) collective-permute-start(bf16[1280,256]{1,0:T(8,128)(2,1)S(1)} %bitcast.71), channel_id=1, source_target_pairs={{0,1},{1,0},{2,3},{3,2},{4,5},{5,4},{6,7},{7,6},{8,9},{9,8},{10,11... | collective-permute-start | bytes 1966088 | tf_op jit(solution)/shard_map/ppermute | solution.py:231
  199.6 18.1 %collective-permute-start.19 = (bf16[4,96,128]{2,1,0:T(8,128)(2,1)S(1)}, bf16[4,96,128]{2,1,0:T(8,128)(2,1)S(1)}, u32[]{:S(2)}, u32[]{:S(2)}) collective-permute-start(bf16[4,96,128]{2,1,0:T(8,128)(2,1)S(1)} %shard_map.68), channel_id=1, source_target_pairs={{0,16},{8,24},{16,0},{24,8},{1,17},{9,25},{17,1},{25,9},{2,18},{10... | collective-permute-start | bytes 294920 | tf_op jit(solution)/shard_map/ppermute | solution.py:249
  206.9 10.7 %collective-permute-start.20 = (bf16[4,96,128]{2,1,0:T(8,128)(2,1)S(1)}, bf16[4,96,128]{2,1,0:T(8,128)(2,1)S(1)}, u32[]{:S(2)}, u32[]{:S(2)}) collective-permute-start(bf16[4,96,128]{2,1,0:T(8,128)(2,1)S(1)} %shard_map.69), channel_id=1, source_target_pairs={{0,24},{8,0},{16,8},{24,16},{1,25},{9,1},{17,9},{25,17},{2,26},{10... | collective-permute-start | bytes 294920 | tf_op jit(solution)/shard_map/ppermute | solution.py:249
  212.4 6.6 %collective-permute-start.21 = (bf16[4,96,128]{2,1,0:T(8,128)(2,1)S(1)}, bf16[4,96,128]{2,1,0:T(8,128)(2,1)S(1)}, u32[]{:S(2)}, u32[]{:S(2)}) collective-permute-start(bf16[4,96,128]{2,1,0:T(8,128)(2,1)S(1)} %shard_map.70), channel_id=1, source_target_pairs={{0,8},{8,16},{16,24},{24,0},{1,9},{9,17},{17,25},{25,1},{2,10},{10... | collective-permute-start | bytes 294920 | tf_op jit(solution)/shard_map/ppermute | solution.py:249

commit v12 on v10

--- a/solution.py
+++ b/solution.py
@@ -11,6 +11,7 @@
 HIDE = -1e30
 CHUNK = 640
 EXTRA = 16
+WHOLE = pltpu.CompilerParams(vmem_limit_bytes=56 * 1024 * 1024)
 LIMIT = pltpu.CompilerParams(vmem_limit_bytes=24 * 1024 * 1024)
 
 
@@ -29,7 +30,7 @@
         in_specs=[pl.BlockSpec((3, 2, ny // steps, part, 2 * HD), lambda i: (0, 0, i, 0, 0))],
         out_specs=pl.BlockSpec((4, ny // steps, part, 3 * HD), lambda i: (0, i, 0, 0)),
         out_shape=jax.ShapeDtypeStruct((4, ny, part, 3 * HD), w.dtype),
-        compiler_params=LIMIT,
+        compiler_params=WHOLE,
         cost_estimate=pl.CostEstimate(flops=0, bytes_accessed=4 * w.size, transcendentals=0),
     )(w.reshape(3, 2, ny, part, 2 * HD))
 
@@ -139,7 +140,7 @@
 
 def attend(start, q, near, far, kpos, half):
     nq, nk = q.shape[0], 2 * near.shape[0]
-    tile = 2 * half
+    tile = 4 * half
     return pl.pallas_call(
         attend_kernel,
         grid=(nq // tile,),
@@ -150,7 +151,7 @@
             pl.BlockSpec((nk // 2, 2 * HD), lambda i: (0, 0)),
             pl.BlockSpec((1, nk), lambda i: (0, 0)),
         ],
-        out_specs=pl.BlockSpec((2, half + EXTRA, HD), lambda i: (i, 0, 0)),
+        out_specs=pl.BlockSpec((4, half + EXTRA, HD), lambda i: (i, 0, 0)),
         out_shape=jax.ShapeDtypeStruct((nq // half, half + EXTRA, HD), jnp.bfloat16),
         scratch_shapes=[pltpu.VMEM((tile, nk), jnp.float32)],
         compiler_params=LIMIT,

time: 223 us -> 222 us (level)
  no operation moved by 1% of the time
where the time goes in v12:
time: 222 us; the launch traced here: 221 us
  starting transfers between devices  93.8 us (42%)
  waiting for transfers between devices  81.8 us (37%)
  Pallas kernels  15.4 us (7%)
  blocking collectives  14.4 us (6%)
  local copies, waits for them, and re-layouts  7.27 us (3%)
  other arithmetic  6.44 us (3%)
    all_to_all x5, waiting for transfers between devices, exchange(): return lax.all_to_all(block, axis, 0, 0, tiled=True)  40.1 us
    ppermute x12, starting transfers between devices, shift(): lax.ppermute(block, axis, [(i, (i + distance) % count) for i in range(cou...  34.1 us
    ppermute x12, waiting for transfers between devices, shift(): lax.ppermute(block, axis, [(i, (i + distance) % count) for i in range(cou...  29.3 us
    all_to_all x5, starting transfers between devices, exchange(): return lax.all_to_all(block, axis, 0, 0, tiled=True)  28.5 us
    ppermute x2, starting transfers between devices, trade(): return lax.ppermute(block, ('zh', 'x', 'zl', 'c'), route)  14.8 us
    all_to_all x1, blocking collectives, exchange(): return lax.all_to_all(block, axis, 0, 0, tiled=True)  14.4 us
    pallas_call x2, Pallas kernels, attend(): pl.pallas_call(attend_kernel, grid=(nq // tile,), in_specs=[pl.BlockSpec(...  8 us
    ppermute x3, starting transfers between devices, swap(): return lax.ppermute(block, axis, [(0, 1), (1, 0)])  6.7 us
  transfers between devices with their start and end apart: 25, of which 16 were waited for; matrix products, arithmetic and copies ran while one was open for 4% of the time, Pallas kernels for 5%

profile of v12, /device:TPU:1, one launch (start us, length us, event | category | flops | bytes accessed | tf_op | source)
XLA Modules:
  0.0 220.6 jit_solution(8148510352173463661)
XLA Ops:
  0.0 3.3 %shard_map.64 = bf16[4,8,128,384]{3,2,1,0:T(8,128)(2,1)} custom-call(bf16[3,2,8,128,256]{4,3,2,1,0:T(8,128)(2,1)} %bitcast.93), custom_call_target="tpu_custom_call" | custom-call | bytes 6291456 | tf_op jit(solution)/shard_map/pallas_call | solution.py:27
  3.3 4.8 %all-to-all-start = ((bf16[4,8,128,384]{3,2,1,0:T(8,128)(2,1)}), bf16[4,8,128,384]{3,2,1,0:T(8,128)(2,1)S(1)}, u32[]{:S(2)}, u32[]{:S(2)}) async-start(bf16[4,8,128,384]{3,2,1,0:T(8,128)(2,1)} %shard_map.64), calls=%async_computation | async-start | bytes 6291456 | tf_op jit(solution)/shard_map/all_to_all | solution.py:228
  8.1 1.3 dynamic-slice_bitcast_fusion.1
  11.3 5.2 %collective-permute-start = (bf16[2,32,2048]{2,1,0:T(8,128)(2,1)}, bf16[2,32,2048]{2,1,0:T(8,128)(2,1)}, u32[]{:S(2)}, u32[]{:S(2)}) collective-permute-start(bf16[2,32,2048]{2,1,0:T(8,128)(2,1)} %get-tuple-element.46), channel_id=1, source_target_pairs={{0,96},{32,0},{64,32},{96,64},{1,97},{33,1},{65,33},{97,65},{2,98}... | collective-permute-start | bytes 786440 | tf_op jit(solution)/shard_map/ppermute | solution.py:242
  16.5 1.9 collective-permute-start.1
  18.5 2.4 %collective-permute-start.2 = (bf16[2,32,2048]{2,1,0:T(8,128)(2,1)}, bf16[2,32,2048]{2,1,0:T(8,128)(2,1)}, u32[]{:S(2)}, u32[]{:S(2)}) collective-permute-start(bf16[2,32,2048]{2,1,0:T(8,128)(2,1)} %get-tuple-element.45), channel_id=1, source_target_pairs={{0,64},{32,96},{64,0},{96,32},{1,65},{33,97},{65,1},{97,33},{2,66}... | collective-permute-start | bytes 786440 | tf_op jit(solution)/shard_map/ppermute | solution.py:242
  20.9 1.1 fusion
  22.1 1.1 fusion.2
  24.3 3.0 %collective-permute-done.1 = bf16[2,32,2048]{2,1,0:T(8,128)(2,1)} collective-permute-done((bf16[2,32,2048]{2,1,0:T(8,128)(2,1)}, bf16[2,32,2048]{2,1,0:T(8,128)(2,1)}, u32[]{:S(2)}, u32[]{:S(2)}) %collective-permute-start.1) | collective-permute-done | bytes 262176 | tf_op jit(solution)/shard_map/ppermute | solution.py:242
  27.3 13.3 %collective-permute-done.2 = bf16[2,32,2048]{2,1,0:T(8,128)(2,1)} collective-permute-done((bf16[2,32,2048]{2,1,0:T(8,128)(2,1)}, bf16[2,32,2048]{2,1,0:T(8,128)(2,1)}, u32[]{:S(2)}, u32[]{:S(2)}) %collective-permute-start.2) | collective-permute-done | bytes 262176 | tf_op jit(solution)/shard_map/ppermute | solution.py:242
  40.6 1.8 fusion.7
  43.3 9.4 %all-to-all-start.1 = ((bf16[8,128,384]{2,1,0:T(8,128)(2,1)}), bf16[8,128,384]{2,1,0:T(8,128)(2,1)S(1)}, u32[]{:S(2)}, u32[]{:S(2)}) async-start(bf16[8,128,384]{2,1,0:T(8,128)(2,1)} %dynamic-slice_bitcast_fusion), calls=%async_computation.1 | async-start | bytes 1572864 | tf_op jit(solution)/shard_map/all_to_all | solution.py:228
  53.5 2.8 %collective-permute-start.3 = (bf16[2,32,512]{2,1,0:T(8,128)(2,1)S(1)}, bf16[2,32,512]{2,1,0:T(8,128)(2,1)S(1)}, u32[]{:S(2)}, u32[]{:S(2)}) collective-permute-start(bf16[2,32,512]{2,1,0:T(8,128)(2,1)S(1)} %bitcast.111), channel_id=1, source_target_pairs={{0,24},{8,0},{16,8},{24,16},{1,25},{9,1},{17,9},{25,17},{2,26},{10... | collective-permute-start | bytes 196616 | tf_op jit(solution)/shard_map/ppermute | solution.py:242
  56.3 2.5 %collective-permute-start.4 = (bf16[2,32,512]{2,1,0:T(8,128)(2,1)S(1)}, bf16[2,32,512]{2,1,0:T(8,128)(2,1)S(1)}, u32[]{:S(2)}, u32[]{:S(2)}) collective-permute-start(bf16[2,32,512]{2,1,0:T(8,128)(2,1)S(1)} %bitcast.112), channel_id=1, source_target_pairs={{0,8},{8,16},{16,24},{24,0},{1,9},{9,17},{17,25},{25,1},{2,10},{10... | collective-permute-start | bytes 196616 | tf_op jit(solution)/shard_map/ppermute | solution.py:242
  58.8 2.5 %collective-permute-start.5 = (bf16[2,32,512]{2,1,0:T(8,128)(2,1)S(1)}, bf16[2,32,512]{2,1,0:T(8,128)(2,1)S(1)}, u32[]{:S(2)}, u32[]{:S(2)}) collective-permute-start(bf16[2,32,512]{2,1,0:T(8,128)(2,1)S(1)} %bitcast.113), channel_id=1, source_target_pairs={{0,16},{8,24},{16,0},{24,8},{1,17},{9,25},{17,1},{25,9},{2,18},{10... | collective-permute-start | bytes 196616 | tf_op jit(solution)/shard_map/ppermute | solution.py:242
  61.4 1.4 collective-permute-done.4
  62.8 2.8 %collective-permute-done.5 = bf16[2,32,512]{2,1,0:T(8,128)(2,1)S(1)} collective-permute-done((bf16[2,32,512]{2,1,0:T(8,128)(2,1)S(1)}, bf16[2,32,512]{2,1,0:T(8,128)(2,1)S(1)}, u32[]{:S(2)}, u32[]{:S(2)}) %collective-permute-start.5) | collective-permute-done | bytes 65568 | tf_op jit(solution)/shard_map/ppermute | solution.py:242
  65.7 4.6 %collective-permute-start.6 = (bf16[32,512]{1,0:T(8,128)(2,1)S(1)}, bf16[32,512]{1,0:T(8,128)(2,1)S(1)}, u32[]{:S(2)}, u32[]{:S(2)}) collective-permute-start(bf16[32,512]{1,0:T(8,128)(2,1)S(1)} %slice_bitcast_fusion), channel_id=1, source_target_pairs={{0,224},{32,192},{64,160},{96,128},{128,96},{160,64},{192,32},{224... | collective-permute-start | bytes 98312 | tf_op jit(solution)/shard_map/ppermute | solution.py:325
  70.3 2.7 %collective-permute-done.6 = bf16[32,512]{1,0:T(8,128)(2,1)S(1)} collective-permute-done((bf16[32,512]{1,0:T(8,128)(2,1)S(1)}, bf16[32,512]{1,0:T(8,128)(2,1)S(1)}, u32[]{:S(2)}, u32[]{:S(2)}) %collective-permute-start.6) | collective-permute-done | bytes 32800 | tf_op jit(solution)/shard_map/ppermute | solution.py:325
  73.1 1.4 all-to-all-done.1
  74.6 12.8 %collective-permute-start.11 = (bf16[128,512]{1,0:T(8,128)(2,1)S(1)}, bf16[128,512]{1,0:T(8,128)(2,1)S(1)}, u32[]{:S(2)}, u32[]{:S(2)}) collective-permute-start(bf16[128,512]{1,0:T(8,128)(2,1)S(1)} %pad_maximum_fusion.4), channel_id=1, source_target_pairs={{0,262},{1,270},{2,260},{3,268},{4,258},{5,266},{6,256},{7,264},{8... | collective-permute-start | bytes 393224 | tf_op jit(solution)/shard_map/ppermute | solution.py:282
  87.4 1.9 collective-permute-start.10
  89.4 3.5 %collective-permute-done.11 = bf16[128,512]{1,0:T(8,128)(2,1)S(1)} collective-permute-done((bf16[128,512]{1,0:T(8,128)(2,1)S(1)}, bf16[128,512]{1,0:T(8,128)(2,1)S(1)}, u32[]{:S(2)}, u32[]{:S(2)}) %collective-permute-start.11) | collective-permute-done | bytes 131104 | tf_op jit(solution)/shard_map/ppermute | solution.py:282
  94.8 7.4 %all-to-all-start.2 = ((bf16[8,128,512]{2,1,0:T(8,128)(2,1)}), bf16[8,128,512]{2,1,0:T(8,128)(2,1)S(1)}, u32[]{:S(2)}, u32[]{:S(2)}) async-start(bf16[8,128,512]{2,1,0:T(8,128)(2,1)} %broadcast_in_dim.2), calls=%async_computation.2 | async-start | bytes 2097152 | tf_op jit(solution)/shard_map/all_to_all | solution.py:228
  102.1 1.9 collective-permute-start.9
  104.0 4.9 %collective-permute-start.8 = (bf16[80,2048]{1,0:T(8,128)(2,1)S(1)}, bf16[80,2048]{1,0:T(8,128)(2,1)S(1)}, u32[]{:S(2)}, u32[]{:S(2)}) collective-permute-start(bf16[80,2048]{1,0:T(8,128)(2,1)S(1)} %fusion.2), channel_id=1, source_target_pairs={{0,16},{8,24},{16,0},{24,8},{1,17},{9,25},{17,1},{25,9},{2,18},{10... | collective-permute-start | bytes 983048 | tf_op jit(solution)/shard_map/ppermute | solution.py:242
  109.0 2.8 %collective-permute-start.7 = (bf16[80,2048]{1,0:T(8,128)(2,1)S(1)}, bf16[80,2048]{1,0:T(8,128)(2,1)S(1)}, u32[]{:S(2)}, u32[]{:S(2)}) collective-permute-start(bf16[80,2048]{1,0:T(8,128)(2,1)S(1)} %fusion.2), channel_id=1, source_target_pairs={{0,8},{8,16},{16,24},{24,0},{1,9},{9,17},{17,25},{25,1},{2,10},{10... | collective-permute-start | bytes 983048 | tf_op jit(solution)/shard_map/ppermute | solution.py:242
  111.7 19.6 %all-to-all-done.2 = bf16[8,128,512]{2,1,0:T(8,128)(2,1)S(1)} async-done(((bf16[8,128,512]{2,1,0:T(8,128)(2,1)}), bf16[8,128,512]{2,1,0:T(8,128)(2,1)S(1)}, u32[]{:S(2)}, u32[]{:S(2)}) %all-to-all-start.2) | async-done | bytes 1048608 | tf_op jit(solution)/shard_map/all_to_all | solution.py:228
  131.4 2.4 %collective-permute-start.12 = (bf16[1024,512]{1,0:T(8,128)(2,1)S(1)}, bf16[1024,512]{1,0:T(8,128)(2,1)S(1)}, u32[]{:S(2)}, u32[]{:S(2)}) collective-permute-start(bf16[1024,512]{1,0:T(8,128)(2,1)S(1)} %bitcast.85), channel_id=1, source_target_pairs={{0,1},{1,0},{2,3},{3,2},{4,5},{5,4},{6,7},{7,6},{8,9},{9,8},{10,11... | collective-permute-start | bytes 3145736 | tf_op jit(solution)/shard_map/ppermute | solution.py:224
  136.0 1.6 shard_map.66
  137.6 3.6 %all-to-all-start.3 = ((bf16[8,320,256]{2,1,0:T(8,128)(2,1)}), bf16[8,320,256]{2,1,0:T(8,128)(2,1)S(1)}, u32[]{:S(2)}, u32[]{:S(2)}) async-start(bf16[8,320,256]{2,1,0:T(8,128)(2,1)} %get-tuple-element.30), calls=%async_computation.3 | async-start | bytes 2621440 | tf_op jit(solution)/shard_map/all_to_all | solution.py:228
  141.2 1.9 collective-permute-start.16
  143.2 1.9 collective-permute-start.15
  145.1 3.4 %collective-permute-start.14 = (bf16[256,512]{1,0:T(8,128)(2,1)S(1)}, bf16[256,512]{1,0:T(8,128)(2,1)S(1)}, u32[]{:S(2)}, u32[]{:S(2)}) collective-permute-start(bf16[256,512]{1,0:T(8,128)(2,1)S(1)} %bitcast.101), channel_id=1, source_target_pairs={{0,8},{8,16},{16,24},{24,0},{1,9},{9,17},{17,25},{25,1},{2,10},{10... | collective-permute-start | bytes 786440 | tf_op jit(solution)/shard_map/ppermute | solution.py:242
  148.5 3.1 %collective-permute-start.13 = (bf16[320,128]{1,0:T(8,128)(2,1)S(1)}, bf16[320,128]{1,0:T(8,128)(2,1)S(1)}, u32[]{:S(2)}, u32[]{:S(2)}) collective-permute-start(bf16[320,128]{1,0:T(8,128)(2,1)S(1)} %get-tuple-element.29.q_ref), channel_id=1, source_target_pairs={{0,262},{2,260},{4,258},{6,256},{256,6},{258,4},{260,2},{262,0},{1... | collective-permute-start | bytes 245768 | tf_op jit(solution)/shard_map/ppermute | solution.py:286
  151.6 2.5 %collective-permute-done.15 = bf16[256,512]{1,0:T(8,128)(2,1)S(1)} collective-permute-done((bf16[256,512]{1,0:T(8,128)(2,1)S(1)}, bf16[256,512]{1,0:T(8,128)(2,1)S(1)}, u32[]{:S(2)}, u32[]{:S(2)}) %collective-permute-start.15) | collective-permute-done | bytes 262176 | tf_op jit(solution)/shard_map/ppermute | solution.py:242
  154.1 6.3 %collective-permute-done.14 = bf16[256,512]{1,0:T(8,128)(2,1)S(1)} collective-permute-done((bf16[256,512]{1,0:T(8,128)(2,1)S(1)}, bf16[256,512]{1,0:T(8,128)(2,1)S(1)}, u32[]{:S(2)}, u32[]{:S(2)}) %collective-permute-start.14) | collective-permute-done | bytes 262176 | tf_op jit(solution)/shard_map/ppermute | solution.py:242
  161.4 14.6 %all-to-all-done.3 = bf16[8,320,256]{2,1,0:T(8,128)(2,1)S(1)} async-done(((bf16[8,320,256]{2,1,0:T(8,128)(2,1)}), bf16[8,320,256]{2,1,0:T(8,128)(2,1)S(1)}, u32[]{:S(2)}, u32[]{:S(2)}) %all-to-all-start.3) | async-done | bytes 1310752 | tf_op jit(solution)/shard_map/all_to_all | solution.py:228
  176.0 2.4 %collective-permute-start.17 = (bf16[2560,256]{1,0:T(8,128)(2,1)S(1)}, bf16[2560,256]{1,0:T(8,128)(2,1)S(1)}, u32[]{:S(2)}, u32[]{:S(2)}) collective-permute-start(bf16[2560,256]{1,0:T(8,128)(2,1)S(1)} %bitcast.88), channel_id=1, source_target_pairs={{0,1},{1,0},{2,3},{3,2},{4,5},{5,4},{6,7},{7,6},{8,9},{9,8},{10,11... | collective-permute-start | bytes 3932168 | tf_op jit(solution)/shard_map/ppermute | solution.py:224
  178.3 1.9 collective-permute-start.19
  181.9 4.0 %shard_map.68 = bf16[4,96,128]{2,1,0:T(8,128)(2,1)S(1)} custom-call(s32[4]{0:T(128)S(1)} %get-tuple-element.34.start_ref, bf16[320,128]{1,0:T(8,128)(2,1)S(1)} %copy-done.1, bf16[2560,256]{1,0:T(8,128)(2,1)S(1)} %bitcast.89, bf16[2560,256]{1,0:T(8,128)(2,1)S(1)} %collective-permute-done.17.far_ref, s32[1,5120]{1,0:T(1,128)S(1)} %bitcast.91), custom_call_target="tpu_custom_call" | custom-call | flops 838860800 | bytes 2621440 | tf_op jit(solution)/shard_map/pallas_call | solution.py:144
  185.9 2.1 collective-permute-start.18
  188.0 4.0 %shard_map.67.near_ref = bf16[4,96,128]{2,1,0:T(8,128)(2,1)S(1)} custom-call(s32[4]{0:T(128)S(1)} %get-tuple-element.21.start_ref, bf16[320,128]{1,0:T(8,128)(2,1)S(1)} %get-tuple-element.29.q_ref, bf16[2560,256]{1,0:T(8,128)(2,1)S(1)} %bitcast.90, bf16[2560,256]{1,0:T(8,128)(2,1)S(1)} %collective-permute-done.17.far_ref, s32[1,5120]{1,0:T(1,128)S(1)} %bitcast.92), custom_call_target="tpu_custom_call" | custom-call | flops 838860800 | bytes 2621440 | tf_op jit(solution)/shard_map/pallas_call | solution.py:144
  192.0 3.7 %collective-permute-done.18.far_ref = bf16[4,96,128]{2,1,0:T(8,128)(2,1)S(1)} collective-permute-done((bf16[4,96,128]{2,1,0:T(8,128)(2,1)S(1)}, bf16[4,96,128]{2,1,0:T(8,128)(2,1)S(1)}, u32[]{:S(2)}, u32[]{:S(2)}) %collective-permute-start.18) | collective-permute-done | bytes 98336 | tf_op jit(solution)/shard_map/ppermute | solution.py:286
  195.7 1.5 shard_map.69
  197.2 3.3 %all-to-all-start.4 = ((bf16[4,80,128]{2,1,0:T(8,128)(2,1)}), bf16[4,80,128]{2,1,0:T(8,128)(2,1)S(1)}, u32[]{:S(2)}, u32[]{:S(2)}) async-start(bf16[4,80,128]{2,1,0:T(8,128)(2,1)} %shard_map.69), calls=%async_computation.4 | async-start | bytes 163840 | tf_op jit(solution)/shard_map/all_to_all | solution.py:228
  200.5 4.5 %all-to-all-done.4.context_ref = bf16[4,80,128]{2,1,0:T(8,128)(2,1)S(1)} async-done(((bf16[4,80,128]{2,1,0:T(8,128)(2,1)}), bf16[4,80,128]{2,1,0:T(8,128)(2,1)S(1)}, u32[]{:S(2)}, u32[]{:S(2)}) %all-to-all-start.4) | async-done | bytes 81952 | tf_op jit(solution)/shard_map/all_to_all | solution.py:228
  205.5 14.4 %all_to_all.30 = bf16[8,80,256]{2,1,0:T(8,128)(2,1)S(1)} all-to-all(bf16[8,80,256]{2,1,0:T(8,128)(2,1)S(1)} %shard_map.70), channel_id=1, replica_groups=mesh['zh'=2,'yh'=2,'yl'=4,'x'=4,'zl'=4,'c'=2] {'zl','c'}, dimensions={0} | all-to-all | bytes 655360 | tf_op jit(solution)/shard_map/all_to_all | solution.py:228
  (64 shorter events, 11.8 us)
Async XLA Ops:
  3.3 39.1 %all-to-all-start = ((bf16[4,8,128,384]{3,2,1,0:T(8,128)(2,1)}), bf16[4,8,128,384]{3,2,1,0:T(8,128)(2,1)S(1)}, u32[]{:S(2)}, u32[]{:S(2)}) async-start(bf16[4,8,128,384]{3,2,1,0:T(8,128)(2,1)} %shard_map.64), calls=%async_computation | async-start | bytes 6291456 | tf_op jit(solution)/shard_map/all_to_all | solution.py:228
  9.4 1.9 copy-start.3
  9.4 11.4 %copy-start.6 = (s32[64]{0:T(128)S(1)}, s32[64]{0:T(128)}, u32[]{:S(2)}) copy-start(s32[64]{0:T(128)} %param.11) | copy-start | bytes 772
  9.5 0.9 copy-start.2
  9.5 12.6 %copy-start.5 = (f32[2048]{0:T(1024)S(1)}, f32[2048]{0:T(1024)}, u32[]{:S(2)}) copy-start(f32[2048]{0:T(1024)} %param.7) | copy-start | bytes 24580
  11.3 13.0 %collective-permute-start = (bf16[2,32,2048]{2,1,0:T(8,128)(2,1)}, bf16[2,32,2048]{2,1,0:T(8,128)(2,1)}, u32[]{:S(2)}, u32[]{:S(2)}) collective-permute-start(bf16[2,32,2048]{2,1,0:T(8,128)(2,1)} %get-tuple-element.46), channel_id=1, source_target_pairs={{0,96},{32,0},{64,32},{96,64},{1,97},{33,1},{65,33},{97,65},{2,98}... | collective-permute-start | bytes 786440 | tf_op jit(solution)/shard_map/ppermute | solution.py:242
  16.5 10.7 %collective-permute-start.1 = (bf16[2,32,2048]{2,1,0:T(8,128)(2,1)}, bf16[2,32,2048]{2,1,0:T(8,128)(2,1)}, u32[]{:S(2)}, u32[]{:S(2)}) collective-permute-start(bf16[2,32,2048]{2,1,0:T(8,128)(2,1)} %get-tuple-element.47), channel_id=1, source_target_pairs={{0,32},{32,64},{64,96},{96,0},{1,33},{33,65},{65,97},{97,1},{2,34}... | collective-permute-start | bytes 786440 | tf_op jit(solution)/shard_map/ppermute | solution.py:242
  18.5 22.1 %collective-permute-start.2 = (bf16[2,32,2048]{2,1,0:T(8,128)(2,1)}, bf16[2,32,2048]{2,1,0:T(8,128)(2,1)}, u32[]{:S(2)}, u32[]{:S(2)}) collective-permute-start(bf16[2,32,2048]{2,1,0:T(8,128)(2,1)} %get-tuple-element.45), channel_id=1, source_target_pairs={{0,64},{32,96},{64,0},{96,32},{1,65},{33,97},{65,1},{97,33},{2,66}... | collective-permute-start | bytes 786440 | tf_op jit(solution)/shard_map/ppermute | solution.py:242
  43.3 9.4 %copy-start.4 = (bf16[2,32,2048]{2,1,0:T(8,128)(2,1)S(1)}, bf16[2,32,2048]{2,1,0:T(8,128)(2,1)}, u32[]{:S(2)}) copy-start(bf16[2,32,2048]{2,1,0:T(8,128)(2,1)} %fusion.7) | copy-start | bytes 786436
  43.3 31.2 %all-to-all-start.1 = ((bf16[8,128,384]{2,1,0:T(8,128)(2,1)}), bf16[8,128,384]{2,1,0:T(8,128)(2,1)S(1)}, u32[]{:S(2)}, u32[]{:S(2)}) async-start(bf16[8,128,384]{2,1,0:T(8,128)(2,1)} %dynamic-slice_bitcast_fusion), calls=%async_computation.1 | async-start | bytes 1572864 | tf_op jit(solution)/shard_map/all_to_all | solution.py:228
  53.5 7.9 %collective-permute-start.3 = (bf16[2,32,512]{2,1,0:T(8,128)(2,1)S(1)}, bf16[2,32,512]{2,1,0:T(8,128)(2,1)S(1)}, u32[]{:S(2)}, u32[]{:S(2)}) collective-permute-start(bf16[2,32,512]{2,1,0:T(8,128)(2,1)S(1)} %bitcast.111), channel_id=1, source_target_pairs={{0,24},{8,0},{16,8},{24,16},{1,25},{9,1},{17,9},{25,17},{2,26},{10... | collective-permute-start | bytes 196616 | tf_op jit(solution)/shard_map/ppermute | solution.py:242
  56.3 6.5 %collective-permute-start.4 = (bf16[2,32,512]{2,1,0:T(8,128)(2,1)S(1)}, bf16[2,32,512]{2,1,0:T(8,128)(2,1)S(1)}, u32[]{:S(2)}, u32[]{:S(2)}) collective-permute-start(bf16[2,32,512]{2,1,0:T(8,128)(2,1)S(1)} %bitcast.112), channel_id=1, source_target_pairs={{0,8},{8,16},{16,24},{24,0},{1,9},{9,17},{17,25},{25,1},{2,10},{10... | collective-permute-start | bytes 196616 | tf_op jit(solution)/shard_map/ppermute | solution.py:242
  58.8 6.8 %collective-permute-start.5 = (bf16[2,32,512]{2,1,0:T(8,128)(2,1)S(1)}, bf16[2,32,512]{2,1,0:T(8,128)(2,1)S(1)}, u32[]{:S(2)}, u32[]{:S(2)}) collective-permute-start(bf16[2,32,512]{2,1,0:T(8,128)(2,1)S(1)} %bitcast.113), channel_id=1, source_target_pairs={{0,16},{8,24},{16,0},{24,8},{1,17},{9,25},{17,1},{25,9},{2,18},{10... | collective-permute-start | bytes 196616 | tf_op jit(solution)/shard_map/ppermute | solution.py:242
  65.7 7.4 %collective-permute-start.6 = (bf16[32,512]{1,0:T(8,128)(2,1)S(1)}, bf16[32,512]{1,0:T(8,128)(2,1)S(1)}, u32[]{:S(2)}, u32[]{:S(2)}) collective-permute-start(bf16[32,512]{1,0:T(8,128)(2,1)S(1)} %slice_bitcast_fusion), channel_id=1, source_target_pairs={{0,224},{32,192},{64,160},{96,128},{128,96},{160,64},{192,32},{224... | collective-permute-start | bytes 98312 | tf_op jit(solution)/shard_map/ppermute | solution.py:325
  74.6 18.3 %collective-permute-start.11 = (bf16[128,512]{1,0:T(8,128)(2,1)S(1)}, bf16[128,512]{1,0:T(8,128)(2,1)S(1)}, u32[]{:S(2)}, u32[]{:S(2)}) collective-permute-start(bf16[128,512]{1,0:T(8,128)(2,1)S(1)} %pad_maximum_fusion.4), channel_id=1, source_target_pairs={{0,262},{1,270},{2,260},{3,268},{4,258},{5,266},{6,256},{7,264},{8... | collective-permute-start | bytes 393224 | tf_op jit(solution)/shard_map/ppermute | solution.py:282
  87.4 6.3 %collective-permute-start.10 = (bf16[128,512]{1,0:T(8,128)(2,1)S(1)}, bf16[128,512]{1,0:T(8,128)(2,1)S(1)}, u32[]{:S(2)}, u32[]{:S(2)}) collective-permute-start(bf16[128,512]{1,0:T(8,128)(2,1)S(1)} %pad_maximum_fusion.4), channel_id=1, source_target_pairs={{1,8},{3,10},{5,12},{7,14},{8,1},{10,3},{12,5},{14,7},{17,24},{19,... | collective-permute-start | bytes 393224 | tf_op jit(solution)/shard_map/ppermute | solution.py:282
  94.8 36.6 %all-to-all-start.2 = ((bf16[8,128,512]{2,1,0:T(8,128)(2,1)}), bf16[8,128,512]{2,1,0:T(8,128)(2,1)S(1)}, u32[]{:S(2)}, u32[]{:S(2)}) async-start(bf16[8,128,512]{2,1,0:T(8,128)(2,1)} %broadcast_in_dim.2), calls=%async_computation.2 | async-start | bytes 2097152 | tf_op jit(solution)/shard_map/all_to_all | solution.py:228
  102.1 31.7 %collective-permute-start.9 = (bf16[80,2048]{1,0:T(8,128)(2,1)S(1)}, bf16[80,2048]{1,0:T(8,128)(2,1)S(1)}, u32[]{:S(2)}, u32[]{:S(2)}) collective-permute-start(bf16[80,2048]{1,0:T(8,128)(2,1)S(1)} %fusion.2), channel_id=1, source_target_pairs={{0,24},{8,0},{16,8},{24,16},{1,25},{9,1},{17,9},{25,17},{2,26},{10... | collective-permute-start | bytes 983048 | tf_op jit(solution)/shard_map/ppermute | solution.py:242
  104.0 29.8 %collective-permute-start.8 = (bf16[80,2048]{1,0:T(8,128)(2,1)S(1)}, bf16[80,2048]{1,0:T(8,128)(2,1)S(1)}, u32[]{:S(2)}, u32[]{:S(2)}) collective-permute-start(bf16[80,2048]{1,0:T(8,128)(2,1)S(1)} %fusion.2), channel_id=1, source_target_pairs={{0,16},{8,24},{16,0},{24,8},{1,17},{9,25},{17,1},{25,9},{2,18},{10... | collective-permute-start | bytes 983048 | tf_op jit(solution)/shard_map/ppermute | solution.py:242
  109.0 24.9 %collective-permute-start.7 = (bf16[80,2048]{1,0:T(8,128)(2,1)S(1)}, bf16[80,2048]{1,0:T(8,128)(2,1)S(1)}, u32[]{:S(2)}, u32[]{:S(2)}) collective-permute-start(bf16[80,2048]{1,0:T(8,128)(2,1)S(1)} %fusion.2), channel_id=1, source_target_pairs={{0,8},{8,16},{16,24},{24,0},{1,9},{9,17},{17,25},{25,1},{2,10},{10... | collective-permute-start | bytes 983048 | tf_op jit(solution)/shard_map/ppermute | solution.py:242
  131.4 4.7 %collective-permute-start.12 = (bf16[1024,512]{1,0:T(8,128)(2,1)S(1)}, bf16[1024,512]{1,0:T(8,128)(2,1)S(1)}, u32[]{:S(2)}, u32[]{:S(2)}) collective-permute-start(bf16[1024,512]{1,0:T(8,128)(2,1)S(1)} %bitcast.85), channel_id=1, source_target_pairs={{0,1},{1,0},{2,3},{3,2},{4,5},{5,4},{6,7},{7,6},{8,9},{9,8},{10,11... | collective-permute-start | bytes 3145736 | tf_op jit(solution)/shard_map/ppermute | solution.py:224
  137.6 38.3 %all-to-all-start.3 = ((bf16[8,320,256]{2,1,0:T(8,128)(2,1)}), bf16[8,320,256]{2,1,0:T(8,128)(2,1)S(1)}, u32[]{:S(2)}, u32[]{:S(2)}) async-start(bf16[8,320,256]{2,1,0:T(8,128)(2,1)} %get-tuple-element.30), calls=%async_computation.3 | async-start | bytes 2621440 | tf_op jit(solution)/shard_map/all_to_all | solution.py:228
  141.2 10.3 %collective-permute-start.16 = (bf16[256,512]{1,0:T(8,128)(2,1)S(1)}, bf16[256,512]{1,0:T(8,128)(2,1)S(1)}, u32[]{:S(2)}, u32[]{:S(2)}) collective-permute-start(bf16[256,512]{1,0:T(8,128)(2,1)S(1)} %bitcast.99), channel_id=1, source_target_pairs={{0,24},{8,0},{16,8},{24,16},{1,25},{9,1},{17,9},{25,17},{2,26},{10... | collective-permute-start | bytes 786440 | tf_op jit(solution)/shard_map/ppermute | solution.py:242
  143.2 11.0 %collective-permute-start.15 = (bf16[256,512]{1,0:T(8,128)(2,1)S(1)}, bf16[256,512]{1,0:T(8,128)(2,1)S(1)}, u32[]{:S(2)}, u32[]{:S(2)}) collective-permute-start(bf16[256,512]{1,0:T(8,128)(2,1)S(1)} %bitcast.100), channel_id=1, source_target_pairs={{0,16},{8,24},{16,0},{24,8},{1,17},{9,25},{17,1},{25,9},{2,18},{10... | collective-permute-start | bytes 786440 | tf_op jit(solution)/shard_map/ppermute | solution.py:242
  145.1 15.3 %collective-permute-start.14 = (bf16[256,512]{1,0:T(8,128)(2,1)S(1)}, bf16[256,512]{1,0:T(8,128)(2,1)S(1)}, u32[]{:S(2)}, u32[]{:S(2)}) collective-permute-start(bf16[256,512]{1,0:T(8,128)(2,1)S(1)} %bitcast.101), channel_id=1, source_target_pairs={{0,8},{8,16},{16,24},{24,0},{1,9},{9,17},{17,25},{25,1},{2,10},{10... | collective-permute-start | bytes 786440 | tf_op jit(solution)/shard_map/ppermute | solution.py:242
  148.5 12.3 %collective-permute-start.13 = (bf16[320,128]{1,0:T(8,128)(2,1)S(1)}, bf16[320,128]{1,0:T(8,128)(2,1)S(1)}, u32[]{:S(2)}, u32[]{:S(2)}) collective-permute-start(bf16[320,128]{1,0:T(8,128)(2,1)S(1)} %get-tuple-element.29.q_ref), channel_id=1, source_target_pairs={{0,262},{2,260},{4,258},{6,256},{256,6},{258,4},{260,2},{262,0},{1... | collective-permute-start | bytes 245768 | tf_op jit(solution)/shard_map/ppermute | solution.py:286
  160.8 0.6 copy-start
  176.0 5.0 %collective-permute-start.17 = (bf16[2560,256]{1,0:T(8,128)(2,1)S(1)}, bf16[2560,256]{1,0:T(8,128)(2,1)S(1)}, u32[]{:S(2)}, u32[]{:S(2)}) collective-permute-start(bf16[2560,256]{1,0:T(8,128)(2,1)S(1)} %bitcast.88), channel_id=1, source_target_pairs={{0,1},{1,0},{2,3},{3,2},{4,5},{5,4},{6,7},{7,6},{8,9},{9,8},{10,11... | collective-permute-start | bytes 3932168 | tf_op jit(solution)/shard_map/ppermute | solution.py:224
  178.3 22.1 %collective-permute-start.19 = (bf16[4,256,512]{2,1,0:T(8,128)(2,1)S(1)}, bf16[4,256,512]{2,1,0:T(8,128)(2,1)S(1)}, u32[]{:S(2)}, u32[]{:S(2)}) collective-permute-start(bf16[4,256,512]{2,1,0:T(8,128)(2,1)S(1)} %pad_maximum_fusion.3.near_ref), channel_id=1, source_target_pairs={{0,1},{1,0},{2,3},{3,2},{4,5},{5,4},{6,7},{7,6},{8,9},{9,8},{10,11... | collective-permute-start | bytes 3145736 | tf_op jit(solution)/shard_map/ppermute | solution.py:224
  181.0 0.9 copy-start.1
  185.9 9.8 %collective-permute-start.18 = (bf16[4,96,128]{2,1,0:T(8,128)(2,1)S(1)}, bf16[4,96,128]{2,1,0:T(8,128)(2,1)S(1)}, u32[]{:S(2)}, u32[]{:S(2)}) collective-permute-start(bf16[4,96,128]{2,1,0:T(8,128)(2,1)S(1)} %shard_map.68), channel_id=1, source_target_pairs={{0,262},{2,260},{4,258},{6,256},{256,6},{258,4},{260,2},{262,0},{1... | collective-permute-start | bytes 294920 | tf_op jit(solution)/shard_map/ppermute | solution.py:286
  197.2 7.8 %all-to-all-start.4 = ((bf16[4,80,128]{2,1,0:T(8,128)(2,1)}), bf16[4,80,128]{2,1,0:T(8,128)(2,1)S(1)}, u32[]{:S(2)}, u32[]{:S(2)}) async-start(bf16[4,80,128]{2,1,0:T(8,128)(2,1)} %shard_map.69), calls=%async_computation.4 | async-start | bytes 163840 | tf_op jit(solution)/shard_map/all_to_all | solution.py:228

commit v13 on v12

--- a/solution.py
+++ b/solution.py
@@ -35,18 +35,21 @@
     )(w.reshape(3, 2, ny, part, 2 * HD))
 
 
-def near_kernel(c_ref, x_ref, w_ref, out_ref):
+def near_kernel(c_ref, *refs):
+    x_refs, w_ref, out_ref = refs[:-2], refs[-2], refs[-1]
     depth = w_ref.shape[0]
     span = pl.ds(pl.multiple_of(c_ref[0] * depth, depth), depth)
-    w = w_ref[:, : out_ref.shape[1]]
-    out_ref[...] = jnp.dot(x_ref[:, span], w, preferred_element_type=jnp.float32)
-
-
-def far_kernel(c_ref, x_ref, w_ref, sum_ref, q_ref, kv_ref):
+    x = jnp.concatenate([ref[:, span] for ref in x_refs])
+    out_ref[...] = jnp.dot(x, w_ref[:, : out_ref.shape[1]], preferred_element_type=jnp.float32)
+
+
+def far_kernel(c_ref, *refs):
+    x_refs, (w_ref, sum_ref, q_ref, kv_ref) = refs[:-4], refs[-4:]
     depth = w_ref.shape[0]
     span = pl.ds(pl.multiple_of((1 - c_ref[0]) * depth, depth), depth)
+    x = jnp.concatenate([ref[:, span] for ref in x_refs])
     w = w_ref[:, : sum_ref.shape[1]]
-    out = sum_ref[...] + jnp.dot(x_ref[:, span], w, preferred_element_type=jnp.float32)
+    out = sum_ref[...] + jnp.dot(x, w, preferred_element_type=jnp.float32)
     q_ref[...] = out[:, :HD].astype(q_ref.dtype)
     kv = out[:, HD:].astype(kv_ref.dtype)
     for i in range(kv_ref.shape[0]):
@@ -54,22 +57,22 @@
 
 
 def project(core, x, near, far, count):
-    n, cols = x.shape[0], 3 * HD
+    n, cols = sum(block.shape[0] for block in x), 3 * HD
     smem, vmem = pl.BlockSpec(memory_space=pltpu.SMEM), pl.BlockSpec(memory_space=pltpu.VMEM)
     cost = pl.CostEstimate(
-        flops=2 * n * near.shape[0] * cols, bytes_accessed=2 * (x.size + near.size), transcendentals=0
+        flops=2 * n * near.shape[0] * cols, bytes_accessed=2 * (2 * n + cols) * near.shape[0], transcendentals=0
     )
     total = pl.pallas_call(
         near_kernel,
-        in_specs=[smem, vmem, vmem],
+        in_specs=[smem] + [vmem] * (len(x) + 1),
         out_specs=vmem,
         out_shape=jax.ShapeDtypeStruct((n, cols), jnp.float32),
         compiler_params=LIMIT,
         cost_estimate=cost,
-    )(core, x, near)
+    )(core, *x, near)
     return pl.pallas_call(
         far_kernel,
-        in_specs=[smem, vmem, vmem, vmem],
+        in_specs=[smem] + [vmem] * (len(x) + 2),
         out_specs=[vmem, vmem],
         out_shape=[
             jax.ShapeDtypeStruct((n, HD), jnp.bfloat16),
@@ -77,7 +80,7 @@
         ],
         compiler_params=LIMIT,
         cost_estimate=cost,
-    )(core, x, far, total)
+    )(core, *x, far, total)
 
 
 def three_parts(value):
@@ -161,33 +164,33 @@
     )(start, q, near, far, kpos)
 
 
-def merge_kernel(near_ref, far_ref, out_ref):
+def merge_kernel(x_ref, near_ref, far_ref, out_ref):
     nx, half = out_ref.shape[0], out_ref.shape[1]
-    for x in range(nx):
+    for s in range(nx):
         tops, totals = [], []
         for ref in (near_ref, far_ref):
-            stat = ref[x, half:, :].astype(jnp.float32)
+            stat = ref[s, half:, :].astype(jnp.float32)
             stat = jnp.concatenate([stat, jnp.zeros((HD - EXTRA, HD), jnp.float32)]).T[:half]
             tops.append(stat[:, 0:1] + stat[:, 1:2] + stat[:, 2:3])
             totals.append(stat[:, 3:4] + stat[:, 4:5] + stat[:, 5:6])
         top = jnp.maximum(tops[0], tops[1])
         a = totals[0] * jnp.exp2(tops[0] - top)
         b = totals[1] * jnp.exp2(tops[1] - top)
-        mixed = near_ref[x, :half, :].astype(jnp.float32) * a + far_ref[x, :half, :].astype(jnp.float32) * b
-        out_ref[x] = (mixed / (a + b)).astype(out_ref.dtype)
-
-
-def merge(near, far):
+        mixed = near_ref[s, :half, :].astype(jnp.float32) * a + far_ref[s, :half, :].astype(jnp.float32) * b
+        out_ref[lax.rem(x_ref[0] + nx - s, nx)] = (mixed / (a + b)).astype(out_ref.dtype)
+
+
+def merge(x, near, far):
     nx, rows = near.shape[0], near.shape[1] - EXTRA
     vmem = pl.BlockSpec(memory_space=pltpu.VMEM)
     return pl.pallas_call(
         merge_kernel,
-        in_specs=[vmem, vmem],
+        in_specs=[pl.BlockSpec(memory_space=pltpu.SMEM), vmem, vmem],
         out_specs=vmem,
         out_shape=jax.ShapeDtypeStruct((nx, rows, HD), jnp.bfloat16),
         compiler_params=LIMIT,
         cost_estimate=pl.CostEstimate(flops=8 * near.size, bytes_accessed=6 * near.size, transcendentals=0),
-    )(near, far)
+    )(x, near, far)
 
 
 def finish_kernel(c_ref, context_ref, near_ref, far_ref, out_ref):
@@ -259,12 +262,14 @@
     return {s: pick(blocks, (here + s) % count) for s in distances(axis)}
 
 
-def gather_by_shifts(block, axis):
-    here, count = lax.axis_index(axis), lax.axis_size(axis)
-    got = {0: block}
-    for s in distances(axis):
-        got[s] = shift(block, axis, s)
-    got = jnp.stack([got[s] for s in range(count)])
+def gather_shifts(block, axis):
+    got = {s: shift(block, axis, s) for s in distances(axis)}
+    return [block] + [got[s] for s in range(1, lax.axis_size(axis))]
+
+
+def in_order(got, axis):
+    here, count = lax.axis_index(axis), len(got)
+    got = jnp.stack(got)
     return jnp.stack([pick(got, (here - i) % count) for i in range(count)])
 
 
@@ -302,13 +307,12 @@
         mine * lax.rsqrt(jnp.mean(mine * mine, axis=-1, keepdims=True) + 1e-06) * norm_gain
     ).astype(jnp.bfloat16)
 
-    order = block_order.reshape(2, ny, nx) * rows
-    offsets = jnp.arange(half, dtype=jnp.int32)
-    kpos = (pick(order, zh)[:, :, None] + offsets).reshape(-1)
-    kpos = jnp.concatenate([kpos + c * half, kpos + (1 - c) * half]).reshape(1, -1)
+    order = block_order.reshape(2, ny, nx) * rows + c * half
+    order = jnp.stack([lax.dynamic_index_in_dim(order, (x + nx - s) % nx, 2, False) for s in range(nx)], axis=2)
+    kpos = (pick(order, zh)[:, :, None] + jnp.arange(half, dtype=jnp.int32)).reshape(-1)
+    kpos = jnp.concatenate([kpos, kpos + (1 - 2 * c) * half]).reshape(1, -1)
     here = lax.dynamic_index_in_dim(order, y, 1, keepdims=False)
-    start = pick(here, zh) + c * half
-    start_other = pick(here, 1 - zh) + c * half
+    start, start_other = pick(here, zh), pick(here, 1 - zh)
 
     part = width // (2 * ny)
     w = fold(snap_qkv[0], ny)
@@ -328,7 +332,8 @@
     w, normed = lax.optimization_barrier((w, normed))
     w = jnp.where(zh == zh0, jnp.where(x % 2 == c, w, trade(w, 0)), trade(w, 1))
     w = spread(w, ys).reshape(ny * part, 4 * HD)
-    normed = gather_by_shifts(normed, "x").reshape(-1, width)
+    normed = gather_shifts(normed, "x")
+    w, normed = lax.optimization_barrier((w, normed))
     q, kv = project(core, normed, w, swap(w, "c"), ny)
     wo = w[:, 3 * HD :].reshape(ny, nx, part // nx, HD)
     wo = jnp.transpose(wo, (0, 2, 1, 3)).reshape(ny * part // nx, nx * HD)
@@ -336,13 +341,13 @@
 
     near = exchange(kv, ys).reshape(-1, 2 * HD)
     q_other = mirror(q)
-    wo = gather_by_shifts(wo, "x")
-    near, q_other, wo = lax.optimization_barrier((near, q_other, wo))
+    wo = in_order(gather_shifts(wo, "x"), "x")
+    wo_far = swap(wo, "c")
+    near, q_other, wo, wo_far = lax.optimization_barrier((near, q_other, wo, wo_far))
     far = swap(near, "c")
-    wo_far = swap(wo, "c")
 
     others = mirror(attend(start_other, q_other, near, far, kpos, half))
-    context = merge(attend(start, q, near, far, kpos, half), others)
+    context = merge(x.reshape(1), attend(start, q, near, far, kpos, half), others)
     context = exchange(context, "x")
     terms = finish(core, context, wo, wo_far)
     terms = exchange(terms, ("zl", "c")).reshape(-1, rows, terms.shape[2])

time: 222 us -> 222 us (level)
  blocking collectives: 14.4 us -> 21.3 us
  other arithmetic: 6.44 us -> 2.35 us
    all_to_all x5 -> x4, waiting for transfers between devices: 40.1 us -> 14 us  [exchange(): return lax.all_to_all(block, axis, 0, 0, tiled=True)]
    ppermute x12, waiting for transfers between devices: 29.3 us -> 44.3 us  [shift(): lax.ppermute(block, axis, [(i, (i + distance) % count) for i in range(cou...]
    ppermute x2, waiting for transfers between devices: 3.67 us -> 10.8 us  [mirror(): return lax.ppermute(block, ('zh', 'zl'), [(i, 7 - i) for i in range(8)])]
    all_to_all x1 -> x2, blocking collectives: 14.4 us -> 21.3 us  [exchange(): return lax.all_to_all(block, axis, 0, 0, tiled=True)]
    ppermute x3, waiting for transfers between devices: 1.6 us -> 4.16 us  [swap(): return lax.ppermute(block, axis, [(0, 1), (1, 0)])]
    all_to_all x5 -> x4, starting transfers between devices: 28.5 us -> 28.1 us  [exchange(): return lax.all_to_all(block, axis, 0, 0, tiled=True)]
  transfers between devices with their start and end apart: 25 -> 24, of which waited for: 16 -> 21; matrix products, arithmetic and copies ran while one was open for 4% -> 1% of each run, Pallas kernels for 5% -> 2%
where the time goes in v13:
time: 222 us; the launch traced here: 221 us
  starting transfers between devices  94 us (42%)
  waiting for transfers between devices  80.7 us (36%)
  blocking collectives  21.3 us (10%)
  Pallas kernels  13.7 us (6%)
  local copies, waits for them, and re-layouts  7.29 us (3%)
  other arithmetic  2.35 us (1%)
    ppermute x12, waiting for transfers between devices, shift(): lax.ppermute(block, axis, [(i, (i + distance) % count) for i in range(cou...  44.3 us
    ppermute x12, starting transfers between devices, shift(): lax.ppermute(block, axis, [(i, (i + distance) % count) for i in range(cou...  35.9 us
    all_to_all x4, starting transfers between devices, exchange(): return lax.all_to_all(block, axis, 0, 0, tiled=True)  28.1 us
    all_to_all x2, blocking collectives, exchange(): return lax.all_to_all(block, axis, 0, 0, tiled=True)  21.3 us
    ppermute x2, starting transfers between devices, trade(): return lax.ppermute(block, ('zh', 'x', 'zl', 'c'), route)  14.1 us
    all_to_all x4, waiting for transfers between devices, exchange(): return lax.all_to_all(block, axis, 0, 0, tiled=True)  14 us
    ppermute x2, waiting for transfers between devices, mirror(): return lax.ppermute(block, ('zh', 'zl'), [(i, 7 - i) for i in range(8)])  10.8 us
    pallas_call x2, Pallas kernels, attend(): pl.pallas_call(attend_kernel, grid=(nq // tile,), in_specs=[pl.BlockSpec(...  7.94 us
  transfers between devices with their start and end apart: 24, of which 21 were waited for; matrix products, arithmetic and copies ran while one was open for 1% of the time, Pallas kernels for 2%

profile of v13, /device:TPU:1, one launch (start us, length us, event | category | flops | bytes accessed | tf_op | source)
XLA Modules:
  0.0 220.8 jit_solution(11299743416949849485)
XLA Ops:
  0.0 3.3 %shard_map.64 = bf16[4,8,128,384]{3,2,1,0:T(8,128)(2,1)} custom-call(bf16[3,2,8,128,256]{4,3,2,1,0:T(8,128)(2,1)} %bitcast.87), custom_call_target="tpu_custom_call" | custom-call | bytes 6291456 | tf_op jit(solution)/shard_map/pallas_call | solution.py:27
  3.4 5.0 %all-to-all-start = ((bf16[4,8,128,384]{3,2,1,0:T(8,128)(2,1)}), bf16[4,8,128,384]{3,2,1,0:T(8,128)(2,1)}, u32[]{:S(2)}, u32[]{:S(2)}) async-start(bf16[4,8,128,384]{3,2,1,0:T(8,128)(2,1)} %shard_map.64), calls=%async_computation | async-start | bytes 6291456 | tf_op jit(solution)/shard_map/all_to_all | solution.py:231
  9.4 5.9 %collective-permute-start = (bf16[2,32,2048]{2,1,0:T(8,128)(2,1)}, bf16[2,32,2048]{2,1,0:T(8,128)(2,1)S(1)}, u32[]{:S(2)}, u32[]{:S(2)}) collective-permute-start(bf16[2,32,2048]{2,1,0:T(8,128)(2,1)} %get-tuple-element.54), channel_id=1, source_target_pairs={{0,96},{32,0},{64,32},{96,64},{1,97},{33,1},{65,33},{97,65},{2,98}... | collective-permute-start | bytes 786440 | tf_op jit(solution)/shard_map/ppermute | solution.py:245
  15.3 1.9 collective-permute-start.1
  17.2 2.3 %collective-permute-start.2 = (bf16[2,32,2048]{2,1,0:T(8,128)(2,1)S(1)}, bf16[2,32,2048]{2,1,0:T(8,128)(2,1)S(1)}, u32[]{:S(2)}, u32[]{:S(2)}) collective-permute-start(bf16[2,32,2048]{2,1,0:T(8,128)(2,1)S(1)} %get-tuple-element.53), channel_id=1, source_target_pairs={{0,64},{32,96},{64,0},{96,32},{1,65},{33,97},{65,1},{97,33},{2,66}... | collective-permute-start | bytes 786440 | tf_op jit(solution)/shard_map/ppermute | solution.py:245
  21.2 4.6 %collective-permute-done.1 = bf16[2,32,2048]{2,1,0:T(8,128)(2,1)S(1)} collective-permute-done((bf16[2,32,2048]{2,1,0:T(8,128)(2,1)S(1)}, bf16[2,32,2048]{2,1,0:T(8,128)(2,1)S(1)}, u32[]{:S(2)}, u32[]{:S(2)}) %collective-permute-start.1) | collective-permute-done | bytes 262176 | tf_op jit(solution)/shard_map/ppermute | solution.py:245
  25.8 12.9 %collective-permute-done.2 = bf16[2,32,2048]{2,1,0:T(8,128)(2,1)S(1)} collective-permute-done((bf16[2,32,2048]{2,1,0:T(8,128)(2,1)S(1)}, bf16[2,32,2048]{2,1,0:T(8,128)(2,1)S(1)}, u32[]{:S(2)}, u32[]{:S(2)}) %collective-permute-start.2) | collective-permute-done | bytes 262176 | tf_op jit(solution)/shard_map/ppermute | solution.py:245
  40.1 2.1 dynamic-slice_bitcast_fusion
  42.2 12.7 %all-to-all-start.1 = ((bf16[8,128,384]{2,1,0:T(8,128)(2,1)}), bf16[8,128,384]{2,1,0:T(8,128)(2,1)S(1)}, u32[]{:S(2)}, u32[]{:S(2)}) async-start(bf16[8,128,384]{2,1,0:T(8,128)(2,1)} %dynamic-slice_bitcast_fusion), calls=%async_computation.1 | async-start | bytes 1572864 | tf_op jit(solution)/shard_map/all_to_all | solution.py:231
  55.7 2.8 %collective-permute-start.3 = (bf16[2,32,512]{2,1,0:T(8,128)(2,1)S(1)}, bf16[2,32,512]{2,1,0:T(8,128)(2,1)S(1)}, u32[]{:S(2)}, u32[]{:S(2)}) collective-permute-start(bf16[2,32,512]{2,1,0:T(8,128)(2,1)S(1)} %bitcast.101), channel_id=1, source_target_pairs={{0,24},{8,0},{16,8},{24,16},{1,25},{9,1},{17,9},{25,17},{2,26},{10... | collective-permute-start | bytes 196616 | tf_op jit(solution)/shard_map/ppermute | solution.py:245
  58.5 2.5 %collective-permute-start.4 = (bf16[2,32,512]{2,1,0:T(8,128)(2,1)S(1)}, bf16[2,32,512]{2,1,0:T(8,128)(2,1)S(1)}, u32[]{:S(2)}, u32[]{:S(2)}) collective-permute-start(bf16[2,32,512]{2,1,0:T(8,128)(2,1)S(1)} %bitcast.102), channel_id=1, source_target_pairs={{0,8},{8,16},{16,24},{24,0},{1,9},{9,17},{17,25},{25,1},{2,10},{10... | collective-permute-start | bytes 196616 | tf_op jit(solution)/shard_map/ppermute | solution.py:245
  61.0 2.5 %collective-permute-start.5 = (bf16[2,32,512]{2,1,0:T(8,128)(2,1)S(1)}, bf16[2,32,512]{2,1,0:T(8,128)(2,1)S(1)}, u32[]{:S(2)}, u32[]{:S(2)}) collective-permute-start(bf16[2,32,512]{2,1,0:T(8,128)(2,1)S(1)} %bitcast.103), channel_id=1, source_target_pairs={{0,16},{8,24},{16,0},{24,8},{1,17},{9,25},{17,1},{25,9},{2,18},{10... | collective-permute-start | bytes 196616 | tf_op jit(solution)/shard_map/ppermute | solution.py:245
  63.6 1.4 collective-permute-done.4
  65.0 2.8 %collective-permute-done.5 = bf16[2,32,512]{2,1,0:T(8,128)(2,1)S(1)} collective-permute-done((bf16[2,32,512]{2,1,0:T(8,128)(2,1)S(1)}, bf16[2,32,512]{2,1,0:T(8,128)(2,1)S(1)}, u32[]{:S(2)}, u32[]{:S(2)}) %collective-permute-start.5) | collective-permute-done | bytes 65568 | tf_op jit(solution)/shard_map/ppermute | solution.py:245
  67.9 4.6 %collective-permute-start.6 = (bf16[32,512]{1,0:T(8,128)(2,1)S(1)}, bf16[32,512]{1,0:T(8,128)(2,1)S(1)}, u32[]{:S(2)}, u32[]{:S(2)}) collective-permute-start(bf16[32,512]{1,0:T(8,128)(2,1)S(1)} %slice_bitcast_fusion), channel_id=1, source_target_pairs={{0,224},{32,192},{64,160},{96,128},{128,96},{160,64},{192,32},{224... | collective-permute-start | bytes 98312 | tf_op jit(solution)/shard_map/ppermute | solution.py:329
  72.5 3.1 %collective-permute-done.6 = bf16[32,512]{1,0:T(8,128)(2,1)S(1)} collective-permute-done((bf16[32,512]{1,0:T(8,128)(2,1)S(1)}, bf16[32,512]{1,0:T(8,128)(2,1)S(1)}, u32[]{:S(2)}, u32[]{:S(2)}) %collective-permute-start.6) | collective-permute-done | bytes 32800 | tf_op jit(solution)/shard_map/ppermute | solution.py:329
  75.6 1.7 all-to-all-done.1
  77.4 12.2 %collective-permute-start.8 = (bf16[128,512]{1,0:T(8,128)(2,1)S(1)}, bf16[128,512]{1,0:T(8,128)(2,1)S(1)}, u32[]{:S(2)}, u32[]{:S(2)}) collective-permute-start(bf16[128,512]{1,0:T(8,128)(2,1)S(1)} %pad_maximum_fusion.2), channel_id=1, source_target_pairs={{0,262},{1,270},{2,260},{3,268},{4,258},{5,266},{6,256},{7,264},{8... | collective-permute-start | bytes 393224 | tf_op jit(solution)/shard_map/ppermute | solution.py:287
  89.6 1.9 collective-permute-start.7
  91.6 3.5 %collective-permute-done.8 = bf16[128,512]{1,0:T(8,128)(2,1)S(1)} collective-permute-done((bf16[128,512]{1,0:T(8,128)(2,1)S(1)}, bf16[128,512]{1,0:T(8,128)(2,1)S(1)}, u32[]{:S(2)}, u32[]{:S(2)}) %collective-permute-start.8) | collective-permute-done | bytes 131104 | tf_op jit(solution)/shard_map/ppermute | solution.py:287
  97.1 6.9 %all-to-all-start.2 = ((bf16[8,128,512]{2,1,0:T(8,128)(2,1)}), bf16[8,128,512]{2,1,0:T(8,128)(2,1)S(1)}, u32[]{:S(2)}, u32[]{:S(2)}) async-start(bf16[8,128,512]{2,1,0:T(8,128)(2,1)} %broadcast_in_dim.2), calls=%async_computation.2 | async-start | bytes 2097152 | tf_op jit(solution)/shard_map/all_to_all | solution.py:231
  104.0 1.9 collective-permute-start.9
  105.9 4.9 %collective-permute-start.10 = (bf16[80,2048]{1,0:T(8,128)(2,1)S(1)}, bf16[80,2048]{1,0:T(8,128)(2,1)S(1)}, u32[]{:S(2)}, u32[]{:S(2)}) collective-permute-start(bf16[80,2048]{1,0:T(8,128)(2,1)S(1)} %fusion.2.refs_0_), channel_id=1, source_target_pairs={{0,16},{8,24},{16,0},{24,8},{1,17},{9,25},{17,1},{25,9},{2,18},{10... | collective-permute-start | bytes 983048 | tf_op jit(solution)/shard_map/ppermute | solution.py:245
  110.8 4.0 %collective-permute-start.11 = (bf16[80,2048]{1,0:T(8,128)(2,1)S(1)}, bf16[80,2048]{1,0:T(8,128)(2,1)S(1)}, u32[]{:S(2)}, u32[]{:S(2)}) collective-permute-start(bf16[80,2048]{1,0:T(8,128)(2,1)S(1)} %fusion.2.refs_0_), channel_id=1, source_target_pairs={{0,24},{8,0},{16,8},{24,16},{1,25},{9,1},{17,9},{25,17},{2,26},{10... | collective-permute-start | bytes 983048 | tf_op jit(solution)/shard_map/ppermute | solution.py:245
  115.9 7.5 %collective-permute-done.10.refs_2_ = bf16[80,2048]{1,0:T(8,128)(2,1)S(1)} collective-permute-done((bf16[80,2048]{1,0:T(8,128)(2,1)S(1)}, bf16[80,2048]{1,0:T(8,128)(2,1)S(1)}, u32[]{:S(2)}, u32[]{:S(2)}) %collective-permute-start.10) | collective-permute-done | bytes 327712 | tf_op jit(solution)/shard_map/ppermute | solution.py:245
  123.3 2.1 collective-permute-done.11.refs_3_
  125.4 7.8 %all-to-all-done.2 = bf16[8,128,512]{2,1,0:T(8,128)(2,1)S(1)} async-done(((bf16[8,128,512]{2,1,0:T(8,128)(2,1)}), bf16[8,128,512]{2,1,0:T(8,128)(2,1)S(1)}, u32[]{:S(2)}, u32[]{:S(2)}) %all-to-all-start.2) | async-done | bytes 1048608 | tf_op jit(solution)/shard_map/all_to_all | solution.py:231
  133.2 2.4 %collective-permute-start.12 = (bf16[1024,512]{1,0:T(8,128)(2,1)S(1)}, bf16[1024,512]{1,0:T(8,128)(2,1)S(1)}, u32[]{:S(2)}, u32[]{:S(2)}) collective-permute-start(bf16[1024,512]{1,0:T(8,128)(2,1)S(1)} %bitcast.79), channel_id=1, source_target_pairs={{0,1},{1,0},{2,3},{3,2},{4,5},{5,4},{6,7},{7,6},{8,9},{9,8},{10,11... | collective-permute-start | bytes 3145736 | tf_op jit(solution)/shard_map/ppermute | solution.py:227
  136.4 1.5 collective-permute-done.12.refs_4_
  139.5 3.6 %all-to-all-start.3 = ((bf16[8,320,256]{2,1,0:T(8,128)(2,1)}), bf16[8,320,256]{2,1,0:T(8,128)(2,1)S(1)}, u32[]{:S(2)}, u32[]{:S(2)}) async-start(bf16[8,320,256]{2,1,0:T(8,128)(2,1)} %copy-done), calls=%async_computation.3 | async-start | bytes 2621440 | tf_op jit(solution)/shard_map/all_to_all | solution.py:231
  143.1 1.9 collective-permute-start.16
  145.0 1.9 collective-permute-start.15
  146.9 3.4 %collective-permute-start.14 = (bf16[256,512]{1,0:T(8,128)(2,1)S(1)}, bf16[256,512]{1,0:T(8,128)(2,1)S(1)}, u32[]{:S(2)}, u32[]{:S(2)}) collective-permute-start(bf16[256,512]{1,0:T(8,128)(2,1)S(1)} %bitcast.94), channel_id=1, source_target_pairs={{0,8},{8,16},{16,24},{24,0},{1,9},{9,17},{17,25},{25,1},{2,10},{10... | collective-permute-start | bytes 786440 | tf_op jit(solution)/shard_map/ppermute | solution.py:245
  150.4 2.1 collective-permute-done.16
  152.5 3.5 %collective-permute-done.15 = bf16[256,512]{1,0:T(8,128)(2,1)S(1)} collective-permute-done((bf16[256,512]{1,0:T(8,128)(2,1)S(1)}, bf16[256,512]{1,0:T(8,128)(2,1)S(1)}, u32[]{:S(2)}, u32[]{:S(2)}) %collective-permute-start.15) | collective-permute-done | bytes 262176 | tf_op jit(solution)/shard_map/ppermute | solution.py:245
  156.0 6.3 %collective-permute-done.14 = bf16[256,512]{1,0:T(8,128)(2,1)S(1)} collective-permute-done((bf16[256,512]{1,0:T(8,128)(2,1)S(1)}, bf16[256,512]{1,0:T(8,128)(2,1)S(1)}, u32[]{:S(2)}, u32[]{:S(2)}) %collective-permute-start.14) | collective-permute-done | bytes 262176 | tf_op jit(solution)/shard_map/ppermute | solution.py:245
  162.6 2.4 %collective-permute-start.17 = (bf16[4,256,512]{2,1,0:T(8,128)(2,1)S(1)}, bf16[4,256,512]{2,1,0:T(8,128)(2,1)S(1)}, u32[]{:S(2)}, u32[]{:S(2)}) collective-permute-start(bf16[4,256,512]{2,1,0:T(8,128)(2,1)S(1)} %pad_maximum_fusion.1.near_ref), channel_id=1, source_target_pairs={{0,1},{1,0},{2,3},{3,2},{4,5},{5,4},{6,7},{7,6},{8,9},{9,8},{10,11... | collective-permute-start | bytes 3145736 | tf_op jit(solution)/shard_map/ppermute | solution.py:227
  165.0 1.9 collective-permute-start.13
  167.0 7.1 %collective-permute-done.13.q_ref = bf16[320,128]{1,0:T(8,128)(2,1)S(1)} collective-permute-done((bf16[320,128]{1,0:T(8,128)(2,1)S(1)}, bf16[320,128]{1,0:T(8,128)(2,1)S(1)}, u32[]{:S(2)}, u32[]{:S(2)}) %collective-permute-start.13) | collective-permute-done | bytes 81952 | tf_op jit(solution)/shard_map/ppermute | solution.py:291
  174.7 3.1 %all-to-all-done.3 = bf16[8,320,256]{2,1,0:T(8,128)(2,1)S(1)} async-done(((bf16[8,320,256]{2,1,0:T(8,128)(2,1)}), bf16[8,320,256]{2,1,0:T(8,128)(2,1)S(1)}, u32[]{:S(2)}, u32[]{:S(2)}) %all-to-all-start.3) | async-done | bytes 1310752 | tf_op jit(solution)/shard_map/all_to_all | solution.py:231
  177.8 2.4 %collective-permute-start.18 = (bf16[2560,256]{1,0:T(8,128)(2,1)S(1)}, bf16[2560,256]{1,0:T(8,128)(2,1)S(1)}, u32[]{:S(2)}, u32[]{:S(2)}) collective-permute-start(bf16[2560,256]{1,0:T(8,128)(2,1)S(1)} %bitcast.82), channel_id=1, source_target_pairs={{0,1},{1,0},{2,3},{3,2},{4,5},{5,4},{6,7},{7,6},{8,9},{9,8},{10,11... | collective-permute-start | bytes 3932168 | tf_op jit(solution)/shard_map/ppermute | solution.py:227
  180.2 2.6 %collective-permute-done.18.far_ref = bf16[2560,256]{1,0:T(8,128)(2,1)S(1)} collective-permute-done((bf16[2560,256]{1,0:T(8,128)(2,1)S(1)}, bf16[2560,256]{1,0:T(8,128)(2,1)S(1)}, u32[]{:S(2)}, u32[]{:S(2)}) %collective-permute-start.18) | collective-permute-done | bytes 1310752 | tf_op jit(solution)/shard_map/ppermute | solution.py:227
  183.7 4.0 %shard_map.68 = bf16[4,96,128]{2,1,0:T(8,128)(2,1)S(1)} custom-call(s32[4]{0:T(128)S(1)} %get-tuple-element.45.start_ref, bf16[320,128]{1,0:T(8,128)(2,1)S(1)} %copy-done.2, bf16[2560,256]{1,0:T(8,128)(2,1)S(1)} %bitcast.83, bf16[2560,256]{1,0:T(8,128)(2,1)S(1)} %collective-permute-done.18.far_ref, s32[1,5120]{1,0:T(1,128)S(1)} %bitcast.85), custom_call_target="tpu_custom_call" | custom-call | flops 838860800 | bytes 2621440 | tf_op jit(solution)/shard_map/pallas_call | solution.py:147
  187.7 2.1 collective-permute-start.19
  189.8 4.0 %shard_map.67.near_ref = bf16[4,96,128]{2,1,0:T(8,128)(2,1)S(1)} custom-call(s32[4]{0:T(128)S(1)} %get-tuple-element.27.start_ref, bf16[320,128]{1,0:T(8,128)(2,1)S(1)} %get-tuple-element.40.q_ref, bf16[2560,256]{1,0:T(8,128)(2,1)S(1)} %bitcast.84, bf16[2560,256]{1,0:T(8,128)(2,1)S(1)} %collective-permute-done.18.far_ref, s32[1,5120]{1,0:T(1,128)S(1)} %bitcast.86), custom_call_target="tpu_custom_call" | custom-call | flops 838860800 | bytes 2621440 | tf_op jit(solution)/shard_map/pallas_call | solution.py:147
  193.8 3.7 %collective-permute-done.19.far_ref = bf16[4,96,128]{2,1,0:T(8,128)(2,1)S(1)} collective-permute-done((bf16[4,96,128]{2,1,0:T(8,128)(2,1)S(1)}, bf16[4,96,128]{2,1,0:T(8,128)(2,1)S(1)}, u32[]{:S(2)}, u32[]{:S(2)}) %collective-permute-start.19) | collective-permute-done | bytes 98336 | tf_op jit(solution)/shard_map/ppermute | solution.py:291
  198.3 6.9 %all_to_all.30.context_ref = bf16[4,80,128]{2,1,0:T(8,128)(2,1)S(1)} all-to-all(bf16[4,80,128]{2,1,0:T(8,128)(2,1)S(1)} %shard_map.69), channel_id=1, replica_groups=mesh['zh'=2,'yh'=2,'yl'=4,'x'=4,'zl'=4,'c'=2] {'x'}, dimensions={0} | all-to-all | bytes 163840 | tf_op jit(solution)/shard_map/all_to_all | solution.py:231
  205.8 14.4 %all_to_all.31 = bf16[8,80,256]{2,1,0:T(8,128)(2,1)S(1)} all-to-all(bf16[8,80,256]{2,1,0:T(8,128)(2,1)S(1)} %shard_map.70), channel_id=1, replica_groups=mesh['zh'=2,'yh'=2,'yl'=4,'x'=4,'zl'=4,'c'=2] {'zl','c'}, dimensions={0} | all-to-all | bytes 655360 | tf_op jit(solution)/shard_map/all_to_all | solution.py:231
  (62 shorter events, 13.3 us)
Async XLA Ops:
  3.3 5.0 %copy-start.3 = (bf16[1,256,2048]{2,1,0:T(8,128)(2,1)S(1)}, bf16[1,256,2048]{2,1,0:T(8,128)(2,1)}, u32[]{:S(2)}) copy-start(bf16[1,256,2048]{2,1,0:T(8,128)(2,1)} %param.9) | copy-start | bytes 3145732
  3.4 36.8 %all-to-all-start = ((bf16[4,8,128,384]{3,2,1,0:T(8,128)(2,1)}), bf16[4,8,128,384]{3,2,1,0:T(8,128)(2,1)}, u32[]{:S(2)}, u32[]{:S(2)}) async-start(bf16[4,8,128,384]{3,2,1,0:T(8,128)(2,1)} %shard_map.64), calls=%async_computation | async-start | bytes 6291456 | tf_op jit(solution)/shard_map/all_to_all | solution.py:231
  8.3 11.3 %copy-start.6 = (s32[64]{0:T(128)S(1)}, s32[64]{0:T(128)}, u32[]{:S(2)}) copy-start(s32[64]{0:T(128)} %param.11) | copy-start | bytes 772
  8.3 11.7 %copy-start.4 = (bf16[160,2048]{1,0:T(8,128)(2,1)S(1)}, bf16[160,2048]{1,0:T(8,128)(2,1)}, u32[]{:S(2)}) copy-start(bf16[160,2048]{1,0:T(8,128)(2,1)} %param.6) | copy-start | bytes 1966084
  8.3 11.9 %copy-start.5 = (f32[2048]{0:T(1024)S(1)}, f32[2048]{0:T(1024)}, u32[]{:S(2)}) copy-start(f32[2048]{0:T(1024)} %param.7) | copy-start | bytes 24580
  9.4 11.8 %collective-permute-start = (bf16[2,32,2048]{2,1,0:T(8,128)(2,1)}, bf16[2,32,2048]{2,1,0:T(8,128)(2,1)S(1)}, u32[]{:S(2)}, u32[]{:S(2)}) collective-permute-start(bf16[2,32,2048]{2,1,0:T(8,128)(2,1)} %get-tuple-element.54), channel_id=1, source_target_pairs={{0,96},{32,0},{64,32},{96,64},{1,97},{33,1},{65,33},{97,65},{2,98}... | collective-permute-start | bytes 786440 | tf_op jit(solution)/shard_map/ppermute | solution.py:245
  15.3 10.6 %collective-permute-start.1 = (bf16[2,32,2048]{2,1,0:T(8,128)(2,1)S(1)}, bf16[2,32,2048]{2,1,0:T(8,128)(2,1)S(1)}, u32[]{:S(2)}, u32[]{:S(2)}) collective-permute-start(bf16[2,32,2048]{2,1,0:T(8,128)(2,1)S(1)} %get-tuple-element.55), channel_id=1, source_target_pairs={{0,32},{32,64},{64,96},{96,0},{1,33},{33,65},{65,97},{97,1},{2,34}... | collective-permute-start | bytes 786440 | tf_op jit(solution)/shard_map/ppermute | solution.py:245
  17.2 21.6 %collective-permute-start.2 = (bf16[2,32,2048]{2,1,0:T(8,128)(2,1)S(1)}, bf16[2,32,2048]{2,1,0:T(8,128)(2,1)S(1)}, u32[]{:S(2)}, u32[]{:S(2)}) collective-permute-start(bf16[2,32,2048]{2,1,0:T(8,128)(2,1)S(1)} %get-tuple-element.53), channel_id=1, source_target_pairs={{0,64},{32,96},{64,0},{96,32},{1,65},{33,97},{65,1},{97,33},{2,66}... | collective-permute-start | bytes 786440 | tf_op jit(solution)/shard_map/ppermute | solution.py:245
  42.2 35.1 %all-to-all-start.1 = ((bf16[8,128,384]{2,1,0:T(8,128)(2,1)}), bf16[8,128,384]{2,1,0:T(8,128)(2,1)S(1)}, u32[]{:S(2)}, u32[]{:S(2)}) async-start(bf16[8,128,384]{2,1,0:T(8,128)(2,1)} %dynamic-slice_bitcast_fusion), calls=%async_computation.1 | async-start | bytes 1572864 | tf_op jit(solution)/shard_map/all_to_all | solution.py:231
  55.7 7.9 %collective-permute-start.3 = (bf16[2,32,512]{2,1,0:T(8,128)(2,1)S(1)}, bf16[2,32,512]{2,1,0:T(8,128)(2,1)S(1)}, u32[]{:S(2)}, u32[]{:S(2)}) collective-permute-start(bf16[2,32,512]{2,1,0:T(8,128)(2,1)S(1)} %bitcast.101), channel_id=1, source_target_pairs={{0,24},{8,0},{16,8},{24,16},{1,25},{9,1},{17,9},{25,17},{2,26},{10... | collective-permute-start | bytes 196616 | tf_op jit(solution)/shard_map/ppermute | solution.py:245
  58.5 6.5 %collective-permute-start.4 = (bf16[2,32,512]{2,1,0:T(8,128)(2,1)S(1)}, bf16[2,32,512]{2,1,0:T(8,128)(2,1)S(1)}, u32[]{:S(2)}, u32[]{:S(2)}) collective-permute-start(bf16[2,32,512]{2,1,0:T(8,128)(2,1)S(1)} %bitcast.102), channel_id=1, source_target_pairs={{0,8},{8,16},{16,24},{24,0},{1,9},{9,17},{17,25},{25,1},{2,10},{10... | collective-permute-start | bytes 196616 | tf_op jit(solution)/shard_map/ppermute | solution.py:245
  61.0 6.8 %collective-permute-start.5 = (bf16[2,32,512]{2,1,0:T(8,128)(2,1)S(1)}, bf16[2,32,512]{2,1,0:T(8,128)(2,1)S(1)}, u32[]{:S(2)}, u32[]{:S(2)}) collective-permute-start(bf16[2,32,512]{2,1,0:T(8,128)(2,1)S(1)} %bitcast.103), channel_id=1, source_target_pairs={{0,16},{8,24},{16,0},{24,8},{1,17},{9,25},{17,1},{25,9},{2,18},{10... | collective-permute-start | bytes 196616 | tf_op jit(solution)/shard_map/ppermute | solution.py:245
  67.9 7.7 %collective-permute-start.6 = (bf16[32,512]{1,0:T(8,128)(2,1)S(1)}, bf16[32,512]{1,0:T(8,128)(2,1)S(1)}, u32[]{:S(2)}, u32[]{:S(2)}) collective-permute-start(bf16[32,512]{1,0:T(8,128)(2,1)S(1)} %slice_bitcast_fusion), channel_id=1, source_target_pairs={{0,224},{32,192},{64,160},{96,128},{128,96},{160,64},{192,32},{224... | collective-permute-start | bytes 98312 | tf_op jit(solution)/shard_map/ppermute | solution.py:329
  77.4 17.7 %collective-permute-start.8 = (bf16[128,512]{1,0:T(8,128)(2,1)S(1)}, bf16[128,512]{1,0:T(8,128)(2,1)S(1)}, u32[]{:S(2)}, u32[]{:S(2)}) collective-permute-start(bf16[128,512]{1,0:T(8,128)(2,1)S(1)} %pad_maximum_fusion.2), channel_id=1, source_target_pairs={{0,262},{1,270},{2,260},{3,268},{4,258},{5,266},{6,256},{7,264},{8... | collective-permute-start | bytes 393224 | tf_op jit(solution)/shard_map/ppermute | solution.py:287
  89.6 6.4 %collective-permute-start.7 = (bf16[128,512]{1,0:T(8,128)(2,1)S(1)}, bf16[128,512]{1,0:T(8,128)(2,1)S(1)}, u32[]{:S(2)}, u32[]{:S(2)}) collective-permute-start(bf16[128,512]{1,0:T(8,128)(2,1)S(1)} %pad_maximum_fusion.2), channel_id=1, source_target_pairs={{1,8},{3,10},{5,12},{7,14},{8,1},{10,3},{12,5},{14,7},{17,24},{19,... | collective-permute-start | bytes 393224 | tf_op jit(solution)/shard_map/ppermute | solution.py:287
  97.1 36.2 %all-to-all-start.2 = ((bf16[8,128,512]{2,1,0:T(8,128)(2,1)}), bf16[8,128,512]{2,1,0:T(8,128)(2,1)S(1)}, u32[]{:S(2)}, u32[]{:S(2)}) async-start(bf16[8,128,512]{2,1,0:T(8,128)(2,1)} %broadcast_in_dim.2), calls=%async_computation.2 | async-start | bytes 2097152 | tf_op jit(solution)/shard_map/all_to_all | solution.py:231
  104.0 11.9 %collective-permute-start.9 = (bf16[80,2048]{1,0:T(8,128)(2,1)S(1)}, bf16[80,2048]{1,0:T(8,128)(2,1)S(1)}, u32[]{:S(2)}, u32[]{:S(2)}) collective-permute-start(bf16[80,2048]{1,0:T(8,128)(2,1)S(1)} %fusion.2.refs_0_), channel_id=1, source_target_pairs={{0,8},{8,16},{16,24},{24,0},{1,9},{9,17},{17,25},{25,1},{2,10},{10... | collective-permute-start | bytes 983048 | tf_op jit(solution)/shard_map/ppermute | solution.py:245
  105.9 17.4 %collective-permute-start.10 = (bf16[80,2048]{1,0:T(8,128)(2,1)S(1)}, bf16[80,2048]{1,0:T(8,128)(2,1)S(1)}, u32[]{:S(2)}, u32[]{:S(2)}) collective-permute-start(bf16[80,2048]{1,0:T(8,128)(2,1)S(1)} %fusion.2.refs_0_), channel_id=1, source_target_pairs={{0,16},{8,24},{16,0},{24,8},{1,17},{9,25},{17,1},{25,9},{2,18},{10... | collective-permute-start | bytes 983048 | tf_op jit(solution)/shard_map/ppermute | solution.py:245
  110.8 14.6 %collective-permute-start.11 = (bf16[80,2048]{1,0:T(8,128)(2,1)S(1)}, bf16[80,2048]{1,0:T(8,128)(2,1)S(1)}, u32[]{:S(2)}, u32[]{:S(2)}) collective-permute-start(bf16[80,2048]{1,0:T(8,128)(2,1)S(1)} %fusion.2.refs_0_), channel_id=1, source_target_pairs={{0,24},{8,0},{16,8},{24,16},{1,25},{9,1},{17,9},{25,17},{2,26},{10... | collective-permute-start | bytes 983048 | tf_op jit(solution)/shard_map/ppermute | solution.py:245
  133.2 4.7 %collective-permute-start.12 = (bf16[1024,512]{1,0:T(8,128)(2,1)S(1)}, bf16[1024,512]{1,0:T(8,128)(2,1)S(1)}, u32[]{:S(2)}, u32[]{:S(2)}) collective-permute-start(bf16[1024,512]{1,0:T(8,128)(2,1)S(1)} %bitcast.79), channel_id=1, source_target_pairs={{0,1},{1,0},{2,3},{3,2},{4,5},{5,4},{6,7},{7,6},{8,9},{9,8},{10,11... | collective-permute-start | bytes 3145736 | tf_op jit(solution)/shard_map/ppermute | solution.py:227
  138.4 1.1 copy-start
  139.5 38.3 %all-to-all-start.3 = ((bf16[8,320,256]{2,1,0:T(8,128)(2,1)}), bf16[8,320,256]{2,1,0:T(8,128)(2,1)S(1)}, u32[]{:S(2)}, u32[]{:S(2)}) async-start(bf16[8,320,256]{2,1,0:T(8,128)(2,1)} %copy-done), calls=%async_computation.3 | async-start | bytes 2621440 | tf_op jit(solution)/shard_map/all_to_all | solution.py:231
  143.1 9.4 %collective-permute-start.16 = (bf16[256,512]{1,0:T(8,128)(2,1)S(1)}, bf16[256,512]{1,0:T(8,128)(2,1)S(1)}, u32[]{:S(2)}, u32[]{:S(2)}) collective-permute-start(bf16[256,512]{1,0:T(8,128)(2,1)S(1)} %bitcast.92), channel_id=1, source_target_pairs={{0,24},{8,0},{16,8},{24,16},{1,25},{9,1},{17,9},{25,17},{2,26},{10... | collective-permute-start | bytes 786440 | tf_op jit(solution)/shard_map/ppermute | solution.py:245
  145.0 11.0 %collective-permute-start.15 = (bf16[256,512]{1,0:T(8,128)(2,1)S(1)}, bf16[256,512]{1,0:T(8,128)(2,1)S(1)}, u32[]{:S(2)}, u32[]{:S(2)}) collective-permute-start(bf16[256,512]{1,0:T(8,128)(2,1)S(1)} %bitcast.93), channel_id=1, source_target_pairs={{0,16},{8,24},{16,0},{24,8},{1,17},{9,25},{17,1},{25,9},{2,18},{10... | collective-permute-start | bytes 786440 | tf_op jit(solution)/shard_map/ppermute | solution.py:245
  146.9 15.3 %collective-permute-start.14 = (bf16[256,512]{1,0:T(8,128)(2,1)S(1)}, bf16[256,512]{1,0:T(8,128)(2,1)S(1)}, u32[]{:S(2)}, u32[]{:S(2)}) collective-permute-start(bf16[256,512]{1,0:T(8,128)(2,1)S(1)} %bitcast.94), channel_id=1, source_target_pairs={{0,8},{8,16},{16,24},{24,0},{1,9},{9,17},{17,25},{25,1},{2,10},{10... | collective-permute-start | bytes 786440 | tf_op jit(solution)/shard_map/ppermute | solution.py:245
  162.6 12.1 %collective-permute-start.17 = (bf16[4,256,512]{2,1,0:T(8,128)(2,1)S(1)}, bf16[4,256,512]{2,1,0:T(8,128)(2,1)S(1)}, u32[]{:S(2)}, u32[]{:S(2)}) collective-permute-start(bf16[4,256,512]{2,1,0:T(8,128)(2,1)S(1)} %pad_maximum_fusion.1.near_ref), channel_id=1, source_target_pairs={{0,1},{1,0},{2,3},{3,2},{4,5},{5,4},{6,7},{7,6},{8,9},{9,8},{10,11... | collective-permute-start | bytes 3145736 | tf_op jit(solution)/shard_map/ppermute | solution.py:227
  165.0 9.0 %collective-permute-start.13 = (bf16[320,128]{1,0:T(8,128)(2,1)S(1)}, bf16[320,128]{1,0:T(8,128)(2,1)S(1)}, u32[]{:S(2)}, u32[]{:S(2)}) collective-permute-start(bf16[320,128]{1,0:T(8,128)(2,1)S(1)} %get-tuple-element.40.q_ref), channel_id=1, source_target_pairs={{0,262},{2,260},{4,258},{6,256},{256,6},{258,4},{260,2},{262,0},{1... | collective-permute-start | bytes 245768 | tf_op jit(solution)/shard_map/ppermute | solution.py:291
  174.1 0.6 copy-start.1
  177.8 5.0 %collective-permute-start.18 = (bf16[2560,256]{1,0:T(8,128)(2,1)S(1)}, bf16[2560,256]{1,0:T(8,128)(2,1)S(1)}, u32[]{:S(2)}, u32[]{:S(2)}) collective-permute-start(bf16[2560,256]{1,0:T(8,128)(2,1)S(1)} %bitcast.82), channel_id=1, source_target_pairs={{0,1},{1,0},{2,3},{3,2},{4,5},{5,4},{6,7},{7,6},{8,9},{9,8},{10,11... | collective-permute-start | bytes 3932168 | tf_op jit(solution)/shard_map/ppermute | solution.py:227
  182.8 0.9 copy-start.2
  187.7 9.8 %collective-permute-start.19 = (bf16[4,96,128]{2,1,0:T(8,128)(2,1)S(1)}, bf16[4,96,128]{2,1,0:T(8,128)(2,1)S(1)}, u32[]{:S(2)}, u32[]{:S(2)}) collective-permute-start(bf16[4,96,128]{2,1,0:T(8,128)(2,1)S(1)} %shard_map.68), channel_id=1, source_target_pairs={{0,262},{2,260},{4,258},{6,256},{256,6},{258,4},{260,2},{262,0},{1... | collective-permute-start | bytes 294920 | tf_op jit(solution)/shard_map/ppermute | solution.py:291

commit v14 on v13

--- a/solution.py
+++ b/solution.py
@@ -1,3 +1,5 @@
+import functools
+
 import jax
 import jax.numpy as jnp
 import numpy as np
@@ -90,50 +92,51 @@
     return first, second, rest - second
 
 
-def attend_kernel(start_ref, q_ref, near_ref, far_ref, kpos_ref, o_ref, s_ref):
+def score(start_ref, q_ref, kv_refs, kpos_refs, s_ref, half):
     factor = float(np.log2(np.e) / HD**0.5)
     rows = q_ref.shape[0]
-    blocks, half = o_ref.shape[0], o_ref.shape[1] - EXTRA
     row = lax.broadcasted_iota(jnp.int32, (rows, 1), 0)
-    first = blocks * pl.program_id(0)
-    qpos = row + start_ref[first]
-    for b in range(1, blocks):
-        qpos = jnp.where(row < b * half, qpos, row - b * half + start_ref[first + b])
-    pieces = [
-        (ref, j * CHUNK, i * ref.shape[0] + j * CHUNK)
-        for i, ref in enumerate((near_ref, far_ref))
-        for j in range(ref.shape[0] // CHUNK)
-    ]
+    qpos = row + start_ref[0]
+    for b in range(1, rows // half):
+        qpos = jnp.where(row < b * half, qpos, row - b * half + start_ref[b])
     q = q_ref[...]
     high = jnp.full((rows, HD), HIDE, jnp.float32)
-    for ref, at, column in pieces:
-        span = pl.ds(column, CHUNK)
-        s = lax.dot_general(
-            q, ref[pl.ds(at, CHUNK), :HD], (((1,), (1,)), ((), ())), preferred_element_type=jnp.float32
-        )
-        s = jnp.where(kpos_ref[:, span] <= qpos, s * factor, HIDE)
-        s_ref[:, span] = s
-        for t in range(CHUNK // HD):
-            high = jnp.maximum(high, s[:, t * HD : (t + 1) * HD])
-    top = jnp.max(high, axis=1, keepdims=True)
+    for i, (kv_ref, kpos_ref) in enumerate(zip(kv_refs, kpos_refs)):
+        for at in range(0, kv_ref.shape[0], CHUNK):
+            s = lax.dot_general(
+                q, kv_ref[pl.ds(at, CHUNK), :HD], (((1,), (1,)), ((), ())), preferred_element_type=jnp.float32
+            )
+            s = jnp.where(kpos_ref[:, pl.ds(at, CHUNK)] <= qpos, s * factor, HIDE)
+            s_ref[:, pl.ds(i * kv_ref.shape[0] + at, CHUNK)] = s
+            for t in range(CHUNK // HD):
+                high = jnp.maximum(high, s[:, t * HD : (t + 1) * HD])
+    return jnp.max(high, axis=1, keepdims=True)
+
+
+def weigh(top, kv_refs, s_ref):
+    rows = s_ref.shape[0]
     base = jnp.where(top <= 0.5 * HIDE, 0.0, top)
     total = jnp.zeros((rows, HD), jnp.float32)
     acc = jnp.zeros((rows, HD), jnp.float32)
-    for ref, at, column in pieces:
-        span = pl.ds(column, CHUNK)
-        p = jnp.exp2(s_ref[:, span] - base)
-        for t in range(CHUNK // HD):
-            total = total + p[:, t * HD : (t + 1) * HD]
-        acc = acc + jnp.dot(
-            p.astype(jnp.bfloat16), ref[pl.ds(at, CHUNK), HD:], preferred_element_type=jnp.float32
-        )
-    total = jnp.sum(total, axis=1, keepdims=True)
+    for i, kv_ref in enumerate(kv_refs):
+        for at in range(0, kv_ref.shape[0], CHUNK):
+            p = jnp.exp2(s_ref[:, pl.ds(i * kv_ref.shape[0] + at, CHUNK)] - base)
+            for t in range(CHUNK // HD):
+                total = total + p[:, t * HD : (t + 1) * HD]
+            acc = acc + jnp.dot(
+                p.astype(jnp.bfloat16), kv_ref[pl.ds(at, CHUNK), HD:], preferred_element_type=jnp.float32
+            )
+    return jnp.sum(total, axis=1, keepdims=True), acc
+
+
+def write_parts(top, total, acc, o_ref):
+    half = o_ref.shape[1] - EXTRA
     o = acc / jnp.where(total == 0.0, 1.0, total)
-    lane = lax.broadcasted_iota(jnp.int32, (rows, HD), 1)
-    stat = jnp.zeros((rows, HD), jnp.float32)
+    lane = lax.broadcasted_iota(jnp.int32, acc.shape, 1)
+    stat = jnp.zeros(acc.shape, jnp.float32)
     for k, piece in enumerate(three_parts(top) + three_parts(total)):
         stat = jnp.where(lane == k, piece, stat)
-    for b in range(blocks):
+    for b in range(o_ref.shape[0]):
         o_ref[b, :half, :] = o[b * half : (b + 1) * half].astype(o_ref.dtype)
         block = jnp.concatenate(
             [stat[b * half : (b + 1) * half], jnp.zeros((HD - half, HD), jnp.float32)]
@@ -141,27 +144,45 @@
         o_ref[b, half:, :] = block.T[:EXTRA].astype(o_ref.dtype)
 
 
-def attend(start, q, near, far, kpos, half):
-    nq, nk = q.shape[0], 2 * near.shape[0]
-    tile = 4 * half
-    return pl.pallas_call(
-        attend_kernel,
-        grid=(nq // tile,),
-        in_specs=[
-            pl.BlockSpec(memory_space=pltpu.SMEM),
-            pl.BlockSpec((tile, HD), lambda i: (i, 0)),
-            pl.BlockSpec((nk // 2, 2 * HD), lambda i: (0, 0)),
-            pl.BlockSpec((nk // 2, 2 * HD), lambda i: (0, 0)),
-            pl.BlockSpec((1, nk), lambda i: (0, 0)),
-        ],
-        out_specs=pl.BlockSpec((4, half + EXTRA, HD), lambda i: (i, 0, 0)),
-        out_shape=jax.ShapeDtypeStruct((nq // half, half + EXTRA, HD), jnp.bfloat16),
-        scratch_shapes=[pltpu.VMEM((tile, nk), jnp.float32)],
+def whole_kernel(half, start_ref, q_ref, near_ref, far_ref, near_pos, far_pos, o_ref, s_ref):
+    kv_refs = (near_ref, far_ref)
+    top = score(start_ref, q_ref, kv_refs, (near_pos, far_pos), s_ref, half)
+    write_parts(top, *weigh(top, kv_refs, s_ref), o_ref)
+
+
+def first_kernel(half, start_ref, q_ref, kv_ref, kpos_ref, acc_ref, stat_ref, s_ref):
+    top = score(start_ref, q_ref, (kv_ref,), (kpos_ref,), s_ref, half)
+    total, acc = weigh(top, (kv_ref,), s_ref)
+    acc_ref[...] = acc
+    stat_ref[...] = jnp.where(lax.broadcasted_iota(jnp.int32, acc.shape, 1) == 0, top, total)
+
+
+def second_kernel(half, start_ref, q_ref, kv_ref, kpos_ref, acc_ref, stat_ref, o_ref, s_ref):
+    before = stat_ref[:, 0:1]
+    top = jnp.maximum(before, score(start_ref, q_ref, (kv_ref,), (kpos_ref,), s_ref, half))
+    total, acc = weigh(top, (kv_ref,), s_ref)
+    keep = jnp.exp2(before - top)
+    write_parts(top, total + stat_ref[:, 1:2] * keep, acc + acc_ref[...] * keep, o_ref)
+
+
+def attend(kernel, half, start, q, kv, kpos, state=()):
+    nq, nk = q.shape[0], sum(block.shape[0] for block in kv)
+    vmem = pl.BlockSpec(memory_space=pltpu.VMEM)
+    if kernel is first_kernel:
+        out_shape = [jax.ShapeDtypeStruct((nq, HD), jnp.float32)] * 2
+    else:
+        out_shape = jax.ShapeDtypeStruct((nq // half, half + EXTRA, HD), jnp.bfloat16)
+    return pl.pallas_call(
+        functools.partial(kernel, half),
+        in_specs=[pl.BlockSpec(memory_space=pltpu.SMEM)] + [vmem] * (1 + 2 * len(kv) + len(state)),
+        out_specs=[vmem, vmem] if kernel is first_kernel else vmem,
+        out_shape=out_shape,
+        scratch_shapes=[pltpu.VMEM((nq, nk), jnp.float32)],
         compiler_params=LIMIT,
         cost_estimate=pl.CostEstimate(
             flops=4 * nq * nk * HD, bytes_accessed=nk * HD * 4, transcendentals=nq * nk
         ),
-    )(start, q, near, far, kpos)
+    )(start, q, *kv, *kpos, *state)
 
 
 def merge_kernel(x_ref, near_ref, far_ref, out_ref):
@@ -310,7 +331,7 @@
     order = block_order.reshape(2, ny, nx) * rows + c * half
     order = jnp.stack([lax.dynamic_index_in_dim(order, (x + nx - s) % nx, 2, False) for s in range(nx)], axis=2)
     kpos = (pick(order, zh)[:, :, None] + jnp.arange(half, dtype=jnp.int32)).reshape(-1)
-    kpos = jnp.concatenate([kpos, kpos + (1 - 2 * c) * half]).reshape(1, -1)
+    kpos = [kpos.reshape(1, -1), (kpos + (1 - 2 * c) * half).reshape(1, -1)]
     here = lax.dynamic_index_in_dim(order, y, 1, keepdims=False)
     start, start_other = pick(here, zh), pick(here, 1 - zh)
 
@@ -337,7 +358,7 @@
     q, kv = project(core, normed, w, swap(w, "c"), ny)
     wo = w[:, 3 * HD :].reshape(ny, nx, part // nx, HD)
     wo = jnp.transpose(wo, (0, 2, 1, 3)).reshape(ny * part // nx, nx * HD)
-    q, kv, wo = lax.optimization_barrier((q, kv, wo))
+    kv, wo = lax.optimization_barrier((kv, wo))
 
     near = exchange(kv, ys).reshape(-1, 2 * HD)
     q_other = mirror(q)
@@ -346,8 +367,9 @@
     near, q_other, wo, wo_far = lax.optimization_barrier((near, q_other, wo, wo_far))
     far = swap(near, "c")
 
-    others = mirror(attend(start_other, q_other, near, far, kpos, half))
-    context = merge(x.reshape(1), attend(start, q, near, far, kpos, half), others)
+    state = attend(first_kernel, half, start_other, q_other, [near], kpos[:1])
+    others = mirror(attend(second_kernel, half, start_other, q_other, [far], kpos[1:], state))
+    context = merge(x.reshape(1), attend(whole_kernel, half, start, q, [near, far], kpos), others)
     context = exchange(context, "x")
     terms = finish(core, context, wo, wo_far)
     terms = exchange(terms, ("zl", "c")).reshape(-1, rows, terms.shape[2])

time: 222 us -> 219 us (0.986)
  waiting for transfers between devices: 80.7 us -> 74.5 us
  other arithmetic: 2.35 us -> 7.32 us
  starting transfers between devices: 94 us -> 90.1 us
    all_to_all x4, starting transfers between devices: 28.1 us -> 23.6 us  [exchange(): return lax.all_to_all(block, axis, 0, 0, tiled=True)]
    ppermute x3, waiting for transfers between devices: 4.16 us -> 1.82 us  [swap(): return lax.ppermute(block, axis, [(0, 1), (1, 0)])]
    pallas_call x2 -> x3, Pallas kernels: 7.94 us -> 8.78 us  [attend(): pl.pallas_call(functools.partial(kernel, half), in_specs=[pl.BlockSpec(me...]
  transfers between devices with their start and end apart: 24 -> 24, of which waited for: 21 -> 20; matrix products, arithmetic and copies ran while one was open for 1% -> 5% of each run, Pallas kernels for 2% -> 3%
where the time goes in v14:
time: 219 us; the launch traced here: 218 us
  starting transfers between devices  90.1 us (41%)
  waiting for transfers between devices  74.5 us (34%)
  blocking collectives  21.3 us (10%)
  Pallas kernels  14.5 us (7%)
  local copies, waits for them, and re-layouts  9.06 us (4%)
  other arithmetic  7.32 us (3%)
    ppermute x12, waiting for transfers between devices, shift(): lax.ppermute(block, axis, [(i, (i + distance) % count) for i in range(cou...  42.8 us
    ppermute x12, starting transfers between devices, shift(): lax.ppermute(block, axis, [(i, (i + distance) % count) for i in range(cou...  35.3 us
    all_to_all x4, starting transfers between devices, exchange(): return lax.all_to_all(block, axis, 0, 0, tiled=True)  23.6 us
    all_to_all x2, blocking collectives, exchange(): return lax.all_to_all(block, axis, 0, 0, tiled=True)  21.3 us
    ppermute x2, starting transfers between devices, trade(): return lax.ppermute(block, ('zh', 'x', 'zl', 'c'), route)  15.2 us
    all_to_all x4, waiting for transfers between devices, exchange(): return lax.all_to_all(block, axis, 0, 0, tiled=True)  12.9 us
    ppermute x2, waiting for transfers between devices, mirror(): return lax.ppermute(block, ('zh', 'zl'), [(i, 7 - i) for i in range(8)])  10.8 us
    pallas_call x3, Pallas kernels, attend(): pl.pallas_call(functools.partial(kernel, half), in_specs=[pl.BlockSpec(me...  8.78 us
  transfers between devices with their start and end apart: 24, of which 20 were waited for; matrix products, arithmetic and copies ran while one was open for 5% of the time, Pallas kernels for 3%

profile of v14, /device:TPU:1, one launch (start us, length us, event | category | flops | bytes accessed | tf_op | source)
XLA Modules:
  0.0 218.2 jit_solution(9323826581188410770)
XLA Ops:
  0.0 3.3 %shard_map.64 = bf16[4,8,128,384]{3,2,1,0:T(8,128)(2,1)} custom-call(bf16[3,2,8,128,256]{4,3,2,1,0:T(8,128)(2,1)} %bitcast.84), custom_call_target="tpu_custom_call" | custom-call | bytes 6291456 | tf_op jit(solution)/shard_map/pallas_call | solution.py:29
  3.3 4.8 %all-to-all-start = ((bf16[4,8,128,384]{3,2,1,0:T(8,128)(2,1)}), bf16[4,8,128,384]{3,2,1,0:T(8,128)(2,1)S(1)}, u32[]{:S(2)}, u32[]{:S(2)}) async-start(bf16[4,8,128,384]{3,2,1,0:T(8,128)(2,1)} %shard_map.64), calls=%async_computation | async-start | bytes 6291456 | tf_op jit(solution)/shard_map/all_to_all | solution.py:252
  8.2 2.1 dynamic-slice_bitcast_fusion.1
  11.1 2.1 fusion.13
  13.3 5.2 %collective-permute-start = (bf16[2,32,2048]{2,1,0:T(8,128)(2,1)}, bf16[2,32,2048]{2,1,0:T(8,128)(2,1)}, u32[]{:S(2)}, u32[]{:S(2)}) collective-permute-start(bf16[2,32,2048]{2,1,0:T(8,128)(2,1)} %get-tuple-element.58), channel_id=1, source_target_pairs={{0,96},{32,0},{64,32},{96,64},{1,97},{33,1},{65,33},{97,65},{2,98}... | collective-permute-start | bytes 786440 | tf_op jit(solution)/shard_map/ppermute | solution.py:266
  18.5 1.9 collective-permute-start.1
  20.4 2.4 %collective-permute-start.2 = (bf16[2,32,2048]{2,1,0:T(8,128)(2,1)}, bf16[2,32,2048]{2,1,0:T(8,128)(2,1)}, u32[]{:S(2)}, u32[]{:S(2)}) collective-permute-start(bf16[2,32,2048]{2,1,0:T(8,128)(2,1)} %get-tuple-element.57), channel_id=1, source_target_pairs={{0,64},{32,96},{64,0},{96,32},{1,65},{33,97},{65,1},{97,33},{2,66}... | collective-permute-start | bytes 786440 | tf_op jit(solution)/shard_map/ppermute | solution.py:266
  26.4 2.8 %collective-permute-done.1 = bf16[2,32,2048]{2,1,0:T(8,128)(2,1)} collective-permute-done((bf16[2,32,2048]{2,1,0:T(8,128)(2,1)}, bf16[2,32,2048]{2,1,0:T(8,128)(2,1)}, u32[]{:S(2)}, u32[]{:S(2)}) %collective-permute-start.1) | collective-permute-done | bytes 262176 | tf_op jit(solution)/shard_map/ppermute | solution.py:266
  29.2 13.3 %collective-permute-done.2 = bf16[2,32,2048]{2,1,0:T(8,128)(2,1)} collective-permute-done((bf16[2,32,2048]{2,1,0:T(8,128)(2,1)}, bf16[2,32,2048]{2,1,0:T(8,128)(2,1)}, u32[]{:S(2)}, u32[]{:S(2)}) %collective-permute-start.2) | collective-permute-done | bytes 262176 | tf_op jit(solution)/shard_map/ppermute | solution.py:266
  42.5 1.7 fusion.7
  45.2 7.4 %all-to-all-start.1 = ((bf16[8,128,384]{2,1,0:T(8,128)(2,1)}), bf16[8,128,384]{2,1,0:T(8,128)(2,1)S(1)}, u32[]{:S(2)}, u32[]{:S(2)}) async-start(bf16[8,128,384]{2,1,0:T(8,128)(2,1)} %dynamic-slice_bitcast_fusion), calls=%async_computation.1 | async-start | bytes 1572864 | tf_op jit(solution)/shard_map/all_to_all | solution.py:252
  54.3 2.8 %collective-permute-start.3 = (bf16[2,32,512]{2,1,0:T(8,128)(2,1)S(1)}, bf16[2,32,512]{2,1,0:T(8,128)(2,1)S(1)}, u32[]{:S(2)}, u32[]{:S(2)}) collective-permute-start(bf16[2,32,512]{2,1,0:T(8,128)(2,1)S(1)} %bitcast.98), channel_id=1, source_target_pairs={{0,24},{8,0},{16,8},{24,16},{1,25},{9,1},{17,9},{25,17},{2,26},{10... | collective-permute-start | bytes 196616 | tf_op jit(solution)/shard_map/ppermute | solution.py:266
  57.1 2.5 %collective-permute-start.4 = (bf16[2,32,512]{2,1,0:T(8,128)(2,1)S(1)}, bf16[2,32,512]{2,1,0:T(8,128)(2,1)S(1)}, u32[]{:S(2)}, u32[]{:S(2)}) collective-permute-start(bf16[2,32,512]{2,1,0:T(8,128)(2,1)S(1)} %bitcast.99), channel_id=1, source_target_pairs={{0,8},{8,16},{16,24},{24,0},{1,9},{9,17},{17,25},{25,1},{2,10},{10... | collective-permute-start | bytes 196616 | tf_op jit(solution)/shard_map/ppermute | solution.py:266
  59.7 2.5 %collective-permute-start.5 = (bf16[2,32,512]{2,1,0:T(8,128)(2,1)S(1)}, bf16[2,32,512]{2,1,0:T(8,128)(2,1)S(1)}, u32[]{:S(2)}, u32[]{:S(2)}) collective-permute-start(bf16[2,32,512]{2,1,0:T(8,128)(2,1)S(1)} %bitcast.100), channel_id=1, source_target_pairs={{0,16},{8,24},{16,0},{24,8},{1,17},{9,25},{17,1},{25,9},{2,18},{10... | collective-permute-start | bytes 196616 | tf_op jit(solution)/shard_map/ppermute | solution.py:266
  63.7 2.8 %collective-permute-done.5 = bf16[2,32,512]{2,1,0:T(8,128)(2,1)S(1)} collective-permute-done((bf16[2,32,512]{2,1,0:T(8,128)(2,1)S(1)}, bf16[2,32,512]{2,1,0:T(8,128)(2,1)S(1)}, u32[]{:S(2)}, u32[]{:S(2)}) %collective-permute-start.5) | collective-permute-done | bytes 65568 | tf_op jit(solution)/shard_map/ppermute | solution.py:266
  66.5 4.6 %collective-permute-start.6 = (bf16[32,512]{1,0:T(8,128)(2,1)S(1)}, bf16[32,512]{1,0:T(8,128)(2,1)S(1)}, u32[]{:S(2)}, u32[]{:S(2)}) collective-permute-start(bf16[32,512]{1,0:T(8,128)(2,1)S(1)} %slice_bitcast_fusion), channel_id=1, source_target_pairs={{0,224},{32,192},{64,160},{96,128},{128,96},{160,64},{192,32},{224... | collective-permute-start | bytes 98312 | tf_op jit(solution)/shard_map/ppermute | solution.py:350
  71.1 1.9 collective-permute-done.6
  74.4 13.3 %collective-permute-start.8 = (bf16[128,512]{1,0:T(8,128)(2,1)S(1)}, bf16[128,512]{1,0:T(8,128)(2,1)S(1)}, u32[]{:S(2)}, u32[]{:S(2)}) collective-permute-start(bf16[128,512]{1,0:T(8,128)(2,1)S(1)} %pad_maximum_fusion.2), channel_id=1, source_target_pairs={{0,262},{1,270},{2,260},{3,268},{4,258},{5,266},{6,256},{7,264},{8... | collective-permute-start | bytes 393224 | tf_op jit(solution)/shard_map/ppermute | solution.py:308
  87.8 1.9 collective-permute-start.7
  89.7 3.5 %collective-permute-done.8 = bf16[128,512]{1,0:T(8,128)(2,1)S(1)} collective-permute-done((bf16[128,512]{1,0:T(8,128)(2,1)S(1)}, bf16[128,512]{1,0:T(8,128)(2,1)S(1)}, u32[]{:S(2)}, u32[]{:S(2)}) %collective-permute-start.8) | collective-permute-done | bytes 131104 | tf_op jit(solution)/shard_map/ppermute | solution.py:308
  95.1 7.8 %all-to-all-start.2 = ((bf16[8,128,512]{2,1,0:T(8,128)(2,1)}), bf16[8,128,512]{2,1,0:T(8,128)(2,1)S(1)}, u32[]{:S(2)}, u32[]{:S(2)}) async-start(bf16[8,128,512]{2,1,0:T(8,128)(2,1)} %broadcast_in_dim.2), calls=%async_computation.2 | async-start | bytes 2097152 | tf_op jit(solution)/shard_map/all_to_all | solution.py:252
  103.0 1.9 collective-permute-start.9
  104.9 4.9 %collective-permute-start.10 = (bf16[80,2048]{1,0:T(8,128)(2,1)S(1)}, bf16[80,2048]{1,0:T(8,128)(2,1)S(1)}, u32[]{:S(2)}, u32[]{:S(2)}) collective-permute-start(bf16[80,2048]{1,0:T(8,128)(2,1)S(1)} %fusion.2.refs_0_), channel_id=1, source_target_pairs={{0,16},{8,24},{16,0},{24,8},{1,17},{9,25},{17,1},{25,9},{2,18},{10... | collective-permute-start | bytes 983048 | tf_op jit(solution)/shard_map/ppermute | solution.py:266
  109.8 4.0 %collective-permute-start.11 = (bf16[80,2048]{1,0:T(8,128)(2,1)S(1)}, bf16[80,2048]{1,0:T(8,128)(2,1)S(1)}, u32[]{:S(2)}, u32[]{:S(2)}) collective-permute-start(bf16[80,2048]{1,0:T(8,128)(2,1)S(1)} %fusion.2.refs_0_), channel_id=1, source_target_pairs={{0,24},{8,0},{16,8},{24,16},{1,25},{9,1},{17,9},{25,17},{2,26},{10... | collective-permute-start | bytes 983048 | tf_op jit(solution)/shard_map/ppermute | solution.py:266
  114.8 7.5 %collective-permute-done.10.refs_2_ = bf16[80,2048]{1,0:T(8,128)(2,1)S(1)} collective-permute-done((bf16[80,2048]{1,0:T(8,128)(2,1)S(1)}, bf16[80,2048]{1,0:T(8,128)(2,1)S(1)}, u32[]{:S(2)}, u32[]{:S(2)}) %collective-permute-start.10) | collective-permute-done | bytes 327712 | tf_op jit(solution)/shard_map/ppermute | solution.py:266
  122.3 2.1 collective-permute-done.11.refs_3_
  124.4 7.8 %all-to-all-done.2 = bf16[8,128,512]{2,1,0:T(8,128)(2,1)S(1)} async-done(((bf16[8,128,512]{2,1,0:T(8,128)(2,1)}), bf16[8,128,512]{2,1,0:T(8,128)(2,1)S(1)}, u32[]{:S(2)}, u32[]{:S(2)}) %all-to-all-start.2) | async-done | bytes 1048608 | tf_op jit(solution)/shard_map/all_to_all | solution.py:252
  132.2 2.4 %collective-permute-start.12 = (bf16[1024,512]{1,0:T(8,128)(2,1)S(1)}, bf16[1024,512]{1,0:T(8,128)(2,1)S(1)}, u32[]{:S(2)}, u32[]{:S(2)}) collective-permute-start(bf16[1024,512]{1,0:T(8,128)(2,1)S(1)} %bitcast.78), channel_id=1, source_target_pairs={{0,1},{1,0},{2,3},{3,2},{4,5},{5,4},{6,7},{7,6},{8,9},{9,8},{10,11... | collective-permute-start | bytes 3145736 | tf_op jit(solution)/shard_map/ppermute | solution.py:248
  135.3 1.5 collective-permute-done.12.refs_4_
  139.1 3.6 %all-to-all-start.3 = ((bf16[8,320,256]{2,1,0:T(8,128)(2,1)}), bf16[8,320,256]{2,1,0:T(8,128)(2,1)S(1)}, u32[]{:S(2)}, u32[]{:S(2)}) async-start(bf16[8,320,256]{2,1,0:T(8,128)(2,1)} %copy-done), calls=%async_computation.3 | async-start | bytes 2621440 | tf_op jit(solution)/shard_map/all_to_all | solution.py:252
  142.7 1.9 collective-permute-start.16
  144.6 1.9 collective-permute-start.15
  146.5 3.4 %collective-permute-start.14 = (bf16[256,512]{1,0:T(8,128)(2,1)S(1)}, bf16[256,512]{1,0:T(8,128)(2,1)S(1)}, u32[]{:S(2)}, u32[]{:S(2)}) collective-permute-start(bf16[256,512]{1,0:T(8,128)(2,1)S(1)} %bitcast.91), channel_id=1, source_target_pairs={{0,8},{8,16},{16,24},{24,0},{1,9},{9,17},{17,25},{25,1},{2,10},{10... | collective-permute-start | bytes 786440 | tf_op jit(solution)/shard_map/ppermute | solution.py:266
  150.0 2.1 collective-permute-done.16
  152.1 3.5 %collective-permute-done.15 = bf16[256,512]{1,0:T(8,128)(2,1)S(1)} collective-permute-done((bf16[256,512]{1,0:T(8,128)(2,1)S(1)}, bf16[256,512]{1,0:T(8,128)(2,1)S(1)}, u32[]{:S(2)}, u32[]{:S(2)}) %collective-permute-start.15) | collective-permute-done | bytes 262176 | tf_op jit(solution)/shard_map/ppermute | solution.py:266
  155.6 6.3 %collective-permute-done.14 = bf16[256,512]{1,0:T(8,128)(2,1)S(1)} collective-permute-done((bf16[256,512]{1,0:T(8,128)(2,1)S(1)}, bf16[256,512]{1,0:T(8,128)(2,1)S(1)}, u32[]{:S(2)}, u32[]{:S(2)}) %collective-permute-start.14) | collective-permute-done | bytes 262176 | tf_op jit(solution)/shard_map/ppermute | solution.py:266
  162.2 2.4 %collective-permute-start.17 = (bf16[4,256,512]{2,1,0:T(8,128)(2,1)S(1)}, bf16[4,256,512]{2,1,0:T(8,128)(2,1)S(1)}, u32[]{:S(2)}, u32[]{:S(2)}) collective-permute-start(bf16[4,256,512]{2,1,0:T(8,128)(2,1)S(1)} %pad_maximum_fusion.1.near_ref), channel_id=1, source_target_pairs={{0,1},{1,0},{2,3},{3,2},{4,5},{5,4},{6,7},{7,6},{8,9},{9,8},{10,11... | collective-permute-start | bytes 3145736 | tf_op jit(solution)/shard_map/ppermute | solution.py:248
  164.6 1.9 collective-permute-start.13
  166.6 7.1 %collective-permute-done.13.q_ref = bf16[320,128]{1,0:T(8,128)(2,1)S(1)} collective-permute-done((bf16[320,128]{1,0:T(8,128)(2,1)S(1)}, bf16[320,128]{1,0:T(8,128)(2,1)S(1)}, u32[]{:S(2)}, u32[]{:S(2)}) %collective-permute-start.13) | collective-permute-done | bytes 81952 | tf_op jit(solution)/shard_map/ppermute | solution.py:312
  173.7 3.7 %all-to-all-done.3 = bf16[8,320,256]{2,1,0:T(8,128)(2,1)S(1)} async-done(((bf16[8,320,256]{2,1,0:T(8,128)(2,1)}), bf16[8,320,256]{2,1,0:T(8,128)(2,1)S(1)}, u32[]{:S(2)}, u32[]{:S(2)}) %all-to-all-start.3) | async-done | bytes 1310752 | tf_op jit(solution)/shard_map/all_to_all | solution.py:252
  177.4 2.5 %collective-permute-start.18 = (bf16[2560,256]{1,0:T(8,128)(2,1)S(1)}, bf16[2560,256]{1,0:T(8,128)(2,1)S(1)}, u32[]{:S(2)}, u32[]{:S(2)}) collective-permute-start(bf16[2560,256]{1,0:T(8,128)(2,1)S(1)} %bitcast.81), channel_id=1, source_target_pairs={{0,1},{1,0},{2,3},{3,2},{4,5},{5,4},{6,7},{7,6},{8,9},{9,8},{10,11... | collective-permute-start | bytes 3932168 | tf_op jit(solution)/shard_map/ppermute | solution.py:248
  179.9 2.3 %shard_map.68 = (f32[320,128]{1,0:T(8,128)S(1)}, f32[320,128]{1,0:T(8,128)S(1)}) custom-call(s32[4]{0:T(128)S(1)} %get-tuple-element.47.start_ref, bf16[320,128]{1,0:T(8,128)(2,1)S(1)} %collective-permute-done.13.q_ref, bf16[2560,256]{1,0:T(8,128)(2,1)S(1)} %bitcast.82, s32[1,2560]{1,0:T(1,128)S(1)} %add.274.near_pos.kpos_ref), custom_call_target="tpu_custom_call" | custom-call | flops 419430400 | bytes 1310720 | tf_op jit(solution)/shard_map/pallas_call | solution.py:175
  182.6 2.5 %shard_map.69 = bf16[4,96,128]{2,1,0:T(8,128)(2,1)S(1)} custom-call(s32[4]{0:T(128)S(1)} %get-tuple-element.47.start_ref, bf16[320,128]{1,0:T(8,128)(2,1)S(1)} %collective-permute-done.13.q_ref, bf16[2560,256]{1,0:T(8,128)(2,1)S(1)} %collective-permute-done.18.far_ref.kv_ref, s32[1,2560]{1,0:T(1,128)S(1)} %broadcast_add_fusion.far_pos.kpos_ref, ...), custom_call_target="tpu_custom_call" | custom-call | flops 419430400 | bytes 1310720 | tf_op jit(solution)/shard_map/pallas_call | solution.py:175
  185.0 2.1 collective-permute-start.19
  187.2 4.0 %shard_map.67.near_ref = bf16[4,96,128]{2,1,0:T(8,128)(2,1)S(1)} custom-call(s32[4]{0:T(128)S(1)} %get-tuple-element.29.start_ref, bf16[320,128]{1,0:T(8,128)(2,1)S(1)} %copy-done.3, bf16[2560,256]{1,0:T(8,128)(2,1)S(1)} %bitcast.83, bf16[2560,256]{1,0:T(8,128)(2,1)S(1)} %collective-permute-done.18.far_ref.kv_ref, s32[1,2560]{1,0:T(1,128)S(1)} %add.274.near_pos.kpos_ref, ...), custom_call_target="tpu_custom_call" | custom-call | flops 838860800 | bytes 2621440 | tf_op jit(solution)/shard_map/pallas_call | solution.py:175
  191.2 3.7 %collective-permute-done.19.far_ref = bf16[4,96,128]{2,1,0:T(8,128)(2,1)S(1)} collective-permute-done((bf16[4,96,128]{2,1,0:T(8,128)(2,1)S(1)}, bf16[4,96,128]{2,1,0:T(8,128)(2,1)S(1)}, u32[]{:S(2)}, u32[]{:S(2)}) %collective-permute-start.19) | collective-permute-done | bytes 98336 | tf_op jit(solution)/shard_map/ppermute | solution.py:312
  195.7 6.9 %all_to_all.30.context_ref = bf16[4,80,128]{2,1,0:T(8,128)(2,1)S(1)} all-to-all(bf16[4,80,128]{2,1,0:T(8,128)(2,1)S(1)} %shard_map.70), channel_id=1, replica_groups=mesh['zh'=2,'yh'=2,'yl'=4,'x'=4,'zl'=4,'c'=2] {'x'}, dimensions={0} | all-to-all | bytes 163840 | tf_op jit(solution)/shard_map/all_to_all | solution.py:252
  203.1 14.4 %all_to_all.31 = bf16[8,80,256]{2,1,0:T(8,128)(2,1)S(1)} all-to-all(bf16[8,80,256]{2,1,0:T(8,128)(2,1)S(1)} %shard_map.71), channel_id=1, replica_groups=mesh['zh'=2,'yh'=2,'yl'=4,'x'=4,'zl'=4,'c'=2] {'zl','c'}, dimensions={0} | all-to-all | bytes 655360 | tf_op jit(solution)/shard_map/all_to_all | solution.py:252
  (60 shorter events, 17.8 us)
Async XLA Ops:
  3.3 40.9 %all-to-all-start = ((bf16[4,8,128,384]{3,2,1,0:T(8,128)(2,1)}), bf16[4,8,128,384]{3,2,1,0:T(8,128)(2,1)S(1)}, u32[]{:S(2)}, u32[]{:S(2)}) async-start(bf16[4,8,128,384]{3,2,1,0:T(8,128)(2,1)} %shard_map.64), calls=%async_computation | async-start | bytes 6291456 | tf_op jit(solution)/shard_map/all_to_all | solution.py:252
  8.2 14.7 %copy-start.5 = (s32[64]{0:T(128)S(1)}, s32[64]{0:T(128)}, u32[]{:S(2)}) copy-start(s32[64]{0:T(128)} %param.11) | copy-start | bytes 772
  8.2 16.3 %copy-start.4 = (f32[2048]{0:T(1024)S(1)}, f32[2048]{0:T(1024)}, u32[]{:S(2)}) copy-start(f32[2048]{0:T(1024)} %param.7) | copy-start | bytes 24580
  13.3 13.1 %collective-permute-start = (bf16[2,32,2048]{2,1,0:T(8,128)(2,1)}, bf16[2,32,2048]{2,1,0:T(8,128)(2,1)}, u32[]{:S(2)}, u32[]{:S(2)}) collective-permute-start(bf16[2,32,2048]{2,1,0:T(8,128)(2,1)} %get-tuple-element.58), channel_id=1, source_target_pairs={{0,96},{32,0},{64,32},{96,64},{1,97},{33,1},{65,33},{97,65},{2,98}... | collective-permute-start | bytes 786440 | tf_op jit(solution)/shard_map/ppermute | solution.py:266
  18.5 10.7 %collective-permute-start.1 = (bf16[2,32,2048]{2,1,0:T(8,128)(2,1)}, bf16[2,32,2048]{2,1,0:T(8,128)(2,1)}, u32[]{:S(2)}, u32[]{:S(2)}) collective-permute-start(bf16[2,32,2048]{2,1,0:T(8,128)(2,1)} %get-tuple-element.59), channel_id=1, source_target_pairs={{0,32},{32,64},{64,96},{96,0},{1,33},{33,65},{65,97},{97,1},{2,34}... | collective-permute-start | bytes 786440 | tf_op jit(solution)/shard_map/ppermute | solution.py:266
  20.4 22.1 %collective-permute-start.2 = (bf16[2,32,2048]{2,1,0:T(8,128)(2,1)}, bf16[2,32,2048]{2,1,0:T(8,128)(2,1)}, u32[]{:S(2)}, u32[]{:S(2)}) collective-permute-start(bf16[2,32,2048]{2,1,0:T(8,128)(2,1)} %get-tuple-element.57), channel_id=1, source_target_pairs={{0,64},{32,96},{64,0},{96,32},{1,65},{33,97},{65,1},{97,33},{2,66}... | collective-permute-start | bytes 786440 | tf_op jit(solution)/shard_map/ppermute | solution.py:266
  45.2 29.2 %all-to-all-start.1 = ((bf16[8,128,384]{2,1,0:T(8,128)(2,1)}), bf16[8,128,384]{2,1,0:T(8,128)(2,1)S(1)}, u32[]{:S(2)}, u32[]{:S(2)}) async-start(bf16[8,128,384]{2,1,0:T(8,128)(2,1)} %dynamic-slice_bitcast_fusion), calls=%async_computation.1 | async-start | bytes 1572864 | tf_op jit(solution)/shard_map/all_to_all | solution.py:252
  54.3 7.9 %collective-permute-start.3 = (bf16[2,32,512]{2,1,0:T(8,128)(2,1)S(1)}, bf16[2,32,512]{2,1,0:T(8,128)(2,1)S(1)}, u32[]{:S(2)}, u32[]{:S(2)}) collective-permute-start(bf16[2,32,512]{2,1,0:T(8,128)(2,1)S(1)} %bitcast.98), channel_id=1, source_target_pairs={{0,24},{8,0},{16,8},{24,16},{1,25},{9,1},{17,9},{25,17},{2,26},{10... | collective-permute-start | bytes 196616 | tf_op jit(solution)/shard_map/ppermute | solution.py:266
  57.1 6.5 %collective-permute-start.4 = (bf16[2,32,512]{2,1,0:T(8,128)(2,1)S(1)}, bf16[2,32,512]{2,1,0:T(8,128)(2,1)S(1)}, u32[]{:S(2)}, u32[]{:S(2)}) collective-permute-start(bf16[2,32,512]{2,1,0:T(8,128)(2,1)S(1)} %bitcast.99), channel_id=1, source_target_pairs={{0,8},{8,16},{16,24},{24,0},{1,9},{9,17},{17,25},{25,1},{2,10},{10... | collective-permute-start | bytes 196616 | tf_op jit(solution)/shard_map/ppermute | solution.py:266
  59.7 6.8 %collective-permute-start.5 = (bf16[2,32,512]{2,1,0:T(8,128)(2,1)S(1)}, bf16[2,32,512]{2,1,0:T(8,128)(2,1)S(1)}, u32[]{:S(2)}, u32[]{:S(2)}) collective-permute-start(bf16[2,32,512]{2,1,0:T(8,128)(2,1)S(1)} %bitcast.100), channel_id=1, source_target_pairs={{0,16},{8,24},{16,0},{24,8},{1,17},{9,25},{17,1},{25,9},{2,18},{10... | collective-permute-start | bytes 196616 | tf_op jit(solution)/shard_map/ppermute | solution.py:266
  66.5 6.5 %collective-permute-start.6 = (bf16[32,512]{1,0:T(8,128)(2,1)S(1)}, bf16[32,512]{1,0:T(8,128)(2,1)S(1)}, u32[]{:S(2)}, u32[]{:S(2)}) collective-permute-start(bf16[32,512]{1,0:T(8,128)(2,1)S(1)} %slice_bitcast_fusion), channel_id=1, source_target_pairs={{0,224},{32,192},{64,160},{96,128},{128,96},{160,64},{192,32},{224... | collective-permute-start | bytes 98312 | tf_op jit(solution)/shard_map/ppermute | solution.py:350
  74.4 18.8 %collective-permute-start.8 = (bf16[128,512]{1,0:T(8,128)(2,1)S(1)}, bf16[128,512]{1,0:T(8,128)(2,1)S(1)}, u32[]{:S(2)}, u32[]{:S(2)}) collective-permute-start(bf16[128,512]{1,0:T(8,128)(2,1)S(1)} %pad_maximum_fusion.2), channel_id=1, source_target_pairs={{0,262},{1,270},{2,260},{3,268},{4,258},{5,266},{6,256},{7,264},{8... | collective-permute-start | bytes 393224 | tf_op jit(solution)/shard_map/ppermute | solution.py:308
  87.8 6.3 %collective-permute-start.7 = (bf16[128,512]{1,0:T(8,128)(2,1)S(1)}, bf16[128,512]{1,0:T(8,128)(2,1)S(1)}, u32[]{:S(2)}, u32[]{:S(2)}) collective-permute-start(bf16[128,512]{1,0:T(8,128)(2,1)S(1)} %pad_maximum_fusion.2), channel_id=1, source_target_pairs={{1,8},{3,10},{5,12},{7,14},{8,1},{10,3},{12,5},{14,7},{17,24},{19,... | collective-permute-start | bytes 393224 | tf_op jit(solution)/shard_map/ppermute | solution.py:308
  95.1 37.1 %all-to-all-start.2 = ((bf16[8,128,512]{2,1,0:T(8,128)(2,1)}), bf16[8,128,512]{2,1,0:T(8,128)(2,1)S(1)}, u32[]{:S(2)}, u32[]{:S(2)}) async-start(bf16[8,128,512]{2,1,0:T(8,128)(2,1)} %broadcast_in_dim.2), calls=%async_computation.2 | async-start | bytes 2097152 | tf_op jit(solution)/shard_map/all_to_all | solution.py:252
  103.0 11.9 %collective-permute-start.9 = (bf16[80,2048]{1,0:T(8,128)(2,1)S(1)}, bf16[80,2048]{1,0:T(8,128)(2,1)S(1)}, u32[]{:S(2)}, u32[]{:S(2)}) collective-permute-start(bf16[80,2048]{1,0:T(8,128)(2,1)S(1)} %fusion.2.refs_0_), channel_id=1, source_target_pairs={{0,8},{8,16},{16,24},{24,0},{1,9},{9,17},{17,25},{25,1},{2,10},{10... | collective-permute-start | bytes 983048 | tf_op jit(solution)/shard_map/ppermute | solution.py:266
  104.9 17.4 %collective-permute-start.10 = (bf16[80,2048]{1,0:T(8,128)(2,1)S(1)}, bf16[80,2048]{1,0:T(8,128)(2,1)S(1)}, u32[]{:S(2)}, u32[]{:S(2)}) collective-permute-start(bf16[80,2048]{1,0:T(8,128)(2,1)S(1)} %fusion.2.refs_0_), channel_id=1, source_target_pairs={{0,16},{8,24},{16,0},{24,8},{1,17},{9,25},{17,1},{25,9},{2,18},{10... | collective-permute-start | bytes 983048 | tf_op jit(solution)/shard_map/ppermute | solution.py:266
  109.8 14.6 %collective-permute-start.11 = (bf16[80,2048]{1,0:T(8,128)(2,1)S(1)}, bf16[80,2048]{1,0:T(8,128)(2,1)S(1)}, u32[]{:S(2)}, u32[]{:S(2)}) collective-permute-start(bf16[80,2048]{1,0:T(8,128)(2,1)S(1)} %fusion.2.refs_0_), channel_id=1, source_target_pairs={{0,24},{8,0},{16,8},{24,16},{1,25},{9,1},{17,9},{25,17},{2,26},{10... | collective-permute-start | bytes 983048 | tf_op jit(solution)/shard_map/ppermute | solution.py:266
  132.2 4.7 %collective-permute-start.12 = (bf16[1024,512]{1,0:T(8,128)(2,1)S(1)}, bf16[1024,512]{1,0:T(8,128)(2,1)S(1)}, u32[]{:S(2)}, u32[]{:S(2)}) collective-permute-start(bf16[1024,512]{1,0:T(8,128)(2,1)S(1)} %bitcast.78), channel_id=1, source_target_pairs={{0,1},{1,0},{2,3},{3,2},{4,5},{5,4},{6,7},{7,6},{8,9},{9,8},{10,11... | collective-permute-start | bytes 3145736 | tf_op jit(solution)/shard_map/ppermute | solution.py:248
  137.4 1.1 copy-start
  138.5 0.6 copy-start.1
  139.1 38.3 %all-to-all-start.3 = ((bf16[8,320,256]{2,1,0:T(8,128)(2,1)}), bf16[8,320,256]{2,1,0:T(8,128)(2,1)S(1)}, u32[]{:S(2)}, u32[]{:S(2)}) async-start(bf16[8,320,256]{2,1,0:T(8,128)(2,1)} %copy-done), calls=%async_computation.3 | async-start | bytes 2621440 | tf_op jit(solution)/shard_map/all_to_all | solution.py:252
  142.7 9.4 %collective-permute-start.16 = (bf16[256,512]{1,0:T(8,128)(2,1)S(1)}, bf16[256,512]{1,0:T(8,128)(2,1)S(1)}, u32[]{:S(2)}, u32[]{:S(2)}) collective-permute-start(bf16[256,512]{1,0:T(8,128)(2,1)S(1)} %bitcast.89), channel_id=1, source_target_pairs={{0,24},{8,0},{16,8},{24,16},{1,25},{9,1},{17,9},{25,17},{2,26},{10... | collective-permute-start | bytes 786440 | tf_op jit(solution)/shard_map/ppermute | solution.py:266
  144.6 11.0 %collective-permute-start.15 = (bf16[256,512]{1,0:T(8,128)(2,1)S(1)}, bf16[256,512]{1,0:T(8,128)(2,1)S(1)}, u32[]{:S(2)}, u32[]{:S(2)}) collective-permute-start(bf16[256,512]{1,0:T(8,128)(2,1)S(1)} %bitcast.90), channel_id=1, source_target_pairs={{0,16},{8,24},{16,0},{24,8},{1,17},{9,25},{17,1},{25,9},{2,18},{10... | collective-permute-start | bytes 786440 | tf_op jit(solution)/shard_map/ppermute | solution.py:266
  146.5 15.3 %collective-permute-start.14 = (bf16[256,512]{1,0:T(8,128)(2,1)S(1)}, bf16[256,512]{1,0:T(8,128)(2,1)S(1)}, u32[]{:S(2)}, u32[]{:S(2)}) collective-permute-start(bf16[256,512]{1,0:T(8,128)(2,1)S(1)} %bitcast.91), channel_id=1, source_target_pairs={{0,8},{8,16},{16,24},{24,0},{1,9},{9,17},{17,25},{25,1},{2,10},{10... | collective-permute-start | bytes 786440 | tf_op jit(solution)/shard_map/ppermute | solution.py:266
  161.9 2.8 %copy-start.2 = (bf16[320,128]{1,0:T(8,128)(2,1)S(1)}, bf16[320,128]{1,0:T(8,128)(2,1)}, u32[]{:S(2)}) copy-start(bf16[320,128]{1,0:T(8,128)(2,1)} %copy-done.1) | copy-start | bytes 245764
  162.2 11.5 %collective-permute-start.17 = (bf16[4,256,512]{2,1,0:T(8,128)(2,1)S(1)}, bf16[4,256,512]{2,1,0:T(8,128)(2,1)S(1)}, u32[]{:S(2)}, u32[]{:S(2)}) collective-permute-start(bf16[4,256,512]{2,1,0:T(8,128)(2,1)S(1)} %pad_maximum_fusion.1.near_ref), channel_id=1, source_target_pairs={{0,1},{1,0},{2,3},{3,2},{4,5},{5,4},{6,7},{7,6},{8,9},{9,8},{10,11... | collective-permute-start | bytes 3145736 | tf_op jit(solution)/shard_map/ppermute | solution.py:248
  164.6 9.0 %collective-permute-start.13 = (bf16[320,128]{1,0:T(8,128)(2,1)S(1)}, bf16[320,128]{1,0:T(8,128)(2,1)S(1)}, u32[]{:S(2)}, u32[]{:S(2)}) collective-permute-start(bf16[320,128]{1,0:T(8,128)(2,1)S(1)} %copy-done.2), channel_id=1, source_target_pairs={{0,262},{2,260},{4,258},{6,256},{256,6},{258,4},{260,2},{262,0},{1... | collective-permute-start | bytes 245768 | tf_op jit(solution)/shard_map/ppermute | solution.py:312
  177.4 9.7 %copy-start.3 = (bf16[320,128]{1,0:T(8,128)(2,1)S(1)}, bf16[320,128]{1,0:T(8,128)(2,1)}, u32[]{:S(2)}) copy-start(bf16[320,128]{1,0:T(8,128)(2,1)} %copy-done.1) | copy-start | bytes 245764
  177.4 5.2 %collective-permute-start.18 = (bf16[2560,256]{1,0:T(8,128)(2,1)S(1)}, bf16[2560,256]{1,0:T(8,128)(2,1)S(1)}, u32[]{:S(2)}, u32[]{:S(2)}) collective-permute-start(bf16[2560,256]{1,0:T(8,128)(2,1)S(1)} %bitcast.81), channel_id=1, source_target_pairs={{0,1},{1,0},{2,3},{3,2},{4,5},{5,4},{6,7},{7,6},{8,9},{9,8},{10,11... | collective-permute-start | bytes 3932168 | tf_op jit(solution)/shard_map/ppermute | solution.py:248
  185.0 9.8 %collective-permute-start.19 = (bf16[4,96,128]{2,1,0:T(8,128)(2,1)S(1)}, bf16[4,96,128]{2,1,0:T(8,128)(2,1)S(1)}, u32[]{:S(2)}, u32[]{:S(2)}) collective-permute-start(bf16[4,96,128]{2,1,0:T(8,128)(2,1)S(1)} %shard_map.69), channel_id=1, source_target_pairs={{0,262},{2,260},{4,258},{6,256},{256,6},{258,4},{260,2},{262,0},{1... | collective-permute-start | bytes 294920 | tf_op jit(solution)/shard_map/ppermute | solution.py:312

commit v15 on v14

--- a/solution.py
+++ b/solution.py
@@ -341,12 +341,13 @@
     wo = snap_out[0].reshape(2, ny // 2, -1, snap_out.shape[2])
     wo = jnp.stack([pick(wo, yh), jnp.flip(pick(wo, 1 - yh), 0)], axis=1)
     wo = take_shifts(pick(wo, yl), ahead(wo, "yl"), "yl", y0 % (ny // 2))
-    w, wo, normed, kpos, start, start_other = lax.optimization_barrier(
-        (w, wo, normed, kpos, start, start_other)
+    wo = jnp.transpose(wo.reshape(2, -1, nx, snap_out.shape[2] // nx), (2, 0, 1, 3))
+    wo, blocks = pick(wo, x), ahead(wo, "x")
+    w, wo, blocks, normed, kpos, start, start_other = lax.optimization_barrier(
+        (w, wo, blocks, normed, kpos, start, start_other)
     )
     w = pick(exchange(w, ys), y0)
-    wo = jnp.transpose(wo.reshape(2, -1, nx, snap_out.shape[2] // nx), (2, 0, 1, 3))
-    wo = take_shifts(pick(wo, x), ahead(wo, "x"), "x", x0)
+    wo = take_shifts(wo, blocks, "x", x0)
     wo = jnp.where(yh == y0 // (ny // 2), wo[0], lax.ppermute(wo[1], ys, [(i, 7 - i) for i in range(8)]))
     wo = jnp.transpose(wo.reshape(wo.shape[0], nx, HD), (1, 0, 2)).reshape(part, HD)
     w = jnp.concatenate([w, wo], axis=1)

time: 219 us -> 221 us (level)
  waiting for transfers between devices: 74.5 us -> 68.8 us
  blocking collectives: 21.3 us -> 25.5 us
  local copies, waits for them, and re-layouts: 9.06 us -> 12.3 us
    ppermute x2, waiting for transfers between devices: 10.8 us -> 3.88 us  [mirror(): return lax.ppermute(block, ('zh', 'zl'), [(i, 7 - i) for i in range(8)])]
    all_to_all x4, starting transfers between devices: 23.6 us -> 17.5 us  [exchange(): return lax.all_to_all(block, axis, 0, 0, tiled=True)]
    all_to_all x2, blocking collectives: 21.3 us -> 25.5 us  [exchange(): return lax.all_to_all(block, axis, 0, 0, tiled=True)]
    ppermute x2, starting transfers between devices: 4.02 us -> 7.3 us  [mirror(): return lax.ppermute(block, ('zh', 'zl'), [(i, 7 - i) for i in range(8)])]
    ppermute x12, starting transfers between devices: 35.3 us -> 38.2 us  [shift(): lax.ppermute(block, axis, [(i, (i + distance) % count) for i in range(cou...]
  transfers between devices with their start and end apart: 24 -> 24, of which waited for: 20 -> 19; matrix products, arithmetic and copies ran while one was open for 5% -> 7% of each run, Pallas kernels for 3% -> 3%
where the time goes in v15:
time: 221 us; the launch traced here: 220 us
  starting transfers between devices  89.3 us (40%)
  waiting for transfers between devices  68.8 us (31%)
  blocking collectives  25.5 us (12%)
  Pallas kernels  14.5 us (7%)
  local copies, waits for them, and re-layouts  12.3 us (6%)
  other arithmetic  8.23 us (4%)
    ppermute x12, waiting for transfers between devices, shift(): lax.ppermute(block, axis, [(i, (i + distance) % count) for i in range(cou...  41.6 us
    ppermute x12, starting transfers between devices, shift(): lax.ppermute(block, axis, [(i, (i + distance) % count) for i in range(cou...  38.2 us
    all_to_all x2, blocking collectives, exchange(): return lax.all_to_all(block, axis, 0, 0, tiled=True)  25.5 us
    all_to_all x4, starting transfers between devices, exchange(): return lax.all_to_all(block, axis, 0, 0, tiled=True)  17.5 us
    ppermute x2, starting transfers between devices, trade(): return lax.ppermute(block, ('zh', 'x', 'zl', 'c'), route)  14.2 us
    all_to_all x4, waiting for transfers between devices, exchange(): return lax.all_to_all(block, axis, 0, 0, tiled=True)  14.1 us
    pallas_call x3, Pallas kernels, attend(): pl.pallas_call(functools.partial(kernel, half), in_specs=[pl.BlockSpec(me...  8.78 us
    ppermute x3, starting transfers between devices, swap(): return lax.ppermute(block, axis, [(0, 1), (1, 0)])  7.51 us
  transfers between devices with their start and end apart: 24, of which 19 were waited for; matrix products, arithmetic and copies ran while one was open for 7% of the time, Pallas kernels for 3%

profile of v15, /device:TPU:1, one launch (start us, length us, event | category | flops | bytes accessed | tf_op | source)
XLA Modules:
  0.0 220.0 jit_solution(15861457495307373358)
XLA Ops:
  0.0 3.3 %shard_map.64 = bf16[4,8,128,384]{3,2,1,0:T(8,128)(2,1)} custom-call(bf16[3,2,8,128,256]{4,3,2,1,0:T(8,128)(2,1)} %bitcast.77), custom_call_target="tpu_custom_call" | custom-call | bytes 6291456 | tf_op jit(solution)/shard_map/pallas_call | solution.py:29
  3.3 4.8 %all-to-all-start = ((bf16[4,8,128,384]{3,2,1,0:T(8,128)(2,1)}), bf16[4,8,128,384]{3,2,1,0:T(8,128)(2,1)S(1)}, u32[]{:S(2)}, u32[]{:S(2)}) async-start(bf16[4,8,128,384]{3,2,1,0:T(8,128)(2,1)} %shard_map.64), calls=%async_computation | async-start | bytes 6291456 | tf_op jit(solution)/shard_map/all_to_all | solution.py:252
  8.2 2.1 dynamic-slice_bitcast_fusion.1
  11.1 2.1 fusion.13
  13.2 5.2 %collective-permute-start = (bf16[2,32,2048]{2,1,0:T(8,128)(2,1)}, bf16[2,32,2048]{2,1,0:T(8,128)(2,1)}, u32[]{:S(2)}, u32[]{:S(2)}) collective-permute-start(bf16[2,32,2048]{2,1,0:T(8,128)(2,1)} %get-tuple-element.64), channel_id=1, source_target_pairs={{0,96},{32,0},{64,32},{96,64},{1,97},{33,1},{65,33},{97,65},{2,98}... | collective-permute-start | bytes 786440 | tf_op jit(solution)/shard_map/ppermute | solution.py:266
  18.5 1.9 collective-permute-start.1
  20.4 2.4 %collective-permute-start.2 = (bf16[2,32,2048]{2,1,0:T(8,128)(2,1)}, bf16[2,32,2048]{2,1,0:T(8,128)(2,1)}, u32[]{:S(2)}, u32[]{:S(2)}) collective-permute-start(bf16[2,32,2048]{2,1,0:T(8,128)(2,1)} %get-tuple-element.63), channel_id=1, source_target_pairs={{0,64},{32,96},{64,0},{96,32},{1,65},{33,97},{65,1},{97,33},{2,66}... | collective-permute-start | bytes 786440 | tf_op jit(solution)/shard_map/ppermute | solution.py:266
  26.4 2.8 %collective-permute-done.1 = bf16[2,32,2048]{2,1,0:T(8,128)(2,1)} collective-permute-done((bf16[2,32,2048]{2,1,0:T(8,128)(2,1)}, bf16[2,32,2048]{2,1,0:T(8,128)(2,1)}, u32[]{:S(2)}, u32[]{:S(2)}) %collective-permute-start.1) | collective-permute-done | bytes 262176 | tf_op jit(solution)/shard_map/ppermute | solution.py:266
  29.2 13.3 %collective-permute-done.2 = bf16[2,32,2048]{2,1,0:T(8,128)(2,1)} collective-permute-done((bf16[2,32,2048]{2,1,0:T(8,128)(2,1)}, bf16[2,32,2048]{2,1,0:T(8,128)(2,1)}, u32[]{:S(2)}, u32[]{:S(2)}) %collective-permute-start.2) | collective-permute-done | bytes 262176 | tf_op jit(solution)/shard_map/ppermute | solution.py:266
  42.5 1.8 fusion.7
  44.3 1.8 reshape.99
  46.1 1.9 constant_dynamic-slice_fusion.11
  50.3 4.7 %all-to-all-start.1 = ((bf16[8,128,384]{2,1,0:T(8,128)(2,1)}), bf16[8,128,384]{2,1,0:T(8,128)(2,1)S(1)}, u32[]{:S(2)}, u32[]{:S(2)}) async-start(bf16[8,128,384]{2,1,0:T(8,128)(2,1)} %dynamic-slice_bitcast_fusion), calls=%async_computation.1 | async-start | bytes 1572864 | tf_op jit(solution)/shard_map/all_to_all | solution.py:252
  55.0 4.6 %collective-permute-start.3 = (bf16[2,32,512]{2,1,0:T(8,128)(2,1)}, bf16[2,32,512]{2,1,0:T(8,128)(2,1)S(1)}, u32[]{:S(2)}, u32[]{:S(2)}) collective-permute-start(bf16[2,32,512]{2,1,0:T(8,128)(2,1)} %get-tuple-element.34), channel_id=1, source_target_pairs={{0,24},{8,0},{16,8},{24,16},{1,25},{9,1},{17,9},{25,17},{2,26},{10... | collective-permute-start | bytes 196616 | tf_op jit(solution)/shard_map/ppermute | solution.py:266
  59.6 2.5 %collective-permute-start.4 = (bf16[2,32,512]{2,1,0:T(8,128)(2,1)}, bf16[2,32,512]{2,1,0:T(8,128)(2,1)S(1)}, u32[]{:S(2)}, u32[]{:S(2)}) collective-permute-start(bf16[2,32,512]{2,1,0:T(8,128)(2,1)} %get-tuple-element.35), channel_id=1, source_target_pairs={{0,16},{8,24},{16,0},{24,8},{1,17},{9,25},{17,1},{25,9},{2,18},{10... | collective-permute-start | bytes 196616 | tf_op jit(solution)/shard_map/ppermute | solution.py:266
  62.1 2.5 %collective-permute-start.5 = (bf16[2,32,512]{2,1,0:T(8,128)(2,1)}, bf16[2,32,512]{2,1,0:T(8,128)(2,1)S(1)}, u32[]{:S(2)}, u32[]{:S(2)}) collective-permute-start(bf16[2,32,512]{2,1,0:T(8,128)(2,1)} %get-tuple-element.36), channel_id=1, source_target_pairs={{0,8},{8,16},{16,24},{24,0},{1,9},{9,17},{17,25},{25,1},{2,10},{10... | collective-permute-start | bytes 196616 | tf_op jit(solution)/shard_map/ppermute | solution.py:266
  64.6 2.0 collective-permute-done.4
  66.6 2.6 %collective-permute-done.5 = bf16[2,32,512]{2,1,0:T(8,128)(2,1)S(1)} collective-permute-done((bf16[2,32,512]{2,1,0:T(8,128)(2,1)}, bf16[2,32,512]{2,1,0:T(8,128)(2,1)S(1)}, u32[]{:S(2)}, u32[]{:S(2)}) %collective-permute-start.5) | collective-permute-done | bytes 65568 | tf_op jit(solution)/shard_map/ppermute | solution.py:266
  70.1 4.6 %collective-permute-start.6 = (bf16[32,512]{1,0:T(8,128)(2,1)S(1)}, bf16[32,512]{1,0:T(8,128)(2,1)S(1)}, u32[]{:S(2)}, u32[]{:S(2)}) collective-permute-start(bf16[32,512]{1,0:T(8,128)(2,1)S(1)} %slice_bitcast_fusion), channel_id=1, source_target_pairs={{0,224},{32,192},{64,160},{96,128},{128,96},{160,64},{192,32},{224... | collective-permute-start | bytes 98312 | tf_op jit(solution)/shard_map/ppermute | solution.py:351
  74.8 2.3 %collective-permute-done.6 = bf16[32,512]{1,0:T(8,128)(2,1)S(1)} collective-permute-done((bf16[32,512]{1,0:T(8,128)(2,1)S(1)}, bf16[32,512]{1,0:T(8,128)(2,1)S(1)}, u32[]{:S(2)}, u32[]{:S(2)}) %collective-permute-start.6) | collective-permute-done | bytes 32800 | tf_op jit(solution)/shard_map/ppermute | solution.py:351
  78.6 12.2 %collective-permute-start.8 = (bf16[128,512]{1,0:T(8,128)(2,1)S(1)}, bf16[128,512]{1,0:T(8,128)(2,1)S(1)}, u32[]{:S(2)}, u32[]{:S(2)}) collective-permute-start(bf16[128,512]{1,0:T(8,128)(2,1)S(1)} %pad_maximum_fusion.2), channel_id=1, source_target_pairs={{0,262},{1,270},{2,260},{3,268},{4,258},{5,266},{6,256},{7,264},{8... | collective-permute-start | bytes 393224 | tf_op jit(solution)/shard_map/ppermute | solution.py:308
  90.8 1.9 collective-permute-start.7
  92.8 4.3 %collective-permute-done.8 = bf16[128,512]{1,0:T(8,128)(2,1)S(1)} collective-permute-done((bf16[128,512]{1,0:T(8,128)(2,1)S(1)}, bf16[128,512]{1,0:T(8,128)(2,1)S(1)}, u32[]{:S(2)}, u32[]{:S(2)}) %collective-permute-start.8) | collective-permute-done | bytes 131104 | tf_op jit(solution)/shard_map/ppermute | solution.py:308
  98.9 4.4 %all-to-all-start.2 = ((bf16[8,128,512]{2,1,0:T(8,128)(2,1)}), bf16[8,128,512]{2,1,0:T(8,128)(2,1)S(1)}, u32[]{:S(2)}, u32[]{:S(2)}) async-start(bf16[8,128,512]{2,1,0:T(8,128)(2,1)} %broadcast_in_dim.2), calls=%async_computation.2 | async-start | bytes 2097152 | tf_op jit(solution)/shard_map/all_to_all | solution.py:252
  103.3 1.9 collective-permute-start.9
  105.2 4.3 %collective-permute-start.10 = (bf16[80,2048]{1,0:T(8,128)(2,1)S(1)}, bf16[80,2048]{1,0:T(8,128)(2,1)S(1)}, u32[]{:S(2)}, u32[]{:S(2)}) collective-permute-start(bf16[80,2048]{1,0:T(8,128)(2,1)S(1)} %fusion.2.refs_0_), channel_id=1, source_target_pairs={{0,16},{8,24},{16,0},{24,8},{1,17},{9,25},{17,1},{25,9},{2,18},{10... | collective-permute-start | bytes 983048 | tf_op jit(solution)/shard_map/ppermute | solution.py:266
  109.5 4.0 %collective-permute-start.11 = (bf16[80,2048]{1,0:T(8,128)(2,1)S(1)}, bf16[80,2048]{1,0:T(8,128)(2,1)S(1)}, u32[]{:S(2)}, u32[]{:S(2)}) collective-permute-start(bf16[80,2048]{1,0:T(8,128)(2,1)S(1)} %fusion.2.refs_0_), channel_id=1, source_target_pairs={{0,24},{8,0},{16,8},{24,16},{1,25},{9,1},{17,9},{25,17},{2,26},{10... | collective-permute-start | bytes 983048 | tf_op jit(solution)/shard_map/ppermute | solution.py:266
  115.2 6.8 %collective-permute-done.10.refs_2_ = bf16[80,2048]{1,0:T(8,128)(2,1)S(1)} collective-permute-done((bf16[80,2048]{1,0:T(8,128)(2,1)S(1)}, bf16[80,2048]{1,0:T(8,128)(2,1)S(1)}, u32[]{:S(2)}, u32[]{:S(2)}) %collective-permute-start.10) | collective-permute-done | bytes 327712 | tf_op jit(solution)/shard_map/ppermute | solution.py:266
  122.0 2.4 %collective-permute-done.11.refs_3_ = bf16[80,2048]{1,0:T(8,128)(2,1)S(1)} collective-permute-done((bf16[80,2048]{1,0:T(8,128)(2,1)S(1)}, bf16[80,2048]{1,0:T(8,128)(2,1)S(1)}, u32[]{:S(2)}, u32[]{:S(2)}) %collective-permute-start.11) | collective-permute-done | bytes 327712 | tf_op jit(solution)/shard_map/ppermute | solution.py:266
  124.5 8.0 %all-to-all-done.2 = bf16[8,128,512]{2,1,0:T(8,128)(2,1)S(1)} async-done(((bf16[8,128,512]{2,1,0:T(8,128)(2,1)}), bf16[8,128,512]{2,1,0:T(8,128)(2,1)S(1)}, u32[]{:S(2)}, u32[]{:S(2)}) %all-to-all-start.2) | async-done | bytes 1048608 | tf_op jit(solution)/shard_map/all_to_all | solution.py:252
  132.5 2.4 %collective-permute-start.12 = (bf16[1024,512]{1,0:T(8,128)(2,1)S(1)}, bf16[1024,512]{1,0:T(8,128)(2,1)S(1)}, u32[]{:S(2)}, u32[]{:S(2)}) collective-permute-start(bf16[1024,512]{1,0:T(8,128)(2,1)S(1)} %bitcast.71), channel_id=1, source_target_pairs={{0,1},{1,0},{2,3},{3,2},{4,5},{5,4},{6,7},{7,6},{8,9},{9,8},{10,11... | collective-permute-start | bytes 3145736 | tf_op jit(solution)/shard_map/ppermute | solution.py:248
  139.4 3.6 %all-to-all-start.3 = ((bf16[8,320,256]{2,1,0:T(8,128)(2,1)}), bf16[8,320,256]{2,1,0:T(8,128)(2,1)S(1)}, u32[]{:S(2)}, u32[]{:S(2)}) async-start(bf16[8,320,256]{2,1,0:T(8,128)(2,1)} %copy-done), calls=%async_computation.3 | async-start | bytes 2621440 | tf_op jit(solution)/shard_map/all_to_all | solution.py:252
  143.0 1.9 collective-permute-start.16
  144.9 4.3 %collective-permute-start.15 = (bf16[256,512]{1,0:T(8,128)(2,1)S(1)}, bf16[256,512]{1,0:T(8,128)(2,1)S(1)}, u32[]{:S(2)}, u32[]{:S(2)}) collective-permute-start(bf16[256,512]{1,0:T(8,128)(2,1)S(1)} %bitcast.83), channel_id=1, source_target_pairs={{0,16},{8,24},{16,0},{24,8},{1,17},{9,25},{17,1},{25,9},{2,18},{10... | collective-permute-start | bytes 786440 | tf_op jit(solution)/shard_map/ppermute | solution.py:266
  149.2 2.8 %collective-permute-start.14 = (bf16[256,512]{1,0:T(8,128)(2,1)S(1)}, bf16[256,512]{1,0:T(8,128)(2,1)S(1)}, u32[]{:S(2)}, u32[]{:S(2)}) collective-permute-start(bf16[256,512]{1,0:T(8,128)(2,1)S(1)} %bitcast.84), channel_id=1, source_target_pairs={{0,8},{8,16},{16,24},{24,0},{1,9},{9,17},{17,25},{25,1},{2,10},{10... | collective-permute-start | bytes 786440 | tf_op jit(solution)/shard_map/ppermute | solution.py:266
  152.4 3.1 %collective-permute-done.15 = bf16[256,512]{1,0:T(8,128)(2,1)S(1)} collective-permute-done((bf16[256,512]{1,0:T(8,128)(2,1)S(1)}, bf16[256,512]{1,0:T(8,128)(2,1)S(1)}, u32[]{:S(2)}, u32[]{:S(2)}) %collective-permute-start.15) | collective-permute-done | bytes 262176 | tf_op jit(solution)/shard_map/ppermute | solution.py:266
  155.5 6.4 %collective-permute-done.14 = bf16[256,512]{1,0:T(8,128)(2,1)S(1)} collective-permute-done((bf16[256,512]{1,0:T(8,128)(2,1)S(1)}, bf16[256,512]{1,0:T(8,128)(2,1)S(1)}, u32[]{:S(2)}, u32[]{:S(2)}) %collective-permute-start.14) | collective-permute-done | bytes 262176 | tf_op jit(solution)/shard_map/ppermute | solution.py:266
  162.3 2.6 %collective-permute-start.17 = (bf16[4,256,512]{2,1,0:T(8,128)(2,1)S(1)}, bf16[4,256,512]{2,1,0:T(8,128)(2,1)S(1)}, u32[]{:S(2)}, u32[]{:S(2)}) collective-permute-start(bf16[4,256,512]{2,1,0:T(8,128)(2,1)S(1)} %pad_maximum_fusion.1.near_ref), channel_id=1, source_target_pairs={{0,1},{1,0},{2,3},{3,2},{4,5},{5,4},{6,7},{7,6},{8,9},{9,8},{10,11... | collective-permute-start | bytes 3145736 | tf_op jit(solution)/shard_map/ppermute | solution.py:248
  164.9 4.2 %collective-permute-start.13 = (bf16[320,128]{1,0:T(8,128)(2,1)S(1)}, bf16[320,128]{1,0:T(8,128)(2,1)S(1)}, u32[]{:S(2)}, u32[]{:S(2)}) collective-permute-start(bf16[320,128]{1,0:T(8,128)(2,1)S(1)} %copy-done.2), channel_id=1, source_target_pairs={{0,262},{2,260},{4,258},{6,256},{256,6},{258,4},{260,2},{262,0},{1... | collective-permute-start | bytes 245768 | tf_op jit(solution)/shard_map/ppermute | solution.py:312
  169.1 3.9 %collective-permute-done.13.q_ref = bf16[320,128]{1,0:T(8,128)(2,1)S(1)} collective-permute-done((bf16[320,128]{1,0:T(8,128)(2,1)S(1)}, bf16[320,128]{1,0:T(8,128)(2,1)S(1)}, u32[]{:S(2)}, u32[]{:S(2)}) %collective-permute-start.13) | collective-permute-done | bytes 81952 | tf_op jit(solution)/shard_map/ppermute | solution.py:312
  173.0 4.7 %all-to-all-done.3 = bf16[8,320,256]{2,1,0:T(8,128)(2,1)S(1)} async-done(((bf16[8,320,256]{2,1,0:T(8,128)(2,1)}), bf16[8,320,256]{2,1,0:T(8,128)(2,1)S(1)}, u32[]{:S(2)}, u32[]{:S(2)}) %all-to-all-start.3) | async-done | bytes 1310752 | tf_op jit(solution)/shard_map/all_to_all | solution.py:252
  177.7 2.5 %collective-permute-start.18 = (bf16[2560,256]{1,0:T(8,128)(2,1)S(1)}, bf16[2560,256]{1,0:T(8,128)(2,1)S(1)}, u32[]{:S(2)}, u32[]{:S(2)}) collective-permute-start(bf16[2560,256]{1,0:T(8,128)(2,1)S(1)} %bitcast.74), channel_id=1, source_target_pairs={{0,1},{1,0},{2,3},{3,2},{4,5},{5,4},{6,7},{7,6},{8,9},{9,8},{10,11... | collective-permute-start | bytes 3932168 | tf_op jit(solution)/shard_map/ppermute | solution.py:248
  180.2 2.3 %shard_map.68 = (f32[320,128]{1,0:T(8,128)S(1)}, f32[320,128]{1,0:T(8,128)S(1)}) custom-call(s32[4]{0:T(128)S(1)} %get-tuple-element.53.start_ref, bf16[320,128]{1,0:T(8,128)(2,1)S(1)} %collective-permute-done.13.q_ref, bf16[2560,256]{1,0:T(8,128)(2,1)S(1)} %bitcast.75, s32[1,2560]{1,0:T(1,128)S(1)} %add.283.near_pos.kpos_ref), custom_call_target="tpu_custom_call" | custom-call | flops 419430400 | bytes 1310720 | tf_op jit(solution)/shard_map/pallas_call | solution.py:175
  182.9 2.5 %shard_map.69 = bf16[4,96,128]{2,1,0:T(8,128)(2,1)S(1)} custom-call(s32[4]{0:T(128)S(1)} %get-tuple-element.53.start_ref, bf16[320,128]{1,0:T(8,128)(2,1)S(1)} %collective-permute-done.13.q_ref, bf16[2560,256]{1,0:T(8,128)(2,1)S(1)} %collective-permute-done.18.far_ref.kv_ref, s32[1,2560]{1,0:T(1,128)S(1)} %broadcast_add_fusion.far_pos.kpos_ref, ...), custom_call_target="tpu_custom_call" | custom-call | flops 419430400 | bytes 1310720 | tf_op jit(solution)/shard_map/pallas_call | solution.py:175
  185.3 3.1 %collective-permute-start.19 = (bf16[4,96,128]{2,1,0:T(8,128)(2,1)S(1)}, bf16[4,96,128]{2,1,0:T(8,128)(2,1)S(1)}, u32[]{:S(2)}, u32[]{:S(2)}) collective-permute-start(bf16[4,96,128]{2,1,0:T(8,128)(2,1)S(1)} %shard_map.69), channel_id=1, source_target_pairs={{0,262},{2,260},{4,258},{6,256},{256,6},{258,4},{260,2},{262,0},{1... | collective-permute-start | bytes 294920 | tf_op jit(solution)/shard_map/ppermute | solution.py:312
  188.4 4.0 %shard_map.67.near_ref = bf16[4,96,128]{2,1,0:T(8,128)(2,1)S(1)} custom-call(s32[4]{0:T(128)S(1)} %get-tuple-element.32.start_ref, bf16[320,128]{1,0:T(8,128)(2,1)S(1)} %copy-done.3, bf16[2560,256]{1,0:T(8,128)(2,1)S(1)} %bitcast.76, bf16[2560,256]{1,0:T(8,128)(2,1)S(1)} %collective-permute-done.18.far_ref.kv_ref, s32[1,2560]{1,0:T(1,128)S(1)} %add.283.near_pos.kpos_ref, ...), custom_call_target="tpu_custom_call" | custom-call | flops 838860800 | bytes 2621440 | tf_op jit(solution)/shard_map/pallas_call | solution.py:175
  193.3 10.7 %all_to_all.30.context_ref = bf16[4,80,128]{2,1,0:T(8,128)(2,1)S(1)} all-to-all(bf16[4,80,128]{2,1,0:T(8,128)(2,1)S(1)} %shard_map.70), channel_id=1, replica_groups=mesh['zh'=2,'yh'=2,'yl'=4,'x'=4,'zl'=4,'c'=2] {'x'}, dimensions={0} | all-to-all | bytes 163840 | tf_op jit(solution)/shard_map/all_to_all | solution.py:252
  204.5 14.8 %all_to_all.31 = bf16[8,80,256]{2,1,0:T(8,128)(2,1)S(1)} all-to-all(bf16[8,80,256]{2,1,0:T(8,128)(2,1)S(1)} %shard_map.71), channel_id=1, replica_groups=mesh['zh'=2,'yh'=2,'yl'=4,'x'=4,'zl'=4,'c'=2] {'zl','c'}, dimensions={0} | all-to-all | bytes 655360 | tf_op jit(solution)/shard_map/all_to_all | solution.py:252
  (59 shorter events, 19.3 us)
Async XLA Ops:
  3.3 46.0 %all-to-all-start = ((bf16[4,8,128,384]{3,2,1,0:T(8,128)(2,1)}), bf16[4,8,128,384]{3,2,1,0:T(8,128)(2,1)S(1)}, u32[]{:S(2)}, u32[]{:S(2)}) async-start(bf16[4,8,128,384]{3,2,1,0:T(8,128)(2,1)} %shard_map.64), calls=%async_computation | async-start | bytes 6291456 | tf_op jit(solution)/shard_map/all_to_all | solution.py:252
  8.1 14.7 %copy-start.5 = (s32[64]{0:T(128)S(1)}, s32[64]{0:T(128)}, u32[]{:S(2)}) copy-start(s32[64]{0:T(128)} %param.11) | copy-start | bytes 772
  8.1 16.3 %copy-start.4 = (f32[2048]{0:T(1024)S(1)}, f32[2048]{0:T(1024)}, u32[]{:S(2)}) copy-start(f32[2048]{0:T(1024)} %param.7) | copy-start | bytes 24580
  13.2 13.1 %collective-permute-start = (bf16[2,32,2048]{2,1,0:T(8,128)(2,1)}, bf16[2,32,2048]{2,1,0:T(8,128)(2,1)}, u32[]{:S(2)}, u32[]{:S(2)}) collective-permute-start(bf16[2,32,2048]{2,1,0:T(8,128)(2,1)} %get-tuple-element.64), channel_id=1, source_target_pairs={{0,96},{32,0},{64,32},{96,64},{1,97},{33,1},{65,33},{97,65},{2,98}... | collective-permute-start | bytes 786440 | tf_op jit(solution)/shard_map/ppermute | solution.py:266
  18.5 10.7 %collective-permute-start.1 = (bf16[2,32,2048]{2,1,0:T(8,128)(2,1)}, bf16[2,32,2048]{2,1,0:T(8,128)(2,1)}, u32[]{:S(2)}, u32[]{:S(2)}) collective-permute-start(bf16[2,32,2048]{2,1,0:T(8,128)(2,1)} %get-tuple-element.65), channel_id=1, source_target_pairs={{0,32},{32,64},{64,96},{96,0},{1,33},{33,65},{65,97},{97,1},{2,34}... | collective-permute-start | bytes 786440 | tf_op jit(solution)/shard_map/ppermute | solution.py:266
  20.4 22.1 %collective-permute-start.2 = (bf16[2,32,2048]{2,1,0:T(8,128)(2,1)}, bf16[2,32,2048]{2,1,0:T(8,128)(2,1)}, u32[]{:S(2)}, u32[]{:S(2)}) collective-permute-start(bf16[2,32,2048]{2,1,0:T(8,128)(2,1)} %get-tuple-element.63), channel_id=1, source_target_pairs={{0,64},{32,96},{64,0},{96,32},{1,65},{33,97},{65,1},{97,33},{2,66}... | collective-permute-start | bytes 786440 | tf_op jit(solution)/shard_map/ppermute | solution.py:266
  50.3 28.3 %all-to-all-start.1 = ((bf16[8,128,384]{2,1,0:T(8,128)(2,1)}), bf16[8,128,384]{2,1,0:T(8,128)(2,1)S(1)}, u32[]{:S(2)}, u32[]{:S(2)}) async-start(bf16[8,128,384]{2,1,0:T(8,128)(2,1)} %dynamic-slice_bitcast_fusion), calls=%async_computation.1 | async-start | bytes 1572864 | tf_op jit(solution)/shard_map/all_to_all | solution.py:252
  55.0 9.6 %collective-permute-start.3 = (bf16[2,32,512]{2,1,0:T(8,128)(2,1)}, bf16[2,32,512]{2,1,0:T(8,128)(2,1)S(1)}, u32[]{:S(2)}, u32[]{:S(2)}) collective-permute-start(bf16[2,32,512]{2,1,0:T(8,128)(2,1)} %get-tuple-element.34), channel_id=1, source_target_pairs={{0,24},{8,0},{16,8},{24,16},{1,25},{9,1},{17,9},{25,17},{2,26},{10... | collective-permute-start | bytes 196616 | tf_op jit(solution)/shard_map/ppermute | solution.py:266
  59.6 7.0 %collective-permute-start.4 = (bf16[2,32,512]{2,1,0:T(8,128)(2,1)}, bf16[2,32,512]{2,1,0:T(8,128)(2,1)S(1)}, u32[]{:S(2)}, u32[]{:S(2)}) collective-permute-start(bf16[2,32,512]{2,1,0:T(8,128)(2,1)} %get-tuple-element.35), channel_id=1, source_target_pairs={{0,16},{8,24},{16,0},{24,8},{1,17},{9,25},{17,1},{25,9},{2,18},{10... | collective-permute-start | bytes 196616 | tf_op jit(solution)/shard_map/ppermute | solution.py:266
  62.1 7.1 %collective-permute-start.5 = (bf16[2,32,512]{2,1,0:T(8,128)(2,1)}, bf16[2,32,512]{2,1,0:T(8,128)(2,1)S(1)}, u32[]{:S(2)}, u32[]{:S(2)}) collective-permute-start(bf16[2,32,512]{2,1,0:T(8,128)(2,1)} %get-tuple-element.36), channel_id=1, source_target_pairs={{0,8},{8,16},{16,24},{24,0},{1,9},{9,17},{17,25},{25,1},{2,10},{10... | collective-permute-start | bytes 196616 | tf_op jit(solution)/shard_map/ppermute | solution.py:266
  70.1 7.0 %collective-permute-start.6 = (bf16[32,512]{1,0:T(8,128)(2,1)S(1)}, bf16[32,512]{1,0:T(8,128)(2,1)S(1)}, u32[]{:S(2)}, u32[]{:S(2)}) collective-permute-start(bf16[32,512]{1,0:T(8,128)(2,1)S(1)} %slice_bitcast_fusion), channel_id=1, source_target_pairs={{0,224},{32,192},{64,160},{96,128},{128,96},{160,64},{192,32},{224... | collective-permute-start | bytes 98312 | tf_op jit(solution)/shard_map/ppermute | solution.py:351
  78.6 18.5 %collective-permute-start.8 = (bf16[128,512]{1,0:T(8,128)(2,1)S(1)}, bf16[128,512]{1,0:T(8,128)(2,1)S(1)}, u32[]{:S(2)}, u32[]{:S(2)}) collective-permute-start(bf16[128,512]{1,0:T(8,128)(2,1)S(1)} %pad_maximum_fusion.2), channel_id=1, source_target_pairs={{0,262},{1,270},{2,260},{3,268},{4,258},{5,266},{6,256},{7,264},{8... | collective-permute-start | bytes 393224 | tf_op jit(solution)/shard_map/ppermute | solution.py:308
  90.8 7.0 %collective-permute-start.7 = (bf16[128,512]{1,0:T(8,128)(2,1)S(1)}, bf16[128,512]{1,0:T(8,128)(2,1)S(1)}, u32[]{:S(2)}, u32[]{:S(2)}) collective-permute-start(bf16[128,512]{1,0:T(8,128)(2,1)S(1)} %pad_maximum_fusion.2), channel_id=1, source_target_pairs={{1,8},{3,10},{5,12},{7,14},{8,1},{10,3},{12,5},{14,7},{17,24},{19,... | collective-permute-start | bytes 393224 | tf_op jit(solution)/shard_map/ppermute | solution.py:308
  98.9 33.6 %all-to-all-start.2 = ((bf16[8,128,512]{2,1,0:T(8,128)(2,1)}), bf16[8,128,512]{2,1,0:T(8,128)(2,1)S(1)}, u32[]{:S(2)}, u32[]{:S(2)}) async-start(bf16[8,128,512]{2,1,0:T(8,128)(2,1)} %broadcast_in_dim.2), calls=%async_computation.2 | async-start | bytes 2097152 | tf_op jit(solution)/shard_map/all_to_all | solution.py:252
  103.3 12.0 %collective-permute-start.9 = (bf16[80,2048]{1,0:T(8,128)(2,1)S(1)}, bf16[80,2048]{1,0:T(8,128)(2,1)S(1)}, u32[]{:S(2)}, u32[]{:S(2)}) collective-permute-start(bf16[80,2048]{1,0:T(8,128)(2,1)S(1)} %fusion.2.refs_0_), channel_id=1, source_target_pairs={{0,8},{8,16},{16,24},{24,0},{1,9},{9,17},{17,25},{25,1},{2,10},{10... | collective-permute-start | bytes 983048 | tf_op jit(solution)/shard_map/ppermute | solution.py:266
  105.2 16.9 %collective-permute-start.10 = (bf16[80,2048]{1,0:T(8,128)(2,1)S(1)}, bf16[80,2048]{1,0:T(8,128)(2,1)S(1)}, u32[]{:S(2)}, u32[]{:S(2)}) collective-permute-start(bf16[80,2048]{1,0:T(8,128)(2,1)S(1)} %fusion.2.refs_0_), channel_id=1, source_target_pairs={{0,16},{8,24},{16,0},{24,8},{1,17},{9,25},{17,1},{25,9},{2,18},{10... | collective-permute-start | bytes 983048 | tf_op jit(solution)/shard_map/ppermute | solution.py:266
  109.5 15.0 %collective-permute-start.11 = (bf16[80,2048]{1,0:T(8,128)(2,1)S(1)}, bf16[80,2048]{1,0:T(8,128)(2,1)S(1)}, u32[]{:S(2)}, u32[]{:S(2)}) collective-permute-start(bf16[80,2048]{1,0:T(8,128)(2,1)S(1)} %fusion.2.refs_0_), channel_id=1, source_target_pairs={{0,24},{8,0},{16,8},{24,16},{1,25},{9,1},{17,9},{25,17},{2,26},{10... | collective-permute-start | bytes 983048 | tf_op jit(solution)/shard_map/ppermute | solution.py:266
  132.5 4.7 %collective-permute-start.12 = (bf16[1024,512]{1,0:T(8,128)(2,1)S(1)}, bf16[1024,512]{1,0:T(8,128)(2,1)S(1)}, u32[]{:S(2)}, u32[]{:S(2)}) collective-permute-start(bf16[1024,512]{1,0:T(8,128)(2,1)S(1)} %bitcast.71), channel_id=1, source_target_pairs={{0,1},{1,0},{2,3},{3,2},{4,5},{5,4},{6,7},{7,6},{8,9},{9,8},{10,11... | collective-permute-start | bytes 3145736 | tf_op jit(solution)/shard_map/ppermute | solution.py:248
  137.7 1.1 copy-start
  138.8 0.6 copy-start.1
  139.4 38.3 %all-to-all-start.3 = ((bf16[8,320,256]{2,1,0:T(8,128)(2,1)}), bf16[8,320,256]{2,1,0:T(8,128)(2,1)S(1)}, u32[]{:S(2)}, u32[]{:S(2)}) async-start(bf16[8,320,256]{2,1,0:T(8,128)(2,1)} %copy-done), calls=%async_computation.3 | async-start | bytes 2621440 | tf_op jit(solution)/shard_map/all_to_all | solution.py:252
  143.0 9.4 %collective-permute-start.16 = (bf16[256,512]{1,0:T(8,128)(2,1)S(1)}, bf16[256,512]{1,0:T(8,128)(2,1)S(1)}, u32[]{:S(2)}, u32[]{:S(2)}) collective-permute-start(bf16[256,512]{1,0:T(8,128)(2,1)S(1)} %bitcast.82), channel_id=1, source_target_pairs={{0,24},{8,0},{16,8},{24,16},{1,25},{9,1},{17,9},{25,17},{2,26},{10... | collective-permute-start | bytes 786440 | tf_op jit(solution)/shard_map/ppermute | solution.py:266
  144.9 10.6 %collective-permute-start.15 = (bf16[256,512]{1,0:T(8,128)(2,1)S(1)}, bf16[256,512]{1,0:T(8,128)(2,1)S(1)}, u32[]{:S(2)}, u32[]{:S(2)}) collective-permute-start(bf16[256,512]{1,0:T(8,128)(2,1)S(1)} %bitcast.83), channel_id=1, source_target_pairs={{0,16},{8,24},{16,0},{24,8},{1,17},{9,25},{17,1},{25,9},{2,18},{10... | collective-permute-start | bytes 786440 | tf_op jit(solution)/shard_map/ppermute | solution.py:266
  149.2 12.7 %collective-permute-start.14 = (bf16[256,512]{1,0:T(8,128)(2,1)S(1)}, bf16[256,512]{1,0:T(8,128)(2,1)S(1)}, u32[]{:S(2)}, u32[]{:S(2)}) collective-permute-start(bf16[256,512]{1,0:T(8,128)(2,1)S(1)} %bitcast.84), channel_id=1, source_target_pairs={{0,8},{8,16},{16,24},{24,0},{1,9},{9,17},{17,25},{25,1},{2,10},{10... | collective-permute-start | bytes 786440 | tf_op jit(solution)/shard_map/ppermute | solution.py:266
  161.9 3.0 %copy-start.2 = (bf16[320,128]{1,0:T(8,128)(2,1)S(1)}, bf16[320,128]{1,0:T(8,128)(2,1)}, u32[]{:S(2)}) copy-start(bf16[320,128]{1,0:T(8,128)(2,1)} %copy-done.1) | copy-start | bytes 245764
  162.3 10.7 %collective-permute-start.17 = (bf16[4,256,512]{2,1,0:T(8,128)(2,1)S(1)}, bf16[4,256,512]{2,1,0:T(8,128)(2,1)S(1)}, u32[]{:S(2)}, u32[]{:S(2)}) collective-permute-start(bf16[4,256,512]{2,1,0:T(8,128)(2,1)S(1)} %pad_maximum_fusion.1.near_ref), channel_id=1, source_target_pairs={{0,1},{1,0},{2,3},{3,2},{4,5},{5,4},{6,7},{7,6},{8,9},{9,8},{10,11... | collective-permute-start | bytes 3145736 | tf_op jit(solution)/shard_map/ppermute | solution.py:248
  164.9 8.1 %collective-permute-start.13 = (bf16[320,128]{1,0:T(8,128)(2,1)S(1)}, bf16[320,128]{1,0:T(8,128)(2,1)S(1)}, u32[]{:S(2)}, u32[]{:S(2)}) collective-permute-start(bf16[320,128]{1,0:T(8,128)(2,1)S(1)} %copy-done.2), channel_id=1, source_target_pairs={{0,262},{2,260},{4,258},{6,256},{256,6},{258,4},{260,2},{262,0},{1... | collective-permute-start | bytes 245768 | tf_op jit(solution)/shard_map/ppermute | solution.py:312
  177.7 10.7 %copy-start.3 = (bf16[320,128]{1,0:T(8,128)(2,1)S(1)}, bf16[320,128]{1,0:T(8,128)(2,1)}, u32[]{:S(2)}) copy-start(bf16[320,128]{1,0:T(8,128)(2,1)} %copy-done.1) | copy-start | bytes 245764
  177.7 5.2 %collective-permute-start.18 = (bf16[2560,256]{1,0:T(8,128)(2,1)S(1)}, bf16[2560,256]{1,0:T(8,128)(2,1)S(1)}, u32[]{:S(2)}, u32[]{:S(2)}) collective-permute-start(bf16[2560,256]{1,0:T(8,128)(2,1)S(1)} %bitcast.74), channel_id=1, source_target_pairs={{0,1},{1,0},{2,3},{3,2},{4,5},{5,4},{6,7},{7,6},{8,9},{9,8},{10,11... | collective-permute-start | bytes 3932168 | tf_op jit(solution)/shard_map/ppermute | solution.py:248
  185.3 7.1 %collective-permute-start.19 = (bf16[4,96,128]{2,1,0:T(8,128)(2,1)S(1)}, bf16[4,96,128]{2,1,0:T(8,128)(2,1)S(1)}, u32[]{:S(2)}, u32[]{:S(2)}) collective-permute-start(bf16[4,96,128]{2,1,0:T(8,128)(2,1)S(1)} %shard_map.69), channel_id=1, source_target_pairs={{0,262},{2,260},{4,258},{6,256},{256,6},{258,4},{260,2},{262,0},{1... | collective-permute-start | bytes 294920 | tf_op jit(solution)/shard_map/ppermute | solution.py:312
